TPU v7x, 32 devices: a whole 2x2x4 slice. The times are simulated.
32 devices in a mesh: clu: 8 (over y, x, core), col: 4 (over z).
Axes of the slice: x: 2, y: 2, z: 4, core: 2. Of those that a mesh axis runs over, the one named last changes fastest.
Arguments:
- positions: float32 [1024, 2, 128], P(('clu', 'col')), may hold values from -4 to 4
- tension: float32 [1024, 128], P(('clu', 'col')), may hold values from -6 to 6
- bending: float32 [1024], P(('clu', 'col')), may hold values from 0.3 to 3
- moved_order: int32 [32, 32], P(('clu', 'col')), may hold values from 0 to 31, each once within a row
- move_destination: int32 [768, 1], P(('clu', 'col')), may hold values from 0 to 7; in each aligned block of 24 rows (0 to 23, 24 to 47, ...) at most 6 rows name the same one
- move_target: int32 [768], P(('clu', 'col')), may hold values from 0 to 31
- far_range: int32 [1024, 1], P(('clu', 'col')), may hold values from 0 to 3; in each aligned block of 32 rows (0 to 31, 32 to 63, ...) at most 16 rows name the same one
- old_basis: bfloat16 [128, 2048], P(None, 'col'), may hold values from -6 to 6
- source_nodes: bfloat16 [2, 2048], P(None, 'col'), may hold values from -4 to 4
Outputs:
- force: float32 [1024, 2, 128], P(('clu', 'col'))
- near_velocity: float32 [1024, 2, 128], P(('clu', 'col'))
- new_basis: float32 [1024, 64, 2, 128], P(('clu', 'col'))
Inputs may be any that keep to these rules, and one draw needn't show every extreme that they name: `moved_order`: each row of a device lists its 32 vesicles once each; the first 24 are the moved ones. `move_destination`: among the 24 rows of one device no cluster is named more than 6 times. `far_range`: among the 32 rows of one device no column range is named more than 16 times.
All inputs are finite; a program needn't handle non-finite values.
Results may differ from a plain program's by a relative error of at most 0.0045.
Values may be sent and summed in bfloat16 or wider, within the bound.
No kernel may reach another device: no remote copies, remote signals or barrier semaphores. Data moves between devices by JAX's collectives and lax.ppermute only.
A program may use at most 64 MiB of HBM per device.

v0:
```python
import math

import jax
import jax.numpy as jnp
from jax import lax
from jax.sharding import PartitionSpec as P

EPS_SQUARED = 0.01


def spectral_tables(node_count):
    half_count = node_count // 2
    node_index = lax.broadcasted_iota(jnp.int32, (node_count, half_count + 1), 0)
    wave_index = lax.broadcasted_iota(jnp.int32, (node_count, half_count + 1), 1)
    phase_angle = (node_index * wave_index % node_count).astype(jnp.float32) * (
        2.0 * math.pi / node_count
    )
    cosine_table = jnp.cos(phase_angle)
    sine_table = jnp.sin(phase_angle)
    wavenumber = lax.broadcasted_iota(jnp.int32, (half_count + 1,), 0).astype(jnp.float32)
    inside = jnp.logical_and(wavenumber > 0, wavenumber < half_count)
    first_weight = jnp.where(inside, 2.0 * wavenumber / half_count, 0.0)
    fourth_weight = jnp.where(
        inside, 2.0 * (wavenumber / half_count) ** 4, jnp.where(wavenumber == half_count, 1.0, 0.0)
    )
    highest = lax.Precision.HIGHEST
    derivative = (
        jnp.dot(cosine_table * first_weight, sine_table.T, precision=highest)
        - jnp.dot(sine_table * first_weight, cosine_table.T, precision=highest)
    ) / node_count
    bending_table = (
        jnp.dot(cosine_table * fourth_weight, cosine_table.T, precision=highest)
        + jnp.dot(sine_table * fourth_weight, sine_table.T, precision=highest)
    ) / node_count
    return (derivative, bending_table)


def membrane_force(positions, tension, bending, derivative, bending_table):
    vesicles, node_count = (positions.shape[0], positions.shape[2])
    highest = lax.Precision.HIGHEST
    flat_rows = positions.reshape(vesicles * 2, node_count)
    slope = jnp.dot(flat_rows, derivative.T, precision=highest).reshape(vesicles, 2, node_count)
    fourth = jnp.dot(flat_rows, bending_table.T, precision=highest).reshape(vesicles, 2, node_count)
    pulled = (tension[:, None, :] * slope).reshape(vesicles * 2, node_count)
    tension_part = jnp.dot(pulled, derivative.T, precision=highest).reshape(vesicles, 2, node_count)
    return tension_part - bending[:, None, None] * fourth


def near_velocity_block(target_nodes, source_nodes, source_force):
    delta_x = target_nodes[0][:, None] - source_nodes[0][None, :]
    delta_y = target_nodes[1][:, None] - source_nodes[1][None, :]
    spread = delta_x * delta_x + delta_y * delta_y + EPS_SQUARED
    log_part = -0.5 * jnp.log(spread)
    push_x = source_force[0][None, :]
    push_y = source_force[1][None, :]
    along = (delta_x * push_x + delta_y * push_y) / spread
    speed_x = jnp.sum(log_part * push_x + delta_x * along, axis=1)
    speed_y = jnp.sum(log_part * push_y + delta_y * along, axis=1)
    return jnp.stack([speed_x, speed_y]) / target_nodes.shape[1]


def far_kernel(targets, sources):
    delta_x = targets[..., 0, None, :] - sources[..., 0, :, None]
    delta_y = targets[..., 1, None, :] - sources[..., 1, :, None]
    spread = delta_x * delta_x + delta_y * delta_y + EPS_SQUARED
    log_part = -0.5 * jnp.log(spread)
    first_first = log_part + delta_x * delta_x / spread
    first_second = delta_x * delta_y / spread
    second_second = log_part + delta_y * delta_y / spread
    upper_rows = jnp.stack([first_first, first_second], axis=-3)
    lower_rows = jnp.stack([first_second, second_second], axis=-3)
    return jnp.stack([upper_rows, lower_rows], axis=-4).astype(jnp.bfloat16)


def group_size():
    return 4


def earlier_count(hot_table):
    return jnp.sum((jnp.cumsum(hot_table, axis=0) - hot_table) * hot_table, axis=1)


def per_device(
    positions,
    tension,
    bending,
    moved_order,
    move_destination,
    move_target,
    far_range,
    old_basis,
    source_nodes,
):
    highest = lax.Precision.HIGHEST
    vesicles, node_count = (positions.shape[0], positions.shape[2])
    rank_count = old_basis.shape[0] // 2
    source_count = old_basis.shape[1]
    derivative, bending_table = spectral_tables(node_count)
    force = membrane_force(positions, tension, bending, derivative, bending_table)
    clu_count = lax.axis_size("clu")
    move_count = move_target.shape[0]
    slot_cap = 2 * ((move_count + clu_count - 1) // clu_count)
    order_row = moved_order[0, :move_count]
    pick_table = (
        order_row[:, None] == lax.broadcasted_iota(jnp.int32, (move_count, vesicles), 1)
    ).astype(jnp.float32)
    carried = jnp.concatenate([positions, force], axis=1).reshape(vesicles, 4 * node_count)
    moving = jnp.dot(pick_table, carried, precision=highest)
    destination = move_destination[:, 0]
    dest_hot = (
        destination[:, None] == lax.broadcasted_iota(jnp.int32, (move_count, clu_count), 1)
    ).astype(jnp.int32)
    slot_index = destination * slot_cap + earlier_count(dest_hot)
    slot_total = clu_count * slot_cap
    pack_table = (
        slot_index[None, :] == lax.broadcasted_iota(jnp.int32, (slot_total, move_count), 0)
    ).astype(jnp.float32)
    packed = jnp.dot(pack_table, moving, precision=highest).reshape(
        clu_count, slot_cap, 4, node_count
    )
    target_tag = jnp.dot(
        pack_table, (move_target + 1).astype(jnp.float32), precision=highest
    ).reshape(clu_count, slot_cap)
    arrived, arrived_tag = (
        lax.all_to_all(packed, "clu", split_axis=0, concat_axis=0, tiled=True),
        lax.all_to_all(target_tag, "clu", split_axis=0, concat_axis=0, tiled=True),
    )
    arrived = arrived.reshape(slot_total, 4, node_count)
    arrived_tag = arrived_tag.reshape(slot_total)
    target_hot = (
        arrived_tag[:, None]
        == (lax.broadcasted_iota(jnp.int32, (slot_total, vesicles), 1) + 1).astype(jnp.float32)
    ).astype(jnp.float32)
    target_nodes = jnp.dot(
        target_hot, positions.reshape(vesicles, 2 * node_count), precision=highest
    ).reshape(slot_total, 2, node_count)
    near_width = group_size()

    def near_group(pieces):
        targets, sources = pieces
        return jax.vmap(near_velocity_block)(targets, sources[:, 0:2], sources[:, 2:4])

    speeds = lax.map(
        near_group,
        (
            target_nodes.reshape(-1, near_width, 2, node_count),
            arrived.reshape(-1, near_width, 4, node_count),
        ),
    )
    speeds = speeds.reshape(slot_total, 2 * node_count)
    near_velocity = jnp.dot(target_hot.T, speeds, precision=highest).reshape(
        vesicles, 2, node_count
    )
    chosen = far_range[:, 0]
    basis_all, sources_all = (
        lax.all_gather(old_basis, "col", axis=1, tiled=True),
        lax.all_gather(source_nodes, "col", axis=1, tiled=True),
    )

    def pull_group(pieces):
        targets, picked = pieces

        def take_range(index):
            start = index * source_count
            return (
                lax.dynamic_slice_in_dim(basis_all, start, source_count, 1),
                lax.dynamic_slice_in_dim(sources_all, start, source_count, 1),
            )

        basis_rows, source_rows = jax.vmap(take_range)(picked)
        kernel = far_kernel(targets, source_rows.astype(jnp.float32))
        stacked = basis_rows.reshape(-1, 2, rank_count, source_count)
        return jnp.einsum("geks,gedsn->gkdn", stacked, kernel, preferred_element_type=jnp.float32)

    sketch = lax.map(pull_group, (positions.reshape(-1, 4, 2, node_count), chosen.reshape(-1, 4)))
    sketch = sketch.reshape(vesicles, rank_count, 2 * node_count)
    local_gram = jnp.einsum("vkm,vjm->kj", sketch, sketch, precision=highest)
    gram = lax.psum(local_gram, ("clu", "col"))
    lower_factor = jnp.linalg.cholesky(gram)
    lower_inverse = jax.scipy.linalg.solve_triangular(
        lower_factor, jnp.eye(rank_count, dtype=jnp.float32), lower=True
    )
    scale_factor = math.sqrt(
        2.0 * node_count * vesicles * lax.axis_size("clu") * lax.axis_size("col")
    )
    new_basis = (
        jnp.einsum("kj,vjm->vkm", lower_inverse, sketch, precision=highest).reshape(
            vesicles, rank_count, 2, node_count
        )
        * scale_factor
    )
    return (force, near_velocity, new_basis)


def solution(mesh):
    placed = (
        P(("clu", "col"), None, None),
        P(("clu", "col"), None),
        P(("clu", "col")),
        P(("clu", "col"), None),
        P(("clu", "col"), None),
        P(("clu", "col")),
        P(("clu", "col"), None),
        P(None, "col"),
        P(None, "col"),
    )
    return jax.shard_map(
        per_device,
        mesh=mesh,
        in_specs=placed,
        out_specs=(
            P(("clu", "col"), None, None),
            P(("clu", "col"), None, None),
            P(("clu", "col"), None, None, None),
        ),
        check_vma=False,
    )
```

profile of v0, /device:TPU:0, one launch (start us, length us, event | category | flops | bytes accessed | tf_op | source)
XLA Modules:
  0.0 225.7 jit_solution(18161108321524255777)
XLA Ops:
  4.5 5.2 %all-to-all-start = ((f32[8,1,6]{2,1,0:T(1,128)}), f32[8,1,6]{2,1,0:T(1,128)S(1)}, u32[]{:S(2)}, u32[]{:S(2)}) async-start(f32[8,1,6]{2,1,0:T(1,128)} %bitcast.35), calls=%async_computation | async-start | bytes 8192 | tf_op jit(solution)/shard_map/all_to_all | solution.py:126
  13.1 16.6 %all_gather.6 = bf16[128,2048]{1,0:T(8,128)(2,1)S(1)} all-gather(bf16[128,512]{1,0:T(8,128)(2,1)S(1)} %copy-done.1), channel_id=1, replica_groups=mesh['clu'=8,'col'=4] {'col'}, dimensions={1}, use_global_device_ids=true | all-gather | bytes 655360 | tf_op jit(solution)/shard_map/all_gather | solution.py:156
  29.6 11.9 %all_gather.7 = bf16[2,2048]{1,0:T(2,128)(2,1)S(1)} all-gather(bf16[2,512]{1,0:T(2,128)(2,1)S(1)} %copy-done.3), channel_id=1, replica_groups=mesh['clu'=8,'col'=4] {'col'}, dimensions={1}, use_global_device_ids=true | all-gather | bytes 10240 | tf_op jit(solution)/shard_map/all_gather | solution.py:157
  42.9 100.4 %while.27 = (s32[]{:T(128)}, f32[8,4,64,2,128]{4,3,2,1,0:T(2,128)}, s32[8,4]{1,0:T(8,128)S(1)}, bf16[128,2048]{1,0:T(8,128)(2,1)S(1)}, f32[8,4,2,128]{3,2,1,0:T(...) while((s32[]{:T(128)}, f32[8,4,64,2,128]{4,3,2,1,0:T(2,128)}, ...), condition=%wide.region_7.8_spmd, body=%wide.region_6.7_spmd.sunk | while | flops 143654928 | bytes 9028579 | solution.py:175
  42.9 4.9 %while.29 = (s32[]{:T(128)}, bf16[2,2048]{1,0:T(2,128)(2,1)S(1)}, s32[4,2]{0,1:T(2,128)S(1)}, bf16[4,2,512]{2,1,0:T(2,128)(2,1)S(1)}, s32[]{:T(128)}) while((s32[]{:T(128)}, bf16[2,2048]{1,0:T(2,128)(2,1)S(1)}, s32[4,2]{0,1:T(2,128)S(1)}, bf16[4,2,512]{2,1,0:T(2,128)(2,1)S(1)}, s32[]{:T(128)}) %tuple.112), condition=%wide.while_cond.1, body=%wide.while_body.1.sunk | while | flops 2 | bytes 4193 | solution.py:167
  48.9 5.1 %while.28 = (s32[]{:T(128)}, bf16[128,2048]{1,0:T(8,128)(2,1)S(1)}, s32[4,2]{0,1:T(2,128)S(1)}, bf16[4,128,512]{2,1,0:T(8,128)(2,1)S(1)}, s32[]{:T(128)}) while((s32[]{:T(128)}, bf16[128,2048]{1,0:T(8,128)(2,1)S(1)}, s32[4,2]{0,1:T(2,128)S(1)}, bf16[4,128,512]{2,1,0:T(8,128)(2,1)S(1)}, s32[]{:T(128)}) %tuple.121), condition=%wide.while_cond, body=%wide.while_body.sunk | while | flops 2 | bytes 262241 | solution.py:166
  55.5 4.9 %while.29 = (s32[]{:T(128)}, bf16[2,2048]{1,0:T(2,128)(2,1)S(1)}, s32[4,2]{0,1:T(2,128)S(1)}, bf16[4,2,512]{2,1,0:T(2,128)(2,1)S(1)}, s32[]{:T(128)}) while((s32[]{:T(128)}, bf16[2,2048]{1,0:T(2,128)(2,1)S(1)}, s32[4,2]{0,1:T(2,128)S(1)}, bf16[4,2,512]{2,1,0:T(2,128)(2,1)S(1)}, s32[]{:T(128)}) %tuple.112), condition=%wide.while_cond.1, body=%wide.while_body.1.sunk | while | flops 2 | bytes 4193 | solution.py:167
  61.5 5.1 %while.28 = (s32[]{:T(128)}, bf16[128,2048]{1,0:T(8,128)(2,1)S(1)}, s32[4,2]{0,1:T(2,128)S(1)}, bf16[4,128,512]{2,1,0:T(8,128)(2,1)S(1)}, s32[]{:T(128)}) while((s32[]{:T(128)}, bf16[128,2048]{1,0:T(8,128)(2,1)S(1)}, s32[4,2]{0,1:T(2,128)S(1)}, bf16[4,128,512]{2,1,0:T(8,128)(2,1)S(1)}, s32[]{:T(128)}) %tuple.121), condition=%wide.while_cond, body=%wide.while_body.sunk | while | flops 2 | bytes 262241 | solution.py:166
  68.0 4.9 %while.29 = (s32[]{:T(128)}, bf16[2,2048]{1,0:T(2,128)(2,1)S(1)}, s32[4,2]{0,1:T(2,128)S(1)}, bf16[4,2,512]{2,1,0:T(2,128)(2,1)S(1)}, s32[]{:T(128)}) while((s32[]{:T(128)}, bf16[2,2048]{1,0:T(2,128)(2,1)S(1)}, s32[4,2]{0,1:T(2,128)S(1)}, bf16[4,2,512]{2,1,0:T(2,128)(2,1)S(1)}, s32[]{:T(128)}) %tuple.112), condition=%wide.while_cond.1, body=%wide.while_body.1.sunk | while | flops 2 | bytes 4193 | solution.py:167
  74.0 5.1 %while.28 = (s32[]{:T(128)}, bf16[128,2048]{1,0:T(8,128)(2,1)S(1)}, s32[4,2]{0,1:T(2,128)S(1)}, bf16[4,128,512]{2,1,0:T(8,128)(2,1)S(1)}, s32[]{:T(128)}) while((s32[]{:T(128)}, bf16[128,2048]{1,0:T(8,128)(2,1)S(1)}, s32[4,2]{0,1:T(2,128)S(1)}, bf16[4,128,512]{2,1,0:T(8,128)(2,1)S(1)}, s32[]{:T(128)}) %tuple.121), condition=%wide.while_cond, body=%wide.while_body.sunk | while | flops 2 | bytes 262241 | solution.py:166
  80.6 4.9 %while.29 = (s32[]{:T(128)}, bf16[2,2048]{1,0:T(2,128)(2,1)S(1)}, s32[4,2]{0,1:T(2,128)S(1)}, bf16[4,2,512]{2,1,0:T(2,128)(2,1)S(1)}, s32[]{:T(128)}) while((s32[]{:T(128)}, bf16[2,2048]{1,0:T(2,128)(2,1)S(1)}, s32[4,2]{0,1:T(2,128)S(1)}, bf16[4,2,512]{2,1,0:T(2,128)(2,1)S(1)}, s32[]{:T(128)}) %tuple.112), condition=%wide.while_cond.1, body=%wide.while_body.1.sunk | while | flops 2 | bytes 4193 | solution.py:167
  86.6 5.1 %while.28 = (s32[]{:T(128)}, bf16[128,2048]{1,0:T(8,128)(2,1)S(1)}, s32[4,2]{0,1:T(2,128)S(1)}, bf16[4,128,512]{2,1,0:T(8,128)(2,1)S(1)}, s32[]{:T(128)}) while((s32[]{:T(128)}, bf16[128,2048]{1,0:T(8,128)(2,1)S(1)}, s32[4,2]{0,1:T(2,128)S(1)}, bf16[4,128,512]{2,1,0:T(8,128)(2,1)S(1)}, s32[]{:T(128)}) %tuple.121), condition=%wide.while_cond, body=%wide.while_body.sunk | while | flops 2 | bytes 262241 | solution.py:166
  92.2 0.9 copy_dynamic-update-slice_fusion.5
  93.1 4.9 %while.29 = (s32[]{:T(128)}, bf16[2,2048]{1,0:T(2,128)(2,1)S(1)}, s32[4,2]{0,1:T(2,128)S(1)}, bf16[4,2,512]{2,1,0:T(2,128)(2,1)S(1)}, s32[]{:T(128)}) while((s32[]{:T(128)}, bf16[2,2048]{1,0:T(2,128)(2,1)S(1)}, s32[4,2]{0,1:T(2,128)S(1)}, bf16[4,2,512]{2,1,0:T(2,128)(2,1)S(1)}, s32[]{:T(128)}) %tuple.112), condition=%wide.while_cond.1, body=%wide.while_body.1.sunk | while | flops 2 | bytes 4193 | solution.py:167
  99.1 5.1 %while.28 = (s32[]{:T(128)}, bf16[128,2048]{1,0:T(8,128)(2,1)S(1)}, s32[4,2]{0,1:T(2,128)S(1)}, bf16[4,128,512]{2,1,0:T(8,128)(2,1)S(1)}, s32[]{:T(128)}) while((s32[]{:T(128)}, bf16[128,2048]{1,0:T(8,128)(2,1)S(1)}, s32[4,2]{0,1:T(2,128)S(1)}, bf16[4,128,512]{2,1,0:T(8,128)(2,1)S(1)}, s32[]{:T(128)}) %tuple.121), condition=%wide.while_cond, body=%wide.while_body.sunk | while | flops 2 | bytes 262241 | solution.py:166
  105.6 4.9 %while.29 = (s32[]{:T(128)}, bf16[2,2048]{1,0:T(2,128)(2,1)S(1)}, s32[4,2]{0,1:T(2,128)S(1)}, bf16[4,2,512]{2,1,0:T(2,128)(2,1)S(1)}, s32[]{:T(128)}) while((s32[]{:T(128)}, bf16[2,2048]{1,0:T(2,128)(2,1)S(1)}, s32[4,2]{0,1:T(2,128)S(1)}, bf16[4,2,512]{2,1,0:T(2,128)(2,1)S(1)}, s32[]{:T(128)}) %tuple.112), condition=%wide.while_cond.1, body=%wide.while_body.1.sunk | while | flops 2 | bytes 4193 | solution.py:167
  111.7 5.1 %while.28 = (s32[]{:T(128)}, bf16[128,2048]{1,0:T(8,128)(2,1)S(1)}, s32[4,2]{0,1:T(2,128)S(1)}, bf16[4,128,512]{2,1,0:T(8,128)(2,1)S(1)}, s32[]{:T(128)}) while((s32[]{:T(128)}, bf16[128,2048]{1,0:T(8,128)(2,1)S(1)}, s32[4,2]{0,1:T(2,128)S(1)}, bf16[4,128,512]{2,1,0:T(8,128)(2,1)S(1)}, s32[]{:T(128)}) %tuple.121), condition=%wide.while_cond, body=%wide.while_body.sunk | while | flops 2 | bytes 262241 | solution.py:166
  117.3 0.9 copy_dynamic-update-slice_fusion.5
  118.2 4.9 %while.29 = (s32[]{:T(128)}, bf16[2,2048]{1,0:T(2,128)(2,1)S(1)}, s32[4,2]{0,1:T(2,128)S(1)}, bf16[4,2,512]{2,1,0:T(2,128)(2,1)S(1)}, s32[]{:T(128)}) while((s32[]{:T(128)}, bf16[2,2048]{1,0:T(2,128)(2,1)S(1)}, s32[4,2]{0,1:T(2,128)S(1)}, bf16[4,2,512]{2,1,0:T(2,128)(2,1)S(1)}, s32[]{:T(128)}) %tuple.112), condition=%wide.while_cond.1, body=%wide.while_body.1.sunk | while | flops 2 | bytes 4193 | solution.py:167
  124.2 5.1 %while.28 = (s32[]{:T(128)}, bf16[128,2048]{1,0:T(8,128)(2,1)S(1)}, s32[4,2]{0,1:T(2,128)S(1)}, bf16[4,128,512]{2,1,0:T(8,128)(2,1)S(1)}, s32[]{:T(128)}) while((s32[]{:T(128)}, bf16[128,2048]{1,0:T(8,128)(2,1)S(1)}, s32[4,2]{0,1:T(2,128)S(1)}, bf16[4,128,512]{2,1,0:T(8,128)(2,1)S(1)}, s32[]{:T(128)}) %tuple.121), condition=%wide.while_cond, body=%wide.while_body.sunk | while | flops 2 | bytes 262241 | solution.py:166
  130.7 4.9 %while.29 = (s32[]{:T(128)}, bf16[2,2048]{1,0:T(2,128)(2,1)S(1)}, s32[4,2]{0,1:T(2,128)S(1)}, bf16[4,2,512]{2,1,0:T(2,128)(2,1)S(1)}, s32[]{:T(128)}) while((s32[]{:T(128)}, bf16[2,2048]{1,0:T(2,128)(2,1)S(1)}, s32[4,2]{0,1:T(2,128)S(1)}, bf16[4,2,512]{2,1,0:T(2,128)(2,1)S(1)}, s32[]{:T(128)}) %tuple.112), condition=%wide.while_cond.1, body=%wide.while_body.1.sunk | while | flops 2 | bytes 4193 | solution.py:167
  136.8 5.1 %while.28 = (s32[]{:T(128)}, bf16[128,2048]{1,0:T(8,128)(2,1)S(1)}, s32[4,2]{0,1:T(2,128)S(1)}, bf16[4,128,512]{2,1,0:T(8,128)(2,1)S(1)}, s32[]{:T(128)}) while((s32[]{:T(128)}, bf16[128,2048]{1,0:T(8,128)(2,1)S(1)}, s32[4,2]{0,1:T(2,128)S(1)}, bf16[4,128,512]{2,1,0:T(8,128)(2,1)S(1)}, s32[]{:T(128)}) %tuple.121), condition=%wide.while_cond, body=%wide.while_body.sunk | while | flops 2 | bytes 262241 | solution.py:166
  143.3 2.9 %reshape.176 = f32[32,64,256]{2,1,0:T(8,128)S(1)} reshape(f32[8,4,64,2,128]{4,3,2,1,0:T(2,128)} %get-tuple-element.58) | data formatting | bytes 4194304 | tf_op jit(solution)/shard_map/reshape | solution.py:176
  146.2 1.8 convolution_bitcast_fusion.1
  148.0 41.1 %psum.7 = f32[64,64]{0,1:T(8,128)S(1)} all-reduce(f32[64,64]{0,1:T(8,128)S(1)} %convolution_bitcast_fusion.1), channel_id=1, replica_groups=mesh['clu'=8,'col'=4] {'clu','col'}, use_global_device_ids=true, to_apply=%region_8.9 | all-reduce | flops 4096 | bytes 32768 | tf_op jit(solution)/shard_map/psum | solution.py:178
  189.2 5.8 %cholesky.17 = f32[64,64]{1,0:T(8,128)S(1)} custom-call(f32[64,64]{1,0:T(8,128)S(1)} %fusion.60), custom_call_target="Cholesky" | custom-call | tf_op jit(solution)/shard_map/jit(cholesky)/cholesky | solution.py:179
  196.4 4.9 %custom-call.7 = f32[1,64,64]{1,2,0:T(8,128)S(1)} custom-call(f32[1,64,64]{2,1,0:T(8,128)S(1)} %fusion.56), custom_call_target="InvertDiagBlocksLowerTriangular" | custom-call | tf_op jit(solution)/shard_map/jit(_solve_triangular)/triangular_solve | solution.py:180
  201.5 3.4 %multiply_bitcast_fusion = f32[32,64,256]{2,1,0:T(8,128)} fusion(f32[32,64,256]{2,1,0:T(8,128)S(1)} %reshape.176, f32[64,64,1]{1,0,2:T(8,128)S(1)} %convolution_bitcast_fusion), kind=kOutput, calls=%fused_computation.65 | convolution fusion | flops 403177472 | bytes 4210688 | tf_op jit(solution)/shard_map/kj,vjm->vkm/dot_general | solution.py:187
  206.2 3.2 %mul.291 = f32[32,64,2,128]{3,2,1,0:T(2,128)} reshape(f32[32,64,256]{2,1,0:T(8,128)} %multiply_bitcast_fusion) | data formatting | bytes 4194304 | tf_op jit(solution)/shard_map/mul | solution.py:187
  209.5 3.6 %all-to-all-start.1 = ((f32[8,6,4,128]{3,2,1,0:T(4,128)}), f32[8,6,4,128]{3,2,1,0:T(4,128)S(1)}, u32[]{:S(2)}, u32[]{:S(2)}) async-start(f32[8,6,4,128]{3,2,1,0:T(4,128)} %reshape.173), calls=%async_computation.1 | async-start | bytes 196608 | tf_op jit(solution)/shard_map/all_to_all | solution.py:125
  214.7 3.5 %all-to-all-done.1 = f32[8,6,4,128]{3,2,1,0:T(4,128)S(1)} async-done(((f32[8,6,4,128]{3,2,1,0:T(4,128)}), f32[8,6,4,128]{3,2,1,0:T(4,128)S(1)}, u32[]{:S(2)}, u32[]{:S(2)}) %all-to-all-start.1) | async-done | bytes 98336 | tf_op jit(solution)/shard_map/all_to_all | solution.py:125
  218.2 6.6 %while.24 = (s32[]{:T(128)}, f32[12,4,2,128]{3,2,1,0:T(2,128)S(1)}, f32[12,4,2,128]{3,0,2,1:T(8,128)S(1)}, f32[12,4,4,128]{3,2,1,0:T(4,128)S(1)}, s32[]{:T(128)}) while((s32[]{:T(128)}, f32[12,4,2,128]{3,2,1,0:T(2,128)S(1)}, f32[12,4,2,128]{3,0,2,1:T(8,128)S(1)}, f32[12,4,4,128]{3,2,1,0:T(4,128)S(1)}, s32[]{:T(128)}) %tuple.123), condition=%wide.region_5.6_spmd, body=%wide.region_2.5_spmd.sunk | while | flops 1181698 | bytes 102473 | solution.py:143
  (459 shorter events, 116.7 us)
Async XLA Ops:
  0.6 11.2 %copy-start = (f32[32,2,128]{2,1,0:T(2,128)S(1)}, f32[32,2,128]{2,1,0:T(2,128)}, u32[]{:S(2)}) copy-start(f32[32,2,128]{2,1,0:T(2,128)} %param.13) | copy-start | bytes 98308
  0.6 11.2 %copy-start.5 = (s32[1,32]{1,0:T(1,128)S(1)}, s32[1,32]{1,0:T(1,128)}, u32[]{:S(2)}) copy-start(s32[1,32]{1,0:T(1,128)} %param.16) | copy-start | bytes 388
  0.7 11.5 %copy-start.2 = (f32[32,128]{1,0:T(8,128)S(1)}, f32[32,128]{1,0:T(8,128)}, u32[]{:S(2)}) copy-start(f32[32,128]{1,0:T(8,128)} %param.14) | copy-start | bytes 49156
  0.7 11.7 %copy-start.4 = (f32[32]{0:T(128)S(1)}, f32[32]{0:T(128)}, u32[]{:S(2)}) copy-start(f32[32]{0:T(128)} %param.15) | copy-start | bytes 388
  0.7 12.4 %copy-start.1 = (bf16[128,512]{1,0:T(8,128)(2,1)S(1)}, bf16[128,512]{1,0:T(8,128)(2,1)}, u32[]{:S(2)}) copy-start(bf16[128,512]{1,0:T(8,128)(2,1)} %param.20) | copy-start | bytes 393220
  0.7 28.9 %copy-start.3 = (bf16[2,512]{1,0:T(2,128)(2,1)S(1)}, bf16[2,512]{1,0:T(2,128)(2,1)}, u32[]{:S(2)}) copy-start(bf16[2,512]{1,0:T(2,128)(2,1)} %param.21) | copy-start | bytes 6148
  0.7 41.4 %copy-start.6 = (s32[32,1]{0,1:T(1,128)S(1)}, s32[32,1]{0,1:T(1,128)}, u32[]{:S(2)}) copy-start(s32[32,1]{0,1:T(1,128)} %param.19) | copy-start | bytes 388
  4.5 204.9 %all-to-all-start = ((f32[8,1,6]{2,1,0:T(1,128)}), f32[8,1,6]{2,1,0:T(1,128)S(1)}, u32[]{:S(2)}, u32[]{:S(2)}) async-start(f32[8,1,6]{2,1,0:T(1,128)} %bitcast.35), calls=%async_computation | async-start | bytes 8192 | tf_op jit(solution)/shard_map/all_to_all | solution.py:126
  209.5 8.8 %all-to-all-start.1 = ((f32[8,6,4,128]{3,2,1,0:T(4,128)}), f32[8,6,4,128]{3,2,1,0:T(4,128)S(1)}, u32[]{:S(2)}, u32[]{:S(2)}) async-start(f32[8,6,4,128]{3,2,1,0:T(4,128)} %reshape.173), calls=%async_computation.1 | async-start | bytes 196608 | tf_op jit(solution)/shard_map/all_to_all | solution.py:125
where the time goes:
time: 227 us; the launch traced here: 226 us
  local copies, waits for them, and re-layouts  97.9 us (43%)
  blocking collectives  69.5 us (31%)
  other arithmetic  29.1 us (13%)
  matrix products  13.6 us (6%)
  starting transfers between devices  8.73 us (4%)
  waiting for transfers between devices  3.54 us (2%)
  loops' own time  2.39 us (1%)
    gather x192, local copies, waits for them, and re-layouts  79.2 us
    psum x1, blocking collectives, per_device(): gram = lax.psum(local_gram, ('clu', 'col'))  41.1 us
    all_gather x1, blocking collectives, per_device(): lax.all_gather(old_basis, 'col', axis=1, tiled=True)  16.6 us
    all_gather x1, blocking collectives, per_device(): lax.all_gather(source_nodes, 'col', axis=1, tiled=True)  11.9 us
    dynamic_update_slice x8, local copies, waits for them, and re-layouts, per_device(): lax.map(pull_group, (positions.reshape(-1, 4, 2, node_count), chosen.resh...  7.3 us
    another operation x8, other arithmetic  6.84 us
    another operation x3, other arithmetic, per_device(): lower_factor = jnp.linalg.cholesky(gram)  6.52 us
    another operation x2, other arithmetic, per_device(): jax.scipy.linalg.solve_triangular(lower_factor, jnp.eye(rank_count, dtype...  5.55 us
  transfers between devices with their start and end apart: 2, of which 1 were waited for; matrix products, arithmetic and copies ran while one was open for 58% of the time, Pallas kernels for 0%

commit v1 on v0

v1 whole, which is shorter than its diff:
```python
import functools
import math

import jax
import jax.numpy as jnp
import numpy as np
from jax import lax
from jax.experimental import pallas as pl
from jax.experimental.pallas import tpu as pltpu
from jax.sharding import PartitionSpec as P

EPS_SQUARED = 0.01
F32 = jnp.float32
BF16 = jnp.bfloat16
HIGHEST = lax.Precision.HIGHEST
BLOCK = 8
MIB = 1 << 20

NT = (((1,), (1,)), ((), ()))
NN = (((1,), (0,)), ((), ()))


def spectral_tables(node_count):
    half = node_count // 2
    j = np.arange(node_count)[:, None]
    k = np.arange(half + 1)[None, :]
    phase = (j * k % node_count) * (2.0 * math.pi / node_count)
    c, s = np.cos(phase), np.sin(phase)
    k = np.arange(half + 1, dtype=np.float64)
    inside = (k > 0) & (k < half)
    u = np.where(inside, 2.0 * k / half, 0.0)
    w = np.where(inside, 2.0 * (k / half) ** 4, np.where(k == half, 1.0, 0.0))
    derivative = ((c * u) @ s.T - (s * u) @ c.T) / node_count
    bending_table = ((c * w) @ c.T + (s * w) @ s.T) / node_count
    return derivative.T.astype(np.float32), bending_table.T.astype(np.float32)


def iota(shape, axis):
    return lax.broadcasted_iota(jnp.int32, shape, axis)


def dot(a, b, dims=NN, precision=None):
    return lax.dot_general(a, b, dims, precision=precision, preferred_element_type=F32)


def reciprocal(x):
    r = pl.reciprocal(x, approx=True)
    return r * (2.0 - x * r)


def force_kernel(clu_count, slot_cap, clu_ref, pos_ref, ten_ref, bend_ref, order_ref, dest_ref,
                 target_ref, deriv_ref, table_ref, force_ref, *piece_refs):
    vesicles = ten_ref.shape[0]
    moves = target_ref.shape[1]
    x = pos_ref[pl.ds(0, vesicles, stride=2), :]
    y = pos_ref[pl.ds(1, vesicles, stride=2), :]
    rows = jnp.concatenate([x, y], axis=0)
    deriv = deriv_ref[...]
    tension = jnp.concatenate([ten_ref[...]] * 2, axis=0)
    eye = iota((vesicles, vesicles), 0) == iota((vesicles, vesicles), 1)
    bend = jnp.sum(jnp.where(eye, bend_ref[...], 0.0), axis=1, keepdims=True)
    bend = jnp.concatenate([bend] * 2, axis=0)
    slope = dot(rows, deriv, precision=HIGHEST)
    fourth = dot(rows, table_ref[...], precision=HIGHEST)
    force = dot(tension * slope, deriv, precision=HIGHEST) - bend * fourth
    force_x, force_y = force[:vesicles], force[vesicles:]
    force_ref[pl.ds(0, vesicles, stride=2), :] = force_x
    force_ref[pl.ds(1, vesicles, stride=2), :] = force_y

    slots = clu_count * BLOCK
    relative = lax.rem(dest_ref[...] - clu_ref[0] + clu_count, clu_count)
    hot = (iota((clu_count, moves), 0) == relative).astype(F32)
    earlier = (iota((moves, moves), 0) < iota((moves, moves), 1)).astype(F32)
    rank = jnp.sum(dot(hot, earlier) * hot, axis=0, keepdims=True).astype(jnp.int32)
    slot = relative * BLOCK + rank
    pack = (iota((slots, moves), 0) == slot).astype(F32)
    pick = (iota((vesicles, moves), 0) == order_ref[:, :moves]).astype(F32)
    select = dot(pack, pick, NT)
    carried = jnp.concatenate([x, y, force_x, force_y], axis=1)
    packed = dot(select, carried, precision=HIGHEST)
    tag = jnp.sum(pack * (target_ref[...] + 1).astype(F32), axis=1, keepdims=True)
    tag = jnp.broadcast_to(tag, (slots, x.shape[1]))
    for k in range(clu_count):
        here = slice(k * BLOCK, (k + 1) * BLOCK)
        piece_refs[k][...] = jnp.concatenate([packed[here], tag[here]], axis=1)


def near_kernel(clu_count, slot_cap, pos_ref, *refs):
    piece_refs, near_ref, arrived, aim_x, aim_y, speed_x, speed_y = (
        refs[:clu_count], *refs[clu_count:])
    vesicles = pos_ref.shape[0] // 2
    nodes = pos_ref.shape[1]
    for k in range(clu_count):
        arrived[k] = piece_refs[k][...]
    slots = clu_count * BLOCK
    tag = arrived[:, :, 4 * nodes:].reshape(slots, nodes)[:, :vesicles]
    hot = (tag == (iota((slots, vesicles), 1) + 1).astype(F32)).astype(F32)
    x = pos_ref[pl.ds(0, vesicles, stride=2), :]
    y = pos_ref[pl.ds(1, vesicles, stride=2), :]
    aim_x[...] = dot(hot, x, precision=HIGHEST).reshape(clu_count, BLOCK, nodes)
    aim_y[...] = dot(hot, y, precision=HIGHEST).reshape(clu_count, BLOCK, nodes)

    def piece(k, _):
        data = arrived[k]
        turned = [data[:, c * nodes:(c + 1) * nodes].T for c in range(4)]
        tx, ty = aim_x[k], aim_y[k]
        rows_x, rows_y = [], []
        for h in range(slot_cap):
            sx, sy, fx, fy = [jnp.broadcast_to(t[:, h:h + 1], (nodes, nodes)) for t in turned]
            dx = tx[h:h + 1] - sx
            dy = ty[h:h + 1] - sy
            spread = dx * dx + dy * dy + EPS_SQUARED
            log_part = -0.5 * jnp.log(spread)
            along = (dx * fx + dy * fy) * reciprocal(spread)
            rows_x.append(jnp.sum(log_part * fx + dx * along, axis=0, keepdims=True))
            rows_y.append(jnp.sum(log_part * fy + dy * along, axis=0, keepdims=True))
        rows_x += [jnp.zeros((1, nodes), F32)] * (BLOCK - slot_cap)
        rows_y += [jnp.zeros((1, nodes), F32)] * (BLOCK - slot_cap)
        speed_x[k] = jnp.concatenate(rows_x, axis=0)
        speed_y[k] = jnp.concatenate(rows_y, axis=0)
        return 0

    lax.fori_loop(0, clu_count, piece, 0)
    turned_hot = hot.T
    near_ref[pl.ds(0, vesicles, stride=2), :] = dot(
        turned_hot, speed_x[...].reshape(slots, nodes), precision=HIGHEST) / nodes
    near_ref[pl.ds(1, vesicles, stride=2), :] = dot(
        turned_hot, speed_y[...].reshape(slots, nodes), precision=HIGHEST) / nodes


def far_kernel(col_count, index_ref, range_ref, pos_ref, own_ref, nodes_ref, *refs):
    count = 2 * (col_count - 1)
    piece_refs, (high_ref, low_ref, gram_ref, basis, spots, wide) = refs[:count], refs[count:]
    vesicles = pos_ref.shape[0] // 2
    nodes = pos_ref.shape[1]
    rows, sources = own_ref.shape
    half, rank = rows // 2, rows // 2
    core, col = index_ref[0], index_ref[1]
    basis[col] = own_ref[...]
    spots[col, 0:2] = nodes_ref[...].astype(F32)
    for k in range(1, col_count):
        where = lax.rem(col - k + col_count, col_count)
        mine, other = piece_refs[2 * k - 2], piece_refs[2 * k - 1]
        basis[where, pl.ds(pl.multiple_of(core * half, half), half), :] = mine[0:half]
        basis[where, pl.ds(pl.multiple_of((1 - core) * half, half), half), :] = other[0:half]
        spots[where, 0:2] = mine[half:half + 16].astype(F32)[0:2]
    for r in range(col_count):
        turned = spots[r].T
        for c in range(2):
            wide[r, c] = jnp.broadcast_to(turned[:, c:c + 1], (sources, nodes))
    gram_ref[...] = jnp.zeros_like(gram_ref)
    chunk = 256 if sources % 256 == 0 else sources

    def vesicle(v, total):
        r = range_ref[v]
        tx = pos_ref[pl.ds(2 * v, 1), :]
        ty = pos_ref[pl.ds(2 * v + 1, 1), :]
        product = None
        for start in range(0, sources, chunk):
            dx = tx - wide[r, 0, start:start + chunk]
            dy = ty - wide[r, 1, start:start + chunk]
            spread = dx * dx + dy * dy + EPS_SQUARED
            log_part = -0.5 * jnp.log(spread)
            inverse = reciprocal(spread)
            dxr = dx * inverse
            ff = (log_part + dx * dxr).astype(BF16)
            fs = (dy * dxr).astype(BF16)
            ss = (log_part + dy * (dy * inverse)).astype(BF16)
            part = dot(basis[r, :, start:start + chunk], jnp.concatenate([ff, fs, ss], axis=1))
            product = part if product is None else product + part
        first = product[:rank, :nodes] + product[rank:, nodes:2 * nodes]
        second = product[:rank, nodes:2 * nodes] + product[rank:, 2 * nodes:]
        high_0, high_1 = first.astype(BF16), second.astype(BF16)
        low_0 = (first - high_0.astype(F32)).astype(BF16)
        low_1 = (second - high_1.astype(F32)).astype(BF16)
        high_ref[v] = jnp.concatenate([high_0, high_1], axis=0)
        low_ref[v] = jnp.concatenate([low_0, low_1], axis=0)
        both = jnp.concatenate([
            jnp.concatenate([high_0, high_1], axis=1),
            jnp.concatenate([low_0, low_1], axis=1)], axis=0)
        return total + dot(both, both, NT)

    total = lax.fori_loop(0, vesicles, vesicle, jnp.zeros((2 * rank, 2 * rank), F32))
    gram = total[:rank, :rank] + total[rank:, rank:] + (total[:rank, rank:] + total[rank:, :rank])
    gram_ref[...] = jnp.concatenate([gram[:rank // 2], gram[rank // 2:]], axis=1)


def lower_inverse(gram):
    size = gram.shape[0]
    eye = (iota((size, size), 0) == iota((size, size), 1)).astype(F32)
    rest = jnp.concatenate([gram, eye], axis=1)
    done = []
    step = 8
    for start in range(0, size, step):
        height = size - start
        columns = [jnp.broadcast_to(rest[:, start + j:start + j + 1], (height, 2 * size))
                   for j in range(step)]
        row_number = iota((height, 2 * size), 0)
        scale = jnp.zeros((step, 2 * size), F32)
        for j in range(step):
            column = columns[j]
            pivot = column[j:j + 1]
            factor = jnp.where(row_number > j, column * reciprocal(pivot), 0.0)
            for later in range(j + 1, step):
                columns[later] = columns[later] - factor * column[later:later + 1]
            rest = rest - factor * rest[j:j + 1]
            root = lax.rsqrt(pivot)
            root = root * (1.5 - 0.5 * pivot * root * root)
            scale = jnp.where(row_number[:step] == j, root, scale)
        done.append(rest[:step] * scale)
        rest = rest[step:]
    return jnp.concatenate(done, axis=0)[:, size:]


def basis_kernel(col_count, scale_factor, *refs):
    gram_refs = refs[:col_count]
    high_ref, low_ref, out_ref, weight = refs[col_count:]
    rank = high_ref.shape[1] // 2

    @pl.when(pl.program_id(0) == 0)
    def _():
        folded = gram_refs[0][...]
        for g in gram_refs[1:]:
            folded = folded + g[...]
        gram = jnp.concatenate([folded[:, :rank], folded[:, rank:]], axis=0)
        inverse = lower_inverse(gram) * scale_factor
        turn = iota((2 * rank, rank), 0) - 2 * iota((2 * rank, rank), 1)
        spread = jnp.concatenate([
            dot((turn == d).astype(F32), inverse, precision=HIGHEST) for d in range(2)], axis=1)
        high = spread.astype(BF16)
        low = (spread - high.astype(F32)).astype(BF16)
        weight[...] = jnp.concatenate([high, high, low], axis=1)

    w = weight[...]
    for v in range(high_ref.shape[0]):
        stacked = jnp.concatenate([high_ref[v], low_ref[v], high_ref[v]], axis=0)
        out_ref[v] = dot(w, stacked)


def whole_spec():
    return pl.BlockSpec(memory_space=pltpu.VMEM)


def scalar_spec():
    return pl.BlockSpec(memory_space=pltpu.SMEM)


def params(mib):
    return pltpu.CompilerParams(vmem_limit_bytes=mib * MIB)


def shifts(count, by):
    return [(i, (i + by) % count) for i in range(count)]


def per_device(positions, tension, bending, moved_order, move_destination, move_target, far_range,
               old_basis, source_nodes):
    vesicles, _, nodes = positions.shape
    rows, sources = old_basis.shape
    rank = rows // 2
    clu_count, col_count = lax.axis_size("clu"), lax.axis_size("col")
    moves = move_target.shape[0]
    slot_cap = 2 * ((moves + clu_count - 1) // clu_count)
    clu, col = lax.axis_index("clu"), lax.axis_index("col")
    core = lax.rem(clu, 2)
    flat = positions.reshape(2 * vesicles, nodes)

    half_rows = lax.dynamic_slice_in_dim(old_basis, core * rank, rank, 0)
    sent = jnp.concatenate(
        [half_rows, source_nodes, jnp.zeros((14, sources), old_basis.dtype)], axis=0)
    swap = [(i, i ^ 1) for i in range(clu_count)]
    pieces = []
    for k in range(1, col_count):
        mine = lax.ppermute(sent, "col", shifts(col_count, k))
        pieces += [mine, lax.ppermute(mine, "clu", swap)]

    deriv, table = spectral_tables(nodes)
    force_out = pl.pallas_call(
        functools.partial(force_kernel, clu_count, slot_cap),
        out_shape=[jax.ShapeDtypeStruct((2 * vesicles, nodes), F32)]
        + [jax.ShapeDtypeStruct((BLOCK, 5 * nodes), F32)] * clu_count,
        in_specs=[scalar_spec()] + [whole_spec()] * 8,
        out_specs=[whole_spec()] * (1 + clu_count),
        compiler_params=params(16),
        cost_estimate=pl.CostEstimate(flops=10**8, bytes_accessed=10**6, transcendentals=0),
    )(clu.reshape(1), flat, tension, bending.reshape(1, vesicles), moved_order,
      move_destination.reshape(1, moves), move_target.reshape(1, moves), deriv, table)
    force, packed = force_out[0], force_out[1:]
    arrived = [packed[0]] + [
        lax.ppermute(packed[k], "clu", shifts(clu_count, k)) for k in range(1, clu_count)]

    near = pl.pallas_call(
        functools.partial(near_kernel, clu_count, slot_cap),
        out_shape=jax.ShapeDtypeStruct((2 * vesicles, nodes), F32),
        in_specs=[whole_spec()] * (1 + clu_count),
        out_specs=whole_spec(),
        scratch_shapes=[pltpu.VMEM((clu_count, BLOCK, 5 * nodes), F32)]
        + [pltpu.VMEM((clu_count, BLOCK, nodes), F32)] * 4,
        compiler_params=params(16),
        cost_estimate=pl.CostEstimate(flops=10**9, bytes_accessed=10**7, transcendentals=10**6),
    )(flat, *arrived)

    high, low, gram = pl.pallas_call(
        functools.partial(far_kernel, col_count),
        out_shape=[jax.ShapeDtypeStruct((vesicles, rows, nodes), BF16)] * 2
        + [jax.ShapeDtypeStruct((rank // 2, 2 * rank), F32)],
        in_specs=[scalar_spec()] * 2 + [whole_spec()] * (3 + 2 * (col_count - 1)),
        out_specs=[whole_spec()] * 3,
        scratch_shapes=[
            pltpu.VMEM((col_count, rows, sources), BF16),
            pltpu.VMEM((col_count, 8, sources), F32),
            pltpu.VMEM((col_count, 2, sources, nodes), F32)],
        compiler_params=params(32),
        cost_estimate=pl.CostEstimate(flops=10**10, bytes_accessed=10**7, transcendentals=10**7),
    )(jnp.stack([core, col]), far_range.reshape(vesicles), flat, old_basis, source_nodes, *pieces)

    for k in range(1, clu_count):
        moved = lax.ppermute(gram, "clu", shifts(clu_count, k))
        total = moved if k == 1 else total + moved
    gram = gram + total
    grams = [gram] + [lax.ppermute(gram, "col", shifts(col_count, k)) for k in range(1, col_count)]

    scale_factor = math.sqrt(2.0 * nodes * vesicles * clu_count * col_count)
    group = 8 if vesicles % 8 == 0 else vesicles
    block = pl.BlockSpec((group, rows, nodes), lambda i: (i, 0, 0))
    new_basis = pl.pallas_call(
        functools.partial(basis_kernel, col_count, scale_factor),
        out_shape=jax.ShapeDtypeStruct((vesicles, rows, nodes), F32),
        grid=(vesicles // group,),
        in_specs=[whole_spec()] * col_count + [block] * 2,
        out_specs=block,
        scratch_shapes=[pltpu.VMEM((rows, 3 * rows), BF16)],
        compiler_params=params(16),
        cost_estimate=pl.CostEstimate(flops=10**9, bytes_accessed=10**7, transcendentals=0),
    )(*grams, high, low)

    return (force.reshape(vesicles, 2, nodes), near.reshape(vesicles, 2, nodes),
            new_basis.reshape(vesicles, rank, 2, nodes))


def solution(mesh):
    both = ("clu", "col")
    placed = (
        P(both, None, None), P(both, None), P(both), P(both, None), P(both, None), P(both),
        P(both, None), P(None, "col"), P(None, "col"),
    )
    return jax.shard_map(
        per_device,
        mesh=mesh,
        in_specs=placed,
        out_specs=(P(both, None, None), P(both, None, None), P(both, None, None, None)),
        check_vma=False,
    )
```

time: 227 us -> 69.3 us (0.31)
  local copies, waits for them, and re-layouts: 97.9 us -> 9.7 us
  blocking collectives: 69.5 us -> 0 us
  Pallas kernels: 0 us -> 31.2 us
  other arithmetic: 29.1 us -> 0.85 us
  starting transfers between devices: 8.73 us -> 25.4 us
  matrix products: 13.6 us -> 0 us
  waiting for transfers between devices: 3.54 us -> 0.9 us
  loops' own time: 2.39 us -> 0 us
    gather x192 -> x0, local copies, waits for them, and re-layouts: 79.2 us -> none
    psum x1 -> x0, blocking collectives: 41.1 us -> none  [per_device(): gram = lax.psum(local_gram, ('clu', 'col'))]
    pallas_call x0 -> x4, Pallas kernels: none -> 31.2 us  [the longest x1 18.8 us: per_device(): pl.pallas_call(functools.partial(far_kernel, col_count), out_shape=[jax.S...]
    all_gather x2 -> x0, blocking collectives: 28.4 us -> none  [the longest x1 16.6 us: per_device(): lax.all_gather(old_basis, 'col', axis=1, tiled=True)]
    ppermute x0 -> x23, starting transfers between devices: none -> 25.4 us  [the longest x7 7.36 us: per_device(): moved = lax.ppermute(gram, 'clu', shifts(clu_count, k))]
    another operation x22 -> x1, other arithmetic: 20.2 us -> 0.07 us  [per_device(): jnp.stack([core, col])]
    dot_general x22 -> x0, matrix products: 13.3 us -> none  [the longest x8 3.82 us: pull_group(): jnp.einsum('geks,gedsn->gkdn', stacked, kernel, preferred_element_type=jn...]
    all_to_all x2 -> x0, starting transfers between devices: 8.73 us -> none  [the longest x1 5.17 us: per_device(): lax.all_to_all(target_tag, 'clu', split_axis=0, concat_axis=0, tiled=True)]
  transfers between devices with their start and end apart: 2 -> 23, of which waited for: 1 -> 3; matrix products, arithmetic and copies ran while one was open for 58% -> 0% of each run, Pallas kernels for 0% -> 38%
where the time goes in v1:
time: 69.3 us; the launch traced here: 68.7 us
  Pallas kernels  31.2 us (45%)
  starting transfers between devices  25.4 us (37%)
  local copies, waits for them, and re-layouts  9.7 us (14%)
  waiting for transfers between devices  0.9 us (1%)
  other arithmetic  0.85 us (1%)
  between operations  0.7 us (1%)
    pallas_call x1, Pallas kernels, per_device(): pl.pallas_call(functools.partial(far_kernel, col_count), out_shape=[jax.S...  18.8 us
    unnamed x24, local copies, waits for them, and re-layouts  8.77 us
    ppermute x7, starting transfers between devices, per_device(): moved = lax.ppermute(gram, 'clu', shifts(clu_count, k))  7.36 us
    pallas_call x1, Pallas kernels, per_device(): pl.pallas_call(functools.partial(near_kernel, clu_count, slot_cap), out_s...  6.19 us
    ppermute x3, starting transfers between devices, per_device(): mine = lax.ppermute(sent, 'col', shifts(col_count, k))  6.13 us
    ppermute x7, starting transfers between devices, per_device(): lax.ppermute(packed[k], 'clu', shifts(clu_count, k))  6.06 us
    pallas_call x1, Pallas kernels, per_device(): pl.pallas_call(functools.partial(basis_kernel, col_count, scale_factor),...  5.13 us
    ppermute x3, starting transfers between devices, per_device(): lax.ppermute(gram, 'col', shifts(col_count, k))  4.08 us
  transfers between devices with their start and end apart: 23, of which 3 were waited for; matrix products, arithmetic and copies ran while one was open for 0% of the time, Pallas kernels for 38%

profile of v1, /device:TPU:0, one launch (start us, length us, event | category | flops | bytes accessed | tf_op | source)
XLA Modules:
  0.0 68.7 jit_solution(17255985648270046767)
XLA Ops:
  0.6 0.8 %constant_dynamic-slice_fusion = bf16[64,512]{1,0:T(8,128)(2,1)S(1)} fusion(bf16[128,512]{1,0:T(8,128)(2,1)} %own_ref.1, s32[]{:T(128)S(6)} %select_n.3), kind=kLoop, calls=%fused_computation.3 | loop fusion | bytes 131076 | tf_op jit(solution)/shard_map/dynamic_slice | solution.py:268
  1.6 0.8 %maximum_maximum_fusion = bf16[80,512]{1,0:T(8,128)(2,1)S(1)} fusion(bf16[2,512]{1,0:T(2,128)(2,1)} %nodes_ref.1, bf16[64,512]{1,0:T(8,128)(2,1)S(1)} %constant_dynamic-slice_fusion, bf16[80]{0:T(256)(128)(2,1)S(1)} %pad.2.clone), kind=kLoop, calls=%fused_computation | loop fusion | flops 245760 | bytes 149664 | tf_op jit(solution)/shard_map/concatenate | solution.py:269
  2.3 4.1 %collective-permute-start.9 = (bf16[80,512]{1,0:T(8,128)(2,1)S(1)}, bf16[80,512]{1,0:T(8,128)(2,1)S(1)}, u32[]{:S(2)}, u32[]{:S(2)}) collective-permute-start(bf16[80,512]{1,0:T(8,128)(2,1)S(1)} %maximum_maximum_fusion), channel_id=1, source_target_pairs={{0,2},{1,3},{2,0},{3,1},{4,6},{5,7},{6,4},{7,5},{8,10},{9,11},{10,... | collective-permute-start | bytes 245768 | tf_op jit(solution)/shard_map/ppermute | solution.py:274
  6.4 1.3 %collective-permute-start.11 = (bf16[80,512]{1,0:T(8,128)(2,1)S(1)}, bf16[80,512]{1,0:T(8,128)(2,1)S(1)}, u32[]{:S(2)}, u32[]{:S(2)}) collective-permute-start(bf16[80,512]{1,0:T(8,128)(2,1)S(1)} %maximum_maximum_fusion), channel_id=1, source_target_pairs={{0,3},{1,0},{2,1},{3,2},{4,7},{5,4},{6,5},{7,6},{8,11},{9,8},{10,9... | collective-permute-start | bytes 245768 | tf_op jit(solution)/shard_map/ppermute | solution.py:274
  7.8 0.7 collective-permute-start.7
  8.5 0.8 %copy-done.2 = f32[32,2,128]{2,1,0:T(2,128)S(1)} copy-done((f32[32,2,128]{2,1,0:T(2,128)S(1)}, f32[32,2,128]{2,1,0:T(2,128)}, u32[]{:S(2)}) %copy-start.2) | copy-done | bytes 32792
  9.2 0.7 %copy-done.4 = f32[32,128]{1,0:T(8,128)S(1)} copy-done((f32[32,128]{1,0:T(8,128)S(1)}, f32[32,128]{1,0:T(8,128)}, u32[]{:S(2)}) %copy-start.4) | copy-done | bytes 16408
  9.9 0.7 copy-done.5
  10.6 0.7 copy-done.6
  11.3 0.7 copy-done.7
  11.9 0.7 copy-done.8
  12.6 0.8 %copy-done.10 = f32[128,128]{1,0:T(8,128)S(1)} copy-done((f32[128,128]{1,0:T(8,128)S(1)}, f32[128,128]{1,0:T(8,128)}, u32[]{:S(2)}) %copy-start.10) | copy-done | bytes 65560
  13.4 0.8 %copy-done.11 = f32[128,128]{1,0:T(8,128)S(1)} copy-done((f32[128,128]{1,0:T(8,128)S(1)}, f32[128,128]{1,0:T(8,128)}, u32[]{:S(2)}) %copy-start.11) | copy-done | bytes 65560
  14.2 1.0 %shard_map.130 = (f32[64,128]{1,0:T(8,128)}, f32[8,640]{1,0:T(8,128)S(1)}, f32[8,640]{1,0:T(8,128)S(1)}, f32[8,640]{1,0:T(8,128)S(1)}, f32[8,640]{1,0:T(8,128)S(...) custom-call(s32[1]{0:T(128)} %bitcast.clu_ref, ...), custom_call_target="tpu_custom_call" | custom-call | flops 100000000 | bytes 1000000 | tf_op jit(solution)/shard_map/pallas_call | solution.py:278
  15.3 1.5 %collective-permute-start.1 = (f32[8,640]{1,0:T(8,128)S(1)}, f32[8,640]{1,0:T(8,128)S(1)}, u32[]{:S(2)}, u32[]{:S(2)}) collective-permute-start(f32[8,640]{1,0:T(8,128)S(1)} %get-tuple-element.18), channel_id=1, source_target_pairs={{0,8},{4,12},{8,16},{12,20},{16,24},{20,28},{24,0},{28,4},{1,9},{5... | collective-permute-start | bytes 61448 | tf_op jit(solution)/shard_map/ppermute | solution.py:290
  16.8 1.3 %collective-permute-start.10 = (bf16[80,512]{1,0:T(8,128)(2,1)S(1)}, bf16[80,512]{1,0:T(8,128)(2,1)S(1)}, u32[]{:S(2)}, u32[]{:S(2)}) collective-permute-start(bf16[80,512]{1,0:T(8,128)(2,1)S(1)} %collective-permute-done.9.refs_2_), channel_id=1, source_target_pairs={{0,4},{4,0},{8,12},{12,8},{16,20},{20,16},{24,28},{28,24},{1,5},{5... | collective-permute-start | bytes 245768 | tf_op jit(solution)/shard_map/ppermute | solution.py:275
  19.5 0.9 %copy-done = bf16[128,512]{1,0:T(8,128)(2,1)S(1)} copy-done((bf16[128,512]{1,0:T(8,128)(2,1)S(1)}, bf16[128,512]{1,0:T(8,128)(2,1)}, u32[]{:S(2)}) %copy-start) | copy-done | bytes 131096
  20.4 0.7 copy-done.1
  21.1 0.8 %copy-done.3 = f32[32,2,128]{2,1,0:T(2,128)S(1)} copy-done((f32[32,2,128]{2,1,0:T(2,128)S(1)}, f32[32,2,128]{2,1,0:T(2,128)}, u32[]{:S(2)}) %copy-start.3) | copy-done | bytes 32792
  22.5 18.8 %shard_map.132 = (bf16[32,128,128]{2,1,0:T(8,128)(2,1)S(1)}, bf16[32,128,128]{2,1,0:T(8,128)(2,1)S(1)}, f32[32,128]{1,0:T(8,128)S(1)}) custom-call(s32[2]{0:T(128)S(1)} %pad_add_fusion.index_ref, s32[32]{0:T(128)S(1)} %bitcast.17, f32[64,128]{1,0:T(8,128)S(1)} %bitcast.12, bf16[128,512]{1,0:T(8,128)(2,1)S(1)} %copy-done, bf16[2,512]{1,0:T(2,128)(2,1)S(1)} %copy-done.1, ...), custom_call_target="tpu_custom_call" | custom-call | flops 10000000000 | bytes 10000000 | tf_op jit(solution)/shard_map/pallas_call | solution.py:303
  41.7 1.5 %collective-permute-start.14 = (f32[32,128]{1,0:T(8,128)S(1)}, f32[32,128]{1,0:T(8,128)S(1)}, u32[]{:S(2)}, u32[]{:S(2)}) collective-permute-start(f32[32,128]{1,0:T(8,128)S(1)} %get-tuple-element.24), channel_id=1, source_target_pairs={{0,8},{4,12},{8,16},{12,20},{16,24},{20,28},{24,0},{28,4},{1,9},{5... | collective-permute-start | bytes 49160 | tf_op jit(solution)/shard_map/ppermute | solution.py:318
  43.2 1.1 %collective-permute-start.15 = (f32[32,128]{1,0:T(8,128)S(1)}, f32[32,128]{1,0:T(8,128)S(1)}, u32[]{:S(2)}, u32[]{:S(2)}) collective-permute-start(f32[32,128]{1,0:T(8,128)S(1)} %get-tuple-element.24), channel_id=1, source_target_pairs={{0,12},{4,16},{8,20},{12,24},{16,28},{20,0},{24,4},{28,8},{1,13},{... | collective-permute-start | bytes 49160 | tf_op jit(solution)/shard_map/ppermute | solution.py:318
  44.3 1.5 %collective-permute-start.16 = (f32[32,128]{1,0:T(8,128)S(1)}, f32[32,128]{1,0:T(8,128)S(1)}, u32[]{:S(2)}, u32[]{:S(2)}) collective-permute-start(f32[32,128]{1,0:T(8,128)S(1)} %get-tuple-element.24), channel_id=1, source_target_pairs={{0,16},{4,20},{8,24},{12,28},{16,0},{20,4},{24,8},{28,12},{1,17},{... | collective-permute-start | bytes 49160 | tf_op jit(solution)/shard_map/ppermute | solution.py:318
  45.8 1.5 %collective-permute-start.18 = (f32[32,128]{1,0:T(8,128)S(1)}, f32[32,128]{1,0:T(8,128)S(1)}, u32[]{:S(2)}, u32[]{:S(2)}) collective-permute-start(f32[32,128]{1,0:T(8,128)S(1)} %get-tuple-element.24), channel_id=1, source_target_pairs={{0,24},{4,28},{8,0},{12,4},{16,8},{20,12},{24,16},{28,20},{1,25},{... | collective-permute-start | bytes 49160 | tf_op jit(solution)/shard_map/ppermute | solution.py:318
  47.3 1.4 %collective-permute-start.19 = (f32[32,128]{1,0:T(8,128)S(1)}, f32[32,128]{1,0:T(8,128)S(1)}, u32[]{:S(2)}, u32[]{:S(2)}) collective-permute-start(f32[32,128]{1,0:T(8,128)S(1)} %get-tuple-element.24), channel_id=1, source_target_pairs={{0,28},{4,0},{8,4},{12,8},{16,12},{20,16},{24,20},{28,24},{1,29},{... | collective-permute-start | bytes 49160 | tf_op jit(solution)/shard_map/ppermute | solution.py:318
  48.8 1.5 %collective-permute-start.3 = (f32[8,640]{1,0:T(8,128)S(1)}, f32[8,640]{1,0:T(8,128)S(1)}, u32[]{:S(2)}, u32[]{:S(2)}) collective-permute-start(f32[8,640]{1,0:T(8,128)S(1)} %get-tuple-element.20), channel_id=1, source_target_pairs={{0,16},{4,20},{8,24},{12,28},{16,0},{20,4},{24,8},{28,12},{1,17},{... | collective-permute-start | bytes 61448 | tf_op jit(solution)/shard_map/ppermute | solution.py:290
  50.2 1.4 %collective-permute-start.4 = (f32[8,640]{1,0:T(8,128)S(1)}, f32[8,640]{1,0:T(8,128)S(1)}, u32[]{:S(2)}, u32[]{:S(2)}) collective-permute-start(f32[8,640]{1,0:T(8,128)S(1)} %get-tuple-element.21), channel_id=1, source_target_pairs={{0,20},{4,24},{8,28},{12,0},{16,4},{20,8},{24,12},{28,16},{1,21},{... | collective-permute-start | bytes 61448 | tf_op jit(solution)/shard_map/ppermute | solution.py:290
  52.2 1.1 %collective-permute-start.6 = (f32[8,640]{1,0:T(8,128)S(1)}, f32[8,640]{1,0:T(8,128)S(1)}, u32[]{:S(2)}, u32[]{:S(2)}) collective-permute-start(f32[8,640]{1,0:T(8,128)S(1)} %get-tuple-element.23), channel_id=1, source_target_pairs={{0,28},{4,0},{8,4},{12,8},{16,12},{20,16},{24,20},{28,24},{1,29},{... | collective-permute-start | bytes 61448 | tf_op jit(solution)/shard_map/ppermute | solution.py:290
  53.3 1.6 %collective-permute-start.20 = (f32[32,128]{1,0:T(8,128)S(1)}, f32[32,128]{1,0:T(8,128)S(1)}, u32[]{:S(2)}, u32[]{:S(2)}) collective-permute-start(f32[32,128]{1,0:T(8,128)S(1)} %add_add_fusion.refs_0_), channel_id=1, source_target_pairs={{0,1},{1,2},{2,3},{3,0},{4,5},{5,6},{6,7},{7,4},{8,9},{9,10},{10,1... | collective-permute-start | bytes 49160 | tf_op jit(solution)/shard_map/ppermute | solution.py:321
  54.9 2.1 %collective-permute-start.21 = (f32[32,128]{1,0:T(8,128)S(1)}, f32[32,128]{1,0:T(8,128)S(1)}, u32[]{:S(2)}, u32[]{:S(2)}) collective-permute-start(f32[32,128]{1,0:T(8,128)S(1)} %add_add_fusion.refs_0_), channel_id=1, source_target_pairs={{0,2},{1,3},{2,0},{3,1},{4,6},{5,7},{6,4},{7,5},{8,10},{9,11},{10,... | collective-permute-start | bytes 49160 | tf_op jit(solution)/shard_map/ppermute | solution.py:321
  57.4 6.2 %shard_map.131 = f32[64,128]{1,0:T(8,128)} custom-call(f32[64,128]{1,0:T(8,128)S(1)} %bitcast.13, f32[8,640]{1,0:T(8,128)S(1)} %get-tuple-element.16.refs_0_, f32[8,640]{1,0:T(8,128)S(1)} %collective-permute-done.refs_1_, f32[8,640]{1,0:T(8,128)S(1)} %collective-permute-done.1.refs_2_, f32[8,640]{1,0:T(8,128)S(1)} %collective-permute-done.2.refs_3_, ...), custom_call_target="tpu_custom_call" | custom-call | flops 1000000000 | bytes 10000000 | tf_op jit(solution)/shard_map/pallas_call | solution.py:292
  63.6 5.1 %shard_map.133 = f32[32,128,128]{2,1,0:T(8,128)} custom-call(f32[32,128]{1,0:T(8,128)S(1)} %add_add_fusion.refs_0_, f32[32,128]{1,0:T(8,128)S(1)} %collective-permute-done.20.refs_1_, f32[32,128]{1,0:T(8,128)S(1)} %collective-permute-done.21.refs_2_, f32[32,128]{1,0:T(8,128)S(1)} %collective-permute-done.22.refs_3_, ...), custom_call_target="tpu_custom_call" | custom-call | flops 1000000000 | bytes 10000000 | tf_op jit(solution)/shard_map/pallas_call | solution.py:326
  (48 shorter events, 3.5 us)
Async XLA Ops:
  2.3 14.5 %collective-permute-start.9 = (bf16[80,512]{1,0:T(8,128)(2,1)S(1)}, bf16[80,512]{1,0:T(8,128)(2,1)S(1)}, u32[]{:S(2)}, u32[]{:S(2)}) collective-permute-start(bf16[80,512]{1,0:T(8,128)(2,1)S(1)} %maximum_maximum_fusion), channel_id=1, source_target_pairs={{0,2},{1,3},{2,0},{3,1},{4,6},{5,7},{6,4},{7,5},{8,10},{9,11},{10,... | collective-permute-start | bytes 245768 | tf_op jit(solution)/shard_map/ppermute | solution.py:274
  6.4 11.7 %collective-permute-start.11 = (bf16[80,512]{1,0:T(8,128)(2,1)S(1)}, bf16[80,512]{1,0:T(8,128)(2,1)S(1)}, u32[]{:S(2)}, u32[]{:S(2)}) collective-permute-start(bf16[80,512]{1,0:T(8,128)(2,1)S(1)} %maximum_maximum_fusion), channel_id=1, source_target_pairs={{0,3},{1,0},{2,1},{3,2},{4,7},{5,4},{6,5},{7,6},{8,11},{9,8},{10,9... | collective-permute-start | bytes 245768 | tf_op jit(solution)/shard_map/ppermute | solution.py:274
  7.8 10.4 %collective-permute-start.7 = (bf16[80,512]{1,0:T(8,128)(2,1)S(1)}, bf16[80,512]{1,0:T(8,128)(2,1)S(1)}, u32[]{:S(2)}, u32[]{:S(2)}) collective-permute-start(bf16[80,512]{1,0:T(8,128)(2,1)S(1)} %maximum_maximum_fusion), channel_id=1, source_target_pairs={{0,1},{1,2},{2,3},{3,0},{4,5},{5,6},{6,7},{7,4},{8,9},{9,10},{10,1... | collective-permute-start | bytes 245768 | tf_op jit(solution)/shard_map/ppermute | solution.py:274
  8.5 0.8 %copy-start.2 = (f32[32,2,128]{2,1,0:T(2,128)S(1)}, f32[32,2,128]{2,1,0:T(2,128)}, u32[]{:S(2)}) copy-start(f32[32,2,128]{2,1,0:T(2,128)} %param.11) | copy-start | bytes 98308
  9.2 0.7 %copy-start.4 = (f32[32,128]{1,0:T(8,128)S(1)}, f32[32,128]{1,0:T(8,128)}, u32[]{:S(2)}) copy-start(f32[32,128]{1,0:T(8,128)} %ten_ref.1) | copy-start | bytes 49156
  9.9 0.7 copy-start.5
  11.3 0.7 copy-start.7
  12.6 0.8 %copy-start.10 = (f32[128,128]{1,0:T(8,128)S(1)}, f32[128,128]{1,0:T(8,128)}, u32[]{:S(2)}) copy-start(f32[128,128]{1,0:T(8,128)} %constant.25.clone.deriv_ref) | copy-start | bytes 196612
  13.4 0.8 %copy-start.11 = (f32[128,128]{1,0:T(8,128)S(1)}, f32[128,128]{1,0:T(8,128)}, u32[]{:S(2)}) copy-start(f32[128,128]{1,0:T(8,128)} %constant.26.clone.table_ref) | copy-start | bytes 196612
  15.3 29.0 %collective-permute-start = (f32[8,640]{1,0:T(8,128)S(1)}, f32[8,640]{1,0:T(8,128)S(1)}, u32[]{:S(2)}, u32[]{:S(2)}) collective-permute-start(f32[8,640]{1,0:T(8,128)S(1)} %get-tuple-element.17), channel_id=1, source_target_pairs={{0,4},{4,8},{8,12},{12,16},{16,20},{20,24},{24,28},{28,0},{1,5},{5... | collective-permute-start | bytes 61448 | tf_op jit(solution)/shard_map/ppermute | solution.py:290
  15.3 30.5 %collective-permute-start.1 = (f32[8,640]{1,0:T(8,128)S(1)}, f32[8,640]{1,0:T(8,128)S(1)}, u32[]{:S(2)}, u32[]{:S(2)}) collective-permute-start(f32[8,640]{1,0:T(8,128)S(1)} %get-tuple-element.18), channel_id=1, source_target_pairs={{0,8},{4,12},{8,16},{12,20},{16,24},{20,28},{24,0},{28,4},{1,9},{5... | collective-permute-start | bytes 61448 | tf_op jit(solution)/shard_map/ppermute | solution.py:290
  16.8 2.2 %collective-permute-start.10 = (bf16[80,512]{1,0:T(8,128)(2,1)S(1)}, bf16[80,512]{1,0:T(8,128)(2,1)S(1)}, u32[]{:S(2)}, u32[]{:S(2)}) collective-permute-start(bf16[80,512]{1,0:T(8,128)(2,1)S(1)} %collective-permute-done.9.refs_2_), channel_id=1, source_target_pairs={{0,4},{4,0},{8,12},{12,8},{16,20},{20,16},{24,28},{28,24},{1,5},{5... | collective-permute-start | bytes 245768 | tf_op jit(solution)/shard_map/ppermute | solution.py:275
  18.1 1.3 %collective-permute-start.12 = (bf16[80,512]{1,0:T(8,128)(2,1)S(1)}, bf16[80,512]{1,0:T(8,128)(2,1)S(1)}, u32[]{:S(2)}, u32[]{:S(2)}) collective-permute-start(bf16[80,512]{1,0:T(8,128)(2,1)S(1)} %collective-permute-done.11.refs_4_), channel_id=1, source_target_pairs={{0,4},{4,0},{8,12},{12,8},{16,20},{20,16},{24,28},{28,24},{1,5},{5... | collective-permute-start | bytes 245768 | tf_op jit(solution)/shard_map/ppermute | solution.py:275
  18.2 1.4 %collective-permute-start.8 = (bf16[80,512]{1,0:T(8,128)(2,1)S(1)}, bf16[80,512]{1,0:T(8,128)(2,1)S(1)}, u32[]{:S(2)}, u32[]{:S(2)}) collective-permute-start(bf16[80,512]{1,0:T(8,128)(2,1)S(1)} %collective-permute-done.7.refs_0_), channel_id=1, source_target_pairs={{0,4},{4,0},{8,12},{12,8},{16,20},{20,16},{24,28},{28,24},{1,5},{5... | collective-permute-start | bytes 245768 | tf_op jit(solution)/shard_map/ppermute | solution.py:275
  19.5 0.9 %copy-start = (bf16[128,512]{1,0:T(8,128)(2,1)S(1)}, bf16[128,512]{1,0:T(8,128)(2,1)}, u32[]{:S(2)}) copy-start(bf16[128,512]{1,0:T(8,128)(2,1)} %own_ref.1) | copy-start | bytes 393220
  20.4 0.7 copy-start.1
  21.1 0.8 %copy-start.3 = (f32[32,2,128]{2,1,0:T(2,128)S(1)}, f32[32,2,128]{2,1,0:T(2,128)}, u32[]{:S(2)}) copy-start(f32[32,2,128]{2,1,0:T(2,128)} %param.11) | copy-start | bytes 98308
  41.3 4.5 %collective-permute-start.13 = (f32[32,128]{1,0:T(8,128)S(1)}, f32[32,128]{1,0:T(8,128)S(1)}, u32[]{:S(2)}, u32[]{:S(2)}) collective-permute-start(f32[32,128]{1,0:T(8,128)S(1)} %get-tuple-element.24), channel_id=1, source_target_pairs={{0,4},{4,8},{8,12},{12,16},{16,20},{20,24},{24,28},{28,0},{1,5},{5... | collective-permute-start | bytes 49160 | tf_op jit(solution)/shard_map/ppermute | solution.py:318
  41.7 5.6 %collective-permute-start.14 = (f32[32,128]{1,0:T(8,128)S(1)}, f32[32,128]{1,0:T(8,128)S(1)}, u32[]{:S(2)}, u32[]{:S(2)}) collective-permute-start(f32[32,128]{1,0:T(8,128)S(1)} %get-tuple-element.24), channel_id=1, source_target_pairs={{0,8},{4,12},{8,16},{12,20},{16,24},{20,28},{24,0},{28,4},{1,9},{5... | collective-permute-start | bytes 49160 | tf_op jit(solution)/shard_map/ppermute | solution.py:318
  43.2 5.5 %collective-permute-start.15 = (f32[32,128]{1,0:T(8,128)S(1)}, f32[32,128]{1,0:T(8,128)S(1)}, u32[]{:S(2)}, u32[]{:S(2)}) collective-permute-start(f32[32,128]{1,0:T(8,128)S(1)} %get-tuple-element.24), channel_id=1, source_target_pairs={{0,12},{4,16},{8,20},{12,24},{16,28},{20,0},{24,4},{28,8},{1,13},{... | collective-permute-start | bytes 49160 | tf_op jit(solution)/shard_map/ppermute | solution.py:318
  44.3 4.5 %collective-permute-start.16 = (f32[32,128]{1,0:T(8,128)S(1)}, f32[32,128]{1,0:T(8,128)S(1)}, u32[]{:S(2)}, u32[]{:S(2)}) collective-permute-start(f32[32,128]{1,0:T(8,128)S(1)} %get-tuple-element.24), channel_id=1, source_target_pairs={{0,16},{4,20},{8,24},{12,28},{16,0},{20,4},{24,8},{28,12},{1,17},{... | collective-permute-start | bytes 49160 | tf_op jit(solution)/shard_map/ppermute | solution.py:318
  45.8 4.4 %collective-permute-start.17 = (f32[32,128]{1,0:T(8,128)S(1)}, f32[32,128]{1,0:T(8,128)S(1)}, u32[]{:S(2)}, u32[]{:S(2)}) collective-permute-start(f32[32,128]{1,0:T(8,128)S(1)} %get-tuple-element.24), channel_id=1, source_target_pairs={{0,20},{4,24},{8,28},{12,0},{16,4},{20,8},{24,12},{28,16},{1,21},{... | collective-permute-start | bytes 49160 | tf_op jit(solution)/shard_map/ppermute | solution.py:318
  45.8 5.8 %collective-permute-start.18 = (f32[32,128]{1,0:T(8,128)S(1)}, f32[32,128]{1,0:T(8,128)S(1)}, u32[]{:S(2)}, u32[]{:S(2)}) collective-permute-start(f32[32,128]{1,0:T(8,128)S(1)} %get-tuple-element.24), channel_id=1, source_target_pairs={{0,24},{4,28},{8,0},{12,4},{16,8},{20,12},{24,16},{28,20},{1,25},{... | collective-permute-start | bytes 49160 | tf_op jit(solution)/shard_map/ppermute | solution.py:318
  47.3 4.9 %collective-permute-start.19 = (f32[32,128]{1,0:T(8,128)S(1)}, f32[32,128]{1,0:T(8,128)S(1)}, u32[]{:S(2)}, u32[]{:S(2)}) collective-permute-start(f32[32,128]{1,0:T(8,128)S(1)} %get-tuple-element.24), channel_id=1, source_target_pairs={{0,28},{4,0},{8,4},{12,8},{16,12},{20,16},{24,20},{28,24},{1,29},{... | collective-permute-start | bytes 49160 | tf_op jit(solution)/shard_map/ppermute | solution.py:318
  48.7 4.6 %collective-permute-start.2 = (f32[8,640]{1,0:T(8,128)S(1)}, f32[8,640]{1,0:T(8,128)S(1)}, u32[]{:S(2)}, u32[]{:S(2)}) collective-permute-start(f32[8,640]{1,0:T(8,128)S(1)} %get-tuple-element.19), channel_id=1, source_target_pairs={{0,12},{4,16},{8,20},{12,24},{16,28},{20,0},{24,4},{28,8},{1,13},{... | collective-permute-start | bytes 61448 | tf_op jit(solution)/shard_map/ppermute | solution.py:290
  48.8 6.2 %collective-permute-start.3 = (f32[8,640]{1,0:T(8,128)S(1)}, f32[8,640]{1,0:T(8,128)S(1)}, u32[]{:S(2)}, u32[]{:S(2)}) collective-permute-start(f32[8,640]{1,0:T(8,128)S(1)} %get-tuple-element.20), channel_id=1, source_target_pairs={{0,16},{4,20},{8,24},{12,28},{16,0},{20,4},{24,8},{28,12},{1,17},{... | collective-permute-start | bytes 61448 | tf_op jit(solution)/shard_map/ppermute | solution.py:290
  50.2 6.8 %collective-permute-start.4 = (f32[8,640]{1,0:T(8,128)S(1)}, f32[8,640]{1,0:T(8,128)S(1)}, u32[]{:S(2)}, u32[]{:S(2)}) collective-permute-start(f32[8,640]{1,0:T(8,128)S(1)} %get-tuple-element.21), channel_id=1, source_target_pairs={{0,20},{4,24},{8,28},{12,0},{16,4},{20,8},{24,12},{28,16},{1,21},{... | collective-permute-start | bytes 61448 | tf_op jit(solution)/shard_map/ppermute | solution.py:290
  51.6 5.7 %collective-permute-start.5 = (f32[8,640]{1,0:T(8,128)S(1)}, f32[8,640]{1,0:T(8,128)S(1)}, u32[]{:S(2)}, u32[]{:S(2)}) collective-permute-start(f32[8,640]{1,0:T(8,128)S(1)} %get-tuple-element.22), channel_id=1, source_target_pairs={{0,24},{4,28},{8,0},{12,4},{16,8},{20,12},{24,16},{28,20},{1,25},{... | collective-permute-start | bytes 61448 | tf_op jit(solution)/shard_map/ppermute | solution.py:290
  52.2 5.2 %collective-permute-start.6 = (f32[8,640]{1,0:T(8,128)S(1)}, f32[8,640]{1,0:T(8,128)S(1)}, u32[]{:S(2)}, u32[]{:S(2)}) collective-permute-start(f32[8,640]{1,0:T(8,128)S(1)} %get-tuple-element.23), channel_id=1, source_target_pairs={{0,28},{4,0},{8,4},{12,8},{16,12},{20,16},{24,20},{28,24},{1,29},{... | collective-permute-start | bytes 61448 | tf_op jit(solution)/shard_map/ppermute | solution.py:290
  53.3 10.3 %collective-permute-start.20 = (f32[32,128]{1,0:T(8,128)S(1)}, f32[32,128]{1,0:T(8,128)S(1)}, u32[]{:S(2)}, u32[]{:S(2)}) collective-permute-start(f32[32,128]{1,0:T(8,128)S(1)} %add_add_fusion.refs_0_), channel_id=1, source_target_pairs={{0,1},{1,2},{2,3},{3,0},{4,5},{5,6},{6,7},{7,4},{8,9},{9,10},{10,1... | collective-permute-start | bytes 49160 | tf_op jit(solution)/shard_map/ppermute | solution.py:321
  54.9 8.7 %collective-permute-start.21 = (f32[32,128]{1,0:T(8,128)S(1)}, f32[32,128]{1,0:T(8,128)S(1)}, u32[]{:S(2)}, u32[]{:S(2)}) collective-permute-start(f32[32,128]{1,0:T(8,128)S(1)} %add_add_fusion.refs_0_), channel_id=1, source_target_pairs={{0,2},{1,3},{2,0},{3,1},{4,6},{5,7},{6,4},{7,5},{8,10},{9,11},{10,... | collective-permute-start | bytes 49160 | tf_op jit(solution)/shard_map/ppermute | solution.py:321
  57.1 6.5 %collective-permute-start.22 = (f32[32,128]{1,0:T(8,128)S(1)}, f32[32,128]{1,0:T(8,128)S(1)}, u32[]{:S(2)}, u32[]{:S(2)}) collective-permute-start(f32[32,128]{1,0:T(8,128)S(1)} %add_add_fusion.refs_0_), channel_id=1, source_target_pairs={{0,3},{1,0},{2,1},{3,2},{4,7},{5,4},{6,5},{7,6},{8,11},{9,8},{10,9... | collective-permute-start | bytes 49160 | tf_op jit(solution)/shard_map/ppermute | solution.py:321
  (3 other events, 2.0 us)

commit v2 on v1

--- a/solution.py
+++ b/solution.py
@@ -44,12 +44,29 @@
 
 
 def reciprocal(x):
-    r = pl.reciprocal(x, approx=True)
-    return r * (2.0 - x * r)
-
-
-def force_kernel(clu_count, slot_cap, clu_ref, pos_ref, ten_ref, bend_ref, order_ref, dest_ref,
-                 target_ref, deriv_ref, table_ref, force_ref, *piece_refs):
+    return pl.reciprocal(x, approx=True)
+
+
+def fetch(sources, targets, sems):
+    copies = [pltpu.make_async_copy(s, t, sems.at[i])
+              for i, (s, t) in enumerate(zip(sources, targets))]
+    for copy in copies:
+        copy.start()
+    for copy in copies:
+        copy.wait()
+
+
+def force_kernel(clu_count, *refs):
+    sources, targets, sems = refs[:10], refs[13:23], refs[23]
+    sent_ref, force_ref, packed_ref = refs[10:13]
+    fetch(sources, targets, sems)
+    (own_ref, nodes_ref, pos_ref, ten_ref, bend_ref, order_ref, dest_ref, target_ref, deriv_ref,
+     table_ref) = targets
+    half = own_ref.shape[0] // 2
+    core = lax.rem(lax.axis_index("clu"), 2)
+    sent_ref[0:half] = own_ref[pl.ds(pl.multiple_of(core * half, half), half), :]
+    spots = jnp.concatenate([nodes_ref[...].astype(F32)] * 8, axis=0)
+    sent_ref[half:half + 16] = spots.astype(BF16)
     vesicles = ten_ref.shape[0]
     moves = target_ref.shape[1]
     x = pos_ref[pl.ds(0, vesicles, stride=2), :]
@@ -68,11 +85,10 @@
     force_ref[pl.ds(1, vesicles, stride=2), :] = force_y
 
     slots = clu_count * BLOCK
-    relative = lax.rem(dest_ref[...] - clu_ref[0] + clu_count, clu_count)
-    hot = (iota((clu_count, moves), 0) == relative).astype(F32)
+    hot = (iota((clu_count, moves), 0) == dest_ref[...]).astype(F32)
     earlier = (iota((moves, moves), 0) < iota((moves, moves), 1)).astype(F32)
     rank = jnp.sum(dot(hot, earlier) * hot, axis=0, keepdims=True).astype(jnp.int32)
-    slot = relative * BLOCK + rank
+    slot = dest_ref[...] * BLOCK + rank
     pack = (iota((slots, moves), 0) == slot).astype(F32)
     pick = (iota((vesicles, moves), 0) == order_ref[:, :moves]).astype(F32)
     select = dot(pack, pick, NT)
@@ -80,18 +96,13 @@
     packed = dot(select, carried, precision=HIGHEST)
     tag = jnp.sum(pack * (target_ref[...] + 1).astype(F32), axis=1, keepdims=True)
     tag = jnp.broadcast_to(tag, (slots, x.shape[1]))
-    for k in range(clu_count):
-        here = slice(k * BLOCK, (k + 1) * BLOCK)
-        piece_refs[k][...] = jnp.concatenate([packed[here], tag[here]], axis=1)
-
-
-def near_kernel(clu_count, slot_cap, pos_ref, *refs):
-    piece_refs, near_ref, arrived, aim_x, aim_y, speed_x, speed_y = (
-        refs[:clu_count], *refs[clu_count:])
+    packed = jnp.concatenate([packed, tag], axis=1)
+    packed_ref[...] = packed.reshape(clu_count, BLOCK, packed.shape[1])
+
+
+def near_kernel(clu_count, slot_cap, pos_ref, arrived, near_ref, aim_x, aim_y, speed_x, speed_y):
     vesicles = pos_ref.shape[0] // 2
     nodes = pos_ref.shape[1]
-    for k in range(clu_count):
-        arrived[k] = piece_refs[k][...]
     slots = clu_count * BLOCK
     tag = arrived[:, :, 4 * nodes:].reshape(slots, nodes)[:, :vesicles]
     hot = (tag == (iota((slots, vesicles), 1) + 1).astype(F32)).astype(F32)
@@ -128,18 +139,20 @@
         turned_hot, speed_y[...].reshape(slots, nodes), precision=HIGHEST) / nodes
 
 
-def far_kernel(col_count, index_ref, range_ref, pos_ref, own_ref, nodes_ref, *refs):
+def far_kernel(col_count, range_in, pos_in, own_in, nodes_in, _, *refs):
     count = 2 * (col_count - 1)
-    piece_refs, (high_ref, low_ref, gram_ref, basis, spots, wide) = refs[:count], refs[count:]
+    piece_refs = refs[:count]
+    (high_ref, low_ref, gram_ref, range_ref, pos_ref, own_nodes, basis, spots, wide, buffer,
+     sums, sems) = refs[count:]
     vesicles = pos_ref.shape[0] // 2
     nodes = pos_ref.shape[1]
-    rows, sources = own_ref.shape
+    _, rows, sources = basis.shape
     half, rank = rows // 2, rows // 2
-    core, col = index_ref[0], index_ref[1]
-    basis[col] = own_ref[...]
-    spots[col, 0:2] = nodes_ref[...].astype(F32)
+    core, col = lax.rem(lax.axis_index("clu"), 2), lax.axis_index("col")
+    fetch([range_in, pos_in, nodes_in, own_in], [range_ref, pos_ref, own_nodes, basis.at[col]], sems)
+    spots[col, 0:2] = own_nodes[...].astype(F32)
     for k in range(1, col_count):
-        where = lax.rem(col - k + col_count, col_count)
+        where = origin(col, k, col_count)
         mine, other = piece_refs[2 * k - 2], piece_refs[2 * k - 1]
         basis[where, pl.ds(pl.multiple_of(core * half, half), half), :] = mine[0:half]
         basis[where, pl.ds(pl.multiple_of((1 - core) * half, half), half), :] = other[0:half]
@@ -148,14 +161,13 @@
         turned = spots[r].T
         for c in range(2):
             wide[r, c] = jnp.broadcast_to(turned[:, c:c + 1], (sources, nodes))
-    gram_ref[...] = jnp.zeros_like(gram_ref)
-    chunk = 256 if sources % 256 == 0 else sources
-
-    def vesicle(v, total):
-        r = range_ref[v]
+    sums[...] = jnp.zeros_like(sums)
+    chunk = 128 if sources % 128 == 0 else sources
+
+    def evaluate(v, slot):
+        r = range_ref[0, v]
         tx = pos_ref[pl.ds(2 * v, 1), :]
         ty = pos_ref[pl.ds(2 * v + 1, 1), :]
-        product = None
         for start in range(0, sources, chunk):
             dx = tx - wide[r, 0, start:start + chunk]
             dy = ty - wide[r, 1, start:start + chunk]
@@ -163,11 +175,13 @@
             log_part = -0.5 * jnp.log(spread)
             inverse = reciprocal(spread)
             dxr = dx * inverse
-            ff = (log_part + dx * dxr).astype(BF16)
-            fs = (dy * dxr).astype(BF16)
-            ss = (log_part + dy * (dy * inverse)).astype(BF16)
-            part = dot(basis[r, :, start:start + chunk], jnp.concatenate([ff, fs, ss], axis=1))
-            product = part if product is None else product + part
+            here = slice(start, start + chunk)
+            buffer[slot, here, 0:nodes] = (log_part + dx * dxr).astype(BF16)
+            buffer[slot, here, nodes:2 * nodes] = (dy * dxr).astype(BF16)
+            buffer[slot, here, 2 * nodes:] = (log_part + dy * (dy * inverse)).astype(BF16)
+
+    def multiply(v, slot):
+        product = dot(basis[range_ref[0, v]], buffer[slot])
         first = product[:rank, :nodes] + product[rank:, nodes:2 * nodes]
         second = product[:rank, nodes:2 * nodes] + product[rank:, 2 * nodes:]
         high_0, high_1 = first.astype(BF16), second.astype(BF16)
@@ -178,9 +192,20 @@
         both = jnp.concatenate([
             jnp.concatenate([high_0, high_1], axis=1),
             jnp.concatenate([low_0, low_1], axis=1)], axis=0)
-        return total + dot(both, both, NT)
-
-    total = lax.fori_loop(0, vesicles, vesicle, jnp.zeros((2 * rank, 2 * rank), F32))
+        sums[...] += dot(both, both, NT)
+
+    evaluate(0, 0)
+
+    def pair(i, _):
+        v = 2 * i
+        evaluate(v + 1, 1)
+        multiply(v, 0)
+        evaluate(jnp.minimum(v + 2, vesicles - 1), 0)
+        multiply(v + 1, 1)
+        return 0
+
+    lax.fori_loop(0, vesicles // 2, pair, 0)
+    total = sums[...]
     gram = total[:rank, :rank] + total[rank:, rank:] + (total[:rank, rank:] + total[rank:, :rank])
     gram_ref[...] = jnp.concatenate([gram[:rank // 2], gram[rank // 2:]], axis=1)
 
@@ -212,16 +237,13 @@
     return jnp.concatenate(done, axis=0)[:, size:]
 
 
-def basis_kernel(col_count, scale_factor, *refs):
-    gram_refs = refs[:col_count]
-    high_ref, low_ref, out_ref, weight = refs[col_count:]
+def basis_kernel(scale_factor, *refs):
+    gram_ref, high_ref, low_ref, out_ref, weight = refs
     rank = high_ref.shape[1] // 2
 
     @pl.when(pl.program_id(0) == 0)
     def _():
-        folded = gram_refs[0][...]
-        for g in gram_refs[1:]:
-            folded = folded + g[...]
+        folded = gram_ref[...]
         gram = jnp.concatenate([folded[:, :rank], folded[:, rank:]], axis=0)
         inverse = lower_inverse(gram) * scale_factor
         turn = iota((2 * rank, rank), 0) - 2 * iota((2 * rank, rank), 1)
@@ -241,16 +263,40 @@
     return pl.BlockSpec(memory_space=pltpu.VMEM)
 
 
-def scalar_spec():
-    return pl.BlockSpec(memory_space=pltpu.SMEM)
+def far_off_spec():
+    return pl.BlockSpec(memory_space=pltpu.HBM)
 
 
 def params(mib):
     return pltpu.CompilerParams(vmem_limit_bytes=mib * MIB)
 
 
-def shifts(count, by):
-    return [(i, (i + by) % count) for i in range(count)]
+def power_of_two(count):
+    return count & (count - 1) == 0
+
+
+def partners(count, step):
+    if power_of_two(count):
+        return [(i, i ^ step) for i in range(count)]
+    return [(i, (i + step) % count) for i in range(count)]
+
+
+def origin(index, step, count):
+    if power_of_two(count):
+        return jnp.bitwise_xor(index, step)
+    return lax.rem(index - step + count, count)
+
+
+def sum_over(value, axis):
+    count = lax.axis_size(axis)
+    if power_of_two(count):
+        step = 1
+        while step < count:
+            value = value + lax.ppermute(value, axis, partners(count, step))
+            step *= 2
+        return value
+    moved = [lax.ppermute(value, axis, partners(count, k)) for k in range(1, count)]
+    return sum(moved, value)
 
 
 def per_device(positions, tension, bending, moved_order, move_destination, move_target, far_range,
@@ -261,78 +307,77 @@
     clu_count, col_count = lax.axis_size("clu"), lax.axis_size("col")
     moves = move_target.shape[0]
     slot_cap = 2 * ((moves + clu_count - 1) // clu_count)
-    clu, col = lax.axis_index("clu"), lax.axis_index("col")
-    core = lax.rem(clu, 2)
     flat = positions.reshape(2 * vesicles, nodes)
 
-    half_rows = lax.dynamic_slice_in_dim(old_basis, core * rank, rank, 0)
-    sent = jnp.concatenate(
-        [half_rows, source_nodes, jnp.zeros((14, sources), old_basis.dtype)], axis=0)
-    swap = [(i, i ^ 1) for i in range(clu_count)]
-    pieces = []
-    for k in range(1, col_count):
-        mine = lax.ppermute(sent, "col", shifts(col_count, k))
-        pieces += [mine, lax.ppermute(mine, "clu", swap)]
-
     deriv, table = spectral_tables(nodes)
-    force_out = pl.pallas_call(
-        functools.partial(force_kernel, clu_count, slot_cap),
-        out_shape=[jax.ShapeDtypeStruct((2 * vesicles, nodes), F32)]
-        + [jax.ShapeDtypeStruct((BLOCK, 5 * nodes), F32)] * clu_count,
-        in_specs=[scalar_spec()] + [whole_spec()] * 8,
-        out_specs=[whole_spec()] * (1 + clu_count),
+    operands = [old_basis, source_nodes, flat, tension, bending.reshape(1, vesicles), moved_order,
+                move_destination.reshape(1, moves), move_target.reshape(1, moves),
+                jnp.asarray(deriv), jnp.asarray(table)]
+    operands = [pltpu.with_memory_space_constraint(o, pltpu.HBM) for o in operands]
+    sent, force, packed = pl.pallas_call(
+        functools.partial(force_kernel, clu_count),
+        out_shape=[jax.ShapeDtypeStruct((rank + 16, sources), BF16),
+                   jax.ShapeDtypeStruct((2 * vesicles, nodes), F32),
+                   jax.ShapeDtypeStruct((clu_count, BLOCK, 5 * nodes), F32)],
+        in_specs=[far_off_spec()] * len(operands),
+        out_specs=[whole_spec()] * 3,
+        scratch_shapes=[pltpu.VMEM(o.shape, o.dtype) for o in operands]
+        + [pltpu.SemaphoreType.DMA((len(operands),))],
         compiler_params=params(16),
         cost_estimate=pl.CostEstimate(flops=10**8, bytes_accessed=10**6, transcendentals=0),
-    )(clu.reshape(1), flat, tension, bending.reshape(1, vesicles), moved_order,
-      move_destination.reshape(1, moves), move_target.reshape(1, moves), deriv, table)
-    force, packed = force_out[0], force_out[1:]
-    arrived = [packed[0]] + [
-        lax.ppermute(packed[k], "clu", shifts(clu_count, k)) for k in range(1, clu_count)]
+    )(*operands)
+
+    moved_halves = [lax.ppermute(sent, "col", partners(col_count, k)) for k in range(1, col_count)]
+    arrived = lax.all_to_all(packed, "clu", split_axis=0, concat_axis=0, tiled=True)
+    pieces = []
+    for mine in moved_halves:
+        pieces += [mine, lax.ppermute(mine, "clu", [(i, i ^ 1) for i in range(clu_count)])]
 
     near = pl.pallas_call(
         functools.partial(near_kernel, clu_count, slot_cap),
         out_shape=jax.ShapeDtypeStruct((2 * vesicles, nodes), F32),
-        in_specs=[whole_spec()] * (1 + clu_count),
+        in_specs=[whole_spec()] * 2,
         out_specs=whole_spec(),
-        scratch_shapes=[pltpu.VMEM((clu_count, BLOCK, 5 * nodes), F32)]
-        + [pltpu.VMEM((clu_count, BLOCK, nodes), F32)] * 4,
+        scratch_shapes=[pltpu.VMEM((clu_count, BLOCK, nodes), F32)] * 4,
         compiler_params=params(16),
         cost_estimate=pl.CostEstimate(flops=10**9, bytes_accessed=10**7, transcendentals=10**6),
-    )(flat, *arrived)
+    )(flat, arrived)
 
     high, low, gram = pl.pallas_call(
         functools.partial(far_kernel, col_count),
         out_shape=[jax.ShapeDtypeStruct((vesicles, rows, nodes), BF16)] * 2
         + [jax.ShapeDtypeStruct((rank // 2, 2 * rank), F32)],
-        in_specs=[scalar_spec()] * 2 + [whole_spec()] * (3 + 2 * (col_count - 1)),
+        in_specs=[far_off_spec()] * 5 + [whole_spec()] * (2 * (col_count - 1)),
         out_specs=[whole_spec()] * 3,
         scratch_shapes=[
+            pltpu.SMEM((1, vesicles), jnp.int32),
+            pltpu.VMEM((2 * vesicles, nodes), F32),
+            pltpu.VMEM((2, sources), BF16),
             pltpu.VMEM((col_count, rows, sources), BF16),
             pltpu.VMEM((col_count, 8, sources), F32),
-            pltpu.VMEM((col_count, 2, sources, nodes), F32)],
+            pltpu.VMEM((col_count, 2, sources, nodes), F32),
+            pltpu.VMEM((2, sources, 3 * nodes), BF16),
+            pltpu.VMEM((rows, rows), F32),
+            pltpu.SemaphoreType.DMA((4,))],
         compiler_params=params(32),
         cost_estimate=pl.CostEstimate(flops=10**10, bytes_accessed=10**7, transcendentals=10**7),
-    )(jnp.stack([core, col]), far_range.reshape(vesicles), flat, old_basis, source_nodes, *pieces)
-
-    for k in range(1, clu_count):
-        moved = lax.ppermute(gram, "clu", shifts(clu_count, k))
-        total = moved if k == 1 else total + moved
-    gram = gram + total
-    grams = [gram] + [lax.ppermute(gram, "col", shifts(col_count, k)) for k in range(1, col_count)]
+    )(pltpu.with_memory_space_constraint(far_range.reshape(1, vesicles), pltpu.HBM), operands[2],
+      operands[0], operands[1], arrived, *pieces)
+    gram = sum_over(sum_over(gram, "clu"), "col")
 
     scale_factor = math.sqrt(2.0 * nodes * vesicles * clu_count * col_count)
     group = 8 if vesicles % 8 == 0 else vesicles
     block = pl.BlockSpec((group, rows, nodes), lambda i: (i, 0, 0))
     new_basis = pl.pallas_call(
-        functools.partial(basis_kernel, col_count, scale_factor),
+        functools.partial(basis_kernel, scale_factor),
         out_shape=jax.ShapeDtypeStruct((vesicles, rows, nodes), F32),
         grid=(vesicles // group,),
-        in_specs=[whole_spec()] * col_count + [block] * 2,
+        in_specs=[whole_spec()] + [block] * 2,
         out_specs=block,
         scratch_shapes=[pltpu.VMEM((rows, 3 * rows), BF16)],
         compiler_params=params(16),
         cost_estimate=pl.CostEstimate(flops=10**9, bytes_accessed=10**7, transcendentals=0),
-    )(*grams, high, low)
+    )(gram, high, low)
 
     return (force.reshape(vesicles, 2, nodes), near.reshape(vesicles, 2, nodes),
             new_basis.reshape(vesicles, rank, 2, nodes))

time: 69.3 us -> 60.1 us (0.87)
  waiting for transfers between devices: 0.9 us -> 14.9 us
  starting transfers between devices: 25.4 us -> 15.2 us
  local copies, waits for them, and re-layouts: 9.7 us -> 0.01 us
  Pallas kernels: 31.2 us -> 29 us
  other arithmetic: 0.85 us -> 0.02 us
    ppermute x23 -> x11, starting transfers between devices: 25.4 us -> 11.3 us  [the longest x3 5.76 us: per_device(): lax.ppermute(sent, 'col', partners(col_count, k))]
    ppermute x23 -> x11, waiting for transfers between devices: 0.9 us -> 11.9 us  [the longest x5 10 us: sum_over(): value = value + lax.ppermute(value, axis, partners(count, step))]
    unnamed x24 -> x2, local copies, waits for them, and re-layouts: 8.77 us -> 0.01 us
    all_to_all x0 -> x1, starting transfers between devices: none -> 3.87 us  [per_device(): lax.all_to_all(packed, 'clu', split_axis=0, concat_axis=0, tiled=True)]
    pallas_call x1, Pallas kernels: 18.8 us -> 15.7 us  [per_device(): pl.pallas_call(functools.partial(far_kernel, col_count), out_shape=[jax.S...]
    all_to_all x0 -> x1, waiting for transfers between devices: none -> 3.02 us  [per_device(): lax.all_to_all(packed, 'clu', split_axis=0, concat_axis=0, tiled=True)]
    pallas_call x2, Pallas kernels: 6.15 us -> 7.32 us  [the longest x1 4.87 us: per_device(): pl.pallas_call(functools.partial(basis_kernel, scale_factor), out_shape=j...]
    dynamic_slice x1 -> x0, local copies, waits for them, and re-layouts: 0.85 us -> none  [per_device(): half_rows = lax.dynamic_slice_in_dim(old_basis, core * rank, rank, 0)]
  transfers between devices with their start and end apart: 23 -> 12, of which waited for: 3 -> 6; matrix products, arithmetic and copies ran while one was open for 0% -> 0% of each run, Pallas kernels for 38% -> 10%
where the time goes in v2:
time: 60.1 us; the launch traced here: 59.8 us
  Pallas kernels  29 us (48%)
  starting transfers between devices  15.2 us (25%)
  waiting for transfers between devices  14.9 us (25%)
  between operations  0.68 us (1%)
    pallas_call x1, Pallas kernels, per_device(): pl.pallas_call(functools.partial(far_kernel, col_count), out_shape=[jax.S...  15.7 us
    ppermute x5, waiting for transfers between devices, sum_over(): value = value + lax.ppermute(value, axis, partners(count, step))  10 us
    pallas_call x1, Pallas kernels, per_device(): pl.pallas_call(functools.partial(near_kernel, clu_count, slot_cap), out_s...  6.01 us
    ppermute x3, starting transfers between devices, per_device(): lax.ppermute(sent, 'col', partners(col_count, k))  5.76 us
    pallas_call x1, Pallas kernels, per_device(): pl.pallas_call(functools.partial(basis_kernel, scale_factor), out_shape=j...  4.87 us
    ppermute x5, starting transfers between devices, sum_over(): value = value + lax.ppermute(value, axis, partners(count, step))  4.58 us
    all_to_all x1, starting transfers between devices, per_device(): lax.all_to_all(packed, 'clu', split_axis=0, concat_axis=0, tiled=True)  3.87 us
    all_to_all x1, waiting for transfers between devices, per_device(): lax.all_to_all(packed, 'clu', split_axis=0, concat_axis=0, tiled=True)  3.02 us
  transfers between devices with their start and end apart: 12, of which 6 were waited for; matrix products, arithmetic and copies ran while one was open for 0% of the time, Pallas kernels for 10%

profile of v2, /device:TPU:0, one launch (start us, length us, event | category | flops | bytes accessed | tf_op | source)
XLA Modules:
  0.0 59.8 jit_solution(17466677388967541776)
XLA Ops:
  0.6 2.4 %shard_map.130 = (bf16[80,512]{1,0:T(8,128)(2,1)S(1)}, f32[64,128]{1,0:T(8,128)}, f32[8,8,640]{2,1,0:T(8,128)}) custom-call(bf16[128,512]{1,0:T(8,128)(2,1)} %own_in.1, bf16[2,512]{1,0:T(2,128)(2,1)} %nodes_in.1, f32[64,128]{1,0:T(8,128)} %bitcast.8, f32[32,128]{1,0:T(8,128)} %refs_3_.1, f32[1,32]{1,0:T(1,128)} %bitcast.12, s32[1,32]{1,0:T(1,128)} %refs_5_.1, ...), custom_call_target="tpu_custom_call" | custom-call | flops 100000000 | bytes 1000000 | tf_op jit(solution)/shard_map/pallas_call | solution.py:317
  3.1 5.1 %collective-permute-start.4 = (bf16[80,512]{1,0:T(8,128)(2,1)S(1)}, bf16[80,512]{1,0:T(8,128)(2,1)S(1)}, u32[]{:S(2)}, u32[]{:S(2)}) collective-permute-start(bf16[80,512]{1,0:T(8,128)(2,1)S(1)} %get-tuple-element.11), channel_id=1, source_target_pairs={{0,3},{1,2},{2,1},{3,0},{4,7},{5,6},{6,5},{7,4},{8,11},{9,10},{10,... | collective-permute-start | bytes 245768 | tf_op jit(solution)/shard_map/ppermute | solution.py:330
  8.2 0.0 collective-permute-start.2
  8.2 0.6 %collective-permute-start = (bf16[80,512]{1,0:T(8,128)(2,1)S(1)}, bf16[80,512]{1,0:T(8,128)(2,1)S(1)}, u32[]{:S(2)}, u32[]{:S(2)}) collective-permute-start(bf16[80,512]{1,0:T(8,128)(2,1)S(1)} %get-tuple-element.11), channel_id=1, source_target_pairs={{0,1},{1,0},{2,3},{3,2},{4,5},{5,4},{6,7},{7,6},{8,9},{9,8},{10,11... | collective-permute-start | bytes 245768 | tf_op jit(solution)/shard_map/ppermute | solution.py:330
  8.8 3.9 %all-to-all-start = ((f32[8,8,640]{2,1,0:T(8,128)}), f32[8,8,640]{2,1,0:T(8,128)S(1)}, u32[]{:S(2)}, u32[]{:S(2)}) async-start(f32[8,8,640]{2,1,0:T(8,128)} %get-tuple-element.10), calls=%async_computation | async-start | bytes 327680 | tf_op jit(solution)/shard_map/all_to_all | solution.py:331
  12.7 0.0 collective-permute-done.4.refs_4_
  12.7 0.5 collective-permute-start.5
  13.2 1.8 %collective-permute-done.2.refs_2_ = bf16[80,512]{1,0:T(8,128)(2,1)S(1)} collective-permute-done((bf16[80,512]{1,0:T(8,128)(2,1)S(1)}, bf16[80,512]{1,0:T(8,128)(2,1)S(1)}, u32[]{:S(2)}, u32[]{:S(2)}) %collective-permute-start.2) | collective-permute-done | bytes 81952 | tf_op jit(solution)/shard_map/ppermute | solution.py:330
  15.1 0.0 collective-permute-start.3
  15.1 0.0 collective-permute-done.refs_0_
  15.1 0.5 collective-permute-start.1
  15.6 3.0 %all-to-all-done.arrived._ = f32[8,8,640]{2,1,0:T(8,128)S(1)} async-done(((f32[8,8,640]{2,1,0:T(8,128)}), f32[8,8,640]{2,1,0:T(8,128)S(1)}, u32[]{:S(2)}, u32[]{:S(2)}) %all-to-all-start) | async-done | bytes 163872 | tf_op jit(solution)/shard_map/all_to_all | solution.py:331
  18.6 0.0 collective-permute-done.5.refs_5_
  18.6 0.0 collective-permute-done.3.refs_3_
  18.6 0.0 collective-permute-done.1.refs_1_
  18.6 0.0 copy-start
  18.6 15.7 %shard_map.132 = (bf16[32,128,128]{2,1,0:T(8,128)(2,1)S(1)}, bf16[32,128,128]{2,1,0:T(8,128)(2,1)S(1)}, f32[32,128]{1,0:T(8,128)S(1)}) custom-call(s32[1,32]{1,0:T(1,128)} %bitcast.15, f32[64,128]{1,0:T(8,128)} %bitcast.9, bf16[128,512]{1,0:T(8,128)(2,1)} %own_in.1, bf16[2,512]{1,0:T(2,128)(2,1)} %nodes_in.1, f32[8,8,640]{2,1,0:T(8,128)S(1)} %all-to-all-done.arrived._, ...), custom_call_target="tpu_custom_call" | custom-call | flops 10000000000 | bytes 10000000 | tf_op jit(solution)/shard_map/pallas_call | solution.py:346
  34.3 0.1 collective-permute-start.6
  34.4 1.2 %collective-permute-done.6 = f32[32,128]{1,0:T(8,128)S(1)} collective-permute-done((f32[32,128]{1,0:T(8,128)S(1)}, f32[32,128]{1,0:T(8,128)S(1)}, u32[]{:S(2)}, u32[]{:S(2)}) %collective-permute-start.6) | collective-permute-done | bytes 16416 | tf_op jit(solution)/shard_map/ppermute | solution.py:295
  35.6 0.6 collective-permute-start.7
  36.1 3.2 %collective-permute-done.7 = f32[32,128]{1,0:T(8,128)S(1)} collective-permute-done((f32[32,128]{1,0:T(8,128)S(1)}, f32[32,128]{1,0:T(8,128)S(1)}, u32[]{:S(2)}, u32[]{:S(2)}) %collective-permute-start.7) | collective-permute-done | bytes 16416 | tf_op jit(solution)/shard_map/ppermute | solution.py:295
  39.3 0.6 collective-permute-start.8
  39.9 3.2 %collective-permute-done.8 = f32[32,128]{1,0:T(8,128)S(1)} collective-permute-done((f32[32,128]{1,0:T(8,128)S(1)}, f32[32,128]{1,0:T(8,128)S(1)}, u32[]{:S(2)}, u32[]{:S(2)}) %collective-permute-start.8) | collective-permute-done | bytes 16416 | tf_op jit(solution)/shard_map/ppermute | solution.py:295
  43.0 1.2 %collective-permute-start.9 = (f32[32,128]{1,0:T(8,128)S(1)}, f32[32,128]{1,0:T(8,128)S(1)}, u32[]{:S(2)}, u32[]{:S(2)}) collective-permute-start(f32[32,128]{1,0:T(8,128)S(1)} %add.17), channel_id=1, source_target_pairs={{0,1},{1,0},{2,3},{3,2},{4,5},{5,4},{6,7},{7,6},{8,9},{9,8},{10,11... | collective-permute-start | bytes 49160 | tf_op jit(solution)/shard_map/ppermute | solution.py:295
  44.3 2.5 %collective-permute-done.9 = f32[32,128]{1,0:T(8,128)S(1)} collective-permute-done((f32[32,128]{1,0:T(8,128)S(1)}, f32[32,128]{1,0:T(8,128)S(1)}, u32[]{:S(2)}, u32[]{:S(2)}) %collective-permute-start.9) | collective-permute-done | bytes 16416 | tf_op jit(solution)/shard_map/ppermute | solution.py:295
  46.8 2.1 %collective-permute-start.10 = (f32[32,128]{1,0:T(8,128)S(1)}, f32[32,128]{1,0:T(8,128)S(1)}, u32[]{:S(2)}, u32[]{:S(2)}) collective-permute-start(f32[32,128]{1,0:T(8,128)S(1)} %add.18), channel_id=1, source_target_pairs={{0,2},{1,3},{2,0},{3,1},{4,6},{5,7},{6,4},{7,5},{8,10},{9,11},{10,... | collective-permute-start | bytes 49160 | tf_op jit(solution)/shard_map/ppermute | solution.py:295
  48.9 0.0 copy-done
  48.9 6.0 %shard_map.131 = f32[64,128]{1,0:T(8,128)} custom-call(f32[64,128]{1,0:T(8,128)S(1)} %bitcast.10, f32[8,8,640]{2,1,0:T(8,128)S(1)} %all-to-all-done.arrived._), custom_call_target="tpu_custom_call" | custom-call | flops 1000000000 | bytes 10000000 | tf_op jit(solution)/shard_map/pallas_call | solution.py:336
  54.9 0.0 collective-permute-done.10
  55.0 4.9 %shard_map.133 = f32[32,128,128]{2,1,0:T(8,128)} custom-call(f32[32,128]{1,0:T(8,128)S(1)} %add.19.refs_0_, bf16[32,128,128]{2,1,0:T(8,128)(2,1)S(1)} %get-tuple-element.13.refs_1_, bf16[32,128,128]{2,1,0:T(8,128)(2,1)S(1)} %get-tuple-element.14.refs_2_), custom_call_target="tpu_custom_call" | custom-call | flops 1000000000 | bytes 10000000 | tf_op jit(solution)/shard_map/pallas_call | solution.py:371
  (5 shorter events, 0.0 us)
Async XLA Ops:
  3.1 9.6 %collective-permute-start.4 = (bf16[80,512]{1,0:T(8,128)(2,1)S(1)}, bf16[80,512]{1,0:T(8,128)(2,1)S(1)}, u32[]{:S(2)}, u32[]{:S(2)}) collective-permute-start(bf16[80,512]{1,0:T(8,128)(2,1)S(1)} %get-tuple-element.11), channel_id=1, source_target_pairs={{0,3},{1,2},{2,1},{3,0},{4,7},{5,6},{6,5},{7,4},{8,11},{9,10},{10,... | collective-permute-start | bytes 245768 | tf_op jit(solution)/shard_map/ppermute | solution.py:330
  8.2 6.9 %collective-permute-start.2 = (bf16[80,512]{1,0:T(8,128)(2,1)S(1)}, bf16[80,512]{1,0:T(8,128)(2,1)S(1)}, u32[]{:S(2)}, u32[]{:S(2)}) collective-permute-start(bf16[80,512]{1,0:T(8,128)(2,1)S(1)} %get-tuple-element.11), channel_id=1, source_target_pairs={{0,2},{1,3},{2,0},{3,1},{4,6},{5,7},{6,4},{7,5},{8,10},{9,11},{10,... | collective-permute-start | bytes 245768 | tf_op jit(solution)/shard_map/ppermute | solution.py:330
  8.2 6.9 %collective-permute-start = (bf16[80,512]{1,0:T(8,128)(2,1)S(1)}, bf16[80,512]{1,0:T(8,128)(2,1)S(1)}, u32[]{:S(2)}, u32[]{:S(2)}) collective-permute-start(bf16[80,512]{1,0:T(8,128)(2,1)S(1)} %get-tuple-element.11), channel_id=1, source_target_pairs={{0,1},{1,0},{2,3},{3,2},{4,5},{5,4},{6,7},{7,6},{8,9},{9,8},{10,11... | collective-permute-start | bytes 245768 | tf_op jit(solution)/shard_map/ppermute | solution.py:330
  8.8 9.8 %all-to-all-start = ((f32[8,8,640]{2,1,0:T(8,128)}), f32[8,8,640]{2,1,0:T(8,128)S(1)}, u32[]{:S(2)}, u32[]{:S(2)}) async-start(f32[8,8,640]{2,1,0:T(8,128)} %get-tuple-element.10), calls=%async_computation | async-start | bytes 327680 | tf_op jit(solution)/shard_map/all_to_all | solution.py:331
  12.7 5.9 %collective-permute-start.5 = (bf16[80,512]{1,0:T(8,128)(2,1)S(1)}, bf16[80,512]{1,0:T(8,128)(2,1)S(1)}, u32[]{:S(2)}, u32[]{:S(2)}) collective-permute-start(bf16[80,512]{1,0:T(8,128)(2,1)S(1)} %collective-permute-done.4.refs_4_), channel_id=1, source_target_pairs={{0,4},{4,0},{8,12},{12,8},{16,20},{20,16},{24,28},{28,24},{1,5},{5... | collective-permute-start | bytes 245768 | tf_op jit(solution)/shard_map/ppermute | solution.py:334
  15.1 3.5 %collective-permute-start.3 = (bf16[80,512]{1,0:T(8,128)(2,1)S(1)}, bf16[80,512]{1,0:T(8,128)(2,1)S(1)}, u32[]{:S(2)}, u32[]{:S(2)}) collective-permute-start(bf16[80,512]{1,0:T(8,128)(2,1)S(1)} %collective-permute-done.2.refs_2_), channel_id=1, source_target_pairs={{0,4},{4,0},{8,12},{12,8},{16,20},{20,16},{24,28},{28,24},{1,5},{5... | collective-permute-start | bytes 245768 | tf_op jit(solution)/shard_map/ppermute | solution.py:334
  15.1 3.5 %collective-permute-start.1 = (bf16[80,512]{1,0:T(8,128)(2,1)S(1)}, bf16[80,512]{1,0:T(8,128)(2,1)S(1)}, u32[]{:S(2)}, u32[]{:S(2)}) collective-permute-start(bf16[80,512]{1,0:T(8,128)(2,1)S(1)} %collective-permute-done.refs_0_), channel_id=1, source_target_pairs={{0,4},{4,0},{8,12},{12,8},{16,20},{20,16},{24,28},{28,24},{1,5},{5... | collective-permute-start | bytes 245768 | tf_op jit(solution)/shard_map/ppermute | solution.py:334
  18.6 30.3 %copy-start = (f32[32,2,128]{2,1,0:T(2,128)S(1)}, f32[32,2,128]{2,1,0:T(2,128)}, u32[]{:S(2)}) copy-start(f32[32,2,128]{2,1,0:T(2,128)} %param.11) | copy-start | bytes 98308
  34.3 1.2 %collective-permute-start.6 = (f32[32,128]{1,0:T(8,128)S(1)}, f32[32,128]{1,0:T(8,128)S(1)}, u32[]{:S(2)}, u32[]{:S(2)}) collective-permute-start(f32[32,128]{1,0:T(8,128)S(1)} %get-tuple-element.12), channel_id=1, source_target_pairs={{0,4},{4,0},{8,12},{12,8},{16,20},{20,16},{24,28},{28,24},{1,5},{5... | collective-permute-start | bytes 49160 | tf_op jit(solution)/shard_map/ppermute | solution.py:295
  35.6 3.7 %collective-permute-start.7 = (f32[32,128]{1,0:T(8,128)S(1)}, f32[32,128]{1,0:T(8,128)S(1)}, u32[]{:S(2)}, u32[]{:S(2)}) collective-permute-start(f32[32,128]{1,0:T(8,128)S(1)} %add.15), channel_id=1, source_target_pairs={{0,8},{4,12},{8,0},{12,4},{16,24},{20,28},{24,16},{28,20},{1,9},{5... | collective-permute-start | bytes 49160 | tf_op jit(solution)/shard_map/ppermute | solution.py:295
  39.3 3.7 %collective-permute-start.8 = (f32[32,128]{1,0:T(8,128)S(1)}, f32[32,128]{1,0:T(8,128)S(1)}, u32[]{:S(2)}, u32[]{:S(2)}) collective-permute-start(f32[32,128]{1,0:T(8,128)S(1)} %add.16), channel_id=1, source_target_pairs={{0,16},{4,20},{8,24},{12,28},{16,0},{20,4},{24,8},{28,12},{1,17},{... | collective-permute-start | bytes 49160 | tf_op jit(solution)/shard_map/ppermute | solution.py:295
  43.0 3.7 %collective-permute-start.9 = (f32[32,128]{1,0:T(8,128)S(1)}, f32[32,128]{1,0:T(8,128)S(1)}, u32[]{:S(2)}, u32[]{:S(2)}) collective-permute-start(f32[32,128]{1,0:T(8,128)S(1)} %add.17), channel_id=1, source_target_pairs={{0,1},{1,0},{2,3},{3,2},{4,5},{5,4},{6,7},{7,6},{8,9},{9,8},{10,11... | collective-permute-start | bytes 49160 | tf_op jit(solution)/shard_map/ppermute | solution.py:295
  46.8 8.2 %collective-permute-start.10 = (f32[32,128]{1,0:T(8,128)S(1)}, f32[32,128]{1,0:T(8,128)S(1)}, u32[]{:S(2)}, u32[]{:S(2)}) collective-permute-start(f32[32,128]{1,0:T(8,128)S(1)} %add.18), channel_id=1, source_target_pairs={{0,2},{1,3},{2,0},{3,1},{4,6},{5,7},{6,4},{7,5},{8,10},{9,11},{10,... | collective-permute-start | bytes 49160 | tf_op jit(solution)/shard_map/ppermute | solution.py:295

commit v3 on v2

--- a/solution.py
+++ b/solution.py
@@ -56,9 +56,38 @@
         copy.wait()
 
 
+def cube_place(destination, own, count):
+    relative = jnp.bitwise_xor(destination, own)
+    place = jnp.zeros_like(relative)
+    bit = 1
+    while bit < count:
+        place = 2 * place + jnp.bitwise_and(relative, bit) // bit
+        bit *= 2
+    return place
+
+
+def cube_exchange(kept, leaving, axis):
+    count = lax.axis_size(axis)
+    assert power_of_two(count)
+    held = [kept]
+    bit = 1
+    while True:
+        held.append(lax.ppermute(leaving, axis, partners(count, bit)))
+        bit *= 2
+        if bit >= count:
+            return held
+        span = count // bit
+        tails = []
+        for h, part in enumerate(held):
+            cut = part.reshape(-1, span, *part.shape[-2:])
+            tails.append(cut[:, span // 2:].reshape(-1, *part.shape[-2:]))
+            held[h] = cut[:, :span // 2].reshape(-1, *part.shape[-2:])
+        leaving = jnp.concatenate(tails, axis=0)
+
+
 def force_kernel(clu_count, *refs):
-    sources, targets, sems = refs[:10], refs[13:23], refs[23]
-    sent_ref, force_ref, packed_ref = refs[10:13]
+    sources, targets, sems = refs[:10], refs[14:24], refs[24]
+    sent_ref, force_ref, kept_ref, leaving_ref = refs[10:14]
     fetch(sources, targets, sems)
     (own_ref, nodes_ref, pos_ref, ten_ref, bend_ref, order_ref, dest_ref, target_ref, deriv_ref,
      table_ref) = targets
@@ -85,10 +114,11 @@
     force_ref[pl.ds(1, vesicles, stride=2), :] = force_y
 
     slots = clu_count * BLOCK
-    hot = (iota((clu_count, moves), 0) == dest_ref[...]).astype(F32)
+    place = cube_place(dest_ref[...], lax.axis_index("clu"), clu_count)
+    hot = (iota((clu_count, moves), 0) == place).astype(F32)
     earlier = (iota((moves, moves), 0) < iota((moves, moves), 1)).astype(F32)
     rank = jnp.sum(dot(hot, earlier) * hot, axis=0, keepdims=True).astype(jnp.int32)
-    slot = dest_ref[...] * BLOCK + rank
+    slot = place * BLOCK + rank
     pack = (iota((slots, moves), 0) == slot).astype(F32)
     pick = (iota((vesicles, moves), 0) == order_ref[:, :moves]).astype(F32)
     select = dot(pack, pick, NT)
@@ -97,19 +127,32 @@
     tag = jnp.sum(pack * (target_ref[...] + 1).astype(F32), axis=1, keepdims=True)
     tag = jnp.broadcast_to(tag, (slots, x.shape[1]))
     packed = jnp.concatenate([packed, tag], axis=1)
-    packed_ref[...] = packed.reshape(clu_count, BLOCK, packed.shape[1])
-
-
-def near_kernel(clu_count, slot_cap, pos_ref, arrived, near_ref, aim_x, aim_y, speed_x, speed_y):
+    packed = packed.reshape(clu_count, BLOCK, packed.shape[1])
+    kept_ref[...] = packed[:clu_count // 2]
+    leaving_ref[...] = packed[clu_count // 2:]
+
+
+def near_kernel(slot_cap, piece_count, pos_ref, *refs):
+    piece_refs = refs[:piece_count]
+    before_ref, near_ref, arrived, aim_x, aim_y, speed_x, speed_y = refs[piece_count:]
     vesicles = pos_ref.shape[0] // 2
     nodes = pos_ref.shape[1]
-    slots = clu_count * BLOCK
+    here = 0
+    for ref in piece_refs:
+        arrived[here:here + ref.shape[0]] = ref[...]
+        here += ref.shape[0]
+    pieces = arrived.shape[0]
+    slots = pieces * BLOCK
     tag = arrived[:, :, 4 * nodes:].reshape(slots, nodes)[:, :vesicles]
     hot = (tag == (iota((slots, vesicles), 1) + 1).astype(F32)).astype(F32)
     x = pos_ref[pl.ds(0, vesicles, stride=2), :]
     y = pos_ref[pl.ds(1, vesicles, stride=2), :]
-    aim_x[...] = dot(hot, x, precision=HIGHEST).reshape(clu_count, BLOCK, nodes)
-    aim_y[...] = dot(hot, y, precision=HIGHEST).reshape(clu_count, BLOCK, nodes)
+    aim_x[...] = dot(hot, x, precision=HIGHEST).reshape(pieces, BLOCK, nodes)
+    aim_y[...] = dot(hot, y, precision=HIGHEST).reshape(pieces, BLOCK, nodes)
+    chunk = 32 if nodes % 32 == 0 else nodes
+
+    def fold(value):
+        return jnp.sum(value.reshape(-1, 8, nodes), axis=0)
 
     def piece(k, _):
         data = arrived[k]
@@ -117,29 +160,59 @@
         tx, ty = aim_x[k], aim_y[k]
         rows_x, rows_y = [], []
         for h in range(slot_cap):
-            sx, sy, fx, fy = [jnp.broadcast_to(t[:, h:h + 1], (nodes, nodes)) for t in turned]
-            dx = tx[h:h + 1] - sx
-            dy = ty[h:h + 1] - sy
-            spread = dx * dx + dy * dy + EPS_SQUARED
-            log_part = -0.5 * jnp.log(spread)
-            along = (dx * fx + dy * fy) * reciprocal(spread)
-            rows_x.append(jnp.sum(log_part * fx + dx * along, axis=0, keepdims=True))
-            rows_y.append(jnp.sum(log_part * fy + dy * along, axis=0, keepdims=True))
+            logs_x = logs_y = pulls_x = pulls_y = jnp.zeros((8, nodes), F32)
+            for start in range(0, nodes, chunk):
+                sx, sy, fx, fy = [
+                    jnp.broadcast_to(t[start:start + chunk, h:h + 1], (chunk, nodes))
+                    for t in turned]
+                dx = tx[h:h + 1] - sx
+                dy = ty[h:h + 1] - sy
+                spread = dx * dx + dy * dy + EPS_SQUARED
+                logs = jnp.log(spread)
+                along = (dx * fx + dy * fy) * reciprocal(spread)
+                logs_x, logs_y = logs_x + fold(logs * fx), logs_y + fold(logs * fy)
+                pulls_x, pulls_y = pulls_x + fold(dx * along), pulls_y + fold(dy * along)
+            rows_x.append(jnp.sum(pulls_x - 0.5 * logs_x, axis=0, keepdims=True))
+            rows_y.append(jnp.sum(pulls_y - 0.5 * logs_y, axis=0, keepdims=True))
         rows_x += [jnp.zeros((1, nodes), F32)] * (BLOCK - slot_cap)
         rows_y += [jnp.zeros((1, nodes), F32)] * (BLOCK - slot_cap)
         speed_x[k] = jnp.concatenate(rows_x, axis=0)
         speed_y[k] = jnp.concatenate(rows_y, axis=0)
         return 0
 
-    lax.fori_loop(0, clu_count, piece, 0)
+    lax.fori_loop(0, pieces, piece, 0)
     turned_hot = hot.T
-    near_ref[pl.ds(0, vesicles, stride=2), :] = dot(
-        turned_hot, speed_x[...].reshape(slots, nodes), precision=HIGHEST) / nodes
-    near_ref[pl.ds(1, vesicles, stride=2), :] = dot(
-        turned_hot, speed_y[...].reshape(slots, nodes), precision=HIGHEST) / nodes
-
-
-def far_kernel(col_count, range_in, pos_in, own_in, nodes_in, _, *refs):
+    near_x = dot(turned_hot, speed_x[...].reshape(slots, nodes), precision=HIGHEST) / nodes
+    near_y = dot(turned_hot, speed_y[...].reshape(slots, nodes), precision=HIGHEST) / nodes
+    if before_ref is not None:
+        near_x = near_x + before_ref[pl.ds(0, vesicles, stride=2), :]
+        near_y = near_y + before_ref[pl.ds(1, vesicles, stride=2), :]
+    near_ref[pl.ds(0, vesicles, stride=2), :] = near_x
+    near_ref[pl.ds(1, vesicles, stride=2), :] = near_y
+
+
+def near_start(slot_cap, piece_count, pos_ref, *refs):
+    near_kernel(slot_cap, piece_count, pos_ref, *refs[:piece_count], None, *refs[piece_count:])
+
+
+def near_part(flat, pieces, before, slot_cap):
+    vesicles, nodes = flat.shape[0] // 2, flat.shape[1]
+    count = sum(p.shape[0] for p in pieces)
+    operands = [flat, *pieces] + ([] if before is None else [before])
+    return pl.pallas_call(
+        functools.partial(near_start if before is None else near_kernel, slot_cap, len(pieces)),
+        out_shape=jax.ShapeDtypeStruct((2 * vesicles, nodes), F32),
+        in_specs=[whole_spec()] * len(operands),
+        out_specs=whole_spec(),
+        scratch_shapes=[pltpu.VMEM((count, BLOCK, 5 * nodes), F32)]
+        + [pltpu.VMEM((count, BLOCK, nodes), F32)] * 4,
+        compiler_params=params(16),
+        cost_estimate=pl.CostEstimate(
+            flops=10**9, bytes_accessed=10**7, transcendentals=10**6),
+    )(*operands)
+
+
+def far_kernel(col_count, range_in, pos_in, own_in, nodes_in, *refs):
     count = 2 * (col_count - 1)
     piece_refs = refs[:count]
     (high_ref, low_ref, gram_ref, range_ref, pos_ref, own_nodes, basis, spots, wide, buffer,
@@ -162,7 +235,7 @@
         for c in range(2):
             wide[r, c] = jnp.broadcast_to(turned[:, c:c + 1], (sources, nodes))
     sums[...] = jnp.zeros_like(sums)
-    chunk = 128 if sources % 128 == 0 else sources
+    chunk = 32 if sources % 32 == 0 else sources
 
     def evaluate(v, slot):
         r = range_ref[0, v]
@@ -189,15 +262,21 @@
         low_1 = (second - high_1.astype(F32)).astype(BF16)
         high_ref[v] = jnp.concatenate([high_0, high_1], axis=0)
         low_ref[v] = jnp.concatenate([low_0, low_1], axis=0)
+
+    def add_gram(v):
         both = jnp.concatenate([
-            jnp.concatenate([high_0, high_1], axis=1),
-            jnp.concatenate([low_0, low_1], axis=1)], axis=0)
+            jnp.concatenate([ref[u, part] for u in (v, v + 1)
+                             for part in (slice(0, rank), slice(rank, rows))], axis=1)
+            for ref in (high_ref, low_ref)], axis=0)
         sums[...] += dot(both, both, NT)
 
     evaluate(0, 0)
+    high_ref[0:2] = jnp.zeros((2, rows, nodes), BF16)
+    low_ref[0:2] = jnp.zeros((2, rows, nodes), BF16)
 
     def pair(i, _):
         v = 2 * i
+        add_gram(jnp.maximum(v - 2, 0))
         evaluate(v + 1, 1)
         multiply(v, 0)
         evaluate(jnp.minimum(v + 2, vesicles - 1), 0)
@@ -205,6 +284,7 @@
         return 0
 
     lax.fori_loop(0, vesicles // 2, pair, 0)
+    add_gram(vesicles - 2)
     total = sums[...]
     gram = total[:rank, :rank] + total[rank:, rank:] + (total[:rank, rank:] + total[rank:, :rank])
     gram_ref[...] = jnp.concatenate([gram[:rank // 2], gram[rank // 2:]], axis=1)
@@ -287,16 +367,24 @@
     return lax.rem(index - step + count, count)
 
 
-def sum_over(value, axis):
+def step_groups(count, single_first):
+    if not power_of_two(count):
+        return [list(range(1, count))]
+    groups, bit = [], 1
+    if single_first and count > 1:
+        groups, bit = [[1]], 2
+    while bit < count:
+        groups.append([bit] if 2 * bit >= count else [bit, 2 * bit, 3 * bit])
+        bit *= 4
+    return groups
+
+
+def sum_over(value, axis, groups):
     count = lax.axis_size(axis)
-    if power_of_two(count):
-        step = 1
-        while step < count:
-            value = value + lax.ppermute(value, axis, partners(count, step))
-            step *= 2
-        return value
-    moved = [lax.ppermute(value, axis, partners(count, k)) for k in range(1, count)]
-    return sum(moved, value)
+    for steps in groups:
+        moved = [lax.ppermute(value, axis, partners(count, k)) for k in steps]
+        value = sum(moved, value)
+    return value
 
 
 def per_device(positions, tension, bending, moved_order, move_destination, move_target, far_range,
@@ -314,13 +402,13 @@
                 move_destination.reshape(1, moves), move_target.reshape(1, moves),
                 jnp.asarray(deriv), jnp.asarray(table)]
     operands = [pltpu.with_memory_space_constraint(o, pltpu.HBM) for o in operands]
-    sent, force, packed = pl.pallas_call(
+    sent, force, kept, leaving = pl.pallas_call(
         functools.partial(force_kernel, clu_count),
         out_shape=[jax.ShapeDtypeStruct((rank + 16, sources), BF16),
                    jax.ShapeDtypeStruct((2 * vesicles, nodes), F32),
-                   jax.ShapeDtypeStruct((clu_count, BLOCK, 5 * nodes), F32)],
+                   *[jax.ShapeDtypeStruct((clu_count // 2, BLOCK, 5 * nodes), F32)] * 2],
         in_specs=[far_off_spec()] * len(operands),
-        out_specs=[whole_spec()] * 3,
+        out_specs=[whole_spec()] * 4,
         scratch_shapes=[pltpu.VMEM(o.shape, o.dtype) for o in operands]
         + [pltpu.SemaphoreType.DMA((len(operands),))],
         compiler_params=params(16),
@@ -328,26 +416,19 @@
     )(*operands)
 
     moved_halves = [lax.ppermute(sent, "col", partners(col_count, k)) for k in range(1, col_count)]
-    arrived = lax.all_to_all(packed, "clu", split_axis=0, concat_axis=0, tiled=True)
+    arrived = cube_exchange(kept, leaving, "clu")
     pieces = []
     for mine in moved_halves:
         pieces += [mine, lax.ppermute(mine, "clu", [(i, i ^ 1) for i in range(clu_count)])]
 
-    near = pl.pallas_call(
-        functools.partial(near_kernel, clu_count, slot_cap),
-        out_shape=jax.ShapeDtypeStruct((2 * vesicles, nodes), F32),
-        in_specs=[whole_spec()] * 2,
-        out_specs=whole_spec(),
-        scratch_shapes=[pltpu.VMEM((clu_count, BLOCK, nodes), F32)] * 4,
-        compiler_params=params(16),
-        cost_estimate=pl.CostEstimate(flops=10**9, bytes_accessed=10**7, transcendentals=10**6),
-    )(flat, arrived)
+    near = near_part(flat, arrived[:-1], None, slot_cap)
+    near = near_part(flat, arrived[-1:], near, slot_cap)
 
     high, low, gram = pl.pallas_call(
         functools.partial(far_kernel, col_count),
         out_shape=[jax.ShapeDtypeStruct((vesicles, rows, nodes), BF16)] * 2
         + [jax.ShapeDtypeStruct((rank // 2, 2 * rank), F32)],
-        in_specs=[far_off_spec()] * 5 + [whole_spec()] * (2 * (col_count - 1)),
+        in_specs=[far_off_spec()] * 4 + [whole_spec()] * (2 * (col_count - 1)),
         out_specs=[whole_spec()] * 3,
         scratch_shapes=[
             pltpu.SMEM((1, vesicles), jnp.int32),
@@ -362,8 +443,9 @@
         compiler_params=params(32),
         cost_estimate=pl.CostEstimate(flops=10**10, bytes_accessed=10**7, transcendentals=10**7),
     )(pltpu.with_memory_space_constraint(far_range.reshape(1, vesicles), pltpu.HBM), operands[2],
-      operands[0], operands[1], arrived, *pieces)
-    gram = sum_over(sum_over(gram, "clu"), "col")
+      operands[0], operands[1], *pieces)
+    gram = sum_over(gram, "clu", step_groups(clu_count, True))
+    gram = sum_over(gram, "col", step_groups(col_count, False))
 
     scale_factor = math.sqrt(2.0 * nodes * vesicles * clu_count * col_count)
     group = 8 if vesicles % 8 == 0 else vesicles

time: 60.1 us -> 53.1 us (0.88)
  waiting for transfers between devices: 14.9 us -> 8.52 us
  Pallas kernels: 29 us -> 26.4 us
  starting transfers between devices: 15.2 us -> 17.2 us
    ppermute x5 -> x10, waiting for transfers between devices: 10 us -> 3.58 us  [the longest x7 2.32 us: sum_over(): moved = [lax.ppermute(value, axis, partners(count, k)) for k in steps]]
    ppermute x5 -> x10, starting transfers between devices: 4.58 us -> 11 us  [the longest x7 7.95 us: sum_over(): moved = [lax.ppermute(value, axis, partners(count, k)) for k in steps]]
    all_to_all x1 -> x0, starting transfers between devices: 3.87 us -> none  [per_device(): lax.all_to_all(packed, 'clu', split_axis=0, concat_axis=0, tiled=True)]
    ppermute x3, waiting for transfers between devices: 1.85 us -> 4.93 us  [per_device(): lax.ppermute(sent, 'col', partners(col_count, k))]
    all_to_all x1 -> x0, waiting for transfers between devices: 3.02 us -> none  [per_device(): lax.all_to_all(packed, 'clu', split_axis=0, concat_axis=0, tiled=True)]
    pallas_call x1, Pallas kernels: 15.7 us -> 13 us  [per_device(): pl.pallas_call(functools.partial(far_kernel, col_count), out_shape=[jax.S...]
    pallas_call x1 -> x2, Pallas kernels: 6.01 us -> 6.35 us  [near_part(): pl.pallas_call(functools.partial(near_start if before is None else near_k...]
  transfers between devices with their start and end apart: 12 -> 16, of which waited for: 6 -> 7; matrix products, arithmetic and copies ran while one was open for 0% -> 0% of each run, Pallas kernels for 10% -> 39%
where the time goes in v3:
time: 53.1 us; the launch traced here: 53 us
  Pallas kernels  26.4 us (50%)
  starting transfers between devices  17.2 us (32%)
  waiting for transfers between devices  8.52 us (16%)
  between operations  0.71 us (1%)
    pallas_call x1, Pallas kernels, per_device(): pl.pallas_call(functools.partial(far_kernel, col_count), out_shape=[jax.S...  13 us
    ppermute x7, starting transfers between devices, sum_over(): moved = [lax.ppermute(value, axis, partners(count, k)) for k in steps]  7.95 us
    pallas_call x2, Pallas kernels, near_part(): pl.pallas_call(functools.partial(near_start if before is None else near_k...  6.35 us
    ppermute x3, starting transfers between devices, per_device(): lax.ppermute(sent, 'col', partners(col_count, k))  5.76 us
    ppermute x3, waiting for transfers between devices, per_device(): lax.ppermute(sent, 'col', partners(col_count, k))  4.93 us
    pallas_call x1, Pallas kernels, per_device(): pl.pallas_call(functools.partial(basis_kernel, scale_factor), out_shape=j...  4.88 us
    ppermute x3, starting transfers between devices, cube_exchange(): held.append(lax.ppermute(leaving, axis, partners(count, bit)))  3.01 us
    ppermute x7, waiting for transfers between devices, sum_over(): moved = [lax.ppermute(value, axis, partners(count, k)) for k in steps]  2.32 us
  transfers between devices with their start and end apart: 16, of which 7 were waited for; matrix products, arithmetic and copies ran while one was open for 0% of the time, Pallas kernels for 39%

profile of v3, /device:TPU:0, one launch (start us, length us, event | category | flops | bytes accessed | tf_op | source)
XLA Modules:
  0.0 53.0 jit_solution(7915067811656732231)
XLA Ops:
  0.6 2.2 %shard_map.130 = (bf16[80,512]{1,0:T(8,128)(2,1)S(1)}, f32[64,128]{1,0:T(8,128)}, f32[4,8,640]{2,1,0:T(8,128)S(1)}, f32[4,8,640]{2,1,0:T(8,128)S(1)}) custom-call(bf16[128,512]{1,0:T(8,128)(2,1)} %own_in.1, bf16[2,512]{1,0:T(2,128)(2,1)} %nodes_in.1, f32[64,128]{1,0:T(8,128)} %bitcast.33, f32[32,128]{1,0:T(8,128)} %refs_3_.1, f32[1,32]{1,0:T(1,128)} %bitcast.41, ...), custom_call_target="tpu_custom_call" | custom-call | flops 100000000 | bytes 1000000 | tf_op jit(solution)/shard_map/pallas_call | solution.py:405
  2.8 5.1 %collective-permute-start.7 = (bf16[80,512]{1,0:T(8,128)(2,1)S(1)}, bf16[80,512]{1,0:T(8,128)(2,1)S(1)}, u32[]{:S(2)}, u32[]{:S(2)}) collective-permute-start(bf16[80,512]{1,0:T(8,128)(2,1)S(1)} %get-tuple-element.13), channel_id=1, source_target_pairs={{0,3},{1,2},{2,1},{3,0},{4,7},{5,6},{6,5},{7,4},{8,11},{9,10},{10,... | collective-permute-start | bytes 245768 | tf_op jit(solution)/shard_map/ppermute | solution.py:418
  7.9 0.0 collective-permute-start.5
  7.9 0.6 %collective-permute-start.3 = (bf16[80,512]{1,0:T(8,128)(2,1)S(1)}, bf16[80,512]{1,0:T(8,128)(2,1)S(1)}, u32[]{:S(2)}, u32[]{:S(2)}) collective-permute-start(bf16[80,512]{1,0:T(8,128)(2,1)S(1)} %get-tuple-element.13), channel_id=1, source_target_pairs={{0,1},{1,0},{2,3},{3,2},{4,5},{5,4},{6,7},{7,6},{8,9},{9,8},{10,11... | collective-permute-start | bytes 245768 | tf_op jit(solution)/shard_map/ppermute | solution.py:418
  8.6 0.0 collective-permute-start
  8.6 1.3 %collective-permute-done = f32[4,8,640]{2,1,0:T(8,128)S(1)} collective-permute-done((f32[4,8,640]{2,1,0:T(8,128)S(1)}, f32[4,8,640]{2,1,0:T(8,128)S(1)}, u32[]{:S(2)}, u32[]{:S(2)}) %collective-permute-start) | collective-permute-done | bytes 81952 | tf_op jit(solution)/shard_map/ppermute | solution.py:75
  9.8 1.1 %collective-permute-done.7.refs_4_ = bf16[80,512]{1,0:T(8,128)(2,1)S(1)} collective-permute-done((bf16[80,512]{1,0:T(8,128)(2,1)S(1)}, bf16[80,512]{1,0:T(8,128)(2,1)S(1)}, u32[]{:S(2)}, u32[]{:S(2)}) %collective-permute-start.7) | collective-permute-done | bytes 81952 | tf_op jit(solution)/shard_map/ppermute | solution.py:418
  10.9 3.8 %collective-permute-done.5.refs_2_ = bf16[80,512]{1,0:T(8,128)(2,1)S(1)} collective-permute-done((bf16[80,512]{1,0:T(8,128)(2,1)S(1)}, bf16[80,512]{1,0:T(8,128)(2,1)S(1)}, u32[]{:S(2)}, u32[]{:S(2)}) %collective-permute-start.5) | collective-permute-done | bytes 81952 | tf_op jit(solution)/shard_map/ppermute | solution.py:418
  14.8 0.0 collective-permute-start.6
  14.8 0.5 collective-permute-start.4
  15.3 1.5 %collective-permute-start.1 = (f32[4,8,640]{2,1,0:T(8,128)S(1)}, f32[4,8,640]{2,1,0:T(8,128)S(1)}, u32[]{:S(2)}, u32[]{:S(2)}) collective-permute-start(f32[4,8,640]{2,1,0:T(8,128)S(1)} %pad_maximum_fusion), channel_id=1, source_target_pairs={{0,8},{4,12},{8,0},{12,4},{16,24},{20,28},{24,16},{28,20},{1,9},{5... | collective-permute-start | bytes 245768 | tf_op jit(solution)/shard_map/ppermute | solution.py:75
  16.8 0.0 copy-start
  16.8 13.0 %shard_map.133 = (bf16[32,128,128]{2,1,0:T(8,128)(2,1)S(1)}, bf16[32,128,128]{2,1,0:T(8,128)(2,1)S(1)}, f32[32,128]{1,0:T(8,128)S(1)}) custom-call(s32[1,32]{1,0:T(1,128)} %bitcast.44, f32[64,128]{1,0:T(8,128)} %bitcast.34, bf16[128,512]{1,0:T(8,128)(2,1)} %own_in.1, bf16[2,512]{1,0:T(2,128)(2,1)} %nodes_in.1, ...), custom_call_target="tpu_custom_call" | custom-call | flops 10000000000 | bytes 10000000 | tf_op jit(solution)/shard_map/pallas_call | solution.py:427
  29.9 0.1 collective-permute-start.9
  29.9 0.0 collective-permute-done.1
  30.0 1.1 %collective-permute-done.9 = f32[32,128]{1,0:T(8,128)S(1)} collective-permute-done((f32[32,128]{1,0:T(8,128)S(1)}, f32[32,128]{1,0:T(8,128)S(1)}, u32[]{:S(2)}, u32[]{:S(2)}) %collective-permute-start.9) | collective-permute-done | bytes 16416 | tf_op jit(solution)/shard_map/ppermute | solution.py:385
  31.1 1.9 %collective-permute-start.12 = (f32[32,128]{1,0:T(8,128)S(1)}, f32[32,128]{1,0:T(8,128)S(1)}, u32[]{:S(2)}, u32[]{:S(2)}) collective-permute-start(f32[32,128]{1,0:T(8,128)S(1)} %add.21), channel_id=1, source_target_pairs={{0,24},{4,28},{8,16},{12,20},{16,8},{20,12},{24,0},{28,4},{1,25},{... | collective-permute-start | bytes 49160 | tf_op jit(solution)/shard_map/ppermute | solution.py:385
  33.0 0.5 collective-permute-start.11
  33.5 1.1 %collective-permute-start.10 = (f32[32,128]{1,0:T(8,128)S(1)}, f32[32,128]{1,0:T(8,128)S(1)}, u32[]{:S(2)}, u32[]{:S(2)}) collective-permute-start(f32[32,128]{1,0:T(8,128)S(1)} %add.21), channel_id=1, source_target_pairs={{0,8},{4,12},{8,0},{12,4},{16,24},{20,28},{24,16},{28,20},{1,9},{5... | collective-permute-start | bytes 49160 | tf_op jit(solution)/shard_map/ppermute | solution.py:385
  34.6 1.5 %collective-permute-start.2 = (f32[4,8,640]{2,1,0:T(8,128)S(1)}, f32[4,8,640]{2,1,0:T(8,128)S(1)}, u32[]{:S(2)}, u32[]{:S(2)}) collective-permute-start(f32[4,8,640]{2,1,0:T(8,128)S(1)} %pad_maximum_fusion.1), channel_id=1, source_target_pairs={{0,16},{4,20},{8,24},{12,28},{16,0},{20,4},{24,8},{28,12},{1,17},{... | collective-permute-start | bytes 245768 | tf_op jit(solution)/shard_map/ppermute | solution.py:75
  36.1 0.0 collective-permute-done.12
  36.1 0.8 %collective-permute-done.11 = f32[32,128]{1,0:T(8,128)S(1)} collective-permute-done((f32[32,128]{1,0:T(8,128)S(1)}, f32[32,128]{1,0:T(8,128)S(1)}, u32[]{:S(2)}, u32[]{:S(2)}) %collective-permute-start.11) | collective-permute-done | bytes 16416 | tf_op jit(solution)/shard_map/ppermute | solution.py:385
  36.9 0.3 collective-permute-done.10
  37.2 2.7 %collective-permute-start.15 = (f32[32,128]{1,0:T(8,128)S(1)}, f32[32,128]{1,0:T(8,128)S(1)}, u32[]{:S(2)}, u32[]{:S(2)}) collective-permute-start(f32[32,128]{1,0:T(8,128)S(1)} %add_add_fusion.1), channel_id=1, source_target_pairs={{0,3},{1,2},{2,1},{3,0},{4,7},{5,6},{6,5},{7,4},{8,11},{9,10},{10,... | collective-permute-start | bytes 49160 | tf_op jit(solution)/shard_map/ppermute | solution.py:385
  39.9 0.0 collective-permute-start.14
  39.9 1.7 %collective-permute-start.13 = (f32[32,128]{1,0:T(8,128)S(1)}, f32[32,128]{1,0:T(8,128)S(1)}, u32[]{:S(2)}, u32[]{:S(2)}) collective-permute-start(f32[32,128]{1,0:T(8,128)S(1)} %add_add_fusion.1), channel_id=1, source_target_pairs={{0,1},{1,0},{2,3},{3,2},{4,5},{5,4},{6,7},{7,6},{8,9},{9,8},{10,11... | collective-permute-start | bytes 49160 | tf_op jit(solution)/shard_map/ppermute | solution.py:385
  41.6 2.9 %shard_map.131.refs_1_ = f32[64,128]{1,0:T(8,128)S(1)} custom-call(f32[64,128]{1,0:T(8,128)S(1)} %bitcast.35, f32[1,8,640]{2,1,0:T(8,128)S(1)} %get-tuple-element.21.refs_0_, f32[1,8,640]{2,1,0:T(8,128)S(1)} %get-tuple-element.19.refs_1_, f32[2,8,640]{2,1,0:T(8,128)S(1)} %get-tuple-element.17.refs_2_), custom_call_target="tpu_custom_call" | custom-call | flops 1000000000 | bytes 10000000 | tf_op jit(solution)/shard_map/pallas_call | solution.py:202
  44.5 0.0 collective-permute-done.15
  44.5 0.1 collective-permute-done.14
  44.6 0.0 collective-permute-done.13
  44.6 4.9 %shard_map.134 = f32[32,128,128]{2,1,0:T(8,128)} custom-call(f32[32,128]{1,0:T(8,128)S(1)} %add_add_fusion.refs_0_, bf16[32,128,128]{2,1,0:T(8,128)(2,1)S(1)} %get-tuple-element.15.refs_1_, bf16[32,128,128]{2,1,0:T(8,128)(2,1)S(1)} %get-tuple-element.16.refs_2_), custom_call_target="tpu_custom_call" | custom-call | flops 1000000000 | bytes 10000000 | tf_op jit(solution)/shard_map/pallas_call | solution.py:453
  49.5 3.5 %shard_map.132 = f32[64,128]{1,0:T(8,128)} custom-call(f32[64,128]{1,0:T(8,128)S(1)} %bitcast.36, f32[4,8,640]{2,1,0:T(8,128)S(1)} %collective-permute-done.2.refs_0_, f32[64,128]{1,0:T(8,128)S(1)} %shard_map.131.refs_1_), custom_call_target="tpu_custom_call" | custom-call | flops 1000000000 | bytes 10000000 | tf_op jit(solution)/shard_map/pallas_call | solution.py:202
  (17 shorter events, 0.1 us)
Async XLA Ops:
  2.8 8.1 %collective-permute-start.7 = (bf16[80,512]{1,0:T(8,128)(2,1)S(1)}, bf16[80,512]{1,0:T(8,128)(2,1)S(1)}, u32[]{:S(2)}, u32[]{:S(2)}) collective-permute-start(bf16[80,512]{1,0:T(8,128)(2,1)S(1)} %get-tuple-element.13), channel_id=1, source_target_pairs={{0,3},{1,2},{2,1},{3,0},{4,7},{5,6},{6,5},{7,4},{8,11},{9,10},{10,... | collective-permute-start | bytes 245768 | tf_op jit(solution)/shard_map/ppermute | solution.py:418
  7.9 6.9 %collective-permute-start.5 = (bf16[80,512]{1,0:T(8,128)(2,1)S(1)}, bf16[80,512]{1,0:T(8,128)(2,1)S(1)}, u32[]{:S(2)}, u32[]{:S(2)}) collective-permute-start(bf16[80,512]{1,0:T(8,128)(2,1)S(1)} %get-tuple-element.13), channel_id=1, source_target_pairs={{0,2},{1,3},{2,0},{3,1},{4,6},{5,7},{6,4},{7,5},{8,10},{9,11},{10,... | collective-permute-start | bytes 245768 | tf_op jit(solution)/shard_map/ppermute | solution.py:418
  7.9 6.9 %collective-permute-start.3 = (bf16[80,512]{1,0:T(8,128)(2,1)S(1)}, bf16[80,512]{1,0:T(8,128)(2,1)S(1)}, u32[]{:S(2)}, u32[]{:S(2)}) collective-permute-start(bf16[80,512]{1,0:T(8,128)(2,1)S(1)} %get-tuple-element.13), channel_id=1, source_target_pairs={{0,1},{1,0},{2,3},{3,2},{4,5},{5,4},{6,7},{7,6},{8,9},{9,8},{10,11... | collective-permute-start | bytes 245768 | tf_op jit(solution)/shard_map/ppermute | solution.py:418
  8.6 1.3 %collective-permute-start = (f32[4,8,640]{2,1,0:T(8,128)S(1)}, f32[4,8,640]{2,1,0:T(8,128)S(1)}, u32[]{:S(2)}, u32[]{:S(2)}) collective-permute-start(f32[4,8,640]{2,1,0:T(8,128)S(1)} %get-tuple-element.12), channel_id=1, source_target_pairs={{0,4},{4,0},{8,12},{12,8},{16,20},{20,16},{24,28},{28,24},{1,5},{5... | collective-permute-start | bytes 245768 | tf_op jit(solution)/shard_map/ppermute | solution.py:75
  10.9 5.8 %collective-permute-start.8 = (bf16[80,512]{1,0:T(8,128)(2,1)S(1)}, bf16[80,512]{1,0:T(8,128)(2,1)S(1)}, u32[]{:S(2)}, u32[]{:S(2)}) collective-permute-start(bf16[80,512]{1,0:T(8,128)(2,1)S(1)} %collective-permute-done.7.refs_4_), channel_id=1, source_target_pairs={{0,4},{4,0},{8,12},{12,8},{16,20},{20,16},{24,28},{28,24},{1,5},{5... | collective-permute-start | bytes 245768 | tf_op jit(solution)/shard_map/ppermute | solution.py:422
  14.8 2.0 %collective-permute-start.6 = (bf16[80,512]{1,0:T(8,128)(2,1)S(1)}, bf16[80,512]{1,0:T(8,128)(2,1)S(1)}, u32[]{:S(2)}, u32[]{:S(2)}) collective-permute-start(bf16[80,512]{1,0:T(8,128)(2,1)S(1)} %collective-permute-done.5.refs_2_), channel_id=1, source_target_pairs={{0,4},{4,0},{8,12},{12,8},{16,20},{20,16},{24,28},{28,24},{1,5},{5... | collective-permute-start | bytes 245768 | tf_op jit(solution)/shard_map/ppermute | solution.py:422
  14.8 2.0 %collective-permute-start.4 = (bf16[80,512]{1,0:T(8,128)(2,1)S(1)}, bf16[80,512]{1,0:T(8,128)(2,1)S(1)}, u32[]{:S(2)}, u32[]{:S(2)}) collective-permute-start(bf16[80,512]{1,0:T(8,128)(2,1)S(1)} %collective-permute-done.3.refs_0_), channel_id=1, source_target_pairs={{0,4},{4,0},{8,12},{12,8},{16,20},{20,16},{24,28},{28,24},{1,5},{5... | collective-permute-start | bytes 245768 | tf_op jit(solution)/shard_map/ppermute | solution.py:422
  15.3 14.7 %collective-permute-start.1 = (f32[4,8,640]{2,1,0:T(8,128)S(1)}, f32[4,8,640]{2,1,0:T(8,128)S(1)}, u32[]{:S(2)}, u32[]{:S(2)}) collective-permute-start(f32[4,8,640]{2,1,0:T(8,128)S(1)} %pad_maximum_fusion), channel_id=1, source_target_pairs={{0,8},{4,12},{8,0},{12,4},{16,24},{20,28},{24,16},{28,20},{1,9},{5... | collective-permute-start | bytes 245768 | tf_op jit(solution)/shard_map/ppermute | solution.py:75
  16.8 24.8 %copy-start = (f32[32,2,128]{2,1,0:T(2,128)S(1)}, f32[32,2,128]{2,1,0:T(2,128)}, u32[]{:S(2)}) copy-start(f32[32,2,128]{2,1,0:T(2,128)} %param.11) | copy-start | bytes 98308
  29.9 1.2 %collective-permute-start.9 = (f32[32,128]{1,0:T(8,128)S(1)}, f32[32,128]{1,0:T(8,128)S(1)}, u32[]{:S(2)}, u32[]{:S(2)}) collective-permute-start(f32[32,128]{1,0:T(8,128)S(1)} %get-tuple-element.14), channel_id=1, source_target_pairs={{0,4},{4,0},{8,12},{12,8},{16,20},{20,16},{24,28},{28,24},{1,5},{5... | collective-permute-start | bytes 49160 | tf_op jit(solution)/shard_map/ppermute | solution.py:385
  31.1 5.0 %collective-permute-start.12 = (f32[32,128]{1,0:T(8,128)S(1)}, f32[32,128]{1,0:T(8,128)S(1)}, u32[]{:S(2)}, u32[]{:S(2)}) collective-permute-start(f32[32,128]{1,0:T(8,128)S(1)} %add.21), channel_id=1, source_target_pairs={{0,24},{4,28},{8,16},{12,20},{16,8},{20,12},{24,0},{28,4},{1,25},{... | collective-permute-start | bytes 49160 | tf_op jit(solution)/shard_map/ppermute | solution.py:385
  33.0 3.9 %collective-permute-start.11 = (f32[32,128]{1,0:T(8,128)S(1)}, f32[32,128]{1,0:T(8,128)S(1)}, u32[]{:S(2)}, u32[]{:S(2)}) collective-permute-start(f32[32,128]{1,0:T(8,128)S(1)} %add.21), channel_id=1, source_target_pairs={{0,16},{4,20},{8,24},{12,28},{16,0},{20,4},{24,8},{28,12},{1,17},{... | collective-permute-start | bytes 49160 | tf_op jit(solution)/shard_map/ppermute | solution.py:385
  33.5 3.7 %collective-permute-start.10 = (f32[32,128]{1,0:T(8,128)S(1)}, f32[32,128]{1,0:T(8,128)S(1)}, u32[]{:S(2)}, u32[]{:S(2)}) collective-permute-start(f32[32,128]{1,0:T(8,128)S(1)} %add.21), channel_id=1, source_target_pairs={{0,8},{4,12},{8,0},{12,4},{16,24},{20,28},{24,16},{28,20},{1,9},{5... | collective-permute-start | bytes 49160 | tf_op jit(solution)/shard_map/ppermute | solution.py:385
  34.6 14.8 %collective-permute-start.2 = (f32[4,8,640]{2,1,0:T(8,128)S(1)}, f32[4,8,640]{2,1,0:T(8,128)S(1)}, u32[]{:S(2)}, u32[]{:S(2)}) collective-permute-start(f32[4,8,640]{2,1,0:T(8,128)S(1)} %pad_maximum_fusion.1), channel_id=1, source_target_pairs={{0,16},{4,20},{8,24},{12,28},{16,0},{20,4},{24,8},{28,12},{1,17},{... | collective-permute-start | bytes 245768 | tf_op jit(solution)/shard_map/ppermute | solution.py:75
  37.2 7.3 %collective-permute-start.15 = (f32[32,128]{1,0:T(8,128)S(1)}, f32[32,128]{1,0:T(8,128)S(1)}, u32[]{:S(2)}, u32[]{:S(2)}) collective-permute-start(f32[32,128]{1,0:T(8,128)S(1)} %add_add_fusion.1), channel_id=1, source_target_pairs={{0,3},{1,2},{2,1},{3,0},{4,7},{5,6},{6,5},{7,4},{8,11},{9,10},{10,... | collective-permute-start | bytes 49160 | tf_op jit(solution)/shard_map/ppermute | solution.py:385
  39.9 4.6 %collective-permute-start.14 = (f32[32,128]{1,0:T(8,128)S(1)}, f32[32,128]{1,0:T(8,128)S(1)}, u32[]{:S(2)}, u32[]{:S(2)}) collective-permute-start(f32[32,128]{1,0:T(8,128)S(1)} %add_add_fusion.1), channel_id=1, source_target_pairs={{0,2},{1,3},{2,0},{3,1},{4,6},{5,7},{6,4},{7,5},{8,10},{9,11},{10,... | collective-permute-start | bytes 49160 | tf_op jit(solution)/shard_map/ppermute | solution.py:385
  39.9 4.6 %collective-permute-start.13 = (f32[32,128]{1,0:T(8,128)S(1)}, f32[32,128]{1,0:T(8,128)S(1)}, u32[]{:S(2)}, u32[]{:S(2)}) collective-permute-start(f32[32,128]{1,0:T(8,128)S(1)} %add_add_fusion.1), channel_id=1, source_target_pairs={{0,1},{1,0},{2,3},{3,2},{4,5},{5,4},{6,7},{7,6},{8,9},{9,8},{10,11... | collective-permute-start | bytes 49160 | tf_op jit(solution)/shard_map/ppermute | solution.py:385

commit v4 on v3

--- a/solution.py
+++ b/solution.py
@@ -56,46 +56,24 @@
         copy.wait()
 
 
-def cube_place(destination, own, count):
-    relative = jnp.bitwise_xor(destination, own)
-    place = jnp.zeros_like(relative)
-    bit = 1
-    while bit < count:
-        place = 2 * place + jnp.bitwise_and(relative, bit) // bit
-        bit *= 2
-    return place
-
-
-def cube_exchange(kept, leaving, axis):
-    count = lax.axis_size(axis)
-    assert power_of_two(count)
-    held = [kept]
-    bit = 1
-    while True:
-        held.append(lax.ppermute(leaving, axis, partners(count, bit)))
-        bit *= 2
-        if bit >= count:
-            return held
-        span = count // bit
-        tails = []
-        for h, part in enumerate(held):
-            cut = part.reshape(-1, span, *part.shape[-2:])
-            tails.append(cut[:, span // 2:].reshape(-1, *part.shape[-2:]))
-            held[h] = cut[:, :span // 2].reshape(-1, *part.shape[-2:])
-        leaving = jnp.concatenate(tails, axis=0)
-
-
 def force_kernel(clu_count, *refs):
-    sources, targets, sems = refs[:10], refs[14:24], refs[24]
-    sent_ref, force_ref, kept_ref, leaving_ref = refs[10:14]
+    sources, targets, sems = refs[:10], refs[13:23], refs[23]
+    sent_ref, force_ref, packed_ref = refs[10:13]
     fetch(sources, targets, sems)
     (own_ref, nodes_ref, pos_ref, ten_ref, bend_ref, order_ref, dest_ref, target_ref, deriv_ref,
      table_ref) = targets
     half = own_ref.shape[0] // 2
     core = lax.rem(lax.axis_index("clu"), 2)
-    sent_ref[0:half] = own_ref[pl.ds(pl.multiple_of(core * half, half), half), :]
-    spots = jnp.concatenate([nodes_ref[...].astype(F32)] * 8, axis=0)
-    sent_ref[half:half + 16] = spots.astype(BF16)
+    mine = own_ref[pl.ds(pl.multiple_of(core * half, half), half), :]
+    spots = nodes_ref[...].astype(F32)
+    lanes = pos_ref.shape[1]
+    columns = own_ref.shape[1] // lanes
+    for c in range(columns):
+        sent_ref[c * half:(c + 1) * half] = mine[:, c * lanes:(c + 1) * lanes]
+    spots = jnp.concatenate([spots[:, c * lanes:(c + 1) * lanes] for c in range(columns)], axis=0)
+    tail = sent_ref.shape[0] - columns * half
+    spots = jnp.concatenate([spots, jnp.zeros((tail - 2 * columns, lanes), F32)], axis=0)
+    sent_ref[columns * half:] = spots.astype(BF16)
     vesicles = ten_ref.shape[0]
     moves = target_ref.shape[1]
     x = pos_ref[pl.ds(0, vesicles, stride=2), :]
@@ -114,11 +92,10 @@
     force_ref[pl.ds(1, vesicles, stride=2), :] = force_y
 
     slots = clu_count * BLOCK
-    place = cube_place(dest_ref[...], lax.axis_index("clu"), clu_count)
-    hot = (iota((clu_count, moves), 0) == place).astype(F32)
+    hot = (iota((clu_count, moves), 0) == dest_ref[...]).astype(F32)
     earlier = (iota((moves, moves), 0) < iota((moves, moves), 1)).astype(F32)
     rank = jnp.sum(dot(hot, earlier) * hot, axis=0, keepdims=True).astype(jnp.int32)
-    slot = place * BLOCK + rank
+    slot = dest_ref[...] * BLOCK + rank
     pack = (iota((slots, moves), 0) == slot).astype(F32)
     pick = (iota((vesicles, moves), 0) == order_ref[:, :moves]).astype(F32)
     select = dot(pack, pick, NT)
@@ -127,21 +104,15 @@
     tag = jnp.sum(pack * (target_ref[...] + 1).astype(F32), axis=1, keepdims=True)
     tag = jnp.broadcast_to(tag, (slots, x.shape[1]))
     packed = jnp.concatenate([packed, tag], axis=1)
-    packed = packed.reshape(clu_count, BLOCK, packed.shape[1])
-    kept_ref[...] = packed[:clu_count // 2]
-    leaving_ref[...] = packed[clu_count // 2:]
-
-
-def near_kernel(slot_cap, piece_count, pos_ref, *refs):
-    piece_refs = refs[:piece_count]
-    before_ref, near_ref, arrived, aim_x, aim_y, speed_x, speed_y = refs[piece_count:]
+    packed_ref[...] = packed.reshape(clu_count, BLOCK, packed.shape[1])
+
+
+def near_kernel(slot_cap, span, pos_ref, all_ref, before_ref, near_ref, aim_x, aim_y, speed_x,
+                speed_y):
     vesicles = pos_ref.shape[0] // 2
     nodes = pos_ref.shape[1]
-    here = 0
-    for ref in piece_refs:
-        arrived[here:here + ref.shape[0]] = ref[...]
-        here += ref.shape[0]
-    pieces = arrived.shape[0]
+    arrived = all_ref.at[span[0]:span[1]]
+    pieces = span[1] - span[0]
     slots = pieces * BLOCK
     tag = arrived[:, :, 4 * nodes:].reshape(slots, nodes)[:, :vesicles]
     hot = (tag == (iota((slots, vesicles), 1) + 1).astype(F32)).astype(F32)
@@ -191,21 +162,19 @@
     near_ref[pl.ds(1, vesicles, stride=2), :] = near_y
 
 
-def near_start(slot_cap, piece_count, pos_ref, *refs):
-    near_kernel(slot_cap, piece_count, pos_ref, *refs[:piece_count], None, *refs[piece_count:])
-
-
-def near_part(flat, pieces, before, slot_cap):
+def near_start(slot_cap, span, pos_ref, all_ref, *refs):
+    near_kernel(slot_cap, span, pos_ref, all_ref, None, *refs)
+
+
+def near_part(flat, arrived, span, before, slot_cap):
     vesicles, nodes = flat.shape[0] // 2, flat.shape[1]
-    count = sum(p.shape[0] for p in pieces)
-    operands = [flat, *pieces] + ([] if before is None else [before])
+    operands = [flat, arrived] + ([] if before is None else [before])
     return pl.pallas_call(
-        functools.partial(near_start if before is None else near_kernel, slot_cap, len(pieces)),
+        functools.partial(near_start if before is None else near_kernel, slot_cap, span),
         out_shape=jax.ShapeDtypeStruct((2 * vesicles, nodes), F32),
         in_specs=[whole_spec()] * len(operands),
         out_specs=whole_spec(),
-        scratch_shapes=[pltpu.VMEM((count, BLOCK, 5 * nodes), F32)]
-        + [pltpu.VMEM((count, BLOCK, nodes), F32)] * 4,
+        scratch_shapes=[pltpu.VMEM((span[1] - span[0], BLOCK, nodes), F32)] * 4,
         compiler_params=params(16),
         cost_estimate=pl.CostEstimate(
             flops=10**9, bytes_accessed=10**7, transcendentals=10**6),
@@ -215,8 +184,8 @@
 def far_kernel(col_count, range_in, pos_in, own_in, nodes_in, *refs):
     count = 2 * (col_count - 1)
     piece_refs = refs[:count]
-    (high_ref, low_ref, gram_ref, range_ref, pos_ref, own_nodes, basis, spots, wide, buffer,
-     sums, sems) = refs[count:]
+    (high_ref, low_ref, gram_ref, range_ref, pos_ref, own_nodes, basis, spots, wide, buffer_0,
+     buffer_1, sums, sems) = refs[count:]
     vesicles = pos_ref.shape[0] // 2
     nodes = pos_ref.shape[1]
     _, rows, sources = basis.shape
@@ -227,9 +196,15 @@
     for k in range(1, col_count):
         where = origin(col, k, col_count)
         mine, other = piece_refs[2 * k - 2], piece_refs[2 * k - 1]
-        basis[where, pl.ds(pl.multiple_of(core * half, half), half), :] = mine[0:half]
-        basis[where, pl.ds(pl.multiple_of((1 - core) * half, half), half), :] = other[0:half]
-        spots[where, 0:2] = mine[half:half + 16].astype(F32)[0:2]
+        columns = sources // nodes
+        ends = mine[columns * half:].astype(F32)
+        for c in range(columns):
+            lanes = slice(c * nodes, (c + 1) * nodes)
+            from_rows = slice(c * half, (c + 1) * half)
+            basis[where, pl.ds(pl.multiple_of(core * half, half), half), lanes] = mine[from_rows]
+            basis[where, pl.ds(pl.multiple_of((1 - core) * half, half), half), lanes] = (
+                other[from_rows])
+            spots[where, 0:2, lanes] = ends[2 * c:2 * c + 2]
     for r in range(col_count):
         turned = spots[r].T
         for c in range(2):
@@ -237,11 +212,11 @@
     sums[...] = jnp.zeros_like(sums)
     chunk = 32 if sources % 32 == 0 else sources
 
-    def evaluate(v, slot):
+    def evaluate(v, buffer, part, parts):
         r = range_ref[0, v]
         tx = pos_ref[pl.ds(2 * v, 1), :]
         ty = pos_ref[pl.ds(2 * v + 1, 1), :]
-        for start in range(0, sources, chunk):
+        for start in range(part * sources // parts, (part + 1) * sources // parts, chunk):
             dx = tx - wide[r, 0, start:start + chunk]
             dy = ty - wide[r, 1, start:start + chunk]
             spread = dx * dx + dy * dy + EPS_SQUARED
@@ -249,19 +224,26 @@
             inverse = reciprocal(spread)
             dxr = dx * inverse
             here = slice(start, start + chunk)
-            buffer[slot, here, 0:nodes] = (log_part + dx * dxr).astype(BF16)
-            buffer[slot, here, nodes:2 * nodes] = (dy * dxr).astype(BF16)
-            buffer[slot, here, 2 * nodes:] = (log_part + dy * (dy * inverse)).astype(BF16)
-
-    def multiply(v, slot):
-        product = dot(basis[range_ref[0, v]], buffer[slot])
-        first = product[:rank, :nodes] + product[rank:, nodes:2 * nodes]
-        second = product[:rank, nodes:2 * nodes] + product[rank:, 2 * nodes:]
-        high_0, high_1 = first.astype(BF16), second.astype(BF16)
-        low_0 = (first - high_0.astype(F32)).astype(BF16)
-        low_1 = (second - high_1.astype(F32)).astype(BF16)
-        high_ref[v] = jnp.concatenate([high_0, high_1], axis=0)
-        low_ref[v] = jnp.concatenate([low_0, low_1], axis=0)
+            buffer[here, 0:nodes] = (log_part + dx * dxr).astype(BF16)
+            buffer[here, nodes:2 * nodes] = (dy * dxr).astype(BF16)
+            buffer[here, 2 * nodes:] = (log_part + dy * (dy * inverse)).astype(BF16)
+
+    def keep(v, d, value):
+        high = value.astype(BF16)
+        high_ref[v, d * rank:(d + 1) * rank] = high
+        low_ref[v, d * rank:(d + 1) * rank] = (value - high.astype(F32)).astype(BF16)
+
+    def step(v, now, following):
+        later = jnp.minimum(v + 1, vesicles - 1)
+        rows_now = basis[range_ref[0, v]]
+        product = dot(rows_now, now[:, :2 * nodes])
+        evaluate(later, following, 0, 4)
+        last = dot(rows_now, now[:, 2 * nodes:])
+        evaluate(later, following, 1, 4)
+        keep(v, 0, product[:rank, :nodes] + product[rank:, nodes:])
+        evaluate(later, following, 2, 4)
+        keep(v, 1, product[:rank, nodes:] + last[rank:])
+        evaluate(later, following, 3, 4)
 
     def add_gram(v):
         both = jnp.concatenate([
@@ -270,17 +252,15 @@
             for ref in (high_ref, low_ref)], axis=0)
         sums[...] += dot(both, both, NT)
 
-    evaluate(0, 0)
+    evaluate(0, buffer_0, 0, 1)
     high_ref[0:2] = jnp.zeros((2, rows, nodes), BF16)
     low_ref[0:2] = jnp.zeros((2, rows, nodes), BF16)
 
     def pair(i, _):
         v = 2 * i
         add_gram(jnp.maximum(v - 2, 0))
-        evaluate(v + 1, 1)
-        multiply(v, 0)
-        evaluate(jnp.minimum(v + 2, vesicles - 1), 0)
-        multiply(v + 1, 1)
+        step(v, buffer_0, buffer_1)
+        step(v + 1, buffer_1, buffer_0)
         return 0
 
     lax.fori_loop(0, vesicles // 2, pair, 0)
@@ -397,18 +377,20 @@
     slot_cap = 2 * ((moves + clu_count - 1) // clu_count)
     flat = positions.reshape(2 * vesicles, nodes)
 
+    columns = sources // nodes
+    sent_rows = columns * rank + (2 * columns + 15) // 16 * 16
     deriv, table = spectral_tables(nodes)
     operands = [old_basis, source_nodes, flat, tension, bending.reshape(1, vesicles), moved_order,
                 move_destination.reshape(1, moves), move_target.reshape(1, moves),
                 jnp.asarray(deriv), jnp.asarray(table)]
     operands = [pltpu.with_memory_space_constraint(o, pltpu.HBM) for o in operands]
-    sent, force, kept, leaving = pl.pallas_call(
+    sent, force, packed = pl.pallas_call(
         functools.partial(force_kernel, clu_count),
-        out_shape=[jax.ShapeDtypeStruct((rank + 16, sources), BF16),
+        out_shape=[jax.ShapeDtypeStruct((sent_rows, nodes), BF16),
                    jax.ShapeDtypeStruct((2 * vesicles, nodes), F32),
-                   *[jax.ShapeDtypeStruct((clu_count // 2, BLOCK, 5 * nodes), F32)] * 2],
+                   jax.ShapeDtypeStruct((clu_count, BLOCK, 5 * nodes), F32)],
         in_specs=[far_off_spec()] * len(operands),
-        out_specs=[whole_spec()] * 4,
+        out_specs=[whole_spec()] * 3,
         scratch_shapes=[pltpu.VMEM(o.shape, o.dtype) for o in operands]
         + [pltpu.SemaphoreType.DMA((len(operands),))],
         compiler_params=params(16),
@@ -416,13 +398,13 @@
     )(*operands)
 
     moved_halves = [lax.ppermute(sent, "col", partners(col_count, k)) for k in range(1, col_count)]
-    arrived = cube_exchange(kept, leaving, "clu")
+    arrived = lax.all_to_all(packed, "clu", split_axis=0, concat_axis=0, tiled=True)
     pieces = []
     for mine in moved_halves:
         pieces += [mine, lax.ppermute(mine, "clu", [(i, i ^ 1) for i in range(clu_count)])]
 
-    near = near_part(flat, arrived[:-1], None, slot_cap)
-    near = near_part(flat, arrived[-1:], near, slot_cap)
+    near = near_part(flat, arrived, (0, clu_count // 2), None, slot_cap)
+    near = near_part(flat, arrived, (clu_count // 2, clu_count), near, slot_cap)
 
     high, low, gram = pl.pallas_call(
         functools.partial(far_kernel, col_count),
@@ -437,7 +419,8 @@
             pltpu.VMEM((col_count, rows, sources), BF16),
             pltpu.VMEM((col_count, 8, sources), F32),
             pltpu.VMEM((col_count, 2, sources, nodes), F32),
-            pltpu.VMEM((2, sources, 3 * nodes), BF16),
+            pltpu.VMEM((sources, 3 * nodes), BF16),
+            pltpu.VMEM((sources, 3 * nodes), BF16),
             pltpu.VMEM((rows, rows), F32),
             pltpu.SemaphoreType.DMA((4,))],
         compiler_params=params(32),

time: 53.1 us -> 53 us (level)
  waiting for transfers between devices: 8.52 us -> 6.83 us
  starting transfers between devices: 17.2 us -> 18.4 us
    all_to_all x0 -> x1, starting transfers between devices: none -> 3.72 us  [per_device(): lax.all_to_all(packed, 'clu', split_axis=0, concat_axis=0, tiled=True)]
    ppermute x3 -> x0, starting transfers between devices: 3.01 us -> none  [cube_exchange(): held.append(lax.ppermute(leaving, axis, partners(count, bit)))]
    ppermute x3 -> x0, waiting for transfers between devices: 1.27 us -> none  [cube_exchange(): held.append(lax.ppermute(leaving, axis, partners(count, bit)))]
    ppermute x7, waiting for transfers between devices: 2.32 us -> 1.55 us  [sum_over(): moved = [lax.ppermute(value, axis, partners(count, k)) for k in steps]]
  transfers between devices with their start and end apart: 16 -> 14, of which waited for: 7 -> 5; matrix products, arithmetic and copies ran while one was open for 0% -> 0% of each run, Pallas kernels for 39% -> 37%
where the time goes in v4:
time: 53 us; the launch traced here: 52.7 us
  Pallas kernels  26.8 us (51%)
  starting transfers between devices  18.4 us (35%)
  waiting for transfers between devices  6.83 us (13%)
  between operations  0.7 us (1%)
    pallas_call x1, Pallas kernels, per_device(): pl.pallas_call(functools.partial(far_kernel, col_count), out_shape=[jax.S...  13.1 us
    ppermute x7, starting transfers between devices, sum_over(): moved = [lax.ppermute(value, axis, partners(count, k)) for k in steps]  8.43 us
    pallas_call x2, Pallas kernels, near_part(): pl.pallas_call(functools.partial(near_start if before is None else near_k...  6.35 us
    ppermute x3, starting transfers between devices, per_device(): lax.ppermute(sent, 'col', partners(col_count, k))  5.76 us
    ppermute x3, waiting for transfers between devices, per_device(): lax.ppermute(sent, 'col', partners(col_count, k))  5.27 us
    pallas_call x1, Pallas kernels, per_device(): pl.pallas_call(functools.partial(basis_kernel, scale_factor), out_shape=j...  4.88 us
    all_to_all x1, starting transfers between devices, per_device(): lax.all_to_all(packed, 'clu', split_axis=0, concat_axis=0, tiled=True)  3.72 us
    pallas_call x1, Pallas kernels, per_device(): pl.pallas_call(functools.partial(force_kernel, clu_count), out_shape=[jax...  2.44 us
  transfers between devices with their start and end apart: 14, of which 5 were waited for; matrix products, arithmetic and copies ran while one was open for 0% of the time, Pallas kernels for 37%

profile of v4, /device:TPU:0, one launch (start us, length us, event | category | flops | bytes accessed | tf_op | source)
XLA Modules:
  0.0 52.7 jit_solution(1948217160529925235)
XLA Ops:
  0.6 2.4 %shard_map.130 = (bf16[272,128]{1,0:T(8,128)(2,1)S(1)}, f32[64,128]{1,0:T(8,128)}, f32[8,8,640]{2,1,0:T(8,128)}) custom-call(bf16[128,512]{1,0:T(8,128)(2,1)} %own_in.1, bf16[2,512]{1,0:T(2,128)(2,1)} %nodes_in.1, f32[64,128]{1,0:T(8,128)} %bitcast.8, f32[32,128]{1,0:T(8,128)} %refs_3_.1, f32[1,32]{1,0:T(1,128)} %bitcast.13, s32[1,32]{1,0:T(1,128)} %refs_5_.1, ...), custom_call_target="tpu_custom_call" | custom-call | flops 100000000 | bytes 1000000 | tf_op jit(solution)/shard_map/pallas_call | solution.py:387
  3.1 5.1 %collective-permute-start.4 = (bf16[272,128]{1,0:T(8,128)(2,1)S(1)}, bf16[272,128]{1,0:T(8,128)(2,1)S(1)}, u32[]{:S(2)}, u32[]{:S(2)}) collective-permute-start(bf16[272,128]{1,0:T(8,128)(2,1)S(1)} %get-tuple-element.11), channel_id=1, source_target_pairs={{0,3},{1,2},{2,1},{3,0},{4,7},{5,6},{6,5},{7,4},{8,11},{9,10},{10,... | collective-permute-start | bytes 208904 | tf_op jit(solution)/shard_map/ppermute | solution.py:400
  8.2 0.0 collective-permute-start.2
  8.2 0.6 %collective-permute-start = (bf16[272,128]{1,0:T(8,128)(2,1)S(1)}, bf16[272,128]{1,0:T(8,128)(2,1)S(1)}, u32[]{:S(2)}, u32[]{:S(2)}) collective-permute-start(bf16[272,128]{1,0:T(8,128)(2,1)S(1)} %get-tuple-element.11), channel_id=1, source_target_pairs={{0,1},{1,0},{2,3},{3,2},{4,5},{5,4},{6,7},{7,6},{8,9},{9,8},{10,11... | collective-permute-start | bytes 208904 | tf_op jit(solution)/shard_map/ppermute | solution.py:400
  8.8 2.0 %collective-permute-done.4.refs_4_ = bf16[272,128]{1,0:T(8,128)(2,1)S(1)} collective-permute-done((bf16[272,128]{1,0:T(8,128)(2,1)S(1)}, bf16[272,128]{1,0:T(8,128)(2,1)S(1)}, u32[]{:S(2)}, u32[]{:S(2)}) %collective-permute-start.4) | collective-permute-done | bytes 69664 | tf_op jit(solution)/shard_map/ppermute | solution.py:400
  10.9 0.0 collective-permute-start.5
  10.9 3.2 %collective-permute-done.2.refs_2_ = bf16[272,128]{1,0:T(8,128)(2,1)S(1)} collective-permute-done((bf16[272,128]{1,0:T(8,128)(2,1)S(1)}, bf16[272,128]{1,0:T(8,128)(2,1)S(1)}, u32[]{:S(2)}, u32[]{:S(2)}) %collective-permute-start.2) | collective-permute-done | bytes 69664 | tf_op jit(solution)/shard_map/ppermute | solution.py:400
  14.1 0.0 collective-permute-start.3
  14.1 0.0 collective-permute-done.refs_0_
  14.1 0.5 collective-permute-start.1
  14.6 3.7 %all-to-all-start = ((f32[8,8,640]{2,1,0:T(8,128)}), f32[8,8,640]{2,1,0:T(8,128)S(1)}, u32[]{:S(2)}, u32[]{:S(2)}) async-start(f32[8,8,640]{2,1,0:T(8,128)} %get-tuple-element.10), calls=%async_computation | async-start | bytes 327680 | tf_op jit(solution)/shard_map/all_to_all | solution.py:401
  18.3 0.0 collective-permute-done.5.refs_5_
  18.4 0.0 collective-permute-done.1.refs_1_
  18.4 0.0 copy-start
  18.4 13.1 %shard_map.133 = (bf16[32,128,128]{2,1,0:T(8,128)(2,1)S(1)}, bf16[32,128,128]{2,1,0:T(8,128)(2,1)S(1)}, f32[32,128]{1,0:T(8,128)S(1)}) custom-call(s32[1,32]{1,0:T(1,128)} %bitcast.16, f32[64,128]{1,0:T(8,128)} %bitcast.9, bf16[128,512]{1,0:T(8,128)(2,1)} %own_in.1, bf16[2,512]{1,0:T(2,128)(2,1)} %nodes_in.1, ...), custom_call_target="tpu_custom_call" | custom-call | flops 10000000000 | bytes 10000000 | tf_op jit(solution)/shard_map/pallas_call | solution.py:409
  31.5 0.6 %collective-permute-start.6 = (f32[32,128]{1,0:T(8,128)S(1)}, f32[32,128]{1,0:T(8,128)S(1)}, u32[]{:S(2)}, u32[]{:S(2)}) collective-permute-start(f32[32,128]{1,0:T(8,128)S(1)} %get-tuple-element.12), channel_id=1, source_target_pairs={{0,4},{4,0},{8,12},{12,8},{16,20},{20,16},{24,28},{28,24},{1,5},{5... | collective-permute-start | bytes 49160 | tf_op jit(solution)/shard_map/ppermute | solution.py:365
  32.0 0.8 %collective-permute-done.6 = f32[32,128]{1,0:T(8,128)S(1)} collective-permute-done((f32[32,128]{1,0:T(8,128)S(1)}, f32[32,128]{1,0:T(8,128)S(1)}, u32[]{:S(2)}, u32[]{:S(2)}) %collective-permute-start.6) | collective-permute-done | bytes 16416 | tf_op jit(solution)/shard_map/ppermute | solution.py:365
  32.9 2.8 %collective-permute-start.9 = (f32[32,128]{1,0:T(8,128)S(1)}, f32[32,128]{1,0:T(8,128)S(1)}, u32[]{:S(2)}, u32[]{:S(2)}) collective-permute-start(f32[32,128]{1,0:T(8,128)S(1)} %add.21), channel_id=1, source_target_pairs={{0,24},{4,28},{8,16},{12,20},{16,8},{20,12},{24,0},{28,4},{1,25},{... | collective-permute-start | bytes 49160 | tf_op jit(solution)/shard_map/ppermute | solution.py:365
  35.6 0.6 %collective-permute-start.8 = (f32[32,128]{1,0:T(8,128)S(1)}, f32[32,128]{1,0:T(8,128)S(1)}, u32[]{:S(2)}, u32[]{:S(2)}) collective-permute-start(f32[32,128]{1,0:T(8,128)S(1)} %add.21), channel_id=1, source_target_pairs={{0,16},{4,20},{8,24},{12,28},{16,0},{20,4},{24,8},{28,12},{1,17},{... | collective-permute-start | bytes 49160 | tf_op jit(solution)/shard_map/ppermute | solution.py:365
  36.2 0.2 collective-permute-start.7
  36.4 2.9 %shard_map.131.before_ref = f32[64,128]{1,0:T(8,128)S(1)} custom-call(f32[64,128]{1,0:T(8,128)S(1)} %bitcast.10, f32[8,8,640]{2,1,0:T(8,128)S(1)} %all-to-all-done.all_ref), custom_call_target="tpu_custom_call" | custom-call | flops 1000000000 | bytes 10000000 | tf_op jit(solution)/shard_map/pallas_call | solution.py:172
  39.2 0.0 collective-permute-done.9
  39.2 0.1 collective-permute-done.8
  39.4 0.6 %collective-permute-done.7 = f32[32,128]{1,0:T(8,128)S(1)} collective-permute-done((f32[32,128]{1,0:T(8,128)S(1)}, f32[32,128]{1,0:T(8,128)S(1)}, u32[]{:S(2)}, u32[]{:S(2)}) %collective-permute-start.7) | collective-permute-done | bytes 16416 | tf_op jit(solution)/shard_map/ppermute | solution.py:365
  40.0 2.7 %collective-permute-start.12 = (f32[32,128]{1,0:T(8,128)S(1)}, f32[32,128]{1,0:T(8,128)S(1)}, u32[]{:S(2)}, u32[]{:S(2)}) collective-permute-start(f32[32,128]{1,0:T(8,128)S(1)} %add_add_fusion.1), channel_id=1, source_target_pairs={{0,3},{1,2},{2,1},{3,0},{4,7},{5,6},{6,5},{7,4},{8,11},{9,10},{10,... | collective-permute-start | bytes 49160 | tf_op jit(solution)/shard_map/ppermute | solution.py:365
  42.7 0.0 collective-permute-start.11
  42.7 1.7 %collective-permute-start.10 = (f32[32,128]{1,0:T(8,128)S(1)}, f32[32,128]{1,0:T(8,128)S(1)}, u32[]{:S(2)}, u32[]{:S(2)}) collective-permute-start(f32[32,128]{1,0:T(8,128)S(1)} %add_add_fusion.1), channel_id=1, source_target_pairs={{0,1},{1,0},{2,3},{3,2},{4,5},{5,4},{6,7},{7,6},{8,9},{9,8},{10,11... | collective-permute-start | bytes 49160 | tf_op jit(solution)/shard_map/ppermute | solution.py:365
  44.3 3.5 %shard_map.132 = f32[64,128]{1,0:T(8,128)} custom-call(f32[64,128]{1,0:T(8,128)S(1)} %bitcast.11, f32[8,8,640]{2,1,0:T(8,128)S(1)} %all-to-all-done.all_ref, f32[64,128]{1,0:T(8,128)S(1)} %shard_map.131.before_ref), custom_call_target="tpu_custom_call" | custom-call | flops 1000000000 | bytes 10000000 | tf_op jit(solution)/shard_map/pallas_call | solution.py:172
  47.8 0.0 collective-permute-done.12
  47.8 0.0 collective-permute-done.11
  47.8 0.0 collective-permute-done.10
  47.9 4.9 %shard_map.134 = f32[32,128,128]{2,1,0:T(8,128)} custom-call(f32[32,128]{1,0:T(8,128)S(1)} %add_add_fusion.refs_0_, bf16[32,128,128]{2,1,0:T(8,128)(2,1)S(1)} %get-tuple-element.13.refs_1_, bf16[32,128,128]{2,1,0:T(8,128)(2,1)S(1)} %get-tuple-element.14.refs_2_), custom_call_target="tpu_custom_call" | custom-call | flops 1000000000 | bytes 10000000 | tf_op jit(solution)/shard_map/pallas_call | solution.py:436
  (6 shorter events, 0.0 us)
Async XLA Ops:
  3.1 7.8 %collective-permute-start.4 = (bf16[272,128]{1,0:T(8,128)(2,1)S(1)}, bf16[272,128]{1,0:T(8,128)(2,1)S(1)}, u32[]{:S(2)}, u32[]{:S(2)}) collective-permute-start(bf16[272,128]{1,0:T(8,128)(2,1)S(1)} %get-tuple-element.11), channel_id=1, source_target_pairs={{0,3},{1,2},{2,1},{3,0},{4,7},{5,6},{6,5},{7,4},{8,11},{9,10},{10,... | collective-permute-start | bytes 208904 | tf_op jit(solution)/shard_map/ppermute | solution.py:400
  8.2 5.9 %collective-permute-start.2 = (bf16[272,128]{1,0:T(8,128)(2,1)S(1)}, bf16[272,128]{1,0:T(8,128)(2,1)S(1)}, u32[]{:S(2)}, u32[]{:S(2)}) collective-permute-start(bf16[272,128]{1,0:T(8,128)(2,1)S(1)} %get-tuple-element.11), channel_id=1, source_target_pairs={{0,2},{1,3},{2,0},{3,1},{4,6},{5,7},{6,4},{7,5},{8,10},{9,11},{10,... | collective-permute-start | bytes 208904 | tf_op jit(solution)/shard_map/ppermute | solution.py:400
  8.2 5.9 %collective-permute-start = (bf16[272,128]{1,0:T(8,128)(2,1)S(1)}, bf16[272,128]{1,0:T(8,128)(2,1)S(1)}, u32[]{:S(2)}, u32[]{:S(2)}) collective-permute-start(bf16[272,128]{1,0:T(8,128)(2,1)S(1)} %get-tuple-element.11), channel_id=1, source_target_pairs={{0,1},{1,0},{2,3},{3,2},{4,5},{5,4},{6,7},{7,6},{8,9},{9,8},{10,11... | collective-permute-start | bytes 208904 | tf_op jit(solution)/shard_map/ppermute | solution.py:400
  10.9 7.5 %collective-permute-start.5 = (bf16[272,128]{1,0:T(8,128)(2,1)S(1)}, bf16[272,128]{1,0:T(8,128)(2,1)S(1)}, u32[]{:S(2)}, u32[]{:S(2)}) collective-permute-start(bf16[272,128]{1,0:T(8,128)(2,1)S(1)} %collective-permute-done.4.refs_4_), channel_id=1, source_target_pairs={{0,4},{4,0},{8,12},{12,8},{16,20},{20,16},{24,28},{28,24},{1,5},{5... | collective-permute-start | bytes 208904 | tf_op jit(solution)/shard_map/ppermute | solution.py:404
  14.1 4.2 %collective-permute-start.3 = (bf16[272,128]{1,0:T(8,128)(2,1)S(1)}, bf16[272,128]{1,0:T(8,128)(2,1)S(1)}, u32[]{:S(2)}, u32[]{:S(2)}) collective-permute-start(bf16[272,128]{1,0:T(8,128)(2,1)S(1)} %collective-permute-done.2.refs_2_), channel_id=1, source_target_pairs={{0,4},{4,0},{8,12},{12,8},{16,20},{20,16},{24,28},{28,24},{1,5},{5... | collective-permute-start | bytes 208904 | tf_op jit(solution)/shard_map/ppermute | solution.py:404
  14.1 4.2 %collective-permute-start.1 = (bf16[272,128]{1,0:T(8,128)(2,1)S(1)}, bf16[272,128]{1,0:T(8,128)(2,1)S(1)}, u32[]{:S(2)}, u32[]{:S(2)}) collective-permute-start(bf16[272,128]{1,0:T(8,128)(2,1)S(1)} %collective-permute-done.refs_0_), channel_id=1, source_target_pairs={{0,4},{4,0},{8,12},{12,8},{16,20},{20,16},{24,28},{28,24},{1,5},{5... | collective-permute-start | bytes 208904 | tf_op jit(solution)/shard_map/ppermute | solution.py:404
  14.6 21.7 %all-to-all-start = ((f32[8,8,640]{2,1,0:T(8,128)}), f32[8,8,640]{2,1,0:T(8,128)S(1)}, u32[]{:S(2)}, u32[]{:S(2)}) async-start(f32[8,8,640]{2,1,0:T(8,128)} %get-tuple-element.10), calls=%async_computation | async-start | bytes 327680 | tf_op jit(solution)/shard_map/all_to_all | solution.py:401
  18.4 18.0 %copy-start = (f32[32,2,128]{2,1,0:T(2,128)S(1)}, f32[32,2,128]{2,1,0:T(2,128)}, u32[]{:S(2)}) copy-start(f32[32,2,128]{2,1,0:T(2,128)} %param.11) | copy-start | bytes 98308
  31.5 1.4 %collective-permute-start.6 = (f32[32,128]{1,0:T(8,128)S(1)}, f32[32,128]{1,0:T(8,128)S(1)}, u32[]{:S(2)}, u32[]{:S(2)}) collective-permute-start(f32[32,128]{1,0:T(8,128)S(1)} %get-tuple-element.12), channel_id=1, source_target_pairs={{0,4},{4,0},{8,12},{12,8},{16,20},{20,16},{24,28},{28,24},{1,5},{5... | collective-permute-start | bytes 49160 | tf_op jit(solution)/shard_map/ppermute | solution.py:365
  32.9 6.4 %collective-permute-start.9 = (f32[32,128]{1,0:T(8,128)S(1)}, f32[32,128]{1,0:T(8,128)S(1)}, u32[]{:S(2)}, u32[]{:S(2)}) collective-permute-start(f32[32,128]{1,0:T(8,128)S(1)} %add.21), channel_id=1, source_target_pairs={{0,24},{4,28},{8,16},{12,20},{16,8},{20,12},{24,0},{28,4},{1,25},{... | collective-permute-start | bytes 49160 | tf_op jit(solution)/shard_map/ppermute | solution.py:365
  35.6 3.7 %collective-permute-start.8 = (f32[32,128]{1,0:T(8,128)S(1)}, f32[32,128]{1,0:T(8,128)S(1)}, u32[]{:S(2)}, u32[]{:S(2)}) collective-permute-start(f32[32,128]{1,0:T(8,128)S(1)} %add.21), channel_id=1, source_target_pairs={{0,16},{4,20},{8,24},{12,28},{16,0},{20,4},{24,8},{28,12},{1,17},{... | collective-permute-start | bytes 49160 | tf_op jit(solution)/shard_map/ppermute | solution.py:365
  36.2 3.7 %collective-permute-start.7 = (f32[32,128]{1,0:T(8,128)S(1)}, f32[32,128]{1,0:T(8,128)S(1)}, u32[]{:S(2)}, u32[]{:S(2)}) collective-permute-start(f32[32,128]{1,0:T(8,128)S(1)} %add.21), channel_id=1, source_target_pairs={{0,8},{4,12},{8,0},{12,4},{16,24},{20,28},{24,16},{28,20},{1,9},{5... | collective-permute-start | bytes 49160 | tf_op jit(solution)/shard_map/ppermute | solution.py:365
  40.0 7.9 %collective-permute-start.12 = (f32[32,128]{1,0:T(8,128)S(1)}, f32[32,128]{1,0:T(8,128)S(1)}, u32[]{:S(2)}, u32[]{:S(2)}) collective-permute-start(f32[32,128]{1,0:T(8,128)S(1)} %add_add_fusion.1), channel_id=1, source_target_pairs={{0,3},{1,2},{2,1},{3,0},{4,7},{5,6},{6,5},{7,4},{8,11},{9,10},{10,... | collective-permute-start | bytes 49160 | tf_op jit(solution)/shard_map/ppermute | solution.py:365
  42.7 5.2 %collective-permute-start.11 = (f32[32,128]{1,0:T(8,128)S(1)}, f32[32,128]{1,0:T(8,128)S(1)}, u32[]{:S(2)}, u32[]{:S(2)}) collective-permute-start(f32[32,128]{1,0:T(8,128)S(1)} %add_add_fusion.1), channel_id=1, source_target_pairs={{0,2},{1,3},{2,0},{3,1},{4,6},{5,7},{6,4},{7,5},{8,10},{9,11},{10,... | collective-permute-start | bytes 49160 | tf_op jit(solution)/shard_map/ppermute | solution.py:365
  42.7 5.2 %collective-permute-start.10 = (f32[32,128]{1,0:T(8,128)S(1)}, f32[32,128]{1,0:T(8,128)S(1)}, u32[]{:S(2)}, u32[]{:S(2)}) collective-permute-start(f32[32,128]{1,0:T(8,128)S(1)} %add_add_fusion.1), channel_id=1, source_target_pairs={{0,1},{1,0},{2,3},{3,2},{4,5},{5,4},{6,7},{7,6},{8,9},{9,8},{10,11... | collective-permute-start | bytes 49160 | tf_op jit(solution)/shard_map/ppermute | solution.py:365

commit v5 on v4

--- a/solution.py
+++ b/solution.py
@@ -14,6 +14,7 @@
 BF16 = jnp.bfloat16
 HIGHEST = lax.Precision.HIGHEST
 BLOCK = 8
+DEPTH = 16
 MIB = 1 << 20
 
 NT = (((1,), (1,)), ((), ()))
@@ -56,17 +57,13 @@
         copy.wait()
 
 
-def force_kernel(clu_count, *refs):
-    sources, targets, sems = refs[:10], refs[13:23], refs[23]
-    sent_ref, force_ref, packed_ref = refs[10:13]
-    fetch(sources, targets, sems)
-    (own_ref, nodes_ref, pos_ref, ten_ref, bend_ref, order_ref, dest_ref, target_ref, deriv_ref,
-     table_ref) = targets
+def piece_kernel(own_in, nodes_in, sent_ref, own_ref, nodes_ref, sems):
+    fetch([own_in, nodes_in], [own_ref, nodes_ref], sems)
     half = own_ref.shape[0] // 2
     core = lax.rem(lax.axis_index("clu"), 2)
     mine = own_ref[pl.ds(pl.multiple_of(core * half, half), half), :]
     spots = nodes_ref[...].astype(F32)
-    lanes = pos_ref.shape[1]
+    lanes = sent_ref.shape[1]
     columns = own_ref.shape[1] // lanes
     for c in range(columns):
         sent_ref[c * half:(c + 1) * half] = mine[:, c * lanes:(c + 1) * lanes]
@@ -74,6 +71,42 @@
     tail = sent_ref.shape[0] - columns * half
     spots = jnp.concatenate([spots, jnp.zeros((tail - 2 * columns, lanes), F32)], axis=0)
     sent_ref[columns * half:] = spots.astype(BF16)
+
+
+def cube_place(destination, own, count):
+    relative = jnp.bitwise_xor(destination, own)
+    place = jnp.zeros_like(relative)
+    bit = 1
+    while bit < count:
+        place = 2 * place + jnp.bitwise_and(relative, bit) // bit
+        bit *= 2
+    return place
+
+
+def cube_exchange(kept, leaving, axis):
+    count = lax.axis_size(axis)
+    assert power_of_two(count)
+    held = [kept]
+    bit = 1
+    while True:
+        held.append(lax.ppermute(leaving, axis, partners(count, bit)))
+        bit *= 2
+        if bit >= count:
+            return held
+        span = count // bit
+        tails = []
+        for h, part in enumerate(held):
+            cut = part.reshape(-1, span, *part.shape[-2:])
+            tails.append(cut[:, span // 2:].reshape(-1, *part.shape[-2:]))
+            held[h] = cut[:, :span // 2].reshape(-1, *part.shape[-2:])
+        leaving = jnp.concatenate(tails, axis=0)
+
+
+def force_kernel(clu_count, *refs):
+    sources, targets, sems = refs[:8], refs[11:19], refs[19]
+    force_ref, kept_ref, leaving_ref = refs[8:11]
+    fetch(sources, targets, sems)
+    (pos_ref, ten_ref, bend_ref, order_ref, dest_ref, target_ref, deriv_ref, table_ref) = targets
     vesicles = ten_ref.shape[0]
     moves = target_ref.shape[1]
     x = pos_ref[pl.ds(0, vesicles, stride=2), :]
@@ -92,10 +125,11 @@
     force_ref[pl.ds(1, vesicles, stride=2), :] = force_y
 
     slots = clu_count * BLOCK
-    hot = (iota((clu_count, moves), 0) == dest_ref[...]).astype(F32)
+    place = cube_place(dest_ref[...], lax.axis_index("clu"), clu_count)
+    hot = (iota((clu_count, moves), 0) == place).astype(F32)
     earlier = (iota((moves, moves), 0) < iota((moves, moves), 1)).astype(F32)
     rank = jnp.sum(dot(hot, earlier) * hot, axis=0, keepdims=True).astype(jnp.int32)
-    slot = dest_ref[...] * BLOCK + rank
+    slot = place * BLOCK + rank
     pack = (iota((slots, moves), 0) == slot).astype(F32)
     pick = (iota((vesicles, moves), 0) == order_ref[:, :moves]).astype(F32)
     select = dot(pack, pick, NT)
@@ -104,15 +138,21 @@
     tag = jnp.sum(pack * (target_ref[...] + 1).astype(F32), axis=1, keepdims=True)
     tag = jnp.broadcast_to(tag, (slots, x.shape[1]))
     packed = jnp.concatenate([packed, tag], axis=1)
-    packed_ref[...] = packed.reshape(clu_count, BLOCK, packed.shape[1])
-
-
-def near_kernel(slot_cap, span, pos_ref, all_ref, before_ref, near_ref, aim_x, aim_y, speed_x,
-                speed_y):
+    packed = packed.reshape(clu_count, BLOCK, packed.shape[1])
+    kept_ref[...] = packed[:clu_count // 2]
+    leaving_ref[...] = packed[clu_count // 2:]
+
+
+def near_kernel(slot_cap, piece_count, pos_ref, *refs):
+    piece_refs = refs[:piece_count]
+    near_ref, arrived, aim_x, aim_y, speed_x, speed_y = refs[piece_count:]
     vesicles = pos_ref.shape[0] // 2
     nodes = pos_ref.shape[1]
-    arrived = all_ref.at[span[0]:span[1]]
-    pieces = span[1] - span[0]
+    here = 0
+    for ref in piece_refs:
+        arrived[here:here + ref.shape[0]] = ref[...]
+        here += ref.shape[0]
+    pieces = arrived.shape[0]
     slots = pieces * BLOCK
     tag = arrived[:, :, 4 * nodes:].reshape(slots, nodes)[:, :vesicles]
     hot = (tag == (iota((slots, vesicles), 1) + 1).astype(F32)).astype(F32)
@@ -155,37 +195,53 @@
     turned_hot = hot.T
     near_x = dot(turned_hot, speed_x[...].reshape(slots, nodes), precision=HIGHEST) / nodes
     near_y = dot(turned_hot, speed_y[...].reshape(slots, nodes), precision=HIGHEST) / nodes
-    if before_ref is not None:
-        near_x = near_x + before_ref[pl.ds(0, vesicles, stride=2), :]
-        near_y = near_y + before_ref[pl.ds(1, vesicles, stride=2), :]
     near_ref[pl.ds(0, vesicles, stride=2), :] = near_x
     near_ref[pl.ds(1, vesicles, stride=2), :] = near_y
 
 
-def near_start(slot_cap, span, pos_ref, all_ref, *refs):
-    near_kernel(slot_cap, span, pos_ref, all_ref, None, *refs)
-
-
-def near_part(flat, arrived, span, before, slot_cap):
-    vesicles, nodes = flat.shape[0] // 2, flat.shape[1]
-    operands = [flat, arrived] + ([] if before is None else [before])
-    return pl.pallas_call(
-        functools.partial(near_start if before is None else near_kernel, slot_cap, span),
-        out_shape=jax.ShapeDtypeStruct((2 * vesicles, nodes), F32),
-        in_specs=[whole_spec()] * len(operands),
-        out_specs=whole_spec(),
-        scratch_shapes=[pltpu.VMEM((span[1] - span[0], BLOCK, nodes), F32)] * 4,
-        compiler_params=params(16),
-        cost_estimate=pl.CostEstimate(
-            flops=10**9, bytes_accessed=10**7, transcendentals=10**6),
-    )(*operands)
+def parts_of(value, count):
+    parts = []
+    for _ in range(count):
+        part = value.astype(BF16).astype(F32)
+        parts.append(part)
+        value = value - part
+    return parts
+
+
+def source_powers(sx, sy):
+    one = jnp.ones_like(sx)
+    rows = [sx] * 3 + [sy] * 3 + [one] * 3
+    for value in (sx * sx, sy * sy, sx * sy):
+        rows += parts_of(value, 2)
+    return jnp.concatenate(rows + [jnp.zeros_like(sx)], axis=0)
+
+
+def target_factors(pos_ref, factors):
+    vesicles, nodes = pos_ref.shape[0] // 2, pos_ref.shape[1]
+    x = pos_ref[pl.ds(0, vesicles, stride=2), :]
+    y = pos_ref[pl.ds(1, vesicles, stride=2), :]
+    zero = jnp.zeros_like(x)
+    wanted = [
+        (-2.0 * x, -2.0 * y, x * x + y * y + EPS_SQUARED, 1.0, 1.0, 0.0),
+        (4.0 * x, zero, -2.0 * (x * x), -2.0, 0.0, 0.0),
+        (2.0 * y, 2.0 * x, -2.0 * (x * y), 0.0, 0.0, -2.0),
+        (zero, 4.0 * y, -2.0 * (y * y), 0.0, -2.0, 0.0),
+    ]
+    for c, entries in enumerate(wanted):
+        rows = []
+        for value in entries[:3]:
+            rows += parts_of(value, 3)
+        for value in entries[3:]:
+            rows += [jnp.full_like(x, value)] * 2
+        for k, row in enumerate(rows + [zero]):
+            factors[c, pl.ds(k, vesicles, stride=DEPTH), :] = row
 
 
 def far_kernel(col_count, range_in, pos_in, own_in, nodes_in, *refs):
     count = 2 * (col_count - 1)
     piece_refs = refs[:count]
-    (high_ref, low_ref, gram_ref, range_ref, pos_ref, own_nodes, basis, spots, wide, buffer_0,
-     buffer_1, sums, sems) = refs[count:]
+    (high_ref, low_ref, gram_ref, range_ref, pos_ref, own_nodes, basis, spots, powers, factors,
+     buffer_0, buffer_1, sums, sems) = refs[count:]
     vesicles = pos_ref.shape[0] // 2
     nodes = pos_ref.shape[1]
     _, rows, sources = basis.shape
@@ -206,27 +262,23 @@
                 other[from_rows])
             spots[where, 0:2, lanes] = ends[2 * c:2 * c + 2]
     for r in range(col_count):
-        turned = spots[r].T
-        for c in range(2):
-            wide[r, c] = jnp.broadcast_to(turned[:, c:c + 1], (sources, nodes))
+        powers[r] = source_powers(spots[r, 0:1], spots[r, 1:2]).T.astype(BF16)
+    target_factors(pos_ref, factors)
     sums[...] = jnp.zeros_like(sums)
-    chunk = 32 if sources % 32 == 0 else sources
 
     def evaluate(v, buffer, part, parts):
         r = range_ref[0, v]
-        tx = pos_ref[pl.ds(2 * v, 1), :]
-        ty = pos_ref[pl.ds(2 * v + 1, 1), :]
-        for start in range(part * sources // parts, (part + 1) * sources // parts, chunk):
-            dx = tx - wide[r, 0, start:start + chunk]
-            dy = ty - wide[r, 1, start:start + chunk]
-            spread = dx * dx + dy * dy + EPS_SQUARED
-            log_part = -0.5 * jnp.log(spread)
-            inverse = reciprocal(spread)
-            dxr = dx * inverse
-            here = slice(start, start + chunk)
-            buffer[here, 0:nodes] = (log_part + dx * dxr).astype(BF16)
-            buffer[here, nodes:2 * nodes] = (dy * dxr).astype(BF16)
-            buffer[here, 2 * nodes:] = (log_part + dy * (dy * inverse)).astype(BF16)
+        rows_here = pl.ds(pl.multiple_of(v * DEPTH, DEPTH), DEPTH)
+        mine = jnp.concatenate([factors[c, rows_here, :] for c in range(4)], axis=1).astype(BF16)
+        size = sources // parts
+        here = slice(part * size, (part + 1) * size)
+        shape = dot(powers[r, here], mine)
+        spread, xx, xy, yy = [shape[:, c * nodes:(c + 1) * nodes] for c in range(4)]
+        log_part = jnp.log(spread)
+        inverse = reciprocal(spread)
+        buffer[here, 0:nodes] = (log_part + inverse * xx).astype(BF16)
+        buffer[here, nodes:2 * nodes] = (inverse * xy).astype(BF16)
+        buffer[here, 2 * nodes:] = (log_part + inverse * yy).astype(BF16)
 
     def keep(v, d, value):
         high = value.astype(BF16)
@@ -252,7 +304,8 @@
             for ref in (high_ref, low_ref)], axis=0)
         sums[...] += dot(both, both, NT)
 
-    evaluate(0, buffer_0, 0, 1)
+    for part in range(4):
+        evaluate(0, buffer_0, part, 4)
     high_ref[0:2] = jnp.zeros((2, rows, nodes), BF16)
     low_ref[0:2] = jnp.zeros((2, rows, nodes), BF16)
 
@@ -380,15 +433,27 @@
     columns = sources // nodes
     sent_rows = columns * rank + (2 * columns + 15) // 16 * 16
     deriv, table = spectral_tables(nodes)
-    operands = [old_basis, source_nodes, flat, tension, bending.reshape(1, vesicles), moved_order,
+    near_by = functools.partial(pltpu.with_memory_space_constraint, memory_space=pltpu.HBM)
+    basis_here, nodes_here, flat_here = near_by(old_basis), near_by(source_nodes), near_by(flat)
+    sent = pl.pallas_call(
+        piece_kernel,
+        out_shape=jax.ShapeDtypeStruct((sent_rows, nodes), BF16),
+        in_specs=[far_off_spec()] * 2,
+        out_specs=whole_spec(),
+        scratch_shapes=[pltpu.VMEM(old_basis.shape, BF16), pltpu.VMEM(source_nodes.shape, BF16),
+                        pltpu.SemaphoreType.DMA((2,))],
+        compiler_params=params(16),
+        cost_estimate=pl.CostEstimate(flops=10**5, bytes_accessed=10**5, transcendentals=0),
+    )(basis_here, nodes_here)
+
+    operands = [flat, tension, bending.reshape(1, vesicles), moved_order,
                 move_destination.reshape(1, moves), move_target.reshape(1, moves),
                 jnp.asarray(deriv), jnp.asarray(table)]
-    operands = [pltpu.with_memory_space_constraint(o, pltpu.HBM) for o in operands]
-    sent, force, packed = pl.pallas_call(
+    operands = [flat_here] + [near_by(o) for o in operands[1:]]
+    force, kept, leaving = pl.pallas_call(
         functools.partial(force_kernel, clu_count),
-        out_shape=[jax.ShapeDtypeStruct((sent_rows, nodes), BF16),
-                   jax.ShapeDtypeStruct((2 * vesicles, nodes), F32),
-                   jax.ShapeDtypeStruct((clu_count, BLOCK, 5 * nodes), F32)],
+        out_shape=[jax.ShapeDtypeStruct((2 * vesicles, nodes), F32),
+                   *[jax.ShapeDtypeStruct((clu_count // 2, BLOCK, 5 * nodes), F32)] * 2],
         in_specs=[far_off_spec()] * len(operands),
         out_specs=[whole_spec()] * 3,
         scratch_shapes=[pltpu.VMEM(o.shape, o.dtype) for o in operands]
@@ -398,13 +463,22 @@
     )(*operands)
 
     moved_halves = [lax.ppermute(sent, "col", partners(col_count, k)) for k in range(1, col_count)]
-    arrived = lax.all_to_all(packed, "clu", split_axis=0, concat_axis=0, tiled=True)
+    arrived = cube_exchange(kept, leaving, "clu")
     pieces = []
     for mine in moved_halves:
         pieces += [mine, lax.ppermute(mine, "clu", [(i, i ^ 1) for i in range(clu_count)])]
 
-    near = near_part(flat, arrived, (0, clu_count // 2), None, slot_cap)
-    near = near_part(flat, arrived, (clu_count // 2, clu_count), near, slot_cap)
+    near = pl.pallas_call(
+        functools.partial(near_kernel, slot_cap, len(arrived)),
+        out_shape=jax.ShapeDtypeStruct((2 * vesicles, nodes), F32),
+        in_specs=[whole_spec()] * (1 + len(arrived)),
+        out_specs=whole_spec(),
+        scratch_shapes=[pltpu.VMEM((clu_count, BLOCK, 5 * nodes), F32)]
+        + [pltpu.VMEM((clu_count, BLOCK, nodes), F32)] * 4,
+        compiler_params=params(16),
+        cost_estimate=pl.CostEstimate(
+            flops=10**9, bytes_accessed=10**7, transcendentals=10**6),
+    )(flat, *arrived)
 
     high, low, gram = pl.pallas_call(
         functools.partial(far_kernel, col_count),
@@ -418,19 +492,19 @@
             pltpu.VMEM((2, sources), BF16),
             pltpu.VMEM((col_count, rows, sources), BF16),
             pltpu.VMEM((col_count, 8, sources), F32),
-            pltpu.VMEM((col_count, 2, sources, nodes), F32),
+            pltpu.VMEM((col_count, sources, DEPTH), BF16),
+            pltpu.VMEM((4, vesicles * DEPTH, nodes), F32),
             pltpu.VMEM((sources, 3 * nodes), BF16),
             pltpu.VMEM((sources, 3 * nodes), BF16),
             pltpu.VMEM((rows, rows), F32),
             pltpu.SemaphoreType.DMA((4,))],
         compiler_params=params(32),
         cost_estimate=pl.CostEstimate(flops=10**10, bytes_accessed=10**7, transcendentals=10**7),
-    )(pltpu.with_memory_space_constraint(far_range.reshape(1, vesicles), pltpu.HBM), operands[2],
-      operands[0], operands[1], *pieces)
+    )(near_by(far_range.reshape(1, vesicles)), flat_here, basis_here, nodes_here, *pieces)
     gram = sum_over(gram, "clu", step_groups(clu_count, True))
     gram = sum_over(gram, "col", step_groups(col_count, False))
 
-    scale_factor = math.sqrt(2.0 * nodes * vesicles * clu_count * col_count)
+    scale_factor = -math.sqrt(2.0 * nodes * vesicles * clu_count * col_count)
     group = 8 if vesicles % 8 == 0 else vesicles
     block = pl.BlockSpec((group, rows, nodes), lambda i: (i, 0, 0))
     new_basis = pl.pallas_call(

time: 53 us -> 57.7 us (1.089)
  waiting for transfers between devices: 6.83 us -> 11.6 us
  starting transfers between devices: 18.4 us -> 16.5 us
  Pallas kernels: 26.8 us -> 28.6 us
    ppermute x7, waiting for transfers between devices: 1.55 us -> 8.08 us  [sum_over(): moved = [lax.ppermute(value, axis, partners(count, k)) for k in steps]]
    all_to_all x1 -> x0, starting transfers between devices: 3.72 us -> none  [per_device(): lax.all_to_all(packed, 'clu', split_axis=0, concat_axis=0, tiled=True)]
    ppermute x0 -> x3, starting transfers between devices: none -> 2.13 us  [cube_exchange(): held.append(lax.ppermute(leaving, axis, partners(count, bit)))]
    ppermute x3, waiting for transfers between devices: 5.27 us -> 3.48 us  [per_device(): lax.ppermute(sent, 'col', partners(col_count, k))]
    pallas_call x1, Pallas kernels: 13.1 us -> 14.7 us  [per_device(): pl.pallas_call(functools.partial(far_kernel, col_count), out_shape=[jax.S...]
    pallas_call x2, Pallas kernels: 6.35 us -> 6.95 us  [the longest x1 6.01 us: per_device(): pl.pallas_call(functools.partial(near_kernel, slot_cap, len(arrived)), ou...]
  transfers between devices with their start and end apart: 14 -> 16, of which waited for: 5 -> 8; matrix products, arithmetic and copies ran while one was open for 0% -> 0% of each run, Pallas kernels for 37% -> 38%
where the time goes in v5:
time: 57.7 us; the launch traced here: 57.5 us
  Pallas kernels  28.6 us (50%)
  starting transfers between devices  16.5 us (29%)
  waiting for transfers between devices  11.6 us (20%)
  between operations  0.73 us (1%)
    pallas_call x1, Pallas kernels, per_device(): pl.pallas_call(functools.partial(far_kernel, col_count), out_shape=[jax.S...  14.7 us
    ppermute x7, starting transfers between devices, sum_over(): moved = [lax.ppermute(value, axis, partners(count, k)) for k in steps]  8.16 us
    ppermute x7, waiting for transfers between devices, sum_over(): moved = [lax.ppermute(value, axis, partners(count, k)) for k in steps]  8.08 us
    pallas_call x1, Pallas kernels, per_device(): pl.pallas_call(functools.partial(near_kernel, slot_cap, len(arrived)), ou...  6.01 us
    ppermute x3, starting transfers between devices, per_device(): lax.ppermute(sent, 'col', partners(col_count, k))  5.68 us
    pallas_call x1, Pallas kernels, per_device(): pl.pallas_call(functools.partial(basis_kernel, scale_factor), out_shape=j...  4.89 us
    ppermute x3, waiting for transfers between devices, per_device(): lax.ppermute(sent, 'col', partners(col_count, k))  3.48 us
    ppermute x3, starting transfers between devices, cube_exchange(): held.append(lax.ppermute(leaving, axis, partners(count, bit)))  2.13 us
  transfers between devices with their start and end apart: 16, of which 8 were waited for; matrix products, arithmetic and copies ran while one was open for 0% of the time, Pallas kernels for 38%

profile of v5, /device:TPU:0, one launch (start us, length us, event | category | flops | bytes accessed | tf_op | source)
XLA Modules:
  0.0 57.5 jit_solution(14289365410808274154)
XLA Ops:
  0.6 0.9 %shard_map.132 = bf16[272,128]{1,0:T(8,128)(2,1)S(1)} custom-call(bf16[128,512]{1,0:T(8,128)(2,1)} %own_in.3, bf16[2,512]{1,0:T(2,128)(2,1)} %nodes_in.3), custom_call_target="tpu_custom_call" | custom-call | flops 100000 | bytes 100000 | tf_op jit(solution)/shard_map/pallas_call | solution.py:438
  1.6 3.1 %collective-permute-start.3 = (bf16[272,128]{1,0:T(8,128)(2,1)S(1)}, bf16[272,128]{1,0:T(8,128)(2,1)S(1)}, u32[]{:S(2)}, u32[]{:S(2)}) collective-permute-start(bf16[272,128]{1,0:T(8,128)(2,1)S(1)} %shard_map.132), channel_id=1, source_target_pairs={{0,1},{1,0},{2,3},{3,2},{4,5},{5,4},{6,7},{7,6},{8,9},{9,8},{10,11... | collective-permute-start | bytes 208904 | tf_op jit(solution)/shard_map/ppermute | solution.py:465
  4.7 2.6 %collective-permute-start.5 = (bf16[272,128]{1,0:T(8,128)(2,1)S(1)}, bf16[272,128]{1,0:T(8,128)(2,1)S(1)}, u32[]{:S(2)}, u32[]{:S(2)}) collective-permute-start(bf16[272,128]{1,0:T(8,128)(2,1)S(1)} %shard_map.132), channel_id=1, source_target_pairs={{0,2},{1,3},{2,0},{3,1},{4,6},{5,7},{6,4},{7,5},{8,10},{9,11},{10,... | collective-permute-start | bytes 208904 | tf_op jit(solution)/shard_map/ppermute | solution.py:465
  7.3 2.1 %shard_map.130 = (f32[64,128]{1,0:T(8,128)}, f32[4,8,640]{2,1,0:T(8,128)S(1)}, f32[4,8,640]{2,1,0:T(8,128)S(1)}) custom-call(f32[64,128]{1,0:T(8,128)} %bitcast.33, f32[32,128]{1,0:T(8,128)} %refs_1_.1, f32[1,32]{1,0:T(1,128)} %bitcast.40, s32[1,32]{1,0:T(1,128)} %refs_3_.1, s32[1,24]{1,0:T(1,128)} %bitcast.41, s32[1,24]{1,0:T(1,128)} %bitcast.42, ...), custom_call_target="tpu_custom_call" | custom-call | flops 100000000 | bytes 1000000 | tf_op jit(solution)/shard_map/pallas_call | solution.py:453
  9.3 0.1 collective-permute-start
  9.4 0.5 collective-permute-start.4
  10.0 2.2 %collective-permute-done.5.refs_2_ = bf16[272,128]{1,0:T(8,128)(2,1)S(1)} collective-permute-done((bf16[272,128]{1,0:T(8,128)(2,1)S(1)}, bf16[272,128]{1,0:T(8,128)(2,1)S(1)}, u32[]{:S(2)}, u32[]{:S(2)}) %collective-permute-start.5) | collective-permute-done | bytes 69664 | tf_op jit(solution)/shard_map/ppermute | solution.py:465
  12.2 1.3 %collective-permute-done.7.refs_4_ = bf16[272,128]{1,0:T(8,128)(2,1)S(1)} collective-permute-done((bf16[272,128]{1,0:T(8,128)(2,1)S(1)}, bf16[272,128]{1,0:T(8,128)(2,1)S(1)}, u32[]{:S(2)}, u32[]{:S(2)}) %collective-permute-start.7) | collective-permute-done | bytes 69664 | tf_op jit(solution)/shard_map/ppermute | solution.py:465
  13.5 1.6 %collective-permute-start.1 = (f32[4,8,640]{2,1,0:T(8,128)S(1)}, f32[4,8,640]{2,1,0:T(8,128)S(1)}, u32[]{:S(2)}, u32[]{:S(2)}) collective-permute-start(f32[4,8,640]{2,1,0:T(8,128)S(1)} %pad_maximum_fusion), channel_id=1, source_target_pairs={{0,8},{4,12},{8,0},{12,4},{16,24},{20,28},{24,16},{28,20},{1,9},{5... | collective-permute-start | bytes 245768 | tf_op jit(solution)/shard_map/ppermute | solution.py:92
  15.1 0.0 collective-permute-done.4.refs_1_
  15.1 0.0 collective-permute-done.6.refs_3_
  15.1 0.0 collective-permute-done.8.refs_5_
  15.1 14.7 %shard_map.133 = (bf16[32,128,128]{2,1,0:T(8,128)(2,1)S(1)}, bf16[32,128,128]{2,1,0:T(8,128)(2,1)S(1)}, f32[32,128]{1,0:T(8,128)S(1)}) custom-call(s32[1,32]{1,0:T(1,128)} %bitcast.43, f32[64,128]{1,0:T(8,128)} %bitcast.34, bf16[128,512]{1,0:T(8,128)(2,1)} %own_in.3, bf16[2,512]{1,0:T(2,128)(2,1)} %nodes_in.3, ...), custom_call_target="tpu_custom_call" | custom-call | flops 10000000000 | bytes 10000000 | tf_op jit(solution)/shard_map/pallas_call | solution.py:483
  29.8 0.3 collective-permute-start.9
  30.1 1.0 %collective-permute-done.9 = f32[32,128]{1,0:T(8,128)S(1)} collective-permute-done((f32[32,128]{1,0:T(8,128)S(1)}, f32[32,128]{1,0:T(8,128)S(1)}, u32[]{:S(2)}, u32[]{:S(2)}) %collective-permute-start.9) | collective-permute-done | bytes 16416 | tf_op jit(solution)/shard_map/ppermute | solution.py:418
  31.1 1.1 %collective-permute-start.10 = (f32[32,128]{1,0:T(8,128)S(1)}, f32[32,128]{1,0:T(8,128)S(1)}, u32[]{:S(2)}, u32[]{:S(2)}) collective-permute-start(f32[32,128]{1,0:T(8,128)S(1)} %add.21), channel_id=1, source_target_pairs={{0,8},{4,12},{8,0},{12,4},{16,24},{20,28},{24,16},{28,20},{1,9},{5... | collective-permute-start | bytes 49160 | tf_op jit(solution)/shard_map/ppermute | solution.py:418
  32.2 1.5 %collective-permute-start.11 = (f32[32,128]{1,0:T(8,128)S(1)}, f32[32,128]{1,0:T(8,128)S(1)}, u32[]{:S(2)}, u32[]{:S(2)}) collective-permute-start(f32[32,128]{1,0:T(8,128)S(1)} %add.21), channel_id=1, source_target_pairs={{0,16},{4,20},{8,24},{12,28},{16,0},{20,4},{24,8},{28,12},{1,17},{... | collective-permute-start | bytes 49160 | tf_op jit(solution)/shard_map/ppermute | solution.py:418
  33.7 0.8 %collective-permute-start.12 = (f32[32,128]{1,0:T(8,128)S(1)}, f32[32,128]{1,0:T(8,128)S(1)}, u32[]{:S(2)}, u32[]{:S(2)}) collective-permute-start(f32[32,128]{1,0:T(8,128)S(1)} %add.21), channel_id=1, source_target_pairs={{0,24},{4,28},{8,16},{12,20},{16,8},{20,12},{24,0},{28,4},{1,25},{... | collective-permute-start | bytes 49160 | tf_op jit(solution)/shard_map/ppermute | solution.py:418
  34.5 0.0 collective-permute-done.1
  34.6 0.2 collective-permute-done.10
  34.8 1.1 %collective-permute-done.11 = f32[32,128]{1,0:T(8,128)S(1)} collective-permute-done((f32[32,128]{1,0:T(8,128)S(1)}, f32[32,128]{1,0:T(8,128)S(1)}, u32[]{:S(2)}, u32[]{:S(2)}) %collective-permute-start.11) | collective-permute-done | bytes 16416 | tf_op jit(solution)/shard_map/ppermute | solution.py:418
  35.9 2.4 %collective-permute-done.12 = f32[32,128]{1,0:T(8,128)S(1)} collective-permute-done((f32[32,128]{1,0:T(8,128)S(1)}, f32[32,128]{1,0:T(8,128)S(1)}, u32[]{:S(2)}, u32[]{:S(2)}) %collective-permute-start.12) | collective-permute-done | bytes 16416 | tf_op jit(solution)/shard_map/ppermute | solution.py:418
  38.4 0.8 %collective-permute-start.13 = (f32[32,128]{1,0:T(8,128)S(1)}, f32[32,128]{1,0:T(8,128)S(1)}, u32[]{:S(2)}, u32[]{:S(2)}) collective-permute-start(f32[32,128]{1,0:T(8,128)S(1)} %add_add_fusion.1), channel_id=1, source_target_pairs={{0,1},{1,0},{2,3},{3,2},{4,5},{5,4},{6,7},{7,6},{8,9},{9,8},{10,11... | collective-permute-start | bytes 49160 | tf_op jit(solution)/shard_map/ppermute | solution.py:418
  39.2 1.9 %collective-permute-start.14 = (f32[32,128]{1,0:T(8,128)S(1)}, f32[32,128]{1,0:T(8,128)S(1)}, u32[]{:S(2)}, u32[]{:S(2)}) collective-permute-start(f32[32,128]{1,0:T(8,128)S(1)} %add_add_fusion.1), channel_id=1, source_target_pairs={{0,2},{1,3},{2,0},{3,1},{4,6},{5,7},{6,4},{7,5},{8,10},{9,11},{10,... | collective-permute-start | bytes 49160 | tf_op jit(solution)/shard_map/ppermute | solution.py:418
  41.1 1.7 %collective-permute-start.15 = (f32[32,128]{1,0:T(8,128)S(1)}, f32[32,128]{1,0:T(8,128)S(1)}, u32[]{:S(2)}, u32[]{:S(2)}) collective-permute-start(f32[32,128]{1,0:T(8,128)S(1)} %add_add_fusion.1), channel_id=1, source_target_pairs={{0,3},{1,2},{2,1},{3,0},{4,7},{5,6},{6,5},{7,4},{8,11},{9,10},{10,... | collective-permute-start | bytes 49160 | tf_op jit(solution)/shard_map/ppermute | solution.py:418
  42.8 0.5 collective-permute-start.2
  43.3 0.0 collective-permute-done.13
  43.3 0.6 %collective-permute-done.14 = f32[32,128]{1,0:T(8,128)S(1)} collective-permute-done((f32[32,128]{1,0:T(8,128)S(1)}, f32[32,128]{1,0:T(8,128)S(1)}, u32[]{:S(2)}, u32[]{:S(2)}) %collective-permute-start.14) | collective-permute-done | bytes 16416 | tf_op jit(solution)/shard_map/ppermute | solution.py:418
  43.9 2.7 %collective-permute-done.15 = f32[32,128]{1,0:T(8,128)S(1)} collective-permute-done((f32[32,128]{1,0:T(8,128)S(1)}, f32[32,128]{1,0:T(8,128)S(1)}, u32[]{:S(2)}, u32[]{:S(2)}) %collective-permute-start.15) | collective-permute-done | bytes 16416 | tf_op jit(solution)/shard_map/ppermute | solution.py:418
  46.6 4.9 %shard_map.134 = f32[32,128,128]{2,1,0:T(8,128)} custom-call(f32[32,128]{1,0:T(8,128)S(1)} %add_add_fusion.refs_0_, bf16[32,128,128]{2,1,0:T(8,128)(2,1)S(1)} %get-tuple-element.13.refs_1_, bf16[32,128,128]{2,1,0:T(8,128)(2,1)S(1)} %get-tuple-element.14.refs_2_), custom_call_target="tpu_custom_call" | custom-call | flops 1000000000 | bytes 10000000 | tf_op jit(solution)/shard_map/pallas_call | solution.py:510
  51.5 0.0 collective-permute-done.2.refs_3_
  51.5 6.0 %shard_map.131 = f32[64,128]{1,0:T(8,128)} custom-call(f32[64,128]{1,0:T(8,128)S(1)} %bitcast.35, f32[1,8,640]{2,1,0:T(8,128)S(1)} %get-tuple-element.16.refs_0_, f32[1,8,640]{2,1,0:T(8,128)S(1)} %get-tuple-element.18.refs_1_, f32[2,8,640]{2,1,0:T(8,128)S(1)} %get-tuple-element.20.refs_2_, f32[4,8,640]{2,1,0:T(8,128)S(1)} %collective-permute-done.2.refs_3_), custom_call_target="tpu_custom_call" | custom-call | flops 1000000000 | bytes 10000000 | tf_op jit(solution)/shard_map/pallas_call | solution.py:471
  (17 shorter events, 0.1 us)
Async XLA Ops:
  1.6 7.9 %collective-permute-start.3 = (bf16[272,128]{1,0:T(8,128)(2,1)S(1)}, bf16[272,128]{1,0:T(8,128)(2,1)S(1)}, u32[]{:S(2)}, u32[]{:S(2)}) collective-permute-start(bf16[272,128]{1,0:T(8,128)(2,1)S(1)} %shard_map.132), channel_id=1, source_target_pairs={{0,1},{1,0},{2,3},{3,2},{4,5},{5,4},{6,7},{7,6},{8,9},{9,8},{10,11... | collective-permute-start | bytes 208904 | tf_op jit(solution)/shard_map/ppermute | solution.py:465
  4.7 7.5 %collective-permute-start.5 = (bf16[272,128]{1,0:T(8,128)(2,1)S(1)}, bf16[272,128]{1,0:T(8,128)(2,1)S(1)}, u32[]{:S(2)}, u32[]{:S(2)}) collective-permute-start(bf16[272,128]{1,0:T(8,128)(2,1)S(1)} %shard_map.132), channel_id=1, source_target_pairs={{0,2},{1,3},{2,0},{3,1},{4,6},{5,7},{6,4},{7,5},{8,10},{9,11},{10,... | collective-permute-start | bytes 208904 | tf_op jit(solution)/shard_map/ppermute | solution.py:465
  7.3 6.2 %collective-permute-start.7 = (bf16[272,128]{1,0:T(8,128)(2,1)S(1)}, bf16[272,128]{1,0:T(8,128)(2,1)S(1)}, u32[]{:S(2)}, u32[]{:S(2)}) collective-permute-start(bf16[272,128]{1,0:T(8,128)(2,1)S(1)} %shard_map.132), channel_id=1, source_target_pairs={{0,3},{1,2},{2,1},{3,0},{4,7},{5,6},{6,5},{7,4},{8,11},{9,10},{10,... | collective-permute-start | bytes 208904 | tf_op jit(solution)/shard_map/ppermute | solution.py:465
  9.3 4.1 %collective-permute-start = (f32[4,8,640]{2,1,0:T(8,128)S(1)}, f32[4,8,640]{2,1,0:T(8,128)S(1)}, u32[]{:S(2)}, u32[]{:S(2)}) collective-permute-start(f32[4,8,640]{2,1,0:T(8,128)S(1)} %get-tuple-element.11), channel_id=1, source_target_pairs={{0,4},{4,0},{8,12},{12,8},{16,20},{20,16},{24,28},{28,24},{1,5},{5... | collective-permute-start | bytes 245768 | tf_op jit(solution)/shard_map/ppermute | solution.py:92
  9.4 5.6 %collective-permute-start.4 = (bf16[272,128]{1,0:T(8,128)(2,1)S(1)}, bf16[272,128]{1,0:T(8,128)(2,1)S(1)}, u32[]{:S(2)}, u32[]{:S(2)}) collective-permute-start(bf16[272,128]{1,0:T(8,128)(2,1)S(1)} %collective-permute-done.3.refs_0_), channel_id=1, source_target_pairs={{0,4},{4,0},{8,12},{12,8},{16,20},{20,16},{24,28},{28,24},{1,5},{5... | collective-permute-start | bytes 208904 | tf_op jit(solution)/shard_map/ppermute | solution.py:469
  12.2 2.9 %collective-permute-start.6 = (bf16[272,128]{1,0:T(8,128)(2,1)S(1)}, bf16[272,128]{1,0:T(8,128)(2,1)S(1)}, u32[]{:S(2)}, u32[]{:S(2)}) collective-permute-start(bf16[272,128]{1,0:T(8,128)(2,1)S(1)} %collective-permute-done.5.refs_2_), channel_id=1, source_target_pairs={{0,4},{4,0},{8,12},{12,8},{16,20},{20,16},{24,28},{28,24},{1,5},{5... | collective-permute-start | bytes 208904 | tf_op jit(solution)/shard_map/ppermute | solution.py:469
  13.5 1.6 %collective-permute-start.8 = (bf16[272,128]{1,0:T(8,128)(2,1)S(1)}, bf16[272,128]{1,0:T(8,128)(2,1)S(1)}, u32[]{:S(2)}, u32[]{:S(2)}) collective-permute-start(bf16[272,128]{1,0:T(8,128)(2,1)S(1)} %collective-permute-done.7.refs_4_), channel_id=1, source_target_pairs={{0,4},{4,0},{8,12},{12,8},{16,20},{20,16},{24,28},{28,24},{1,5},{5... | collective-permute-start | bytes 208904 | tf_op jit(solution)/shard_map/ppermute | solution.py:469
  13.5 21.0 %collective-permute-start.1 = (f32[4,8,640]{2,1,0:T(8,128)S(1)}, f32[4,8,640]{2,1,0:T(8,128)S(1)}, u32[]{:S(2)}, u32[]{:S(2)}) collective-permute-start(f32[4,8,640]{2,1,0:T(8,128)S(1)} %pad_maximum_fusion), channel_id=1, source_target_pairs={{0,8},{4,12},{8,0},{12,4},{16,24},{20,28},{24,16},{28,20},{1,9},{5... | collective-permute-start | bytes 245768 | tf_op jit(solution)/shard_map/ppermute | solution.py:92
  29.8 1.2 %collective-permute-start.9 = (f32[32,128]{1,0:T(8,128)S(1)}, f32[32,128]{1,0:T(8,128)S(1)}, u32[]{:S(2)}, u32[]{:S(2)}) collective-permute-start(f32[32,128]{1,0:T(8,128)S(1)} %get-tuple-element.12), channel_id=1, source_target_pairs={{0,4},{4,0},{8,12},{12,8},{16,20},{20,16},{24,28},{28,24},{1,5},{5... | collective-permute-start | bytes 49160 | tf_op jit(solution)/shard_map/ppermute | solution.py:418
  31.1 3.7 %collective-permute-start.10 = (f32[32,128]{1,0:T(8,128)S(1)}, f32[32,128]{1,0:T(8,128)S(1)}, u32[]{:S(2)}, u32[]{:S(2)}) collective-permute-start(f32[32,128]{1,0:T(8,128)S(1)} %add.21), channel_id=1, source_target_pairs={{0,8},{4,12},{8,0},{12,4},{16,24},{20,28},{24,16},{28,20},{1,9},{5... | collective-permute-start | bytes 49160 | tf_op jit(solution)/shard_map/ppermute | solution.py:418
  32.2 3.7 %collective-permute-start.11 = (f32[32,128]{1,0:T(8,128)S(1)}, f32[32,128]{1,0:T(8,128)S(1)}, u32[]{:S(2)}, u32[]{:S(2)}) collective-permute-start(f32[32,128]{1,0:T(8,128)S(1)} %add.21), channel_id=1, source_target_pairs={{0,16},{4,20},{8,24},{12,28},{16,0},{20,4},{24,8},{28,12},{1,17},{... | collective-permute-start | bytes 49160 | tf_op jit(solution)/shard_map/ppermute | solution.py:418
  33.7 4.6 %collective-permute-start.12 = (f32[32,128]{1,0:T(8,128)S(1)}, f32[32,128]{1,0:T(8,128)S(1)}, u32[]{:S(2)}, u32[]{:S(2)}) collective-permute-start(f32[32,128]{1,0:T(8,128)S(1)} %add.21), channel_id=1, source_target_pairs={{0,24},{4,28},{8,16},{12,20},{16,8},{20,12},{24,0},{28,4},{1,25},{... | collective-permute-start | bytes 49160 | tf_op jit(solution)/shard_map/ppermute | solution.py:418
  38.4 4.9 %collective-permute-start.13 = (f32[32,128]{1,0:T(8,128)S(1)}, f32[32,128]{1,0:T(8,128)S(1)}, u32[]{:S(2)}, u32[]{:S(2)}) collective-permute-start(f32[32,128]{1,0:T(8,128)S(1)} %add_add_fusion.1), channel_id=1, source_target_pairs={{0,1},{1,0},{2,3},{3,2},{4,5},{5,4},{6,7},{7,6},{8,9},{9,8},{10,11... | collective-permute-start | bytes 49160 | tf_op jit(solution)/shard_map/ppermute | solution.py:418
  39.2 4.7 %collective-permute-start.14 = (f32[32,128]{1,0:T(8,128)S(1)}, f32[32,128]{1,0:T(8,128)S(1)}, u32[]{:S(2)}, u32[]{:S(2)}) collective-permute-start(f32[32,128]{1,0:T(8,128)S(1)} %add_add_fusion.1), channel_id=1, source_target_pairs={{0,2},{1,3},{2,0},{3,1},{4,6},{5,7},{6,4},{7,5},{8,10},{9,11},{10,... | collective-permute-start | bytes 49160 | tf_op jit(solution)/shard_map/ppermute | solution.py:418
  41.1 5.5 %collective-permute-start.15 = (f32[32,128]{1,0:T(8,128)S(1)}, f32[32,128]{1,0:T(8,128)S(1)}, u32[]{:S(2)}, u32[]{:S(2)}) collective-permute-start(f32[32,128]{1,0:T(8,128)S(1)} %add_add_fusion.1), channel_id=1, source_target_pairs={{0,3},{1,2},{2,1},{3,0},{4,7},{5,6},{6,5},{7,4},{8,11},{9,10},{10,... | collective-permute-start | bytes 49160 | tf_op jit(solution)/shard_map/ppermute | solution.py:418
  42.8 8.7 %collective-permute-start.2 = (f32[4,8,640]{2,1,0:T(8,128)S(1)}, f32[4,8,640]{2,1,0:T(8,128)S(1)}, u32[]{:S(2)}, u32[]{:S(2)}) collective-permute-start(f32[4,8,640]{2,1,0:T(8,128)S(1)} %pad_maximum_fusion.1), channel_id=1, source_target_pairs={{0,16},{4,20},{8,24},{12,28},{16,0},{20,4},{24,8},{28,12},{1,17},{... | collective-permute-start | bytes 245768 | tf_op jit(solution)/shard_map/ppermute | solution.py:92
  46.6 4.9 %copy-start = (f32[32,2,128]{2,1,0:T(2,128)S(1)}, f32[32,2,128]{2,1,0:T(2,128)}, u32[]{:S(2)}) copy-start(f32[32,2,128]{2,1,0:T(2,128)} %param.11) | copy-start | bytes 98308

commit v6 on v3

--- a/solution.py
+++ b/solution.py
@@ -54,6 +54,22 @@
         copy.start()
     for copy in copies:
         copy.wait()
+
+
+def piece_kernel(own_in, nodes_in, sent_ref, own_ref, nodes_ref, sems):
+    fetch([own_in, nodes_in], [own_ref, nodes_ref], sems)
+    half = own_ref.shape[0] // 2
+    core = lax.rem(lax.axis_index("clu"), 2)
+    mine = own_ref[pl.ds(pl.multiple_of(core * half, half), half), :]
+    spots = nodes_ref[...].astype(F32)
+    lanes = sent_ref.shape[1]
+    columns = own_ref.shape[1] // lanes
+    for c in range(columns):
+        sent_ref[c * half:(c + 1) * half] = mine[:, c * lanes:(c + 1) * lanes]
+    spots = jnp.concatenate([spots[:, c * lanes:(c + 1) * lanes] for c in range(columns)], axis=0)
+    tail = sent_ref.shape[0] - columns * half
+    spots = jnp.concatenate([spots, jnp.zeros((tail - 2 * columns, lanes), F32)], axis=0)
+    sent_ref[columns * half:] = spots.astype(BF16)
 
 
 def cube_place(destination, own, count):
@@ -86,16 +102,10 @@
 
 
 def force_kernel(clu_count, *refs):
-    sources, targets, sems = refs[:10], refs[14:24], refs[24]
-    sent_ref, force_ref, kept_ref, leaving_ref = refs[10:14]
+    sources, targets, sems = refs[:8], refs[11:19], refs[19]
+    force_ref, kept_ref, leaving_ref = refs[8:11]
     fetch(sources, targets, sems)
-    (own_ref, nodes_ref, pos_ref, ten_ref, bend_ref, order_ref, dest_ref, target_ref, deriv_ref,
-     table_ref) = targets
-    half = own_ref.shape[0] // 2
-    core = lax.rem(lax.axis_index("clu"), 2)
-    sent_ref[0:half] = own_ref[pl.ds(pl.multiple_of(core * half, half), half), :]
-    spots = jnp.concatenate([nodes_ref[...].astype(F32)] * 8, axis=0)
-    sent_ref[half:half + 16] = spots.astype(BF16)
+    (pos_ref, ten_ref, bend_ref, order_ref, dest_ref, target_ref, deriv_ref, table_ref) = targets
     vesicles = ten_ref.shape[0]
     moves = target_ref.shape[1]
     x = pos_ref[pl.ds(0, vesicles, stride=2), :]
@@ -215,72 +225,79 @@
 def far_kernel(col_count, range_in, pos_in, own_in, nodes_in, *refs):
     count = 2 * (col_count - 1)
     piece_refs = refs[:count]
-    (high_ref, low_ref, gram_ref, range_ref, pos_ref, own_nodes, basis, spots, wide, buffer,
-     sums, sems) = refs[count:]
+    (high_ref, low_ref, gram_ref, range_ref, pos_ref, own_nodes, own_rows, basis, spots, wide,
+     buffer_0, buffer_1, sums, sems) = refs[count:]
     vesicles = pos_ref.shape[0] // 2
     nodes = pos_ref.shape[1]
-    _, rows, sources = basis.shape
-    half, rank = rows // 2, rows // 2
+    rank, sources = own_rows.shape[0] // 2, own_rows.shape[1]
+    rows = 2 * rank
     core, col = lax.rem(lax.axis_index("clu"), 2), lax.axis_index("col")
-    fetch([range_in, pos_in, nodes_in, own_in], [range_ref, pos_ref, own_nodes, basis.at[col]], sems)
+    fetch([range_in, pos_in, nodes_in, own_in], [range_ref, pos_ref, own_nodes, own_rows], sems)
+    basis[col, :, :sources] = own_rows[:rank]
+    basis[col, :, sources:] = own_rows[rank:]
     spots[col, 0:2] = own_nodes[...].astype(F32)
     for k in range(1, col_count):
         where = origin(col, k, col_count)
         mine, other = piece_refs[2 * k - 2], piece_refs[2 * k - 1]
-        basis[where, pl.ds(pl.multiple_of(core * half, half), half), :] = mine[0:half]
-        basis[where, pl.ds(pl.multiple_of((1 - core) * half, half), half), :] = other[0:half]
-        spots[where, 0:2] = mine[half:half + 16].astype(F32)[0:2]
+        columns = sources // nodes
+        ends = mine[columns * rank:].astype(F32)
+        for c in range(columns):
+            lanes = slice(c * nodes, (c + 1) * nodes)
+            from_rows = slice(c * rank, (c + 1) * rank)
+            for ref, part in ((mine, core), (other, 1 - core)):
+                there = pl.multiple_of(part * sources + c * nodes, nodes)
+                basis[where, :, pl.ds(there, nodes)] = ref[from_rows]
+            spots[where, 0:2, lanes] = ends[2 * c:2 * c + 2]
     for r in range(col_count):
         turned = spots[r].T
         for c in range(2):
             wide[r, c] = jnp.broadcast_to(turned[:, c:c + 1], (sources, nodes))
     sums[...] = jnp.zeros_like(sums)
+
     chunk = 32 if sources % 32 == 0 else sources
 
-    def evaluate(v, slot):
+    def evaluate(v, buffer, part, parts):
         r = range_ref[0, v]
         tx = pos_ref[pl.ds(2 * v, 1), :]
         ty = pos_ref[pl.ds(2 * v + 1, 1), :]
-        for start in range(0, sources, chunk):
+        for start in range(part * sources // parts, (part + 1) * sources // parts, chunk):
             dx = tx - wide[r, 0, start:start + chunk]
             dy = ty - wide[r, 1, start:start + chunk]
             spread = dx * dx + dy * dy + EPS_SQUARED
             log_part = -0.5 * jnp.log(spread)
             inverse = reciprocal(spread)
             dxr = dx * inverse
-            here = slice(start, start + chunk)
-            buffer[slot, here, 0:nodes] = (log_part + dx * dxr).astype(BF16)
-            buffer[slot, here, nodes:2 * nodes] = (dy * dxr).astype(BF16)
-            buffer[slot, here, 2 * nodes:] = (log_part + dy * (dy * inverse)).astype(BF16)
-
-    def multiply(v, slot):
-        product = dot(basis[range_ref[0, v]], buffer[slot])
-        first = product[:rank, :nodes] + product[rank:, nodes:2 * nodes]
-        second = product[:rank, nodes:2 * nodes] + product[rank:, 2 * nodes:]
-        high_0, high_1 = first.astype(BF16), second.astype(BF16)
-        low_0 = (first - high_0.astype(F32)).astype(BF16)
-        low_1 = (second - high_1.astype(F32)).astype(BF16)
-        high_ref[v] = jnp.concatenate([high_0, high_1], axis=0)
-        low_ref[v] = jnp.concatenate([low_0, low_1], axis=0)
+            upper = slice(start, start + chunk)
+            lower = slice(sources + start, sources + start + chunk)
+            cross = (dy * dxr).astype(BF16)
+            buffer[upper, :nodes] = (log_part + dx * dxr).astype(BF16)
+            buffer[upper, nodes:] = cross
+            buffer[lower, :nodes] = cross
+            buffer[lower, nodes:] = (log_part + dy * (dy * inverse)).astype(BF16)
+
+    def step(v, now, following):
+        later = jnp.minimum(v + 1, vesicles - 1)
+        product = dot(basis[range_ref[0, v]], now[...])
+        evaluate(later, following, 0, 2)
+        high = product.astype(BF16)
+        high_ref[v] = high
+        low_ref[v] = (product - high.astype(F32)).astype(BF16)
+        evaluate(later, following, 1, 2)
 
     def add_gram(v):
         both = jnp.concatenate([
-            jnp.concatenate([ref[u, part] for u in (v, v + 1)
-                             for part in (slice(0, rank), slice(rank, rows))], axis=1)
-            for ref in (high_ref, low_ref)], axis=0)
+            jnp.concatenate([ref[v], ref[v + 1]], axis=1) for ref in (high_ref, low_ref)], axis=0)
         sums[...] += dot(both, both, NT)
 
-    evaluate(0, 0)
-    high_ref[0:2] = jnp.zeros((2, rows, nodes), BF16)
-    low_ref[0:2] = jnp.zeros((2, rows, nodes), BF16)
+    evaluate(0, buffer_0, 0, 1)
+    high_ref[0:2] = jnp.zeros((2, rank, 2 * nodes), BF16)
+    low_ref[0:2] = jnp.zeros((2, rank, 2 * nodes), BF16)
 
     def pair(i, _):
         v = 2 * i
         add_gram(jnp.maximum(v - 2, 0))
-        evaluate(v + 1, 1)
-        multiply(v, 0)
-        evaluate(jnp.minimum(v + 2, vesicles - 1), 0)
-        multiply(v + 1, 1)
+        step(v, buffer_0, buffer_1)
+        step(v + 1, buffer_1, buffer_0)
         return 0
 
     lax.fori_loop(0, vesicles // 2, pair, 0)
@@ -317,26 +334,23 @@
     return jnp.concatenate(done, axis=0)[:, size:]
 
 
-def basis_kernel(scale_factor, *refs):
-    gram_ref, high_ref, low_ref, out_ref, weight = refs
-    rank = high_ref.shape[1] // 2
+def basis_kernel(scale_factor, gram_ref, high_ref, low_ref, _, out_ref, weight):
+    rank, nodes = high_ref.shape[1], high_ref.shape[2] // 2
 
     @pl.when(pl.program_id(0) == 0)
     def _():
         folded = gram_ref[...]
         gram = jnp.concatenate([folded[:, :rank], folded[:, rank:]], axis=0)
         inverse = lower_inverse(gram) * scale_factor
-        turn = iota((2 * rank, rank), 0) - 2 * iota((2 * rank, rank), 1)
-        spread = jnp.concatenate([
-            dot((turn == d).astype(F32), inverse, precision=HIGHEST) for d in range(2)], axis=1)
-        high = spread.astype(BF16)
-        low = (spread - high.astype(F32)).astype(BF16)
+        high = inverse.astype(BF16)
+        low = (inverse - high.astype(F32)).astype(BF16)
         weight[...] = jnp.concatenate([high, high, low], axis=1)
 
     w = weight[...]
     for v in range(high_ref.shape[0]):
-        stacked = jnp.concatenate([high_ref[v], low_ref[v], high_ref[v]], axis=0)
-        out_ref[v] = dot(w, stacked)
+        fresh = dot(w, jnp.concatenate([high_ref[v], low_ref[v], high_ref[v]], axis=0))
+        for d in range(2):
+            out_ref[v, pl.ds(d, rank, stride=2), :] = fresh[:, d * nodes:(d + 1) * nodes]
 
 
 def whole_spec():
@@ -379,11 +393,32 @@
     return groups
 
 
-def sum_over(value, axis, groups):
+def add_kernel(first, *refs):
+    total = first[...]
+    for ref in refs[:-2]:
+        total = total + ref[...]
+    refs[-1][...] = total
+
+
+def add_after(terms, other):
+    return pl.pallas_call(
+        add_kernel,
+        out_shape=jax.ShapeDtypeStruct(terms[0].shape, terms[0].dtype),
+        in_specs=[whole_spec()] * len(terms) + [far_off_spec()],
+        out_specs=whole_spec(),
+        compiler_params=params(16),
+        cost_estimate=pl.CostEstimate(flops=10**4, bytes_accessed=10**5, transcendentals=0),
+    )(*terms, other)
+
+
+def sum_over(value, axis, groups, other=None):
     count = lax.axis_size(axis)
-    for steps in groups:
-        moved = [lax.ppermute(value, axis, partners(count, k)) for k in steps]
-        value = sum(moved, value)
+    for g, steps in enumerate(groups):
+        terms = [value] + [lax.ppermute(value, axis, partners(count, k)) for k in steps]
+        if other is not None and g == len(groups) - 1:
+            value = add_after(terms, other)
+        else:
+            value = sum(terms[1:], value)
     return value
 
 
@@ -397,18 +432,32 @@
     slot_cap = 2 * ((moves + clu_count - 1) // clu_count)
     flat = positions.reshape(2 * vesicles, nodes)
 
+    columns = sources // nodes
+    sent_rows = columns * rank + (2 * columns + 15) // 16 * 16
     deriv, table = spectral_tables(nodes)
-    operands = [old_basis, source_nodes, flat, tension, bending.reshape(1, vesicles), moved_order,
+    near_by = functools.partial(pltpu.with_memory_space_constraint, memory_space=pltpu.HBM)
+    basis_here, nodes_here, flat_here = near_by(old_basis), near_by(source_nodes), near_by(flat)
+    sent = pl.pallas_call(
+        piece_kernel,
+        out_shape=jax.ShapeDtypeStruct((sent_rows, nodes), BF16),
+        in_specs=[far_off_spec()] * 2,
+        out_specs=whole_spec(),
+        scratch_shapes=[pltpu.VMEM(old_basis.shape, BF16), pltpu.VMEM(source_nodes.shape, BF16),
+                        pltpu.SemaphoreType.DMA((2,))],
+        compiler_params=params(16),
+        cost_estimate=pl.CostEstimate(flops=10**5, bytes_accessed=10**5, transcendentals=0),
+    )(basis_here, nodes_here)
+
+    operands = [flat, tension, bending.reshape(1, vesicles), moved_order,
                 move_destination.reshape(1, moves), move_target.reshape(1, moves),
                 jnp.asarray(deriv), jnp.asarray(table)]
-    operands = [pltpu.with_memory_space_constraint(o, pltpu.HBM) for o in operands]
-    sent, force, kept, leaving = pl.pallas_call(
+    operands = [flat_here] + [near_by(o) for o in operands[1:]]
+    force, kept, leaving = pl.pallas_call(
         functools.partial(force_kernel, clu_count),
-        out_shape=[jax.ShapeDtypeStruct((rank + 16, sources), BF16),
-                   jax.ShapeDtypeStruct((2 * vesicles, nodes), F32),
+        out_shape=[jax.ShapeDtypeStruct((2 * vesicles, nodes), F32),
                    *[jax.ShapeDtypeStruct((clu_count // 2, BLOCK, 5 * nodes), F32)] * 2],
         in_specs=[far_off_spec()] * len(operands),
-        out_specs=[whole_spec()] * 4,
+        out_specs=[whole_spec()] * 3,
         scratch_shapes=[pltpu.VMEM(o.shape, o.dtype) for o in operands]
         + [pltpu.SemaphoreType.DMA((len(operands),))],
         compiler_params=params(16),
@@ -421,12 +470,12 @@
     for mine in moved_halves:
         pieces += [mine, lax.ppermute(mine, "clu", [(i, i ^ 1) for i in range(clu_count)])]
 
-    near = near_part(flat, arrived[:-1], None, slot_cap)
-    near = near_part(flat, arrived[-1:], near, slot_cap)
+    near_first = near_part(flat, arrived[:-1], None, slot_cap)
+    near = near_part(flat, arrived[-1:], near_first, slot_cap)
 
     high, low, gram = pl.pallas_call(
         functools.partial(far_kernel, col_count),
-        out_shape=[jax.ShapeDtypeStruct((vesicles, rows, nodes), BF16)] * 2
+        out_shape=[jax.ShapeDtypeStruct((vesicles, rank, 2 * nodes), BF16)] * 2
         + [jax.ShapeDtypeStruct((rank // 2, 2 * rank), F32)],
         in_specs=[far_off_spec()] * 4 + [whole_spec()] * (2 * (col_count - 1)),
         out_specs=[whole_spec()] * 3,
@@ -434,32 +483,34 @@
             pltpu.SMEM((1, vesicles), jnp.int32),
             pltpu.VMEM((2 * vesicles, nodes), F32),
             pltpu.VMEM((2, sources), BF16),
-            pltpu.VMEM((col_count, rows, sources), BF16),
+            pltpu.VMEM((rows, sources), BF16),
+            pltpu.VMEM((col_count, rank, 2 * sources), BF16),
             pltpu.VMEM((col_count, 8, sources), F32),
             pltpu.VMEM((col_count, 2, sources, nodes), F32),
-            pltpu.VMEM((2, sources, 3 * nodes), BF16),
+            pltpu.VMEM((2 * sources, 2 * nodes), BF16),
+            pltpu.VMEM((2 * sources, 2 * nodes), BF16),
             pltpu.VMEM((rows, rows), F32),
             pltpu.SemaphoreType.DMA((4,))],
         compiler_params=params(32),
         cost_estimate=pl.CostEstimate(flops=10**10, bytes_accessed=10**7, transcendentals=10**7),
-    )(pltpu.with_memory_space_constraint(far_range.reshape(1, vesicles), pltpu.HBM), operands[2],
-      operands[0], operands[1], *pieces)
-    gram = sum_over(gram, "clu", step_groups(clu_count, True))
+    )(near_by(far_range.reshape(1, vesicles)), flat_here, basis_here, nodes_here, *pieces)
+    gram = sum_over(gram, "clu", step_groups(clu_count, True), near_first)
     gram = sum_over(gram, "col", step_groups(col_count, False))
 
     scale_factor = math.sqrt(2.0 * nodes * vesicles * clu_count * col_count)
     group = 8 if vesicles % 8 == 0 else vesicles
     block = pl.BlockSpec((group, rows, nodes), lambda i: (i, 0, 0))
+    held = pl.BlockSpec((group, rank, 2 * nodes), lambda i: (i, 0, 0))
     new_basis = pl.pallas_call(
         functools.partial(basis_kernel, scale_factor),
         out_shape=jax.ShapeDtypeStruct((vesicles, rows, nodes), F32),
         grid=(vesicles // group,),
-        in_specs=[whole_spec()] + [block] * 2,
+        in_specs=[whole_spec(), held, held, far_off_spec()],
         out_specs=block,
-        scratch_shapes=[pltpu.VMEM((rows, 3 * rows), BF16)],
+        scratch_shapes=[pltpu.VMEM((rank, 3 * rank), BF16)],
         compiler_params=params(16),
         cost_estimate=pl.CostEstimate(flops=10**9, bytes_accessed=10**7, transcendentals=0),
-    )(gram, high, low)
+    )(gram, high, low, near)
 
     return (force.reshape(vesicles, 2, nodes), near.reshape(vesicles, 2, nodes),
             new_basis.reshape(vesicles, rank, 2, nodes))

time: 53.1 us -> 53.4 us (level)
  waiting for transfers between devices: 8.52 us -> 6.64 us
  starting transfers between devices: 17.2 us -> 18 us
  local copies, waits for them, and re-layouts: 0.03 us -> 0.79 us
    ppermute x3, waiting for transfers between devices: 4.93 us -> 2.54 us  [per_device(): lax.ppermute(sent, 'col', partners(col_count, k))]
    pallas_call x0 -> x2, Pallas kernels: none -> 0.95 us  [the longest x1 0.94 us: per_device(): pl.pallas_call(piece_kernel, out_shape=jax.ShapeDtypeStruct((sent_rows, n...]
    unnamed x2 -> x4, local copies, waits for them, and re-layouts: 0.01 us -> 0.76 us
    pallas_call x1, Pallas kernels: 4.88 us -> 4.24 us  [per_device(): pl.pallas_call(functools.partial(basis_kernel, scale_factor), out_shape=j...]
    ppermute x3, starting transfers between devices: 0.51 us -> 1.06 us  [per_device(): lax.ppermute(mine, 'clu', [(i, i ^ 1) for i in range(clu_count)])]
  transfers between devices with their start and end apart: 16 -> 16, of which waited for: 7 -> 4; matrix products, arithmetic and copies ran while one was open for 0% -> 0% of each run, Pallas kernels for 39% -> 34%
where the time goes in v6:
time: 53.4 us; the launch traced here: 53.1 us
  Pallas kernels  26.9 us (50%)
  starting transfers between devices  18 us (34%)
  waiting for transfers between devices  6.64 us (12%)
  local copies, waits for them, and re-layouts  0.79 us (1%)
  between operations  0.77 us (1%)
    pallas_call x1, Pallas kernels, per_device(): pl.pallas_call(functools.partial(far_kernel, col_count), out_shape=[jax.S...  13.3 us
    ppermute x7, starting transfers between devices, sum_over(): lax.ppermute(value, axis, partners(count, k))  8.01 us
    pallas_call x2, Pallas kernels, near_part(): pl.pallas_call(functools.partial(near_start if before is None else near_k...  6.35 us
    ppermute x3, starting transfers between devices, per_device(): lax.ppermute(sent, 'col', partners(col_count, k))  5.76 us
    pallas_call x1, Pallas kernels, per_device(): pl.pallas_call(functools.partial(basis_kernel, scale_factor), out_shape=j...  4.24 us
    ppermute x3, starting transfers between devices, cube_exchange(): held.append(lax.ppermute(leaving, axis, partners(count, bit)))  3.15 us
    ppermute x7, waiting for transfers between devices, sum_over(): lax.ppermute(value, axis, partners(count, k))  2.62 us
    ppermute x3, waiting for transfers between devices, per_device(): lax.ppermute(sent, 'col', partners(col_count, k))  2.54 us
  transfers between devices with their start and end apart: 16, of which 4 were waited for; matrix products, arithmetic and copies ran while one was open for 0% of the time, Pallas kernels for 34%

profile of v6, /device:TPU:0, one launch (start us, length us, event | category | flops | bytes accessed | tf_op | source)
XLA Modules:
  0.0 53.1 jit_solution(5687801518451297509)
XLA Ops:
  0.6 0.9 %shard_map.133 = bf16[272,128]{1,0:T(8,128)(2,1)S(1)} custom-call(bf16[128,512]{1,0:T(8,128)(2,1)} %own_in.3, bf16[2,512]{1,0:T(2,128)(2,1)} %nodes_in.3), custom_call_target="tpu_custom_call" | custom-call | flops 100000 | bytes 100000 | tf_op jit(solution)/shard_map/pallas_call | solution.py:440
  1.6 5.1 %collective-permute-start.7 = (bf16[272,128]{1,0:T(8,128)(2,1)S(1)}, bf16[272,128]{1,0:T(8,128)(2,1)S(1)}, u32[]{:S(2)}, u32[]{:S(2)}) collective-permute-start(bf16[272,128]{1,0:T(8,128)(2,1)S(1)} %shard_map.133), channel_id=1, source_target_pairs={{0,3},{1,2},{2,1},{3,0},{4,7},{5,6},{6,5},{7,4},{8,11},{9,10},{10,... | collective-permute-start | bytes 208904 | tf_op jit(solution)/shard_map/ppermute | solution.py:467
  6.7 0.6 %collective-permute-start.3 = (bf16[272,128]{1,0:T(8,128)(2,1)S(1)}, bf16[272,128]{1,0:T(8,128)(2,1)S(1)}, u32[]{:S(2)}, u32[]{:S(2)}) collective-permute-start(bf16[272,128]{1,0:T(8,128)(2,1)S(1)} %shard_map.133), channel_id=1, source_target_pairs={{0,1},{1,0},{2,3},{3,2},{4,5},{5,4},{6,7},{7,6},{8,9},{9,8},{10,11... | collective-permute-start | bytes 208904 | tf_op jit(solution)/shard_map/ppermute | solution.py:467
  7.3 2.1 %shard_map.130 = (f32[64,128]{1,0:T(8,128)}, f32[4,8,640]{2,1,0:T(8,128)S(1)}, f32[4,8,640]{2,1,0:T(8,128)S(1)}) custom-call(f32[64,128]{1,0:T(8,128)} %bitcast.34, f32[32,128]{1,0:T(8,128)} %refs_1_.1, f32[1,32]{1,0:T(1,128)} %bitcast.42, s32[1,32]{1,0:T(1,128)} %refs_3_.1, s32[1,24]{1,0:T(1,128)} %bitcast.43, s32[1,24]{1,0:T(1,128)} %bitcast.44, ...), custom_call_target="tpu_custom_call" | custom-call | flops 100000000 | bytes 1000000 | tf_op jit(solution)/shard_map/pallas_call | solution.py:455
  9.4 0.1 collective-permute-start
  9.5 0.0 collective-permute-done.7.refs_4_
  9.5 0.5 %collective-permute-start.8 = (bf16[272,128]{1,0:T(8,128)(2,1)S(1)}, bf16[272,128]{1,0:T(8,128)(2,1)S(1)}, u32[]{:S(2)}, u32[]{:S(2)}) collective-permute-start(bf16[272,128]{1,0:T(8,128)(2,1)S(1)} %collective-permute-done.7.refs_4_), channel_id=1, source_target_pairs={{0,4},{4,0},{8,12},{12,8},{16,20},{20,16},{24,28},{28,24},{1,5},{5... | collective-permute-start | bytes 208904 | tf_op jit(solution)/shard_map/ppermute | solution.py:471
  10.1 2.5 %collective-permute-done.5.refs_2_ = bf16[272,128]{1,0:T(8,128)(2,1)S(1)} collective-permute-done((bf16[272,128]{1,0:T(8,128)(2,1)S(1)}, bf16[272,128]{1,0:T(8,128)(2,1)S(1)}, u32[]{:S(2)}, u32[]{:S(2)}) %collective-permute-start.5) | collective-permute-done | bytes 69664 | tf_op jit(solution)/shard_map/ppermute | solution.py:467
  12.6 0.0 collective-permute-done.3.refs_0_
  12.6 0.5 collective-permute-start.4
  13.1 0.0 collective-permute-done
  13.1 1.6 %collective-permute-start.1 = (f32[4,8,640]{2,1,0:T(8,128)S(1)}, f32[4,8,640]{2,1,0:T(8,128)S(1)}, u32[]{:S(2)}, u32[]{:S(2)}) collective-permute-start(f32[4,8,640]{2,1,0:T(8,128)S(1)} %pad_maximum_fusion), channel_id=1, source_target_pairs={{0,8},{4,12},{8,0},{12,4},{16,24},{20,28},{24,16},{28,20},{1,9},{5... | collective-permute-start | bytes 245768 | tf_op jit(solution)/shard_map/ppermute | solution.py:91
  14.7 0.0 collective-permute-done.8.refs_5_
  14.7 0.0 collective-permute-done.6.refs_3_
  14.7 0.0 collective-permute-done.4.refs_1_
  14.7 0.0 copy-start.1
  14.7 13.3 %shard_map.134 = (bf16[32,64,256]{2,1,0:T(8,128)(2,1)S(1)}, bf16[32,64,256]{2,1,0:T(8,128)(2,1)S(1)}, f32[32,128]{1,0:T(8,128)S(1)}) custom-call(s32[1,32]{1,0:T(1,128)} %bitcast.45, f32[64,128]{1,0:T(8,128)} %bitcast.35, bf16[128,512]{1,0:T(8,128)(2,1)} %own_in.3, bf16[2,512]{1,0:T(2,128)(2,1)} %nodes_in.3, ...), custom_call_target="tpu_custom_call" | custom-call | flops 10000000000 | bytes 10000000 | tf_op jit(solution)/shard_map/pallas_call | solution.py:476
  28.1 0.1 collective-permute-start.9
  28.1 1.2 %collective-permute-done.9 = f32[32,128]{1,0:T(8,128)S(1)} collective-permute-done((f32[32,128]{1,0:T(8,128)S(1)}, f32[32,128]{1,0:T(8,128)S(1)}, u32[]{:S(2)}, u32[]{:S(2)}) %collective-permute-start.9) | collective-permute-done | bytes 16416 | tf_op jit(solution)/shard_map/ppermute | solution.py:417
  29.3 1.8 %collective-permute-start.12 = (f32[32,128]{1,0:T(8,128)S(1)}, f32[32,128]{1,0:T(8,128)S(1)}, u32[]{:S(2)}, u32[]{:S(2)}) collective-permute-start(f32[32,128]{1,0:T(8,128)S(1)} %add.12.first), channel_id=1, source_target_pairs={{0,24},{4,28},{8,16},{12,20},{16,8},{20,12},{24,0},{28,4},{1,25},{... | collective-permute-start | bytes 49160 | tf_op jit(solution)/shard_map/ppermute | solution.py:417
  31.1 0.5 collective-permute-start.11
  31.6 1.2 %collective-permute-start.10 = (f32[32,128]{1,0:T(8,128)S(1)}, f32[32,128]{1,0:T(8,128)S(1)}, u32[]{:S(2)}, u32[]{:S(2)}) collective-permute-start(f32[32,128]{1,0:T(8,128)S(1)} %add.12.first), channel_id=1, source_target_pairs={{0,8},{4,12},{8,0},{12,4},{16,24},{20,28},{24,16},{28,20},{1,9},{5... | collective-permute-start | bytes 49160 | tf_op jit(solution)/shard_map/ppermute | solution.py:417
  32.8 2.9 %shard_map.131.refs_1_.refs_3_ = f32[64,128]{1,0:T(8,128)S(1)} custom-call(f32[64,128]{1,0:T(8,128)S(1)} %bitcast.36, f32[1,8,640]{2,1,0:T(8,128)S(1)} %get-tuple-element.19.refs_0_, f32[1,8,640]{2,1,0:T(8,128)S(1)} %get-tuple-element.17.refs_1_, f32[2,8,640]{2,1,0:T(8,128)S(1)} %get-tuple-element.15.refs_2_), custom_call_target="tpu_custom_call" | custom-call | flops 1000000000 | bytes 10000000 | tf_op jit(solution)/shard_map/pallas_call | solution.py:212
  35.7 0.0 collective-permute-done.11.refs_1_
  35.7 2.8 %collective-permute-start.15 = (f32[32,128]{1,0:T(8,128)S(1)}, f32[32,128]{1,0:T(8,128)S(1)}, u32[]{:S(2)}, u32[]{:S(2)}) collective-permute-start(f32[32,128]{1,0:T(8,128)S(1)} %shard_map.135), channel_id=1, source_target_pairs={{0,3},{1,2},{2,1},{3,0},{4,7},{5,6},{6,5},{7,4},{8,11},{9,10},{10,... | collective-permute-start | bytes 49160 | tf_op jit(solution)/shard_map/ppermute | solution.py:417
  38.5 1.7 %collective-permute-start.13 = (f32[32,128]{1,0:T(8,128)S(1)}, f32[32,128]{1,0:T(8,128)S(1)}, u32[]{:S(2)}, u32[]{:S(2)}) collective-permute-start(f32[32,128]{1,0:T(8,128)S(1)} %shard_map.135), channel_id=1, source_target_pairs={{0,1},{1,0},{2,3},{3,2},{4,5},{5,4},{6,7},{7,6},{8,9},{9,8},{10,11... | collective-permute-start | bytes 49160 | tf_op jit(solution)/shard_map/ppermute | solution.py:417
  40.2 1.5 %collective-permute-start.2 = (f32[4,8,640]{2,1,0:T(8,128)S(1)}, f32[4,8,640]{2,1,0:T(8,128)S(1)}, u32[]{:S(2)}, u32[]{:S(2)}) collective-permute-start(f32[4,8,640]{2,1,0:T(8,128)S(1)} %pad_maximum_fusion.1), channel_id=1, source_target_pairs={{0,16},{4,20},{8,24},{12,28},{16,0},{20,4},{24,8},{28,12},{1,17},{... | collective-permute-start | bytes 245768 | tf_op jit(solution)/shard_map/ppermute | solution.py:91
  41.7 1.4 %collective-permute-done.14 = f32[32,128]{1,0:T(8,128)S(1)} collective-permute-done((f32[32,128]{1,0:T(8,128)S(1)}, f32[32,128]{1,0:T(8,128)S(1)}, u32[]{:S(2)}, u32[]{:S(2)}) %collective-permute-start.14) | collective-permute-done | bytes 16416 | tf_op jit(solution)/shard_map/ppermute | solution.py:417
  43.2 1.5 %collective-permute-done.2.refs_0_ = f32[4,8,640]{2,1,0:T(8,128)S(1)} collective-permute-done((f32[4,8,640]{2,1,0:T(8,128)S(1)}, f32[4,8,640]{2,1,0:T(8,128)S(1)}, u32[]{:S(2)}, u32[]{:S(2)}) %collective-permute-start.2) | collective-permute-done | bytes 81952 | tf_op jit(solution)/shard_map/ppermute | solution.py:91
  44.6 3.5 %shard_map.132._ = f32[64,128]{1,0:T(8,128)} custom-call(f32[64,128]{1,0:T(8,128)S(1)} %bitcast.37, f32[4,8,640]{2,1,0:T(8,128)S(1)} %collective-permute-done.2.refs_0_, f32[64,128]{1,0:T(8,128)S(1)} %shard_map.131.refs_1_.refs_3_), custom_call_target="tpu_custom_call" | custom-call | flops 1000000000 | bytes 10000000 | tf_op jit(solution)/shard_map/pallas_call | solution.py:212
  48.1 0.8 %copy-done = f32[64,128]{1,0:T(8,128)S(1)} copy-done((f32[64,128]{1,0:T(8,128)S(1)}, f32[64,128]{1,0:T(8,128)}, u32[]{:S(2)}) %copy-start) | copy-done | bytes 32792
  48.9 4.2 %shard_map.136 = f32[32,128,128]{2,1,0:T(8,128)} custom-call(f32[32,128]{1,0:T(8,128)S(1)} %add_add_fusion.gram_ref, bf16[32,64,256]{2,1,0:T(8,128)(2,1)S(1)} %get-tuple-element.13.high_ref, bf16[32,64,256]{2,1,0:T(8,128)(2,1)S(1)} %get-tuple-element.14.low_ref, f32[64,128]{1,0:T(8,128)S(1)} %copy-done), custom_call_target="tpu_custom_call" | custom-call | flops 1000000000 | bytes 10000000 | tf_op jit(solution)/shard_map/pallas_call | solution.py:504
  (20 shorter events, 0.1 us)
Async XLA Ops:
  1.6 7.9 %collective-permute-start.7 = (bf16[272,128]{1,0:T(8,128)(2,1)S(1)}, bf16[272,128]{1,0:T(8,128)(2,1)S(1)}, u32[]{:S(2)}, u32[]{:S(2)}) collective-permute-start(bf16[272,128]{1,0:T(8,128)(2,1)S(1)} %shard_map.133), channel_id=1, source_target_pairs={{0,3},{1,2},{2,1},{3,0},{4,7},{5,6},{6,5},{7,4},{8,11},{9,10},{10,... | collective-permute-start | bytes 208904 | tf_op jit(solution)/shard_map/ppermute | solution.py:467
  6.7 5.9 %collective-permute-start.5 = (bf16[272,128]{1,0:T(8,128)(2,1)S(1)}, bf16[272,128]{1,0:T(8,128)(2,1)S(1)}, u32[]{:S(2)}, u32[]{:S(2)}) collective-permute-start(bf16[272,128]{1,0:T(8,128)(2,1)S(1)} %shard_map.133), channel_id=1, source_target_pairs={{0,2},{1,3},{2,0},{3,1},{4,6},{5,7},{6,4},{7,5},{8,10},{9,11},{10,... | collective-permute-start | bytes 208904 | tf_op jit(solution)/shard_map/ppermute | solution.py:467
  6.7 5.9 %collective-permute-start.3 = (bf16[272,128]{1,0:T(8,128)(2,1)S(1)}, bf16[272,128]{1,0:T(8,128)(2,1)S(1)}, u32[]{:S(2)}, u32[]{:S(2)}) collective-permute-start(bf16[272,128]{1,0:T(8,128)(2,1)S(1)} %shard_map.133), channel_id=1, source_target_pairs={{0,1},{1,0},{2,3},{3,2},{4,5},{5,4},{6,7},{7,6},{8,9},{9,8},{10,11... | collective-permute-start | bytes 208904 | tf_op jit(solution)/shard_map/ppermute | solution.py:467
  9.4 3.7 %collective-permute-start = (f32[4,8,640]{2,1,0:T(8,128)S(1)}, f32[4,8,640]{2,1,0:T(8,128)S(1)}, u32[]{:S(2)}, u32[]{:S(2)}) collective-permute-start(f32[4,8,640]{2,1,0:T(8,128)S(1)} %get-tuple-element.11), channel_id=1, source_target_pairs={{0,4},{4,0},{8,12},{12,8},{16,20},{20,16},{24,28},{28,24},{1,5},{5... | collective-permute-start | bytes 245768 | tf_op jit(solution)/shard_map/ppermute | solution.py:91
  9.5 5.2 %collective-permute-start.8 = (bf16[272,128]{1,0:T(8,128)(2,1)S(1)}, bf16[272,128]{1,0:T(8,128)(2,1)S(1)}, u32[]{:S(2)}, u32[]{:S(2)}) collective-permute-start(bf16[272,128]{1,0:T(8,128)(2,1)S(1)} %collective-permute-done.7.refs_4_), channel_id=1, source_target_pairs={{0,4},{4,0},{8,12},{12,8},{16,20},{20,16},{24,28},{28,24},{1,5},{5... | collective-permute-start | bytes 208904 | tf_op jit(solution)/shard_map/ppermute | solution.py:471
  12.6 2.1 %collective-permute-start.6 = (bf16[272,128]{1,0:T(8,128)(2,1)S(1)}, bf16[272,128]{1,0:T(8,128)(2,1)S(1)}, u32[]{:S(2)}, u32[]{:S(2)}) collective-permute-start(bf16[272,128]{1,0:T(8,128)(2,1)S(1)} %collective-permute-done.5.refs_2_), channel_id=1, source_target_pairs={{0,4},{4,0},{8,12},{12,8},{16,20},{20,16},{24,28},{28,24},{1,5},{5... | collective-permute-start | bytes 208904 | tf_op jit(solution)/shard_map/ppermute | solution.py:471
  12.6 2.1 %collective-permute-start.4 = (bf16[272,128]{1,0:T(8,128)(2,1)S(1)}, bf16[272,128]{1,0:T(8,128)(2,1)S(1)}, u32[]{:S(2)}, u32[]{:S(2)}) collective-permute-start(bf16[272,128]{1,0:T(8,128)(2,1)S(1)} %collective-permute-done.3.refs_0_), channel_id=1, source_target_pairs={{0,4},{4,0},{8,12},{12,8},{16,20},{20,16},{24,28},{28,24},{1,5},{5... | collective-permute-start | bytes 208904 | tf_op jit(solution)/shard_map/ppermute | solution.py:471
  13.1 19.7 %collective-permute-start.1 = (f32[4,8,640]{2,1,0:T(8,128)S(1)}, f32[4,8,640]{2,1,0:T(8,128)S(1)}, u32[]{:S(2)}, u32[]{:S(2)}) collective-permute-start(f32[4,8,640]{2,1,0:T(8,128)S(1)} %pad_maximum_fusion), channel_id=1, source_target_pairs={{0,8},{4,12},{8,0},{12,4},{16,24},{20,28},{24,16},{28,20},{1,9},{5... | collective-permute-start | bytes 245768 | tf_op jit(solution)/shard_map/ppermute | solution.py:91
  14.7 18.1 %copy-start.1 = (f32[32,2,128]{2,1,0:T(2,128)S(1)}, f32[32,2,128]{2,1,0:T(2,128)}, u32[]{:S(2)}) copy-start(f32[32,2,128]{2,1,0:T(2,128)} %param.11) | copy-start | bytes 98308
  28.1 1.2 %collective-permute-start.9 = (f32[32,128]{1,0:T(8,128)S(1)}, f32[32,128]{1,0:T(8,128)S(1)}, u32[]{:S(2)}, u32[]{:S(2)}) collective-permute-start(f32[32,128]{1,0:T(8,128)S(1)} %get-tuple-element.12), channel_id=1, source_target_pairs={{0,4},{4,0},{8,12},{12,8},{16,20},{20,16},{24,28},{28,24},{1,5},{5... | collective-permute-start | bytes 49160 | tf_op jit(solution)/shard_map/ppermute | solution.py:417
  29.3 6.4 %collective-permute-start.12 = (f32[32,128]{1,0:T(8,128)S(1)}, f32[32,128]{1,0:T(8,128)S(1)}, u32[]{:S(2)}, u32[]{:S(2)}) collective-permute-start(f32[32,128]{1,0:T(8,128)S(1)} %add.12.first), channel_id=1, source_target_pairs={{0,24},{4,28},{8,16},{12,20},{16,8},{20,12},{24,0},{28,4},{1,25},{... | collective-permute-start | bytes 49160 | tf_op jit(solution)/shard_map/ppermute | solution.py:417
  31.1 4.6 %collective-permute-start.11 = (f32[32,128]{1,0:T(8,128)S(1)}, f32[32,128]{1,0:T(8,128)S(1)}, u32[]{:S(2)}, u32[]{:S(2)}) collective-permute-start(f32[32,128]{1,0:T(8,128)S(1)} %add.12.first), channel_id=1, source_target_pairs={{0,16},{4,20},{8,24},{12,28},{16,0},{20,4},{24,8},{28,12},{1,17},{... | collective-permute-start | bytes 49160 | tf_op jit(solution)/shard_map/ppermute | solution.py:417
  31.6 4.1 %collective-permute-start.10 = (f32[32,128]{1,0:T(8,128)S(1)}, f32[32,128]{1,0:T(8,128)S(1)}, u32[]{:S(2)}, u32[]{:S(2)}) collective-permute-start(f32[32,128]{1,0:T(8,128)S(1)} %add.12.first), channel_id=1, source_target_pairs={{0,8},{4,12},{8,0},{12,4},{16,24},{20,28},{24,16},{28,20},{1,9},{5... | collective-permute-start | bytes 49160 | tf_op jit(solution)/shard_map/ppermute | solution.py:417
  35.7 6.0 %collective-permute-start.15 = (f32[32,128]{1,0:T(8,128)S(1)}, f32[32,128]{1,0:T(8,128)S(1)}, u32[]{:S(2)}, u32[]{:S(2)}) collective-permute-start(f32[32,128]{1,0:T(8,128)S(1)} %shard_map.135), channel_id=1, source_target_pairs={{0,3},{1,2},{2,1},{3,0},{4,7},{5,6},{6,5},{7,4},{8,11},{9,10},{10,... | collective-permute-start | bytes 49160 | tf_op jit(solution)/shard_map/ppermute | solution.py:417
  38.5 4.6 %collective-permute-start.14 = (f32[32,128]{1,0:T(8,128)S(1)}, f32[32,128]{1,0:T(8,128)S(1)}, u32[]{:S(2)}, u32[]{:S(2)}) collective-permute-start(f32[32,128]{1,0:T(8,128)S(1)} %shard_map.135), channel_id=1, source_target_pairs={{0,2},{1,3},{2,0},{3,1},{4,6},{5,7},{6,4},{7,5},{8,10},{9,11},{10,... | collective-permute-start | bytes 49160 | tf_op jit(solution)/shard_map/ppermute | solution.py:417
  38.5 4.6 %collective-permute-start.13 = (f32[32,128]{1,0:T(8,128)S(1)}, f32[32,128]{1,0:T(8,128)S(1)}, u32[]{:S(2)}, u32[]{:S(2)}) collective-permute-start(f32[32,128]{1,0:T(8,128)S(1)} %shard_map.135), channel_id=1, source_target_pairs={{0,1},{1,0},{2,3},{3,2},{4,5},{5,4},{6,7},{7,6},{8,9},{9,8},{10,11... | collective-permute-start | bytes 49160 | tf_op jit(solution)/shard_map/ppermute | solution.py:417
  40.2 4.4 %collective-permute-start.2 = (f32[4,8,640]{2,1,0:T(8,128)S(1)}, f32[4,8,640]{2,1,0:T(8,128)S(1)}, u32[]{:S(2)}, u32[]{:S(2)}) collective-permute-start(f32[4,8,640]{2,1,0:T(8,128)S(1)} %pad_maximum_fusion.1), channel_id=1, source_target_pairs={{0,16},{4,20},{8,24},{12,28},{16,0},{20,4},{24,8},{28,12},{1,17},{... | collective-permute-start | bytes 245768 | tf_op jit(solution)/shard_map/ppermute | solution.py:91
  48.1 0.8 %copy-start = (f32[64,128]{1,0:T(8,128)S(1)}, f32[64,128]{1,0:T(8,128)}, u32[]{:S(2)}) copy-start(f32[64,128]{1,0:T(8,128)} %shard_map.132._) | copy-start | bytes 98308

commit v7 on v6

--- a/solution.py
+++ b/solution.py
@@ -226,7 +226,7 @@
     count = 2 * (col_count - 1)
     piece_refs = refs[:count]
     (high_ref, low_ref, gram_ref, range_ref, pos_ref, own_nodes, own_rows, basis, spots, wide,
-     buffer_0, buffer_1, sums, sems) = refs[count:]
+     sums, sems) = refs[count:]
     vesicles = pos_ref.shape[0] // 2
     nodes = pos_ref.shape[1]
     rank, sources = own_rows.shape[0] // 2, own_rows.shape[1]
@@ -255,53 +255,54 @@
     sums[...] = jnp.zeros_like(sums)
 
     chunk = 32 if sources % 32 == 0 else sources
-
-    def evaluate(v, buffer, part, parts):
+    depth = 256 if sources % 256 == 0 else sources
+
+    def evaluate(v, start):
         r = range_ref[0, v]
         tx = pos_ref[pl.ds(2 * v, 1), :]
         ty = pos_ref[pl.ds(2 * v + 1, 1), :]
-        for start in range(part * sources // parts, (part + 1) * sources // parts, chunk):
-            dx = tx - wide[r, 0, start:start + chunk]
-            dy = ty - wide[r, 1, start:start + chunk]
-            spread = dx * dx + dy * dy + EPS_SQUARED
-            log_part = -0.5 * jnp.log(spread)
-            inverse = reciprocal(spread)
-            dxr = dx * inverse
-            upper = slice(start, start + chunk)
-            lower = slice(sources + start, sources + start + chunk)
-            cross = (dy * dxr).astype(BF16)
-            buffer[upper, :nodes] = (log_part + dx * dxr).astype(BF16)
-            buffer[upper, nodes:] = cross
-            buffer[lower, :nodes] = cross
-            buffer[lower, nodes:] = (log_part + dy * (dy * inverse)).astype(BF16)
-
-    def step(v, now, following):
-        later = jnp.minimum(v + 1, vesicles - 1)
-        product = dot(basis[range_ref[0, v]], now[...])
-        evaluate(later, following, 0, 2)
-        high = product.astype(BF16)
-        high_ref[v] = high
-        low_ref[v] = (product - high.astype(F32)).astype(BF16)
-        evaluate(later, following, 1, 2)
-
-    def add_gram(v):
+        dx = tx - wide[r, 0, start:start + chunk]
+        dy = ty - wide[r, 1, start:start + chunk]
+        spread = dx * dx + dy * dy + EPS_SQUARED
+        log_part = -0.5 * jnp.log(spread)
+        inverse = reciprocal(spread)
+        dxr = dx * inverse
+        return ((log_part + dx * dxr).astype(BF16), (dy * dxr).astype(BF16),
+                (log_part + dy * (dy * inverse)).astype(BF16))
+
+    def sketch(v):
+        r = range_ref[0, v]
+        total = None
+        for start in range(0, sources, depth):
+            ff, fs, ss = [jnp.concatenate(p, axis=0) for p in zip(
+                *[evaluate(v, start + c) for c in range(0, depth, chunk)])]
+            part = dot(basis[r, :, start:start + depth], jnp.concatenate([ff, fs], axis=1))
+            part += dot(basis[r, :, sources + start:sources + start + depth],
+                        jnp.concatenate([fs, ss], axis=1))
+            total = part if total is None else total + part
+        return total
+
+    def pair_gram(v):
         both = jnp.concatenate([
             jnp.concatenate([ref[v], ref[v + 1]], axis=1) for ref in (high_ref, low_ref)], axis=0)
-        sums[...] += dot(both, both, NT)
-
-    evaluate(0, buffer_0, 0, 1)
+        return dot(both, both, NT)
+
     high_ref[0:2] = jnp.zeros((2, rank, 2 * nodes), BF16)
     low_ref[0:2] = jnp.zeros((2, rank, 2 * nodes), BF16)
 
     def pair(i, _):
         v = 2 * i
-        add_gram(jnp.maximum(v - 2, 0))
-        step(v, buffer_0, buffer_1)
-        step(v + 1, buffer_1, buffer_0)
+        before = pair_gram(jnp.maximum(v - 2, 0))
+        made = [sketch(v), sketch(v + 1)]
+        sums[...] += before
+        for c, value in enumerate(made):
+            high = value.astype(BF16)
+            high_ref[v + c] = high
+            low_ref[v + c] = (value - high.astype(F32)).astype(BF16)
         return 0
 
     lax.fori_loop(0, vesicles // 2, pair, 0)
-    add_gram(vesicles - 2)
+    sums[...] += pair_gram(vesicles - 2)
     total = sums[...]
     gram = total[:rank, :rank] + total[rank:, rank:] + (total[:rank, rank:] + total[rank:, :rank])
     gram_ref[...] = jnp.concatenate([gram[:rank // 2], gram[rank // 2:]], axis=1)
@@ -487,8 +488,6 @@
             pltpu.VMEM((col_count, rank, 2 * sources), BF16),
             pltpu.VMEM((col_count, 8, sources), F32),
             pltpu.VMEM((col_count, 2, sources, nodes), F32),
-            pltpu.VMEM((2 * sources, 2 * nodes), BF16),
-            pltpu.VMEM((2 * sources, 2 * nodes), BF16),
             pltpu.VMEM((rows, rows), F32),
             pltpu.SemaphoreType.DMA((4,))],
         compiler_params=params(32),
@@ -510,7 +509,7 @@
         scratch_shapes=[pltpu.VMEM((rank, 3 * rank), BF16)],
         compiler_params=params(16),
         cost_estimate=pl.CostEstimate(flops=10**9, bytes_accessed=10**7, transcendentals=0),
-    )(gram, high, low, near)
+    )(gram, high, low, near_by(near))
 
     return (force.reshape(vesicles, 2, nodes), near.reshape(vesicles, 2, nodes),
             new_basis.reshape(vesicles, rank, 2, nodes))

time: 53.4 us -> 50.3 us (0.942)
  Pallas kernels: 26.9 us -> 24.7 us
  local copies, waits for them, and re-layouts: 0.79 us -> 0.03 us
    pallas_call x1, Pallas kernels: 13.3 us -> 11.1 us  [per_device(): pl.pallas_call(functools.partial(far_kernel, col_count), out_shape=[jax.S...]
    unnamed x4 -> x2, local copies, waits for them, and re-layouts: 0.76 us -> 0.01 us
  transfers between devices with their start and end apart: 16 -> 16, of which waited for: 4 -> 4; matrix products, arithmetic and copies ran while one was open for 0% -> 0% of each run, Pallas kernels for 34% -> 32%
where the time goes in v7:
time: 50.3 us; the launch traced here: 50.1 us
  Pallas kernels  24.7 us (49%)
  starting transfers between devices  18 us (36%)
  waiting for transfers between devices  6.64 us (13%)
  between operations  0.77 us (2%)
    pallas_call x1, Pallas kernels, per_device(): pl.pallas_call(functools.partial(far_kernel, col_count), out_shape=[jax.S...  11.1 us
    ppermute x7, starting transfers between devices, sum_over(): lax.ppermute(value, axis, partners(count, k))  8.01 us
    pallas_call x2, Pallas kernels, near_part(): pl.pallas_call(functools.partial(near_start if before is None else near_k...  6.35 us
    ppermute x3, starting transfers between devices, per_device(): lax.ppermute(sent, 'col', partners(col_count, k))  5.76 us
    pallas_call x1, Pallas kernels, per_device(): pl.pallas_call(functools.partial(basis_kernel, scale_factor), out_shape=j...  4.24 us
    ppermute x3, starting transfers between devices, cube_exchange(): held.append(lax.ppermute(leaving, axis, partners(count, bit)))  3.15 us
    ppermute x7, waiting for transfers between devices, sum_over(): lax.ppermute(value, axis, partners(count, k))  2.61 us
    ppermute x3, waiting for transfers between devices, per_device(): lax.ppermute(sent, 'col', partners(col_count, k))  2.54 us
  transfers between devices with their start and end apart: 16, of which 4 were waited for; matrix products, arithmetic and copies ran while one was open for 0% of the time, Pallas kernels for 32%

profile of v7, /device:TPU:0, one launch (start us, length us, event | category | flops | bytes accessed | tf_op | source)
XLA Modules:
  0.0 50.1 jit_solution(1724242660474539278)
XLA Ops:
  0.6 0.9 %shard_map.133 = bf16[272,128]{1,0:T(8,128)(2,1)S(1)} custom-call(bf16[128,512]{1,0:T(8,128)(2,1)} %own_in.3, bf16[2,512]{1,0:T(2,128)(2,1)} %nodes_in.3), custom_call_target="tpu_custom_call" | custom-call | flops 100000 | bytes 100000 | tf_op jit(solution)/shard_map/pallas_call | solution.py:441
  1.6 5.1 %collective-permute-start.7 = (bf16[272,128]{1,0:T(8,128)(2,1)S(1)}, bf16[272,128]{1,0:T(8,128)(2,1)S(1)}, u32[]{:S(2)}, u32[]{:S(2)}) collective-permute-start(bf16[272,128]{1,0:T(8,128)(2,1)S(1)} %shard_map.133), channel_id=1, source_target_pairs={{0,3},{1,2},{2,1},{3,0},{4,7},{5,6},{6,5},{7,4},{8,11},{9,10},{10,... | collective-permute-start | bytes 208904 | tf_op jit(solution)/shard_map/ppermute | solution.py:468
  6.7 0.6 %collective-permute-start.3 = (bf16[272,128]{1,0:T(8,128)(2,1)S(1)}, bf16[272,128]{1,0:T(8,128)(2,1)S(1)}, u32[]{:S(2)}, u32[]{:S(2)}) collective-permute-start(bf16[272,128]{1,0:T(8,128)(2,1)S(1)} %shard_map.133), channel_id=1, source_target_pairs={{0,1},{1,0},{2,3},{3,2},{4,5},{5,4},{6,7},{7,6},{8,9},{9,8},{10,11... | collective-permute-start | bytes 208904 | tf_op jit(solution)/shard_map/ppermute | solution.py:468
  7.3 2.1 %shard_map.130 = (f32[64,128]{1,0:T(8,128)}, f32[4,8,640]{2,1,0:T(8,128)S(1)}, f32[4,8,640]{2,1,0:T(8,128)S(1)}) custom-call(f32[64,128]{1,0:T(8,128)} %bitcast.33, f32[32,128]{1,0:T(8,128)} %refs_1_.1, f32[1,32]{1,0:T(1,128)} %bitcast.42, s32[1,32]{1,0:T(1,128)} %refs_3_.1, s32[1,24]{1,0:T(1,128)} %bitcast.43, s32[1,24]{1,0:T(1,128)} %bitcast.44, ...), custom_call_target="tpu_custom_call" | custom-call | flops 100000000 | bytes 1000000 | tf_op jit(solution)/shard_map/pallas_call | solution.py:456
  9.4 0.1 collective-permute-start
  9.5 0.0 collective-permute-done.7.refs_4_
  9.5 0.5 %collective-permute-start.8 = (bf16[272,128]{1,0:T(8,128)(2,1)S(1)}, bf16[272,128]{1,0:T(8,128)(2,1)S(1)}, u32[]{:S(2)}, u32[]{:S(2)}) collective-permute-start(bf16[272,128]{1,0:T(8,128)(2,1)S(1)} %collective-permute-done.7.refs_4_), channel_id=1, source_target_pairs={{0,4},{4,0},{8,12},{12,8},{16,20},{20,16},{24,28},{28,24},{1,5},{5... | collective-permute-start | bytes 208904 | tf_op jit(solution)/shard_map/ppermute | solution.py:472
  10.1 2.5 %collective-permute-done.5.refs_2_ = bf16[272,128]{1,0:T(8,128)(2,1)S(1)} collective-permute-done((bf16[272,128]{1,0:T(8,128)(2,1)S(1)}, bf16[272,128]{1,0:T(8,128)(2,1)S(1)}, u32[]{:S(2)}, u32[]{:S(2)}) %collective-permute-start.5) | collective-permute-done | bytes 69664 | tf_op jit(solution)/shard_map/ppermute | solution.py:468
  12.6 0.0 collective-permute-start.6
  12.6 0.0 collective-permute-done.3.refs_0_
  12.6 0.5 %collective-permute-start.4 = (bf16[272,128]{1,0:T(8,128)(2,1)S(1)}, bf16[272,128]{1,0:T(8,128)(2,1)S(1)}, u32[]{:S(2)}, u32[]{:S(2)}) collective-permute-start(bf16[272,128]{1,0:T(8,128)(2,1)S(1)} %collective-permute-done.3.refs_0_), channel_id=1, source_target_pairs={{0,4},{4,0},{8,12},{12,8},{16,20},{20,16},{24,28},{28,24},{1,5},{5... | collective-permute-start | bytes 208904 | tf_op jit(solution)/shard_map/ppermute | solution.py:472
  13.1 0.0 collective-permute-done
  13.1 1.6 %collective-permute-start.1 = (f32[4,8,640]{2,1,0:T(8,128)S(1)}, f32[4,8,640]{2,1,0:T(8,128)S(1)}, u32[]{:S(2)}, u32[]{:S(2)}) collective-permute-start(f32[4,8,640]{2,1,0:T(8,128)S(1)} %pad_maximum_fusion), channel_id=1, source_target_pairs={{0,8},{4,12},{8,0},{12,4},{16,24},{20,28},{24,16},{28,20},{1,9},{5... | collective-permute-start | bytes 245768 | tf_op jit(solution)/shard_map/ppermute | solution.py:91
  14.7 0.0 collective-permute-done.8.refs_5_
  14.7 0.0 collective-permute-done.6.refs_3_
  14.7 0.0 collective-permute-done.4.refs_1_
  14.7 0.0 copy-start
  14.7 11.1 %shard_map.134 = (bf16[32,64,256]{2,1,0:T(8,128)(2,1)S(1)}, bf16[32,64,256]{2,1,0:T(8,128)(2,1)S(1)}, f32[32,128]{1,0:T(8,128)S(1)}) custom-call(s32[1,32]{1,0:T(1,128)} %bitcast.45, f32[64,128]{1,0:T(8,128)} %bitcast.34, bf16[128,512]{1,0:T(8,128)(2,1)} %own_in.3, bf16[2,512]{1,0:T(2,128)(2,1)} %nodes_in.3, ...), custom_call_target="tpu_custom_call" | custom-call | flops 10000000000 | bytes 10000000 | tf_op jit(solution)/shard_map/pallas_call | solution.py:477
  25.8 0.1 collective-permute-start.9
  25.9 1.2 %collective-permute-done.9 = f32[32,128]{1,0:T(8,128)S(1)} collective-permute-done((f32[32,128]{1,0:T(8,128)S(1)}, f32[32,128]{1,0:T(8,128)S(1)}, u32[]{:S(2)}, u32[]{:S(2)}) %collective-permute-start.9) | collective-permute-done | bytes 16416 | tf_op jit(solution)/shard_map/ppermute | solution.py:418
  27.1 1.8 %collective-permute-start.12 = (f32[32,128]{1,0:T(8,128)S(1)}, f32[32,128]{1,0:T(8,128)S(1)}, u32[]{:S(2)}, u32[]{:S(2)}) collective-permute-start(f32[32,128]{1,0:T(8,128)S(1)} %add.12.first), channel_id=1, source_target_pairs={{0,24},{4,28},{8,16},{12,20},{16,8},{20,12},{24,0},{28,4},{1,25},{... | collective-permute-start | bytes 49160 | tf_op jit(solution)/shard_map/ppermute | solution.py:418
  28.8 0.5 %collective-permute-start.11 = (f32[32,128]{1,0:T(8,128)S(1)}, f32[32,128]{1,0:T(8,128)S(1)}, u32[]{:S(2)}, u32[]{:S(2)}) collective-permute-start(f32[32,128]{1,0:T(8,128)S(1)} %add.12.first), channel_id=1, source_target_pairs={{0,16},{4,20},{8,24},{12,28},{16,0},{20,4},{24,8},{28,12},{1,17},{... | collective-permute-start | bytes 49160 | tf_op jit(solution)/shard_map/ppermute | solution.py:418
  29.3 1.2 %collective-permute-start.10 = (f32[32,128]{1,0:T(8,128)S(1)}, f32[32,128]{1,0:T(8,128)S(1)}, u32[]{:S(2)}, u32[]{:S(2)}) collective-permute-start(f32[32,128]{1,0:T(8,128)S(1)} %add.12.first), channel_id=1, source_target_pairs={{0,8},{4,12},{8,0},{12,4},{16,24},{20,28},{24,16},{28,20},{1,9},{5... | collective-permute-start | bytes 49160 | tf_op jit(solution)/shard_map/ppermute | solution.py:418
  30.6 2.9 %shard_map.131.refs_1_.refs_3_ = f32[64,128]{1,0:T(8,128)S(1)} custom-call(f32[64,128]{1,0:T(8,128)S(1)} %bitcast.35, f32[1,8,640]{2,1,0:T(8,128)S(1)} %get-tuple-element.19.refs_0_, f32[1,8,640]{2,1,0:T(8,128)S(1)} %get-tuple-element.17.refs_1_, f32[2,8,640]{2,1,0:T(8,128)S(1)} %get-tuple-element.15.refs_2_), custom_call_target="tpu_custom_call" | custom-call | flops 1000000000 | bytes 10000000 | tf_op jit(solution)/shard_map/pallas_call | solution.py:212
  33.4 0.0 collective-permute-done.11.refs_1_
  33.5 2.8 %collective-permute-start.15 = (f32[32,128]{1,0:T(8,128)S(1)}, f32[32,128]{1,0:T(8,128)S(1)}, u32[]{:S(2)}, u32[]{:S(2)}) collective-permute-start(f32[32,128]{1,0:T(8,128)S(1)} %shard_map.135), channel_id=1, source_target_pairs={{0,3},{1,2},{2,1},{3,0},{4,7},{5,6},{6,5},{7,4},{8,11},{9,10},{10,... | collective-permute-start | bytes 49160 | tf_op jit(solution)/shard_map/ppermute | solution.py:418
  36.3 1.7 %collective-permute-start.13 = (f32[32,128]{1,0:T(8,128)S(1)}, f32[32,128]{1,0:T(8,128)S(1)}, u32[]{:S(2)}, u32[]{:S(2)}) collective-permute-start(f32[32,128]{1,0:T(8,128)S(1)} %shard_map.135), channel_id=1, source_target_pairs={{0,1},{1,0},{2,3},{3,2},{4,5},{5,4},{6,7},{7,6},{8,9},{9,8},{10,11... | collective-permute-start | bytes 49160 | tf_op jit(solution)/shard_map/ppermute | solution.py:418
  37.9 1.5 %collective-permute-start.2 = (f32[4,8,640]{2,1,0:T(8,128)S(1)}, f32[4,8,640]{2,1,0:T(8,128)S(1)}, u32[]{:S(2)}, u32[]{:S(2)}) collective-permute-start(f32[4,8,640]{2,1,0:T(8,128)S(1)} %pad_maximum_fusion.1), channel_id=1, source_target_pairs={{0,16},{4,20},{8,24},{12,28},{16,0},{20,4},{24,8},{28,12},{1,17},{... | collective-permute-start | bytes 245768 | tf_op jit(solution)/shard_map/ppermute | solution.py:91
  39.5 1.4 %collective-permute-done.14 = f32[32,128]{1,0:T(8,128)S(1)} collective-permute-done((f32[32,128]{1,0:T(8,128)S(1)}, f32[32,128]{1,0:T(8,128)S(1)}, u32[]{:S(2)}, u32[]{:S(2)}) %collective-permute-start.14) | collective-permute-done | bytes 16416 | tf_op jit(solution)/shard_map/ppermute | solution.py:418
  40.9 1.5 %collective-permute-done.2.refs_0_ = f32[4,8,640]{2,1,0:T(8,128)S(1)} collective-permute-done((f32[4,8,640]{2,1,0:T(8,128)S(1)}, f32[4,8,640]{2,1,0:T(8,128)S(1)}, u32[]{:S(2)}, u32[]{:S(2)}) %collective-permute-start.2) | collective-permute-done | bytes 81952 | tf_op jit(solution)/shard_map/ppermute | solution.py:91
  42.4 3.5 %shard_map.132._ = f32[64,128]{1,0:T(8,128)} custom-call(f32[64,128]{1,0:T(8,128)S(1)} %bitcast.36, f32[4,8,640]{2,1,0:T(8,128)S(1)} %collective-permute-done.2.refs_0_, f32[64,128]{1,0:T(8,128)S(1)} %shard_map.131.refs_1_.refs_3_), custom_call_target="tpu_custom_call" | custom-call | flops 1000000000 | bytes 10000000 | tf_op jit(solution)/shard_map/pallas_call | solution.py:212
  45.9 4.2 %shard_map.136 = f32[32,128,128]{2,1,0:T(8,128)} custom-call(f32[32,128]{1,0:T(8,128)S(1)} %add_add_fusion.gram_ref, bf16[32,64,256]{2,1,0:T(8,128)(2,1)S(1)} %get-tuple-element.13.high_ref, bf16[32,64,256]{2,1,0:T(8,128)(2,1)S(1)} %get-tuple-element.14.low_ref, f32[64,128]{1,0:T(8,128)} %shard_map.132._), custom_call_target="tpu_custom_call" | custom-call | flops 1000000000 | bytes 10000000 | tf_op jit(solution)/shard_map/pallas_call | solution.py:503
  (18 shorter events, 0.1 us)
Async XLA Ops:
  1.6 7.9 %collective-permute-start.7 = (bf16[272,128]{1,0:T(8,128)(2,1)S(1)}, bf16[272,128]{1,0:T(8,128)(2,1)S(1)}, u32[]{:S(2)}, u32[]{:S(2)}) collective-permute-start(bf16[272,128]{1,0:T(8,128)(2,1)S(1)} %shard_map.133), channel_id=1, source_target_pairs={{0,3},{1,2},{2,1},{3,0},{4,7},{5,6},{6,5},{7,4},{8,11},{9,10},{10,... | collective-permute-start | bytes 208904 | tf_op jit(solution)/shard_map/ppermute | solution.py:468
  6.7 5.9 %collective-permute-start.5 = (bf16[272,128]{1,0:T(8,128)(2,1)S(1)}, bf16[272,128]{1,0:T(8,128)(2,1)S(1)}, u32[]{:S(2)}, u32[]{:S(2)}) collective-permute-start(bf16[272,128]{1,0:T(8,128)(2,1)S(1)} %shard_map.133), channel_id=1, source_target_pairs={{0,2},{1,3},{2,0},{3,1},{4,6},{5,7},{6,4},{7,5},{8,10},{9,11},{10,... | collective-permute-start | bytes 208904 | tf_op jit(solution)/shard_map/ppermute | solution.py:468
  6.7 5.9 %collective-permute-start.3 = (bf16[272,128]{1,0:T(8,128)(2,1)S(1)}, bf16[272,128]{1,0:T(8,128)(2,1)S(1)}, u32[]{:S(2)}, u32[]{:S(2)}) collective-permute-start(bf16[272,128]{1,0:T(8,128)(2,1)S(1)} %shard_map.133), channel_id=1, source_target_pairs={{0,1},{1,0},{2,3},{3,2},{4,5},{5,4},{6,7},{7,6},{8,9},{9,8},{10,11... | collective-permute-start | bytes 208904 | tf_op jit(solution)/shard_map/ppermute | solution.py:468
  9.4 3.7 %collective-permute-start = (f32[4,8,640]{2,1,0:T(8,128)S(1)}, f32[4,8,640]{2,1,0:T(8,128)S(1)}, u32[]{:S(2)}, u32[]{:S(2)}) collective-permute-start(f32[4,8,640]{2,1,0:T(8,128)S(1)} %get-tuple-element.11), channel_id=1, source_target_pairs={{0,4},{4,0},{8,12},{12,8},{16,20},{20,16},{24,28},{28,24},{1,5},{5... | collective-permute-start | bytes 245768 | tf_op jit(solution)/shard_map/ppermute | solution.py:91
  9.5 5.2 %collective-permute-start.8 = (bf16[272,128]{1,0:T(8,128)(2,1)S(1)}, bf16[272,128]{1,0:T(8,128)(2,1)S(1)}, u32[]{:S(2)}, u32[]{:S(2)}) collective-permute-start(bf16[272,128]{1,0:T(8,128)(2,1)S(1)} %collective-permute-done.7.refs_4_), channel_id=1, source_target_pairs={{0,4},{4,0},{8,12},{12,8},{16,20},{20,16},{24,28},{28,24},{1,5},{5... | collective-permute-start | bytes 208904 | tf_op jit(solution)/shard_map/ppermute | solution.py:472
  12.6 2.1 %collective-permute-start.6 = (bf16[272,128]{1,0:T(8,128)(2,1)S(1)}, bf16[272,128]{1,0:T(8,128)(2,1)S(1)}, u32[]{:S(2)}, u32[]{:S(2)}) collective-permute-start(bf16[272,128]{1,0:T(8,128)(2,1)S(1)} %collective-permute-done.5.refs_2_), channel_id=1, source_target_pairs={{0,4},{4,0},{8,12},{12,8},{16,20},{20,16},{24,28},{28,24},{1,5},{5... | collective-permute-start | bytes 208904 | tf_op jit(solution)/shard_map/ppermute | solution.py:472
  12.6 2.1 %collective-permute-start.4 = (bf16[272,128]{1,0:T(8,128)(2,1)S(1)}, bf16[272,128]{1,0:T(8,128)(2,1)S(1)}, u32[]{:S(2)}, u32[]{:S(2)}) collective-permute-start(bf16[272,128]{1,0:T(8,128)(2,1)S(1)} %collective-permute-done.3.refs_0_), channel_id=1, source_target_pairs={{0,4},{4,0},{8,12},{12,8},{16,20},{20,16},{24,28},{28,24},{1,5},{5... | collective-permute-start | bytes 208904 | tf_op jit(solution)/shard_map/ppermute | solution.py:472
  13.1 17.4 %collective-permute-start.1 = (f32[4,8,640]{2,1,0:T(8,128)S(1)}, f32[4,8,640]{2,1,0:T(8,128)S(1)}, u32[]{:S(2)}, u32[]{:S(2)}) collective-permute-start(f32[4,8,640]{2,1,0:T(8,128)S(1)} %pad_maximum_fusion), channel_id=1, source_target_pairs={{0,8},{4,12},{8,0},{12,4},{16,24},{20,28},{24,16},{28,20},{1,9},{5... | collective-permute-start | bytes 245768 | tf_op jit(solution)/shard_map/ppermute | solution.py:91
  14.7 15.9 %copy-start = (f32[32,2,128]{2,1,0:T(2,128)S(1)}, f32[32,2,128]{2,1,0:T(2,128)}, u32[]{:S(2)}) copy-start(f32[32,2,128]{2,1,0:T(2,128)} %param.11) | copy-start | bytes 98308
  25.8 1.2 %collective-permute-start.9 = (f32[32,128]{1,0:T(8,128)S(1)}, f32[32,128]{1,0:T(8,128)S(1)}, u32[]{:S(2)}, u32[]{:S(2)}) collective-permute-start(f32[32,128]{1,0:T(8,128)S(1)} %get-tuple-element.12), channel_id=1, source_target_pairs={{0,4},{4,0},{8,12},{12,8},{16,20},{20,16},{24,28},{28,24},{1,5},{5... | collective-permute-start | bytes 49160 | tf_op jit(solution)/shard_map/ppermute | solution.py:418
  27.1 6.4 %collective-permute-start.12 = (f32[32,128]{1,0:T(8,128)S(1)}, f32[32,128]{1,0:T(8,128)S(1)}, u32[]{:S(2)}, u32[]{:S(2)}) collective-permute-start(f32[32,128]{1,0:T(8,128)S(1)} %add.12.first), channel_id=1, source_target_pairs={{0,24},{4,28},{8,16},{12,20},{16,8},{20,12},{24,0},{28,4},{1,25},{... | collective-permute-start | bytes 49160 | tf_op jit(solution)/shard_map/ppermute | solution.py:418
  28.8 4.6 %collective-permute-start.11 = (f32[32,128]{1,0:T(8,128)S(1)}, f32[32,128]{1,0:T(8,128)S(1)}, u32[]{:S(2)}, u32[]{:S(2)}) collective-permute-start(f32[32,128]{1,0:T(8,128)S(1)} %add.12.first), channel_id=1, source_target_pairs={{0,16},{4,20},{8,24},{12,28},{16,0},{20,4},{24,8},{28,12},{1,17},{... | collective-permute-start | bytes 49160 | tf_op jit(solution)/shard_map/ppermute | solution.py:418
  29.3 4.1 %collective-permute-start.10 = (f32[32,128]{1,0:T(8,128)S(1)}, f32[32,128]{1,0:T(8,128)S(1)}, u32[]{:S(2)}, u32[]{:S(2)}) collective-permute-start(f32[32,128]{1,0:T(8,128)S(1)} %add.12.first), channel_id=1, source_target_pairs={{0,8},{4,12},{8,0},{12,4},{16,24},{20,28},{24,16},{28,20},{1,9},{5... | collective-permute-start | bytes 49160 | tf_op jit(solution)/shard_map/ppermute | solution.py:418
  33.5 6.0 %collective-permute-start.15 = (f32[32,128]{1,0:T(8,128)S(1)}, f32[32,128]{1,0:T(8,128)S(1)}, u32[]{:S(2)}, u32[]{:S(2)}) collective-permute-start(f32[32,128]{1,0:T(8,128)S(1)} %shard_map.135), channel_id=1, source_target_pairs={{0,3},{1,2},{2,1},{3,0},{4,7},{5,6},{6,5},{7,4},{8,11},{9,10},{10,... | collective-permute-start | bytes 49160 | tf_op jit(solution)/shard_map/ppermute | solution.py:418
  36.3 4.6 %collective-permute-start.14 = (f32[32,128]{1,0:T(8,128)S(1)}, f32[32,128]{1,0:T(8,128)S(1)}, u32[]{:S(2)}, u32[]{:S(2)}) collective-permute-start(f32[32,128]{1,0:T(8,128)S(1)} %shard_map.135), channel_id=1, source_target_pairs={{0,2},{1,3},{2,0},{3,1},{4,6},{5,7},{6,4},{7,5},{8,10},{9,11},{10,... | collective-permute-start | bytes 49160 | tf_op jit(solution)/shard_map/ppermute | solution.py:418
  36.3 4.6 %collective-permute-start.13 = (f32[32,128]{1,0:T(8,128)S(1)}, f32[32,128]{1,0:T(8,128)S(1)}, u32[]{:S(2)}, u32[]{:S(2)}) collective-permute-start(f32[32,128]{1,0:T(8,128)S(1)} %shard_map.135), channel_id=1, source_target_pairs={{0,1},{1,0},{2,3},{3,2},{4,5},{5,4},{6,7},{7,6},{8,9},{9,8},{10,11... | collective-permute-start | bytes 49160 | tf_op jit(solution)/shard_map/ppermute | solution.py:418
  37.9 4.4 %collective-permute-start.2 = (f32[4,8,640]{2,1,0:T(8,128)S(1)}, f32[4,8,640]{2,1,0:T(8,128)S(1)}, u32[]{:S(2)}, u32[]{:S(2)}) collective-permute-start(f32[4,8,640]{2,1,0:T(8,128)S(1)} %pad_maximum_fusion.1), channel_id=1, source_target_pairs={{0,16},{4,20},{8,24},{12,28},{16,0},{20,4},{24,8},{28,12},{1,17},{... | collective-permute-start | bytes 245768 | tf_op jit(solution)/shard_map/ppermute | solution.py:91

commit v8 on v7

--- a/solution.py
+++ b/solution.py
@@ -142,84 +142,100 @@
     leaving_ref[...] = packed[clu_count // 2:]
 
 
+def near_piece(data, tx, ty, slot_cap):
+    nodes = tx.shape[1]
+    chunk = 32 if nodes % 32 == 0 else nodes
+    turned = [data[:, c * nodes:(c + 1) * nodes].T for c in range(4)]
+
+    def fold(value):
+        return jnp.sum(value.reshape(-1, 8, nodes), axis=0)
+
+    rows_x, rows_y = [], []
+    for h in range(slot_cap):
+        logs_x = logs_y = pulls_x = pulls_y = jnp.zeros((8, nodes), F32)
+        for start in range(0, nodes, chunk):
+            sx, sy, fx, fy = [
+                jnp.broadcast_to(t[start:start + chunk, h:h + 1], (chunk, nodes)) for t in turned]
+            dx = tx[h:h + 1] - sx
+            dy = ty[h:h + 1] - sy
+            spread = dx * dx + dy * dy + EPS_SQUARED
+            logs = jnp.log(spread)
+            along = (dx * fx + dy * fy) * reciprocal(spread)
+            logs_x, logs_y = logs_x + fold(logs * fx), logs_y + fold(logs * fy)
+            pulls_x, pulls_y = pulls_x + fold(dx * along), pulls_y + fold(dy * along)
+        rows_x.append(jnp.sum(pulls_x - 0.5 * logs_x, axis=0, keepdims=True))
+        rows_y.append(jnp.sum(pulls_y - 0.5 * logs_y, axis=0, keepdims=True))
+    rest = [jnp.zeros((BLOCK - slot_cap, nodes), F32)] if slot_cap < BLOCK else []
+    return jnp.concatenate(rows_x + rest, axis=0), jnp.concatenate(rows_y + rest, axis=0)
+
+
+def target_table(tag, vesicles):
+    tag = tag.reshape(-1, tag.shape[-1])[:, :vesicles]
+    return (tag == (iota(tag.shape, 1) + 1).astype(F32)).astype(F32)
+
+
+def axis_rows(vesicles, axis):
+    return pl.ds(axis, vesicles, stride=2)
+
+
 def near_kernel(slot_cap, piece_count, pos_ref, *refs):
     piece_refs = refs[:piece_count]
-    before_ref, near_ref, arrived, aim_x, aim_y, speed_x, speed_y = refs[piece_count:]
-    vesicles = pos_ref.shape[0] // 2
-    nodes = pos_ref.shape[1]
+    near_ref, arrived, aim_x, aim_y, speed_x, speed_y = refs[piece_count:]
+    vesicles, nodes = pos_ref.shape[0] // 2, pos_ref.shape[1]
     here = 0
     for ref in piece_refs:
         arrived[here:here + ref.shape[0]] = ref[...]
         here += ref.shape[0]
     pieces = arrived.shape[0]
-    slots = pieces * BLOCK
-    tag = arrived[:, :, 4 * nodes:].reshape(slots, nodes)[:, :vesicles]
-    hot = (tag == (iota((slots, vesicles), 1) + 1).astype(F32)).astype(F32)
-    x = pos_ref[pl.ds(0, vesicles, stride=2), :]
-    y = pos_ref[pl.ds(1, vesicles, stride=2), :]
-    aim_x[...] = dot(hot, x, precision=HIGHEST).reshape(pieces, BLOCK, nodes)
-    aim_y[...] = dot(hot, y, precision=HIGHEST).reshape(pieces, BLOCK, nodes)
-    chunk = 32 if nodes % 32 == 0 else nodes
-
-    def fold(value):
-        return jnp.sum(value.reshape(-1, 8, nodes), axis=0)
-
-    def piece(k, _):
-        data = arrived[k]
-        turned = [data[:, c * nodes:(c + 1) * nodes].T for c in range(4)]
-        tx, ty = aim_x[k], aim_y[k]
-        rows_x, rows_y = [], []
-        for h in range(slot_cap):
-            logs_x = logs_y = pulls_x = pulls_y = jnp.zeros((8, nodes), F32)
-            for start in range(0, nodes, chunk):
-                sx, sy, fx, fy = [
-                    jnp.broadcast_to(t[start:start + chunk, h:h + 1], (chunk, nodes))
-                    for t in turned]
-                dx = tx[h:h + 1] - sx
-                dy = ty[h:h + 1] - sy
-                spread = dx * dx + dy * dy + EPS_SQUARED
-                logs = jnp.log(spread)
-                along = (dx * fx + dy * fy) * reciprocal(spread)
-                logs_x, logs_y = logs_x + fold(logs * fx), logs_y + fold(logs * fy)
-                pulls_x, pulls_y = pulls_x + fold(dx * along), pulls_y + fold(dy * along)
-            rows_x.append(jnp.sum(pulls_x - 0.5 * logs_x, axis=0, keepdims=True))
-            rows_y.append(jnp.sum(pulls_y - 0.5 * logs_y, axis=0, keepdims=True))
-        rows_x += [jnp.zeros((1, nodes), F32)] * (BLOCK - slot_cap)
-        rows_y += [jnp.zeros((1, nodes), F32)] * (BLOCK - slot_cap)
-        speed_x[k] = jnp.concatenate(rows_x, axis=0)
-        speed_y[k] = jnp.concatenate(rows_y, axis=0)
+    hot = target_table(arrived[:, :, 4 * nodes:], vesicles)
+    for axis, aim in enumerate((aim_x, aim_y)):
+        aim[...] = dot(hot, pos_ref[axis_rows(vesicles, axis), :], precision=HIGHEST).reshape(
+            pieces, BLOCK, nodes)
+    many = 2 if pieces % 2 == 0 else 1
+
+    def group(i, _):
+        speeds = [near_piece(arrived[i * many + c], aim_x[i * many + c], aim_y[i * many + c],
+                             slot_cap) for c in range(many)]
+        for c, (value_x, value_y) in enumerate(speeds):
+            speed_x[i * many + c] = value_x
+            speed_y[i * many + c] = value_y
         return 0
 
-    lax.fori_loop(0, pieces, piece, 0)
+    lax.fori_loop(0, pieces // many, group, 0)
     turned_hot = hot.T
-    near_x = dot(turned_hot, speed_x[...].reshape(slots, nodes), precision=HIGHEST) / nodes
-    near_y = dot(turned_hot, speed_y[...].reshape(slots, nodes), precision=HIGHEST) / nodes
-    if before_ref is not None:
-        near_x = near_x + before_ref[pl.ds(0, vesicles, stride=2), :]
-        near_y = near_y + before_ref[pl.ds(1, vesicles, stride=2), :]
-    near_ref[pl.ds(0, vesicles, stride=2), :] = near_x
-    near_ref[pl.ds(1, vesicles, stride=2), :] = near_y
-
-
-def near_start(slot_cap, piece_count, pos_ref, *refs):
-    near_kernel(slot_cap, piece_count, pos_ref, *refs[:piece_count], None, *refs[piece_count:])
-
-
-def near_part(flat, pieces, before, slot_cap):
+    for axis, speed in enumerate((speed_x, speed_y)):
+        near_ref[axis_rows(vesicles, axis), :] = dot(
+            turned_hot, speed[...].reshape(-1, nodes), precision=HIGHEST) / nodes
+
+
+def near_part(flat, pieces, slot_cap):
     vesicles, nodes = flat.shape[0] // 2, flat.shape[1]
     count = sum(p.shape[0] for p in pieces)
-    operands = [flat, *pieces] + ([] if before is None else [before])
     return pl.pallas_call(
-        functools.partial(near_start if before is None else near_kernel, slot_cap, len(pieces)),
+        functools.partial(near_kernel, slot_cap, len(pieces)),
         out_shape=jax.ShapeDtypeStruct((2 * vesicles, nodes), F32),
-        in_specs=[whole_spec()] * len(operands),
+        in_specs=[whole_spec()] * (1 + len(pieces)),
         out_specs=whole_spec(),
         scratch_shapes=[pltpu.VMEM((count, BLOCK, 5 * nodes), F32)]
         + [pltpu.VMEM((count, BLOCK, nodes), F32)] * 4,
         compiler_params=params(16),
         cost_estimate=pl.CostEstimate(
             flops=10**9, bytes_accessed=10**7, transcendentals=10**6),
-    )(*operands)
+    )(flat, *pieces)
+
+
+def near_rest(slot_cap, pos_ref, piece_ref, before_ref, near_ref):
+    vesicles, nodes = pos_ref.shape[0] // 2, pos_ref.shape[1]
+    hot = target_table(piece_ref[:, :, 4 * nodes:], vesicles)
+    aims = [dot(hot, pos_ref[axis_rows(vesicles, axis), :], precision=HIGHEST)
+            for axis in range(2)]
+    speeds = [near_piece(piece_ref[k], *[aim[k * BLOCK:(k + 1) * BLOCK] for aim in aims], slot_cap)
+              for k in range(piece_ref.shape[0])]
+    turned_hot = hot.T
+    for axis in range(2):
+        rows = axis_rows(vesicles, axis)
+        speed = jnp.concatenate([pieces[axis] for pieces in speeds], axis=0)
+        near_ref[rows, :] = before_ref[rows, :] + dot(turned_hot, speed, precision=HIGHEST) / nodes
 
 
 def far_kernel(col_count, range_in, pos_in, own_in, nodes_in, *refs):
@@ -263,12 +279,12 @@
         ty = pos_ref[pl.ds(2 * v + 1, 1), :]
         dx = tx - wide[r, 0, start:start + chunk]
         dy = ty - wide[r, 1, start:start + chunk]
-        spread = dx * dx + dy * dy + EPS_SQUARED
+        xx, yy = dx * dx, dy * dy
+        spread = xx + yy + EPS_SQUARED
         log_part = -0.5 * jnp.log(spread)
         inverse = reciprocal(spread)
-        dxr = dx * inverse
-        return ((log_part + dx * dxr).astype(BF16), (dy * dxr).astype(BF16),
-                (log_part + dy * (dy * inverse)).astype(BF16))
+        return ((log_part + xx * inverse).astype(BF16), (dx * dy * inverse).astype(BF16),
+                (log_part + yy * inverse).astype(BF16))
 
     def sketch(v):
         r = range_ref[0, v]
@@ -282,18 +298,21 @@
             total = part if total is None else total + part
         return total
 
-    def pair_gram(v):
+    many = math.gcd(vesicles, 4)
+
+    def group_gram(v):
         both = jnp.concatenate([
-            jnp.concatenate([ref[v], ref[v + 1]], axis=1) for ref in (high_ref, low_ref)], axis=0)
+            jnp.concatenate([ref[v + c] for c in range(many)], axis=1)
+            for ref in (high_ref, low_ref)], axis=0)
         return dot(both, both, NT)
 
-    high_ref[0:2] = jnp.zeros((2, rank, 2 * nodes), BF16)
-    low_ref[0:2] = jnp.zeros((2, rank, 2 * nodes), BF16)
-
-    def pair(i, _):
-        v = 2 * i
-        before = pair_gram(jnp.maximum(v - 2, 0))
-        made = [sketch(v), sketch(v + 1)]
+    high_ref[0:many] = jnp.zeros((many, rank, 2 * nodes), BF16)
+    low_ref[0:many] = jnp.zeros((many, rank, 2 * nodes), BF16)
+
+    def group(i, _):
+        v = many * i
+        before = group_gram(jnp.maximum(v - many, 0))
+        made = [sketch(v + c) for c in range(many)]
         sums[...] += before
         for c, value in enumerate(made):
             high = value.astype(BF16)
@@ -301,8 +320,8 @@
             low_ref[v + c] = (value - high.astype(F32)).astype(BF16)
         return 0
 
-    lax.fori_loop(0, vesicles // 2, pair, 0)
-    sums[...] += pair_gram(vesicles - 2)
+    lax.fori_loop(0, vesicles // many, group, 0)
+    sums[...] += group_gram(vesicles - many)
     total = sums[...]
     gram = total[:rank, :rank] + total[rank:, rank:] + (total[:rank, rank:] + total[rank:, :rank])
     gram_ref[...] = jnp.concatenate([gram[:rank // 2], gram[rank // 2:]], axis=1)
@@ -335,11 +354,13 @@
     return jnp.concatenate(done, axis=0)[:, size:]
 
 
-def basis_kernel(scale_factor, gram_ref, high_ref, low_ref, _, out_ref, weight):
+def basis_kernel(scale_factor, slot_cap, gram_ref, high_ref, low_ref, pos_ref, piece_ref,
+                 before_ref, out_ref, near_ref, weight):
     rank, nodes = high_ref.shape[1], high_ref.shape[2] // 2
 
     @pl.when(pl.program_id(0) == 0)
     def _():
+        near_rest(slot_cap, pos_ref, piece_ref, before_ref, near_ref)
         folded = gram_ref[...]
         gram = jnp.concatenate([folded[:, :rank], folded[:, rank:]], axis=0)
         inverse = lower_inverse(gram) * scale_factor
@@ -394,30 +415,30 @@
     return groups
 
 
-def add_kernel(first, *refs):
-    total = first[...]
-    for ref in refs[:-2]:
+def add_kernel(count, *refs):
+    total = refs[0][...]
+    for ref in refs[1:count]:
         total = total + ref[...]
     refs[-1][...] = total
 
 
-def add_after(terms, other):
+def add_after(terms, others):
     return pl.pallas_call(
-        add_kernel,
+        functools.partial(add_kernel, len(terms)),
         out_shape=jax.ShapeDtypeStruct(terms[0].shape, terms[0].dtype),
-        in_specs=[whole_spec()] * len(terms) + [far_off_spec()],
+        in_specs=[whole_spec()] * len(terms) + [far_off_spec()] * len(others),
         out_specs=whole_spec(),
         compiler_params=params(16),
         cost_estimate=pl.CostEstimate(flops=10**4, bytes_accessed=10**5, transcendentals=0),
-    )(*terms, other)
-
-
-def sum_over(value, axis, groups, other=None):
+    )(*terms, *others)
+
+
+def sum_over(value, axis, groups, others=None):
     count = lax.axis_size(axis)
     for g, steps in enumerate(groups):
         terms = [value] + [lax.ppermute(value, axis, partners(count, k)) for k in steps]
-        if other is not None and g == len(groups) - 1:
-            value = add_after(terms, other)
+        if others is not None and g == len(groups) - 1:
+            value = add_after(terms, others)
         else:
             value = sum(terms[1:], value)
     return value
@@ -471,8 +492,7 @@
     for mine in moved_halves:
         pieces += [mine, lax.ppermute(mine, "clu", [(i, i ^ 1) for i in range(clu_count)])]
 
-    near_first = near_part(flat, arrived[:-1], None, slot_cap)
-    near = near_part(flat, arrived[-1:], near_first, slot_cap)
+    near_first = near_part(flat, arrived[:-1], slot_cap)
 
     high, low, gram = pl.pallas_call(
         functools.partial(far_kernel, col_count),
@@ -493,23 +513,24 @@
         compiler_params=params(32),
         cost_estimate=pl.CostEstimate(flops=10**10, bytes_accessed=10**7, transcendentals=10**7),
     )(near_by(far_range.reshape(1, vesicles)), flat_here, basis_here, nodes_here, *pieces)
-    gram = sum_over(gram, "clu", step_groups(clu_count, True), near_first)
+    gram = sum_over(gram, "clu", step_groups(clu_count, True), [near_first, arrived[-1]])
     gram = sum_over(gram, "col", step_groups(col_count, False))
 
     scale_factor = math.sqrt(2.0 * nodes * vesicles * clu_count * col_count)
     group = 8 if vesicles % 8 == 0 else vesicles
     block = pl.BlockSpec((group, rows, nodes), lambda i: (i, 0, 0))
     held = pl.BlockSpec((group, rank, 2 * nodes), lambda i: (i, 0, 0))
-    new_basis = pl.pallas_call(
-        functools.partial(basis_kernel, scale_factor),
-        out_shape=jax.ShapeDtypeStruct((vesicles, rows, nodes), F32),
+    new_basis, near = pl.pallas_call(
+        functools.partial(basis_kernel, scale_factor, slot_cap),
+        out_shape=[jax.ShapeDtypeStruct((vesicles, rows, nodes), F32),
+                   jax.ShapeDtypeStruct((2 * vesicles, nodes), F32)],
         grid=(vesicles // group,),
-        in_specs=[whole_spec(), held, held, far_off_spec()],
-        out_specs=block,
+        in_specs=[whole_spec(), held, held] + [whole_spec()] * 3,
+        out_specs=[block, whole_spec()],
         scratch_shapes=[pltpu.VMEM((rank, 3 * rank), BF16)],
         compiler_params=params(16),
         cost_estimate=pl.CostEstimate(flops=10**9, bytes_accessed=10**7, transcendentals=0),
-    )(gram, high, low, near_by(near))
+    )(gram, high, low, flat, arrived[-1], near_first)
 
     return (force.reshape(vesicles, 2, nodes), near.reshape(vesicles, 2, nodes),
             new_basis.reshape(vesicles, rank, 2, nodes))

time: 50.3 us -> 48.6 us (0.966)
  Pallas kernels: 24.7 us -> 22.6 us
    ppermute x7, waiting for transfers between devices: 2.61 us -> 4.14 us  [sum_over(): lax.ppermute(value, axis, partners(count, k))]
    pallas_call x1, Pallas kernels: 11.1 us -> 9.68 us  [per_device(): pl.pallas_call(functools.partial(far_kernel, col_count), out_shape=[jax.S...]
    ppermute x3, waiting for transfers between devices: 1.48 us -> 0.3 us  [cube_exchange(): held.append(lax.ppermute(leaving, axis, partners(count, bit)))]
    pallas_call x4 -> x3, Pallas kernels: 10.6 us -> 9.91 us  [the longest x1 7.31 us: per_device(): pl.pallas_call(functools.partial(basis_kernel, scale_factor, slot_cap), o...]
  transfers between devices with their start and end apart: 16 -> 16, of which waited for: 4 -> 5; matrix products, arithmetic and copies ran while one was open for 0% -> 0% of each run, Pallas kernels for 32% -> 30%
where the time goes in v8:
time: 48.6 us; the launch traced here: 48.4 us
  Pallas kernels  22.6 us (47%)
  starting transfers between devices  18 us (37%)
  waiting for transfers between devices  6.98 us (14%)
  between operations  0.76 us (2%)
    pallas_call x1, Pallas kernels, per_device(): pl.pallas_call(functools.partial(far_kernel, col_count), out_shape=[jax.S...  9.68 us
    ppermute x7, starting transfers between devices, sum_over(): lax.ppermute(value, axis, partners(count, k))  7.95 us
    pallas_call x1, Pallas kernels, per_device(): pl.pallas_call(functools.partial(basis_kernel, scale_factor, slot_cap), o...  7.31 us
    ppermute x3, starting transfers between devices, per_device(): lax.ppermute(sent, 'col', partners(col_count, k))  5.76 us
    ppermute x7, waiting for transfers between devices, sum_over(): lax.ppermute(value, axis, partners(count, k))  4.14 us
    ppermute x3, starting transfers between devices, cube_exchange(): held.append(lax.ppermute(leaving, axis, partners(count, bit)))  3.21 us
    pallas_call x1, Pallas kernels, near_part(): pl.pallas_call(functools.partial(near_kernel, slot_cap, len(pieces)), out...  2.6 us
    ppermute x3, waiting for transfers between devices, per_device(): lax.ppermute(sent, 'col', partners(col_count, k))  2.54 us
  transfers between devices with their start and end apart: 16, of which 5 were waited for; matrix products, arithmetic and copies ran while one was open for 0% of the time, Pallas kernels for 30%

profile of v8, /device:TPU:0, one launch (start us, length us, event | category | flops | bytes accessed | tf_op | source)
XLA Modules:
  0.0 48.4 jit_solution(3817410292604342333)
XLA Ops:
  0.6 0.9 %shard_map.131 = bf16[272,128]{1,0:T(8,128)(2,1)S(1)} custom-call(bf16[128,512]{1,0:T(8,128)(2,1)} %own_in.3, bf16[2,512]{1,0:T(2,128)(2,1)} %nodes_in.3), custom_call_target="tpu_custom_call" | custom-call | flops 100000 | bytes 100000 | tf_op jit(solution)/shard_map/pallas_call | solution.py:462
  1.6 5.1 %collective-permute-start.4 = (bf16[272,128]{1,0:T(8,128)(2,1)S(1)}, bf16[272,128]{1,0:T(8,128)(2,1)S(1)}, u32[]{:S(2)}, u32[]{:S(2)}) collective-permute-start(bf16[272,128]{1,0:T(8,128)(2,1)S(1)} %shard_map.131), channel_id=1, source_target_pairs={{0,3},{1,2},{2,1},{3,0},{4,7},{5,6},{6,5},{7,4},{8,11},{9,10},{10,... | collective-permute-start | bytes 208904 | tf_op jit(solution)/shard_map/ppermute | solution.py:489
  6.7 0.0 collective-permute-start.2
  6.7 0.6 %collective-permute-start = (bf16[272,128]{1,0:T(8,128)(2,1)S(1)}, bf16[272,128]{1,0:T(8,128)(2,1)S(1)}, u32[]{:S(2)}, u32[]{:S(2)}) collective-permute-start(bf16[272,128]{1,0:T(8,128)(2,1)S(1)} %shard_map.131), channel_id=1, source_target_pairs={{0,1},{1,0},{2,3},{3,2},{4,5},{5,4},{6,7},{7,6},{8,9},{9,8},{10,11... | collective-permute-start | bytes 208904 | tf_op jit(solution)/shard_map/ppermute | solution.py:489
  7.3 2.1 %shard_map.130 = (f32[64,128]{1,0:T(8,128)}, f32[4,8,640]{2,1,0:T(8,128)S(1)}, f32[4,8,640]{2,1,0:T(8,128)S(1)}) custom-call(f32[64,128]{1,0:T(8,128)} %bitcast.33, f32[32,128]{1,0:T(8,128)} %refs_1_.1, f32[1,32]{1,0:T(1,128)} %bitcast.40, s32[1,32]{1,0:T(1,128)} %refs_3_.1, s32[1,24]{1,0:T(1,128)} %bitcast.41, s32[1,24]{1,0:T(1,128)} %bitcast.42, ...), custom_call_target="tpu_custom_call" | custom-call | flops 100000000 | bytes 1000000 | tf_op jit(solution)/shard_map/pallas_call | solution.py:477
  9.4 0.1 collective-permute-start.10
  9.5 0.0 collective-permute-done.4.refs_4_
  9.5 0.5 %collective-permute-start.5 = (bf16[272,128]{1,0:T(8,128)(2,1)S(1)}, bf16[272,128]{1,0:T(8,128)(2,1)S(1)}, u32[]{:S(2)}, u32[]{:S(2)}) collective-permute-start(bf16[272,128]{1,0:T(8,128)(2,1)S(1)} %collective-permute-done.4.refs_4_), channel_id=1, source_target_pairs={{0,4},{4,0},{8,12},{12,8},{16,20},{20,16},{24,28},{28,24},{1,5},{5... | collective-permute-start | bytes 208904 | tf_op jit(solution)/shard_map/ppermute | solution.py:493
  10.1 2.5 %collective-permute-done.2.refs_2_ = bf16[272,128]{1,0:T(8,128)(2,1)S(1)} collective-permute-done((bf16[272,128]{1,0:T(8,128)(2,1)S(1)}, bf16[272,128]{1,0:T(8,128)(2,1)S(1)}, u32[]{:S(2)}, u32[]{:S(2)}) %collective-permute-start.2) | collective-permute-done | bytes 69664 | tf_op jit(solution)/shard_map/ppermute | solution.py:489
  12.6 0.0 collective-permute-start.3
  12.6 0.0 collective-permute-done.refs_0_
  12.6 0.5 %collective-permute-start.1 = (bf16[272,128]{1,0:T(8,128)(2,1)S(1)}, bf16[272,128]{1,0:T(8,128)(2,1)S(1)}, u32[]{:S(2)}, u32[]{:S(2)}) collective-permute-start(bf16[272,128]{1,0:T(8,128)(2,1)S(1)} %collective-permute-done.refs_0_), channel_id=1, source_target_pairs={{0,4},{4,0},{8,12},{12,8},{16,20},{20,16},{24,28},{28,24},{1,5},{5... | collective-permute-start | bytes 208904 | tf_op jit(solution)/shard_map/ppermute | solution.py:493
  13.1 0.0 collective-permute-done.10
  13.1 1.6 %collective-permute-start.11 = (f32[4,8,640]{2,1,0:T(8,128)S(1)}, f32[4,8,640]{2,1,0:T(8,128)S(1)}, u32[]{:S(2)}, u32[]{:S(2)}) collective-permute-start(f32[4,8,640]{2,1,0:T(8,128)S(1)} %pad_maximum_fusion), channel_id=1, source_target_pairs={{0,8},{4,12},{8,0},{12,4},{16,24},{20,28},{24,16},{28,20},{1,9},{5... | collective-permute-start | bytes 245768 | tf_op jit(solution)/shard_map/ppermute | solution.py:91
  14.7 0.0 collective-permute-done.5.refs_5_
  14.7 0.0 copy-start
  14.7 9.7 %shard_map.132 = (bf16[32,64,256]{2,1,0:T(8,128)(2,1)S(1)}, bf16[32,64,256]{2,1,0:T(8,128)(2,1)S(1)}, f32[32,128]{1,0:T(8,128)S(1)}) custom-call(s32[1,32]{1,0:T(1,128)} %bitcast.43, f32[64,128]{1,0:T(8,128)} %bitcast.34, bf16[128,512]{1,0:T(8,128)(2,1)} %own_in.3, bf16[2,512]{1,0:T(2,128)(2,1)} %nodes_in.3, ...), custom_call_target="tpu_custom_call" | custom-call | flops 10000000000 | bytes 10000000 | tf_op jit(solution)/shard_map/pallas_call | solution.py:497
  24.4 0.1 collective-permute-start.6
  24.5 1.2 %collective-permute-done.6 = f32[32,128]{1,0:T(8,128)S(1)} collective-permute-done((f32[32,128]{1,0:T(8,128)S(1)}, f32[32,128]{1,0:T(8,128)S(1)}, u32[]{:S(2)}, u32[]{:S(2)}) %collective-permute-start.6) | collective-permute-done | bytes 16416 | tf_op jit(solution)/shard_map/ppermute | solution.py:439
  25.7 1.8 %collective-permute-start.9 = (f32[32,128]{1,0:T(8,128)S(1)}, f32[32,128]{1,0:T(8,128)S(1)}, u32[]{:S(2)}, u32[]{:S(2)}) collective-permute-start(f32[32,128]{1,0:T(8,128)S(1)} %add.12.refs_0_), channel_id=1, source_target_pairs={{0,24},{4,28},{8,16},{12,20},{16,8},{20,12},{24,0},{28,4},{1,25},{... | collective-permute-start | bytes 49160 | tf_op jit(solution)/shard_map/ppermute | solution.py:439
  27.4 0.5 %collective-permute-start.8 = (f32[32,128]{1,0:T(8,128)S(1)}, f32[32,128]{1,0:T(8,128)S(1)}, u32[]{:S(2)}, u32[]{:S(2)}) collective-permute-start(f32[32,128]{1,0:T(8,128)S(1)} %add.12.refs_0_), channel_id=1, source_target_pairs={{0,16},{4,20},{8,24},{12,28},{16,0},{20,4},{24,8},{28,12},{1,17},{... | collective-permute-start | bytes 49160 | tf_op jit(solution)/shard_map/ppermute | solution.py:439
  27.9 1.2 %collective-permute-start.7 = (f32[32,128]{1,0:T(8,128)S(1)}, f32[32,128]{1,0:T(8,128)S(1)}, u32[]{:S(2)}, u32[]{:S(2)}) collective-permute-start(f32[32,128]{1,0:T(8,128)S(1)} %add.12.refs_0_), channel_id=1, source_target_pairs={{0,8},{4,12},{8,0},{12,4},{16,24},{20,28},{24,16},{28,20},{1,9},{5... | collective-permute-start | bytes 49160 | tf_op jit(solution)/shard_map/ppermute | solution.py:439
  29.2 0.0 collective-permute-done.11
  29.2 1.6 %collective-permute-start.12 = (f32[4,8,640]{2,1,0:T(8,128)S(1)}, f32[4,8,640]{2,1,0:T(8,128)S(1)}, u32[]{:S(2)}, u32[]{:S(2)}) collective-permute-start(f32[4,8,640]{2,1,0:T(8,128)S(1)} %pad_maximum_fusion.1), channel_id=1, source_target_pairs={{0,16},{4,20},{8,24},{12,28},{16,0},{20,4},{24,8},{28,12},{1,17},{... | collective-permute-start | bytes 245768 | tf_op jit(solution)/shard_map/ppermute | solution.py:91
  30.8 2.6 %shard_map.133.refs_4_.before_ref = f32[64,128]{1,0:T(8,128)S(1)} custom-call(f32[64,128]{1,0:T(8,128)S(1)} %bitcast.35, f32[1,8,640]{2,1,0:T(8,128)S(1)} %get-tuple-element.20.refs_0_, f32[1,8,640]{2,1,0:T(8,128)S(1)} %get-tuple-element.22.refs_1_, f32[2,8,640]{2,1,0:T(8,128)S(1)} %get-tuple-element.24.refs_2_), custom_call_target="tpu_custom_call" | custom-call | flops 1000000000 | bytes 10000000 | tf_op jit(solution)/shard_map/pallas_call | solution.py:214
  33.4 0.0 collective-permute-done.8.refs_2_
  33.4 0.3 collective-permute-done.12.refs_5_.piece_ref
  33.7 2.7 %collective-permute-start.15 = (f32[32,128]{1,0:T(8,128)S(1)}, f32[32,128]{1,0:T(8,128)S(1)}, u32[]{:S(2)}, u32[]{:S(2)}) collective-permute-start(f32[32,128]{1,0:T(8,128)S(1)} %shard_map.134), channel_id=1, source_target_pairs={{0,3},{1,2},{2,1},{3,0},{4,7},{5,6},{6,5},{7,4},{8,11},{9,10},{10,... | collective-permute-start | bytes 49160 | tf_op jit(solution)/shard_map/ppermute | solution.py:439
  36.4 1.7 %collective-permute-start.13 = (f32[32,128]{1,0:T(8,128)S(1)}, f32[32,128]{1,0:T(8,128)S(1)}, u32[]{:S(2)}, u32[]{:S(2)}) collective-permute-start(f32[32,128]{1,0:T(8,128)S(1)} %shard_map.134), channel_id=1, source_target_pairs={{0,1},{1,0},{2,3},{3,2},{4,5},{5,4},{6,7},{7,6},{8,9},{9,8},{10,11... | collective-permute-start | bytes 49160 | tf_op jit(solution)/shard_map/ppermute | solution.py:439
  38.1 1.1 %collective-permute-done.15 = f32[32,128]{1,0:T(8,128)S(1)} collective-permute-done((f32[32,128]{1,0:T(8,128)S(1)}, f32[32,128]{1,0:T(8,128)S(1)}, u32[]{:S(2)}, u32[]{:S(2)}) %collective-permute-start.15) | collective-permute-done | bytes 16416 | tf_op jit(solution)/shard_map/ppermute | solution.py:439
  39.2 1.8 %collective-permute-done.14 = f32[32,128]{1,0:T(8,128)S(1)} collective-permute-done((f32[32,128]{1,0:T(8,128)S(1)}, f32[32,128]{1,0:T(8,128)S(1)}, u32[]{:S(2)}, u32[]{:S(2)}) %collective-permute-start.14) | collective-permute-done | bytes 16416 | tf_op jit(solution)/shard_map/ppermute | solution.py:439
  41.1 7.3 %shard_map.135 = (f32[32,128,128]{2,1,0:T(8,128)}, f32[64,128]{1,0:T(8,128)}) custom-call(f32[32,128]{1,0:T(8,128)S(1)} %add_add_fusion.gram_ref, bf16[32,64,256]{2,1,0:T(8,128)(2,1)S(1)} %get-tuple-element.15.high_ref, bf16[32,64,256]{2,1,0:T(8,128)(2,1)S(1)} %get-tuple-element.16.low_ref, f32[64,128]{1,0:T(8,128)S(1)} %bitcast.36, ...), custom_call_target="tpu_custom_call" | custom-call | flops 1000000000 | bytes 10000000 | tf_op jit(solution)/shard_map/pallas_call | solution.py:523
  (17 shorter events, 0.1 us)
Async XLA Ops:
  1.6 7.9 %collective-permute-start.4 = (bf16[272,128]{1,0:T(8,128)(2,1)S(1)}, bf16[272,128]{1,0:T(8,128)(2,1)S(1)}, u32[]{:S(2)}, u32[]{:S(2)}) collective-permute-start(bf16[272,128]{1,0:T(8,128)(2,1)S(1)} %shard_map.131), channel_id=1, source_target_pairs={{0,3},{1,2},{2,1},{3,0},{4,7},{5,6},{6,5},{7,4},{8,11},{9,10},{10,... | collective-permute-start | bytes 208904 | tf_op jit(solution)/shard_map/ppermute | solution.py:489
  6.7 5.9 %collective-permute-start.2 = (bf16[272,128]{1,0:T(8,128)(2,1)S(1)}, bf16[272,128]{1,0:T(8,128)(2,1)S(1)}, u32[]{:S(2)}, u32[]{:S(2)}) collective-permute-start(bf16[272,128]{1,0:T(8,128)(2,1)S(1)} %shard_map.131), channel_id=1, source_target_pairs={{0,2},{1,3},{2,0},{3,1},{4,6},{5,7},{6,4},{7,5},{8,10},{9,11},{10,... | collective-permute-start | bytes 208904 | tf_op jit(solution)/shard_map/ppermute | solution.py:489
  6.7 5.9 %collective-permute-start = (bf16[272,128]{1,0:T(8,128)(2,1)S(1)}, bf16[272,128]{1,0:T(8,128)(2,1)S(1)}, u32[]{:S(2)}, u32[]{:S(2)}) collective-permute-start(bf16[272,128]{1,0:T(8,128)(2,1)S(1)} %shard_map.131), channel_id=1, source_target_pairs={{0,1},{1,0},{2,3},{3,2},{4,5},{5,4},{6,7},{7,6},{8,9},{9,8},{10,11... | collective-permute-start | bytes 208904 | tf_op jit(solution)/shard_map/ppermute | solution.py:489
  9.4 3.7 %collective-permute-start.10 = (f32[4,8,640]{2,1,0:T(8,128)S(1)}, f32[4,8,640]{2,1,0:T(8,128)S(1)}, u32[]{:S(2)}, u32[]{:S(2)}) collective-permute-start(f32[4,8,640]{2,1,0:T(8,128)S(1)} %get-tuple-element.14), channel_id=1, source_target_pairs={{0,4},{4,0},{8,12},{12,8},{16,20},{20,16},{24,28},{28,24},{1,5},{5... | collective-permute-start | bytes 245768 | tf_op jit(solution)/shard_map/ppermute | solution.py:91
  9.5 5.2 %collective-permute-start.5 = (bf16[272,128]{1,0:T(8,128)(2,1)S(1)}, bf16[272,128]{1,0:T(8,128)(2,1)S(1)}, u32[]{:S(2)}, u32[]{:S(2)}) collective-permute-start(bf16[272,128]{1,0:T(8,128)(2,1)S(1)} %collective-permute-done.4.refs_4_), channel_id=1, source_target_pairs={{0,4},{4,0},{8,12},{12,8},{16,20},{20,16},{24,28},{28,24},{1,5},{5... | collective-permute-start | bytes 208904 | tf_op jit(solution)/shard_map/ppermute | solution.py:493
  12.6 2.1 %collective-permute-start.3 = (bf16[272,128]{1,0:T(8,128)(2,1)S(1)}, bf16[272,128]{1,0:T(8,128)(2,1)S(1)}, u32[]{:S(2)}, u32[]{:S(2)}) collective-permute-start(bf16[272,128]{1,0:T(8,128)(2,1)S(1)} %collective-permute-done.2.refs_2_), channel_id=1, source_target_pairs={{0,4},{4,0},{8,12},{12,8},{16,20},{20,16},{24,28},{28,24},{1,5},{5... | collective-permute-start | bytes 208904 | tf_op jit(solution)/shard_map/ppermute | solution.py:493
  12.6 2.1 %collective-permute-start.1 = (bf16[272,128]{1,0:T(8,128)(2,1)S(1)}, bf16[272,128]{1,0:T(8,128)(2,1)S(1)}, u32[]{:S(2)}, u32[]{:S(2)}) collective-permute-start(bf16[272,128]{1,0:T(8,128)(2,1)S(1)} %collective-permute-done.refs_0_), channel_id=1, source_target_pairs={{0,4},{4,0},{8,12},{12,8},{16,20},{20,16},{24,28},{28,24},{1,5},{5... | collective-permute-start | bytes 208904 | tf_op jit(solution)/shard_map/ppermute | solution.py:493
  13.1 16.0 %collective-permute-start.11 = (f32[4,8,640]{2,1,0:T(8,128)S(1)}, f32[4,8,640]{2,1,0:T(8,128)S(1)}, u32[]{:S(2)}, u32[]{:S(2)}) collective-permute-start(f32[4,8,640]{2,1,0:T(8,128)S(1)} %pad_maximum_fusion), channel_id=1, source_target_pairs={{0,8},{4,12},{8,0},{12,4},{16,24},{20,28},{24,16},{28,20},{1,9},{5... | collective-permute-start | bytes 245768 | tf_op jit(solution)/shard_map/ppermute | solution.py:91
  14.7 16.1 %copy-start = (f32[32,2,128]{2,1,0:T(2,128)S(1)}, f32[32,2,128]{2,1,0:T(2,128)}, u32[]{:S(2)}) copy-start(f32[32,2,128]{2,1,0:T(2,128)} %param.11) | copy-start | bytes 98308
  24.4 1.2 %collective-permute-start.6 = (f32[32,128]{1,0:T(8,128)S(1)}, f32[32,128]{1,0:T(8,128)S(1)}, u32[]{:S(2)}, u32[]{:S(2)}) collective-permute-start(f32[32,128]{1,0:T(8,128)S(1)} %get-tuple-element.12), channel_id=1, source_target_pairs={{0,4},{4,0},{8,12},{12,8},{16,20},{20,16},{24,28},{28,24},{1,5},{5... | collective-permute-start | bytes 49160 | tf_op jit(solution)/shard_map/ppermute | solution.py:439
  25.7 7.7 %collective-permute-start.9 = (f32[32,128]{1,0:T(8,128)S(1)}, f32[32,128]{1,0:T(8,128)S(1)}, u32[]{:S(2)}, u32[]{:S(2)}) collective-permute-start(f32[32,128]{1,0:T(8,128)S(1)} %add.12.refs_0_), channel_id=1, source_target_pairs={{0,24},{4,28},{8,16},{12,20},{16,8},{20,12},{24,0},{28,4},{1,25},{... | collective-permute-start | bytes 49160 | tf_op jit(solution)/shard_map/ppermute | solution.py:439
  27.4 5.9 %collective-permute-start.8 = (f32[32,128]{1,0:T(8,128)S(1)}, f32[32,128]{1,0:T(8,128)S(1)}, u32[]{:S(2)}, u32[]{:S(2)}) collective-permute-start(f32[32,128]{1,0:T(8,128)S(1)} %add.12.refs_0_), channel_id=1, source_target_pairs={{0,16},{4,20},{8,24},{12,28},{16,0},{20,4},{24,8},{28,12},{1,17},{... | collective-permute-start | bytes 49160 | tf_op jit(solution)/shard_map/ppermute | solution.py:439
  27.9 5.4 %collective-permute-start.7 = (f32[32,128]{1,0:T(8,128)S(1)}, f32[32,128]{1,0:T(8,128)S(1)}, u32[]{:S(2)}, u32[]{:S(2)}) collective-permute-start(f32[32,128]{1,0:T(8,128)S(1)} %add.12.refs_0_), channel_id=1, source_target_pairs={{0,8},{4,12},{8,0},{12,4},{16,24},{20,28},{24,16},{28,20},{1,9},{5... | collective-permute-start | bytes 49160 | tf_op jit(solution)/shard_map/ppermute | solution.py:439
  29.2 4.5 %collective-permute-start.12 = (f32[4,8,640]{2,1,0:T(8,128)S(1)}, f32[4,8,640]{2,1,0:T(8,128)S(1)}, u32[]{:S(2)}, u32[]{:S(2)}) collective-permute-start(f32[4,8,640]{2,1,0:T(8,128)S(1)} %pad_maximum_fusion.1), channel_id=1, source_target_pairs={{0,16},{4,20},{8,24},{12,28},{16,0},{20,4},{24,8},{28,12},{1,17},{... | collective-permute-start | bytes 245768 | tf_op jit(solution)/shard_map/ppermute | solution.py:91
  33.7 5.5 %collective-permute-start.15 = (f32[32,128]{1,0:T(8,128)S(1)}, f32[32,128]{1,0:T(8,128)S(1)}, u32[]{:S(2)}, u32[]{:S(2)}) collective-permute-start(f32[32,128]{1,0:T(8,128)S(1)} %shard_map.134), channel_id=1, source_target_pairs={{0,3},{1,2},{2,1},{3,0},{4,7},{5,6},{6,5},{7,4},{8,11},{9,10},{10,... | collective-permute-start | bytes 49160 | tf_op jit(solution)/shard_map/ppermute | solution.py:439
  36.4 4.6 %collective-permute-start.14 = (f32[32,128]{1,0:T(8,128)S(1)}, f32[32,128]{1,0:T(8,128)S(1)}, u32[]{:S(2)}, u32[]{:S(2)}) collective-permute-start(f32[32,128]{1,0:T(8,128)S(1)} %shard_map.134), channel_id=1, source_target_pairs={{0,2},{1,3},{2,0},{3,1},{4,6},{5,7},{6,4},{7,5},{8,10},{9,11},{10,... | collective-permute-start | bytes 49160 | tf_op jit(solution)/shard_map/ppermute | solution.py:439
  36.4 4.6 %collective-permute-start.13 = (f32[32,128]{1,0:T(8,128)S(1)}, f32[32,128]{1,0:T(8,128)S(1)}, u32[]{:S(2)}, u32[]{:S(2)}) collective-permute-start(f32[32,128]{1,0:T(8,128)S(1)} %shard_map.134), channel_id=1, source_target_pairs={{0,1},{1,0},{2,3},{3,2},{4,5},{5,4},{6,7},{7,6},{8,9},{9,8},{10,11... | collective-permute-start | bytes 49160 | tf_op jit(solution)/shard_map/ppermute | solution.py:439

commit v9 on v8

--- a/solution.py
+++ b/solution.py
@@ -47,11 +47,13 @@
     return pl.reciprocal(x, approx=True)
 
 
-def fetch(sources, targets, sems):
+def fetch(sources, targets, sems, meanwhile=None):
     copies = [pltpu.make_async_copy(s, t, sems.at[i])
               for i, (s, t) in enumerate(zip(sources, targets))]
     for copy in copies:
         copy.start()
+    if meanwhile is not None:
+        meanwhile()
     for copy in copies:
         copy.wait()
 
@@ -142,31 +144,39 @@
     leaving_ref[...] = packed[clu_count // 2:]
 
 
+def near_slot(turned, tx, ty):
+    nodes = tx.shape[1]
+    chunk = 32 if nodes % 32 == 0 else nodes
+
+    def fold(value):
+        return jnp.sum(value.reshape(-1, 8, nodes), axis=0)
+
+    logs_x = logs_y = pulls_x = pulls_y = jnp.zeros((8, nodes), F32)
+    for start in range(0, nodes, chunk):
+        sx, sy, fx, fy = [
+            jnp.broadcast_to(t[start:start + chunk], (chunk, nodes)) for t in turned]
+        dx = tx - sx
+        dy = ty - sy
+        spread = dx * dx + dy * dy + EPS_SQUARED
+        logs = jnp.log(spread)
+        along = (dx * fx + dy * fy) * reciprocal(spread)
+        logs_x, logs_y = logs_x + fold(logs * fx), logs_y + fold(logs * fy)
+        pulls_x, pulls_y = pulls_x + fold(dx * along), pulls_y + fold(dy * along)
+    return (jnp.sum(pulls_x - 0.5 * logs_x, axis=0, keepdims=True),
+            jnp.sum(pulls_y - 0.5 * logs_y, axis=0, keepdims=True))
+
+
 def near_piece(data, tx, ty, slot_cap):
     nodes = tx.shape[1]
-    chunk = 32 if nodes % 32 == 0 else nodes
     turned = [data[:, c * nodes:(c + 1) * nodes].T for c in range(4)]
-
-    def fold(value):
-        return jnp.sum(value.reshape(-1, 8, nodes), axis=0)
-
-    rows_x, rows_y = [], []
-    for h in range(slot_cap):
-        logs_x = logs_y = pulls_x = pulls_y = jnp.zeros((8, nodes), F32)
-        for start in range(0, nodes, chunk):
-            sx, sy, fx, fy = [
-                jnp.broadcast_to(t[start:start + chunk, h:h + 1], (chunk, nodes)) for t in turned]
-            dx = tx[h:h + 1] - sx
-            dy = ty[h:h + 1] - sy
-            spread = dx * dx + dy * dy + EPS_SQUARED
-            logs = jnp.log(spread)
-            along = (dx * fx + dy * fy) * reciprocal(spread)
-            logs_x, logs_y = logs_x + fold(logs * fx), logs_y + fold(logs * fy)
-            pulls_x, pulls_y = pulls_x + fold(dx * along), pulls_y + fold(dy * along)
-        rows_x.append(jnp.sum(pulls_x - 0.5 * logs_x, axis=0, keepdims=True))
-        rows_y.append(jnp.sum(pulls_y - 0.5 * logs_y, axis=0, keepdims=True))
-    rest = [jnp.zeros((BLOCK - slot_cap, nodes), F32)] if slot_cap < BLOCK else []
-    return jnp.concatenate(rows_x + rest, axis=0), jnp.concatenate(rows_y + rest, axis=0)
+    return [functools.partial(near_slot, [t[:, h:h + 1] for t in turned], tx[h:h + 1], ty[h:h + 1])
+            for h in range(slot_cap)]
+
+
+def gather_rows(slots, axis):
+    nodes = slots[0][axis].shape[1]
+    rest = [jnp.zeros((BLOCK - len(slots), nodes), F32)] if len(slots) < BLOCK else []
+    return jnp.concatenate([slot[axis] for slot in slots] + rest, axis=0)
 
 
 def target_table(tag, vesicles):
@@ -191,14 +201,15 @@
     for axis, aim in enumerate((aim_x, aim_y)):
         aim[...] = dot(hot, pos_ref[axis_rows(vesicles, axis), :], precision=HIGHEST).reshape(
             pieces, BLOCK, nodes)
-    many = 2 if pieces % 2 == 0 else 1
+    many = math.gcd(pieces, 4)
 
     def group(i, _):
-        speeds = [near_piece(arrived[i * many + c], aim_x[i * many + c], aim_y[i * many + c],
-                             slot_cap) for c in range(many)]
-        for c, (value_x, value_y) in enumerate(speeds):
-            speed_x[i * many + c] = value_x
-            speed_y[i * many + c] = value_y
+        calls = [near_piece(arrived[i * many + c], aim_x[i * many + c], aim_y[i * many + c],
+                            slot_cap) for c in range(many)]
+        slots = [[call() for call in piece] for piece in calls]
+        for c, piece in enumerate(slots):
+            speed_x[i * many + c] = gather_rows(piece, 0)
+            speed_y[i * many + c] = gather_rows(piece, 1)
         return 0
 
     lax.fori_loop(0, pieces // many, group, 0)
@@ -224,18 +235,24 @@
     )(flat, *pieces)
 
 
-def near_rest(slot_cap, pos_ref, piece_ref, before_ref, near_ref):
+def near_rest(slot_cap, pos_ref, piece_ref, before_ref):
     vesicles, nodes = pos_ref.shape[0] // 2, pos_ref.shape[1]
     hot = target_table(piece_ref[:, :, 4 * nodes:], vesicles)
     aims = [dot(hot, pos_ref[axis_rows(vesicles, axis), :], precision=HIGHEST)
             for axis in range(2)]
-    speeds = [near_piece(piece_ref[k], *[aim[k * BLOCK:(k + 1) * BLOCK] for aim in aims], slot_cap)
-              for k in range(piece_ref.shape[0])]
+    before = [before_ref[axis_rows(vesicles, axis), :] for axis in range(2)]
+    calls = [call for k in range(piece_ref.shape[0]) for call in near_piece(
+        piece_ref[k], *[aim[k * BLOCK:(k + 1) * BLOCK] for aim in aims], slot_cap)]
     turned_hot = hot.T
-    for axis in range(2):
-        rows = axis_rows(vesicles, axis)
-        speed = jnp.concatenate([pieces[axis] for pieces in speeds], axis=0)
-        near_ref[rows, :] = before_ref[rows, :] + dot(turned_hot, speed, precision=HIGHEST) / nodes
+
+    def finish(slots):
+        pieces = [slots[k:k + slot_cap] for k in range(0, len(slots), slot_cap)]
+        speeds = [jnp.concatenate([gather_rows(piece, axis) for piece in pieces], axis=0)
+                  for axis in range(2)]
+        return [b + dot(turned_hot, speed, precision=HIGHEST) / nodes
+                for b, speed in zip(before, speeds)]
+
+    return calls, finish
 
 
 def far_kernel(col_count, range_in, pos_in, own_in, nodes_in, *refs):
@@ -248,26 +265,33 @@
     rank, sources = own_rows.shape[0] // 2, own_rows.shape[1]
     rows = 2 * rank
     core, col = lax.rem(lax.axis_index("clu"), 2), lax.axis_index("col")
-    fetch([range_in, pos_in, nodes_in, own_in], [range_ref, pos_ref, own_nodes, own_rows], sems)
+    columns = sources // nodes
+
+    def widen(r):
+        turned = spots[r].T
+        for c in range(2):
+            wide[r, c] = jnp.broadcast_to(turned[:, c:c + 1], (sources, nodes))
+
+    def lay_out_received():
+        for k in range(1, col_count):
+            where = origin(col, k, col_count)
+            mine, other = piece_refs[2 * k - 2], piece_refs[2 * k - 1]
+            ends = mine[columns * rank:].astype(F32)
+            for c in range(columns):
+                lanes = slice(c * nodes, (c + 1) * nodes)
+                from_rows = slice(c * rank, (c + 1) * rank)
+                for ref, part in ((mine, core), (other, 1 - core)):
+                    there = pl.multiple_of(part * sources + c * nodes, nodes)
+                    basis[where, :, pl.ds(there, nodes)] = ref[from_rows]
+                spots[where, 0:2, lanes] = ends[2 * c:2 * c + 2]
+            widen(where)
+
+    fetch([range_in, pos_in, nodes_in, own_in], [range_ref, pos_ref, own_nodes, own_rows], sems,
+          lay_out_received)
     basis[col, :, :sources] = own_rows[:rank]
     basis[col, :, sources:] = own_rows[rank:]
     spots[col, 0:2] = own_nodes[...].astype(F32)
-    for k in range(1, col_count):
-        where = origin(col, k, col_count)
-        mine, other = piece_refs[2 * k - 2], piece_refs[2 * k - 1]
-        columns = sources // nodes
-        ends = mine[columns * rank:].astype(F32)
-        for c in range(columns):
-            lanes = slice(c * nodes, (c + 1) * nodes)
-            from_rows = slice(c * rank, (c + 1) * rank)
-            for ref, part in ((mine, core), (other, 1 - core)):
-                there = pl.multiple_of(part * sources + c * nodes, nodes)
-                basis[where, :, pl.ds(there, nodes)] = ref[from_rows]
-            spots[where, 0:2, lanes] = ends[2 * c:2 * c + 2]
-    for r in range(col_count):
-        turned = spots[r].T
-        for c in range(2):
-            wide[r, c] = jnp.broadcast_to(turned[:, c:c + 1], (sources, nodes))
+    widen(col)
     sums[...] = jnp.zeros_like(sums)
 
     chunk = 32 if sources % 32 == 0 else sources
@@ -298,7 +322,7 @@
             total = part if total is None else total + part
         return total
 
-    many = math.gcd(vesicles, 4)
+    many = math.gcd(vesicles, 8)
 
     def group_gram(v):
         both = jnp.concatenate([
@@ -327,7 +351,7 @@
     gram_ref[...] = jnp.concatenate([gram[:rank // 2], gram[rank // 2:]], axis=1)
 
 
-def lower_inverse(gram):
+def lower_inverse(gram, beside):
     size = gram.shape[0]
     eye = (iota((size, size), 0) == iota((size, size), 1)).astype(F32)
     rest = jnp.concatenate([gram, eye], axis=1)
@@ -335,6 +359,7 @@
     step = 8
     for start in range(0, size, step):
         height = size - start
+        beside(start // step, size // step)
         columns = [jnp.broadcast_to(rest[:, start + j:start + j + 1], (height, 2 * size))
                    for j in range(step)]
         row_number = iota((height, 2 * size), 0)
@@ -360,19 +385,30 @@
 
     @pl.when(pl.program_id(0) == 0)
     def _():
-        near_rest(slot_cap, pos_ref, piece_ref, before_ref, near_ref)
         folded = gram_ref[...]
+        calls, finish = near_rest(slot_cap, pos_ref, piece_ref, before_ref)
+        slots = []
+
+        def beside(i, n):
+            slots.extend(call() for call in calls[len(calls) * i // n:len(calls) * (i + 1) // n])
+
         gram = jnp.concatenate([folded[:, :rank], folded[:, rank:]], axis=0)
-        inverse = lower_inverse(gram) * scale_factor
+        inverse = lower_inverse(gram, beside) * scale_factor
+        near = finish(slots)
         high = inverse.astype(BF16)
         low = (inverse - high.astype(F32)).astype(BF16)
         weight[...] = jnp.concatenate([high, high, low], axis=1)
+        for axis in range(2):
+            near_ref[axis_rows(near[axis].shape[0], axis), :] = near[axis]
 
     w = weight[...]
-    for v in range(high_ref.shape[0]):
-        fresh = dot(w, jnp.concatenate([high_ref[v], low_ref[v], high_ref[v]], axis=0))
-        for d in range(2):
-            out_ref[v, pl.ds(d, rank, stride=2), :] = fresh[:, d * nodes:(d + 1) * nodes]
+    many = math.gcd(high_ref.shape[0], 2)
+    for v in range(0, high_ref.shape[0], many):
+        fresh = [dot(w, jnp.concatenate([high_ref[u], low_ref[u], high_ref[u]], axis=0))
+                 for u in range(v, v + many)]
+        for u, value in enumerate(fresh):
+            for d in range(2):
+                out_ref[v + u, pl.ds(d, rank, stride=2), :] = value[:, d * nodes:(d + 1) * nodes]
 
 
 def whole_spec():

time: 48.6 us -> 46.2 us (0.951)
  Pallas kernels: 22.6 us -> 19.9 us
    pallas_call x1, Pallas kernels: 7.31 us -> 6.05 us  [per_device(): pl.pallas_call(functools.partial(basis_kernel, scale_factor, slot_cap), o...]
    pallas_call x1, Pallas kernels: 9.68 us -> 8.6 us  [per_device(): pl.pallas_call(functools.partial(far_kernel, col_count), out_shape=[jax.S...]
  transfers between devices with their start and end apart: 16 -> 16, of which waited for: 5 -> 5; matrix products, arithmetic and copies ran while one was open for 0% -> 0% of each run, Pallas kernels for 30% -> 28%
where the time goes in v9:
time: 46.2 us; the launch traced here: 46 us
  Pallas kernels  19.9 us (43%)
  starting transfers between devices  18 us (39%)
  waiting for transfers between devices  7.33 us (16%)
  between operations  0.76 us (2%)
    pallas_call x1, Pallas kernels, per_device(): pl.pallas_call(functools.partial(far_kernel, col_count), out_shape=[jax.S...  8.6 us
    ppermute x7, starting transfers between devices, sum_over(): lax.ppermute(value, axis, partners(count, k))  7.95 us
    pallas_call x1, Pallas kernels, per_device(): pl.pallas_call(functools.partial(basis_kernel, scale_factor, slot_cap), o...  6.05 us
    ppermute x3, starting transfers between devices, per_device(): lax.ppermute(sent, 'col', partners(col_count, k))  5.76 us
    ppermute x7, waiting for transfers between devices, sum_over(): lax.ppermute(value, axis, partners(count, k))  4.15 us
    ppermute x3, starting transfers between devices, cube_exchange(): held.append(lax.ppermute(leaving, axis, partners(count, bit)))  3.2 us
    ppermute x3, waiting for transfers between devices, per_device(): lax.ppermute(sent, 'col', partners(col_count, k))  2.54 us
    pallas_call x1, Pallas kernels, near_part(): pl.pallas_call(functools.partial(near_kernel, slot_cap, len(pieces)), out...  2.27 us
  transfers between devices with their start and end apart: 16, of which 5 were waited for; matrix products, arithmetic and copies ran while one was open for 0% of the time, Pallas kernels for 28%

profile of v9, /device:TPU:0, one launch (start us, length us, event | category | flops | bytes accessed | tf_op | source)
XLA Modules:
  0.0 46.0 jit_solution(18255783843899613628)
XLA Ops:
  0.6 0.9 %shard_map.131 = bf16[272,128]{1,0:T(8,128)(2,1)S(1)} custom-call(bf16[128,512]{1,0:T(8,128)(2,1)} %own_in.3, bf16[2,512]{1,0:T(2,128)(2,1)} %nodes_in.3), custom_call_target="tpu_custom_call" | custom-call | flops 100000 | bytes 100000 | tf_op jit(solution)/shard_map/pallas_call | solution.py:498
  1.6 5.1 %collective-permute-start.4 = (bf16[272,128]{1,0:T(8,128)(2,1)S(1)}, bf16[272,128]{1,0:T(8,128)(2,1)S(1)}, u32[]{:S(2)}, u32[]{:S(2)}) collective-permute-start(bf16[272,128]{1,0:T(8,128)(2,1)S(1)} %shard_map.131), channel_id=1, source_target_pairs={{0,3},{1,2},{2,1},{3,0},{4,7},{5,6},{6,5},{7,4},{8,11},{9,10},{10,... | collective-permute-start | bytes 208904 | tf_op jit(solution)/shard_map/ppermute | solution.py:525
  6.7 0.0 collective-permute-start.2
  6.7 0.6 %collective-permute-start = (bf16[272,128]{1,0:T(8,128)(2,1)S(1)}, bf16[272,128]{1,0:T(8,128)(2,1)S(1)}, u32[]{:S(2)}, u32[]{:S(2)}) collective-permute-start(bf16[272,128]{1,0:T(8,128)(2,1)S(1)} %shard_map.131), channel_id=1, source_target_pairs={{0,1},{1,0},{2,3},{3,2},{4,5},{5,4},{6,7},{7,6},{8,9},{9,8},{10,11... | collective-permute-start | bytes 208904 | tf_op jit(solution)/shard_map/ppermute | solution.py:525
  7.3 2.1 %shard_map.130 = (f32[64,128]{1,0:T(8,128)}, f32[4,8,640]{2,1,0:T(8,128)S(1)}, f32[4,8,640]{2,1,0:T(8,128)S(1)}) custom-call(f32[64,128]{1,0:T(8,128)} %bitcast.33, f32[32,128]{1,0:T(8,128)} %refs_1_.1, f32[1,32]{1,0:T(1,128)} %bitcast.40, s32[1,32]{1,0:T(1,128)} %refs_3_.1, s32[1,24]{1,0:T(1,128)} %bitcast.41, s32[1,24]{1,0:T(1,128)} %bitcast.42, ...), custom_call_target="tpu_custom_call" | custom-call | flops 100000000 | bytes 1000000 | tf_op jit(solution)/shard_map/pallas_call | solution.py:513
  9.4 0.1 collective-permute-start.10
  9.5 0.0 collective-permute-done.4.refs_4_
  9.5 0.5 %collective-permute-start.5 = (bf16[272,128]{1,0:T(8,128)(2,1)S(1)}, bf16[272,128]{1,0:T(8,128)(2,1)S(1)}, u32[]{:S(2)}, u32[]{:S(2)}) collective-permute-start(bf16[272,128]{1,0:T(8,128)(2,1)S(1)} %collective-permute-done.4.refs_4_), channel_id=1, source_target_pairs={{0,4},{4,0},{8,12},{12,8},{16,20},{20,16},{24,28},{28,24},{1,5},{5... | collective-permute-start | bytes 208904 | tf_op jit(solution)/shard_map/ppermute | solution.py:529
  10.1 2.5 %collective-permute-done.2.refs_2_ = bf16[272,128]{1,0:T(8,128)(2,1)S(1)} collective-permute-done((bf16[272,128]{1,0:T(8,128)(2,1)S(1)}, bf16[272,128]{1,0:T(8,128)(2,1)S(1)}, u32[]{:S(2)}, u32[]{:S(2)}) %collective-permute-start.2) | collective-permute-done | bytes 69664 | tf_op jit(solution)/shard_map/ppermute | solution.py:525
  12.6 0.0 collective-permute-start.3
  12.6 0.0 collective-permute-done.refs_0_
  12.6 0.5 %collective-permute-start.1 = (bf16[272,128]{1,0:T(8,128)(2,1)S(1)}, bf16[272,128]{1,0:T(8,128)(2,1)S(1)}, u32[]{:S(2)}, u32[]{:S(2)}) collective-permute-start(bf16[272,128]{1,0:T(8,128)(2,1)S(1)} %collective-permute-done.refs_0_), channel_id=1, source_target_pairs={{0,4},{4,0},{8,12},{12,8},{16,20},{20,16},{24,28},{28,24},{1,5},{5... | collective-permute-start | bytes 208904 | tf_op jit(solution)/shard_map/ppermute | solution.py:529
  13.1 0.0 collective-permute-done.10
  13.1 1.6 %collective-permute-start.11 = (f32[4,8,640]{2,1,0:T(8,128)S(1)}, f32[4,8,640]{2,1,0:T(8,128)S(1)}, u32[]{:S(2)}, u32[]{:S(2)}) collective-permute-start(f32[4,8,640]{2,1,0:T(8,128)S(1)} %pad_maximum_fusion), channel_id=1, source_target_pairs={{0,8},{4,12},{8,0},{12,4},{16,24},{20,28},{24,16},{28,20},{1,9},{5... | collective-permute-start | bytes 245768 | tf_op jit(solution)/shard_map/ppermute | solution.py:93
  14.7 0.0 copy-start
  14.7 8.6 %shard_map.132 = (bf16[32,64,256]{2,1,0:T(8,128)(2,1)S(1)}, bf16[32,64,256]{2,1,0:T(8,128)(2,1)S(1)}, f32[32,128]{1,0:T(8,128)S(1)}) custom-call(s32[1,32]{1,0:T(1,128)} %bitcast.43, f32[64,128]{1,0:T(8,128)} %bitcast.34, bf16[128,512]{1,0:T(8,128)(2,1)} %own_in.3, bf16[2,512]{1,0:T(2,128)(2,1)} %nodes_in.3, ...), custom_call_target="tpu_custom_call" | custom-call | flops 10000000000 | bytes 10000000 | tf_op jit(solution)/shard_map/pallas_call | solution.py:533
  23.3 0.1 collective-permute-start.6
  23.4 1.2 %collective-permute-done.6 = f32[32,128]{1,0:T(8,128)S(1)} collective-permute-done((f32[32,128]{1,0:T(8,128)S(1)}, f32[32,128]{1,0:T(8,128)S(1)}, u32[]{:S(2)}, u32[]{:S(2)}) %collective-permute-start.6) | collective-permute-done | bytes 16416 | tf_op jit(solution)/shard_map/ppermute | solution.py:475
  24.6 1.8 %collective-permute-start.9 = (f32[32,128]{1,0:T(8,128)S(1)}, f32[32,128]{1,0:T(8,128)S(1)}, u32[]{:S(2)}, u32[]{:S(2)}) collective-permute-start(f32[32,128]{1,0:T(8,128)S(1)} %add.12.refs_0_), channel_id=1, source_target_pairs={{0,24},{4,28},{8,16},{12,20},{16,8},{20,12},{24,0},{28,4},{1,25},{... | collective-permute-start | bytes 49160 | tf_op jit(solution)/shard_map/ppermute | solution.py:475
  26.4 0.5 %collective-permute-start.8 = (f32[32,128]{1,0:T(8,128)S(1)}, f32[32,128]{1,0:T(8,128)S(1)}, u32[]{:S(2)}, u32[]{:S(2)}) collective-permute-start(f32[32,128]{1,0:T(8,128)S(1)} %add.12.refs_0_), channel_id=1, source_target_pairs={{0,16},{4,20},{8,24},{12,28},{16,0},{20,4},{24,8},{28,12},{1,17},{... | collective-permute-start | bytes 49160 | tf_op jit(solution)/shard_map/ppermute | solution.py:475
  26.9 1.2 %collective-permute-start.7 = (f32[32,128]{1,0:T(8,128)S(1)}, f32[32,128]{1,0:T(8,128)S(1)}, u32[]{:S(2)}, u32[]{:S(2)}) collective-permute-start(f32[32,128]{1,0:T(8,128)S(1)} %add.12.refs_0_), channel_id=1, source_target_pairs={{0,8},{4,12},{8,0},{12,4},{16,24},{20,28},{24,16},{28,20},{1,9},{5... | collective-permute-start | bytes 49160 | tf_op jit(solution)/shard_map/ppermute | solution.py:475
  28.1 1.6 %collective-permute-start.12 = (f32[4,8,640]{2,1,0:T(8,128)S(1)}, f32[4,8,640]{2,1,0:T(8,128)S(1)}, u32[]{:S(2)}, u32[]{:S(2)}) collective-permute-start(f32[4,8,640]{2,1,0:T(8,128)S(1)} %pad_maximum_fusion.1), channel_id=1, source_target_pairs={{0,16},{4,20},{8,24},{12,28},{16,0},{20,4},{24,8},{28,12},{1,17},{... | collective-permute-start | bytes 245768 | tf_op jit(solution)/shard_map/ppermute | solution.py:93
  29.7 2.3 %shard_map.133.refs_4_.before_ref = f32[64,128]{1,0:T(8,128)S(1)} custom-call(f32[64,128]{1,0:T(8,128)S(1)} %bitcast.35, f32[1,8,640]{2,1,0:T(8,128)S(1)} %get-tuple-element.20.refs_0_, f32[1,8,640]{2,1,0:T(8,128)S(1)} %get-tuple-element.22.refs_1_, f32[2,8,640]{2,1,0:T(8,128)S(1)} %get-tuple-element.24.refs_2_), custom_call_target="tpu_custom_call" | custom-call | flops 1000000000 | bytes 10000000 | tf_op jit(solution)/shard_map/pallas_call | solution.py:225
  31.9 0.0 collective-permute-done.9.refs_3_
  31.9 0.0 collective-permute-done.8.refs_2_
  32.0 0.0 collective-permute-done.7.refs_1_
  32.0 0.6 %collective-permute-done.12.refs_5_.piece_ref = f32[4,8,640]{2,1,0:T(8,128)S(1)} collective-permute-done((f32[4,8,640]{2,1,0:T(8,128)S(1)}, f32[4,8,640]{2,1,0:T(8,128)S(1)}, u32[]{:S(2)}, u32[]{:S(2)}) %collective-permute-start.12) | collective-permute-done | bytes 81952 | tf_op jit(solution)/shard_map/ppermute | solution.py:93
  32.6 2.7 %collective-permute-start.15 = (f32[32,128]{1,0:T(8,128)S(1)}, f32[32,128]{1,0:T(8,128)S(1)}, u32[]{:S(2)}, u32[]{:S(2)}) collective-permute-start(f32[32,128]{1,0:T(8,128)S(1)} %shard_map.134), channel_id=1, source_target_pairs={{0,3},{1,2},{2,1},{3,0},{4,7},{5,6},{6,5},{7,4},{8,11},{9,10},{10,... | collective-permute-start | bytes 49160 | tf_op jit(solution)/shard_map/ppermute | solution.py:475
  35.3 1.7 %collective-permute-start.13 = (f32[32,128]{1,0:T(8,128)S(1)}, f32[32,128]{1,0:T(8,128)S(1)}, u32[]{:S(2)}, u32[]{:S(2)}) collective-permute-start(f32[32,128]{1,0:T(8,128)S(1)} %shard_map.134), channel_id=1, source_target_pairs={{0,1},{1,0},{2,3},{3,2},{4,5},{5,4},{6,7},{7,6},{8,9},{9,8},{10,11... | collective-permute-start | bytes 49160 | tf_op jit(solution)/shard_map/ppermute | solution.py:475
  37.0 1.1 %collective-permute-done.15 = f32[32,128]{1,0:T(8,128)S(1)} collective-permute-done((f32[32,128]{1,0:T(8,128)S(1)}, f32[32,128]{1,0:T(8,128)S(1)}, u32[]{:S(2)}, u32[]{:S(2)}) %collective-permute-start.15) | collective-permute-done | bytes 16416 | tf_op jit(solution)/shard_map/ppermute | solution.py:475
  38.2 1.8 %collective-permute-done.14 = f32[32,128]{1,0:T(8,128)S(1)} collective-permute-done((f32[32,128]{1,0:T(8,128)S(1)}, f32[32,128]{1,0:T(8,128)S(1)}, u32[]{:S(2)}, u32[]{:S(2)}) %collective-permute-start.14) | collective-permute-done | bytes 16416 | tf_op jit(solution)/shard_map/ppermute | solution.py:475
  40.0 6.1 %shard_map.135 = (f32[32,128,128]{2,1,0:T(8,128)}, f32[64,128]{1,0:T(8,128)}) custom-call(f32[32,128]{1,0:T(8,128)S(1)} %add_add_fusion.gram_ref, bf16[32,64,256]{2,1,0:T(8,128)(2,1)S(1)} %get-tuple-element.15.high_ref, bf16[32,64,256]{2,1,0:T(8,128)(2,1)S(1)} %get-tuple-element.16.low_ref, f32[64,128]{1,0:T(8,128)S(1)} %bitcast.36, ...), custom_call_target="tpu_custom_call" | custom-call | flops 1000000000 | bytes 10000000 | tf_op jit(solution)/shard_map/pallas_call | solution.py:559
  (17 shorter events, 0.1 us)
Async XLA Ops:
  1.6 7.9 %collective-permute-start.4 = (bf16[272,128]{1,0:T(8,128)(2,1)S(1)}, bf16[272,128]{1,0:T(8,128)(2,1)S(1)}, u32[]{:S(2)}, u32[]{:S(2)}) collective-permute-start(bf16[272,128]{1,0:T(8,128)(2,1)S(1)} %shard_map.131), channel_id=1, source_target_pairs={{0,3},{1,2},{2,1},{3,0},{4,7},{5,6},{6,5},{7,4},{8,11},{9,10},{10,... | collective-permute-start | bytes 208904 | tf_op jit(solution)/shard_map/ppermute | solution.py:525
  6.7 5.9 %collective-permute-start.2 = (bf16[272,128]{1,0:T(8,128)(2,1)S(1)}, bf16[272,128]{1,0:T(8,128)(2,1)S(1)}, u32[]{:S(2)}, u32[]{:S(2)}) collective-permute-start(bf16[272,128]{1,0:T(8,128)(2,1)S(1)} %shard_map.131), channel_id=1, source_target_pairs={{0,2},{1,3},{2,0},{3,1},{4,6},{5,7},{6,4},{7,5},{8,10},{9,11},{10,... | collective-permute-start | bytes 208904 | tf_op jit(solution)/shard_map/ppermute | solution.py:525
  6.7 5.9 %collective-permute-start = (bf16[272,128]{1,0:T(8,128)(2,1)S(1)}, bf16[272,128]{1,0:T(8,128)(2,1)S(1)}, u32[]{:S(2)}, u32[]{:S(2)}) collective-permute-start(bf16[272,128]{1,0:T(8,128)(2,1)S(1)} %shard_map.131), channel_id=1, source_target_pairs={{0,1},{1,0},{2,3},{3,2},{4,5},{5,4},{6,7},{7,6},{8,9},{9,8},{10,11... | collective-permute-start | bytes 208904 | tf_op jit(solution)/shard_map/ppermute | solution.py:525
  9.4 3.7 %collective-permute-start.10 = (f32[4,8,640]{2,1,0:T(8,128)S(1)}, f32[4,8,640]{2,1,0:T(8,128)S(1)}, u32[]{:S(2)}, u32[]{:S(2)}) collective-permute-start(f32[4,8,640]{2,1,0:T(8,128)S(1)} %get-tuple-element.14), channel_id=1, source_target_pairs={{0,4},{4,0},{8,12},{12,8},{16,20},{20,16},{24,28},{28,24},{1,5},{5... | collective-permute-start | bytes 245768 | tf_op jit(solution)/shard_map/ppermute | solution.py:93
  9.5 5.2 %collective-permute-start.5 = (bf16[272,128]{1,0:T(8,128)(2,1)S(1)}, bf16[272,128]{1,0:T(8,128)(2,1)S(1)}, u32[]{:S(2)}, u32[]{:S(2)}) collective-permute-start(bf16[272,128]{1,0:T(8,128)(2,1)S(1)} %collective-permute-done.4.refs_4_), channel_id=1, source_target_pairs={{0,4},{4,0},{8,12},{12,8},{16,20},{20,16},{24,28},{28,24},{1,5},{5... | collective-permute-start | bytes 208904 | tf_op jit(solution)/shard_map/ppermute | solution.py:529
  12.6 2.1 %collective-permute-start.3 = (bf16[272,128]{1,0:T(8,128)(2,1)S(1)}, bf16[272,128]{1,0:T(8,128)(2,1)S(1)}, u32[]{:S(2)}, u32[]{:S(2)}) collective-permute-start(bf16[272,128]{1,0:T(8,128)(2,1)S(1)} %collective-permute-done.2.refs_2_), channel_id=1, source_target_pairs={{0,4},{4,0},{8,12},{12,8},{16,20},{20,16},{24,28},{28,24},{1,5},{5... | collective-permute-start | bytes 208904 | tf_op jit(solution)/shard_map/ppermute | solution.py:529
  12.6 2.1 %collective-permute-start.1 = (bf16[272,128]{1,0:T(8,128)(2,1)S(1)}, bf16[272,128]{1,0:T(8,128)(2,1)S(1)}, u32[]{:S(2)}, u32[]{:S(2)}) collective-permute-start(bf16[272,128]{1,0:T(8,128)(2,1)S(1)} %collective-permute-done.refs_0_), channel_id=1, source_target_pairs={{0,4},{4,0},{8,12},{12,8},{16,20},{20,16},{24,28},{28,24},{1,5},{5... | collective-permute-start | bytes 208904 | tf_op jit(solution)/shard_map/ppermute | solution.py:529
  13.1 14.9 %collective-permute-start.11 = (f32[4,8,640]{2,1,0:T(8,128)S(1)}, f32[4,8,640]{2,1,0:T(8,128)S(1)}, u32[]{:S(2)}, u32[]{:S(2)}) collective-permute-start(f32[4,8,640]{2,1,0:T(8,128)S(1)} %pad_maximum_fusion), channel_id=1, source_target_pairs={{0,8},{4,12},{8,0},{12,4},{16,24},{20,28},{24,16},{28,20},{1,9},{5... | collective-permute-start | bytes 245768 | tf_op jit(solution)/shard_map/ppermute | solution.py:93
  14.7 15.0 %copy-start = (f32[32,2,128]{2,1,0:T(2,128)S(1)}, f32[32,2,128]{2,1,0:T(2,128)}, u32[]{:S(2)}) copy-start(f32[32,2,128]{2,1,0:T(2,128)} %param.11) | copy-start | bytes 98308
  23.3 1.2 %collective-permute-start.6 = (f32[32,128]{1,0:T(8,128)S(1)}, f32[32,128]{1,0:T(8,128)S(1)}, u32[]{:S(2)}, u32[]{:S(2)}) collective-permute-start(f32[32,128]{1,0:T(8,128)S(1)} %get-tuple-element.12), channel_id=1, source_target_pairs={{0,4},{4,0},{8,12},{12,8},{16,20},{20,16},{24,28},{28,24},{1,5},{5... | collective-permute-start | bytes 49160 | tf_op jit(solution)/shard_map/ppermute | solution.py:475
  24.6 7.4 %collective-permute-start.9 = (f32[32,128]{1,0:T(8,128)S(1)}, f32[32,128]{1,0:T(8,128)S(1)}, u32[]{:S(2)}, u32[]{:S(2)}) collective-permute-start(f32[32,128]{1,0:T(8,128)S(1)} %add.12.refs_0_), channel_id=1, source_target_pairs={{0,24},{4,28},{8,16},{12,20},{16,8},{20,12},{24,0},{28,4},{1,25},{... | collective-permute-start | bytes 49160 | tf_op jit(solution)/shard_map/ppermute | solution.py:475
  26.4 5.6 %collective-permute-start.8 = (f32[32,128]{1,0:T(8,128)S(1)}, f32[32,128]{1,0:T(8,128)S(1)}, u32[]{:S(2)}, u32[]{:S(2)}) collective-permute-start(f32[32,128]{1,0:T(8,128)S(1)} %add.12.refs_0_), channel_id=1, source_target_pairs={{0,16},{4,20},{8,24},{12,28},{16,0},{20,4},{24,8},{28,12},{1,17},{... | collective-permute-start | bytes 49160 | tf_op jit(solution)/shard_map/ppermute | solution.py:475
  26.9 5.1 %collective-permute-start.7 = (f32[32,128]{1,0:T(8,128)S(1)}, f32[32,128]{1,0:T(8,128)S(1)}, u32[]{:S(2)}, u32[]{:S(2)}) collective-permute-start(f32[32,128]{1,0:T(8,128)S(1)} %add.12.refs_0_), channel_id=1, source_target_pairs={{0,8},{4,12},{8,0},{12,4},{16,24},{20,28},{24,16},{28,20},{1,9},{5... | collective-permute-start | bytes 49160 | tf_op jit(solution)/shard_map/ppermute | solution.py:475
  28.1 4.5 %collective-permute-start.12 = (f32[4,8,640]{2,1,0:T(8,128)S(1)}, f32[4,8,640]{2,1,0:T(8,128)S(1)}, u32[]{:S(2)}, u32[]{:S(2)}) collective-permute-start(f32[4,8,640]{2,1,0:T(8,128)S(1)} %pad_maximum_fusion.1), channel_id=1, source_target_pairs={{0,16},{4,20},{8,24},{12,28},{16,0},{20,4},{24,8},{28,12},{1,17},{... | collective-permute-start | bytes 245768 | tf_op jit(solution)/shard_map/ppermute | solution.py:93
  32.6 5.5 %collective-permute-start.15 = (f32[32,128]{1,0:T(8,128)S(1)}, f32[32,128]{1,0:T(8,128)S(1)}, u32[]{:S(2)}, u32[]{:S(2)}) collective-permute-start(f32[32,128]{1,0:T(8,128)S(1)} %shard_map.134), channel_id=1, source_target_pairs={{0,3},{1,2},{2,1},{3,0},{4,7},{5,6},{6,5},{7,4},{8,11},{9,10},{10,... | collective-permute-start | bytes 49160 | tf_op jit(solution)/shard_map/ppermute | solution.py:475
  35.3 4.6 %collective-permute-start.14 = (f32[32,128]{1,0:T(8,128)S(1)}, f32[32,128]{1,0:T(8,128)S(1)}, u32[]{:S(2)}, u32[]{:S(2)}) collective-permute-start(f32[32,128]{1,0:T(8,128)S(1)} %shard_map.134), channel_id=1, source_target_pairs={{0,2},{1,3},{2,0},{3,1},{4,6},{5,7},{6,4},{7,5},{8,10},{9,11},{10,... | collective-permute-start | bytes 49160 | tf_op jit(solution)/shard_map/ppermute | solution.py:475
  35.3 4.6 %collective-permute-start.13 = (f32[32,128]{1,0:T(8,128)S(1)}, f32[32,128]{1,0:T(8,128)S(1)}, u32[]{:S(2)}, u32[]{:S(2)}) collective-permute-start(f32[32,128]{1,0:T(8,128)S(1)} %shard_map.134), channel_id=1, source_target_pairs={{0,1},{1,0},{2,3},{3,2},{4,5},{5,4},{6,7},{7,6},{8,9},{9,8},{10,11... | collective-permute-start | bytes 49160 | tf_op jit(solution)/shard_map/ppermute | solution.py:475

commit v10 on v9

--- a/solution.py
+++ b/solution.py
@@ -189,8 +189,8 @@
 
 
 def near_kernel(slot_cap, piece_count, pos_ref, *refs):
-    piece_refs = refs[:piece_count]
-    near_ref, arrived, aim_x, aim_y, speed_x, speed_y = refs[piece_count:]
+    piece_refs, before_refs = refs[:piece_count], refs[piece_count:-6]
+    near_ref, arrived, aim_x, aim_y, speed_x, speed_y = refs[-6:]
     vesicles, nodes = pos_ref.shape[0] // 2, pos_ref.shape[1]
     here = 0
     for ref in piece_refs:
@@ -215,44 +215,27 @@
     lax.fori_loop(0, pieces // many, group, 0)
     turned_hot = hot.T
     for axis, speed in enumerate((speed_x, speed_y)):
-        near_ref[axis_rows(vesicles, axis), :] = dot(
-            turned_hot, speed[...].reshape(-1, nodes), precision=HIGHEST) / nodes
-
-
-def near_part(flat, pieces, slot_cap):
+        rows = axis_rows(vesicles, axis)
+        near = dot(turned_hot, speed[...].reshape(-1, nodes), precision=HIGHEST) / nodes
+        for before_ref in before_refs:
+            near = near + before_ref[rows, :]
+        near_ref[rows, :] = near
+
+
+def near_part(flat, pieces, before, slot_cap):
     vesicles, nodes = flat.shape[0] // 2, flat.shape[1]
     count = sum(p.shape[0] for p in pieces)
     return pl.pallas_call(
         functools.partial(near_kernel, slot_cap, len(pieces)),
         out_shape=jax.ShapeDtypeStruct((2 * vesicles, nodes), F32),
-        in_specs=[whole_spec()] * (1 + len(pieces)),
+        in_specs=[whole_spec()] * (1 + len(pieces) + len(before)),
         out_specs=whole_spec(),
         scratch_shapes=[pltpu.VMEM((count, BLOCK, 5 * nodes), F32)]
         + [pltpu.VMEM((count, BLOCK, nodes), F32)] * 4,
         compiler_params=params(16),
         cost_estimate=pl.CostEstimate(
             flops=10**9, bytes_accessed=10**7, transcendentals=10**6),
-    )(flat, *pieces)
-
-
-def near_rest(slot_cap, pos_ref, piece_ref, before_ref):
-    vesicles, nodes = pos_ref.shape[0] // 2, pos_ref.shape[1]
-    hot = target_table(piece_ref[:, :, 4 * nodes:], vesicles)
-    aims = [dot(hot, pos_ref[axis_rows(vesicles, axis), :], precision=HIGHEST)
-            for axis in range(2)]
-    before = [before_ref[axis_rows(vesicles, axis), :] for axis in range(2)]
-    calls = [call for k in range(piece_ref.shape[0]) for call in near_piece(
-        piece_ref[k], *[aim[k * BLOCK:(k + 1) * BLOCK] for aim in aims], slot_cap)]
-    turned_hot = hot.T
-
-    def finish(slots):
-        pieces = [slots[k:k + slot_cap] for k in range(0, len(slots), slot_cap)]
-        speeds = [jnp.concatenate([gather_rows(piece, axis) for piece in pieces], axis=0)
-                  for axis in range(2)]
-        return [b + dot(turned_hot, speed, precision=HIGHEST) / nodes
-                for b, speed in zip(before, speeds)]
-
-    return calls, finish
+    )(flat, *pieces, *before)
 
 
 def far_kernel(col_count, range_in, pos_in, own_in, nodes_in, *refs):
@@ -351,7 +334,7 @@
     gram_ref[...] = jnp.concatenate([gram[:rank // 2], gram[rank // 2:]], axis=1)
 
 
-def lower_inverse(gram, beside):
+def lower_inverse(gram):
     size = gram.shape[0]
     eye = (iota((size, size), 0) == iota((size, size), 1)).astype(F32)
     rest = jnp.concatenate([gram, eye], axis=1)
@@ -359,7 +342,6 @@
     step = 8
     for start in range(0, size, step):
         height = size - start
-        beside(start // step, size // step)
         columns = [jnp.broadcast_to(rest[:, start + j:start + j + 1], (height, 2 * size))
                    for j in range(step)]
         row_number = iota((height, 2 * size), 0)
@@ -379,36 +361,29 @@
     return jnp.concatenate(done, axis=0)[:, size:]
 
 
-def basis_kernel(scale_factor, slot_cap, gram_ref, high_ref, low_ref, pos_ref, piece_ref,
-                 before_ref, out_ref, near_ref, weight):
-    rank, nodes = high_ref.shape[1], high_ref.shape[2] // 2
-
-    @pl.when(pl.program_id(0) == 0)
-    def _():
-        folded = gram_ref[...]
-        calls, finish = near_rest(slot_cap, pos_ref, piece_ref, before_ref)
-        slots = []
-
-        def beside(i, n):
-            slots.extend(call() for call in calls[len(calls) * i // n:len(calls) * (i + 1) // n])
-
-        gram = jnp.concatenate([folded[:, :rank], folded[:, rank:]], axis=0)
-        inverse = lower_inverse(gram, beside) * scale_factor
-        near = finish(slots)
-        high = inverse.astype(BF16)
-        low = (inverse - high.astype(F32)).astype(BF16)
-        weight[...] = jnp.concatenate([high, high, low], axis=1)
-        for axis in range(2):
-            near_ref[axis_rows(near[axis].shape[0], axis), :] = near[axis]
-
-    w = weight[...]
-    many = math.gcd(high_ref.shape[0], 2)
-    for v in range(0, high_ref.shape[0], many):
-        fresh = [dot(w, jnp.concatenate([high_ref[u], low_ref[u], high_ref[u]], axis=0))
-                 for u in range(v, v + many)]
-        for u, value in enumerate(fresh):
-            for d in range(2):
-                out_ref[v + u, pl.ds(d, rank, stride=2), :] = value[:, d * nodes:(d + 1) * nodes]
+def basis_kernel(scale_factor, groups, gram_ref, high_ref, low_ref, _, out_ref, made, sems):
+    vesicles, rank, nodes = high_ref.shape[0], high_ref.shape[1], high_ref.shape[2] // 2
+    folded = gram_ref[...]
+    gram = jnp.concatenate([folded[:, :rank], folded[:, rank:]], axis=0)
+    inverse = lower_inverse(gram) * scale_factor
+    high = inverse.astype(BF16)
+    low = (inverse - high.astype(F32)).astype(BF16)
+    weight = jnp.concatenate([high, high, low], axis=1)
+    size = vesicles // groups
+    many = math.gcd(size, 4)
+    copies = []
+    for g in range(groups):
+        for v in range(g * size, (g + 1) * size, many):
+            fresh = [dot(weight, jnp.concatenate([high_ref[u], low_ref[u], high_ref[u]], axis=0))
+                     for u in range(v, v + many)]
+            for u, value in enumerate(fresh):
+                for d in range(2):
+                    made[v + u, pl.ds(d, rank, stride=2), :] = value[:, d * nodes:(d + 1) * nodes]
+        here = slice(g * size, (g + 1) * size)
+        copies.append(pltpu.make_async_copy(made.at[here], out_ref.at[here], sems.at[g]))
+        copies[-1].start()
+    for copy in copies:
+        copy.wait()
 
 
 def whole_spec():
@@ -528,7 +503,8 @@
     for mine in moved_halves:
         pieces += [mine, lax.ppermute(mine, "clu", [(i, i ^ 1) for i in range(clu_count)])]
 
-    near_first = near_part(flat, arrived[:-1], slot_cap)
+    near_first = near_part(flat, arrived[:-1], [], slot_cap)
+    near = near_part(flat, arrived[-1:], [near_first], slot_cap)
 
     high, low, gram = pl.pallas_call(
         functools.partial(far_kernel, col_count),
@@ -553,20 +529,17 @@
     gram = sum_over(gram, "col", step_groups(col_count, False))
 
     scale_factor = math.sqrt(2.0 * nodes * vesicles * clu_count * col_count)
-    group = 8 if vesicles % 8 == 0 else vesicles
-    block = pl.BlockSpec((group, rows, nodes), lambda i: (i, 0, 0))
-    held = pl.BlockSpec((group, rank, 2 * nodes), lambda i: (i, 0, 0))
-    new_basis, near = pl.pallas_call(
-        functools.partial(basis_kernel, scale_factor, slot_cap),
-        out_shape=[jax.ShapeDtypeStruct((vesicles, rows, nodes), F32),
-                   jax.ShapeDtypeStruct((2 * vesicles, nodes), F32)],
-        grid=(vesicles // group,),
-        in_specs=[whole_spec(), held, held] + [whole_spec()] * 3,
-        out_specs=[block, whole_spec()],
-        scratch_shapes=[pltpu.VMEM((rank, 3 * rank), BF16)],
+    groups = math.gcd(vesicles, 8)
+    new_basis = pl.pallas_call(
+        functools.partial(basis_kernel, scale_factor, groups),
+        out_shape=jax.ShapeDtypeStruct((vesicles, rows, nodes), F32),
+        in_specs=[whole_spec()] * 3 + [far_off_spec()],
+        out_specs=far_off_spec(),
+        scratch_shapes=[pltpu.VMEM((vesicles, rows, nodes), F32),
+                        pltpu.SemaphoreType.DMA((groups,))],
         compiler_params=params(16),
         cost_estimate=pl.CostEstimate(flops=10**9, bytes_accessed=10**7, transcendentals=0),
-    )(gram, high, low, flat, arrived[-1], near_first)
+    )(gram, high, low, near_by(near))
 
     return (force.reshape(vesicles, 2, nodes), near.reshape(vesicles, 2, nodes),
             new_basis.reshape(vesicles, rank, 2, nodes))

time: 46.2 us -> 43.6 us (0.944)
  waiting for transfers between devices: 7.33 us -> 4.42 us
    ppermute x7, waiting for transfers between devices: 4.15 us -> 1.24 us  [sum_over(): lax.ppermute(value, axis, partners(count, k))]
    pallas_call x1 -> x2, Pallas kernels: 2.27 us -> 5.17 us  [near_part(): pl.pallas_call(functools.partial(near_kernel, slot_cap, len(pieces)), out...]
    pallas_call x1, Pallas kernels: 6.05 us -> 3.42 us  [per_device(): pl.pallas_call(functools.partial(basis_kernel, scale_factor, groups), out...]
  transfers between devices with their start and end apart: 16 -> 16, of which waited for: 5 -> 4; matrix products, arithmetic and copies ran while one was open for 0% -> 0% of each run, Pallas kernels for 28% -> 36%
where the time goes in v10:
time: 43.6 us; the launch traced here: 43.4 us
  Pallas kernels  20.2 us (46%)
  starting transfers between devices  18 us (41%)
  waiting for transfers between devices  4.42 us (10%)
  between operations  0.76 us (2%)
    pallas_call x1, Pallas kernels, per_device(): pl.pallas_call(functools.partial(far_kernel, col_count), out_shape=[jax.S...  8.6 us
    ppermute x7, starting transfers between devices, sum_over(): lax.ppermute(value, axis, partners(count, k))  7.95 us
    ppermute x3, starting transfers between devices, per_device(): lax.ppermute(sent, 'col', partners(col_count, k))  5.76 us
    pallas_call x2, Pallas kernels, near_part(): pl.pallas_call(functools.partial(near_kernel, slot_cap, len(pieces)), out...  5.17 us
    pallas_call x1, Pallas kernels, per_device(): pl.pallas_call(functools.partial(basis_kernel, scale_factor, groups), out...  3.42 us
    ppermute x3, starting transfers between devices, cube_exchange(): held.append(lax.ppermute(leaving, axis, partners(count, bit)))  3.2 us
    ppermute x3, waiting for transfers between devices, per_device(): lax.ppermute(sent, 'col', partners(col_count, k))  2.54 us
    pallas_call x1, Pallas kernels, per_device(): pl.pallas_call(functools.partial(force_kernel, clu_count), out_shape=[jax...  2.06 us
  transfers between devices with their start and end apart: 16, of which 4 were waited for; matrix products, arithmetic and copies ran while one was open for 0% of the time, Pallas kernels for 36%

profile of v10, /device:TPU:0, one launch (start us, length us, event | category | flops | bytes accessed | tf_op | source)
XLA Modules:
  0.0 43.4 jit_solution(13782350365001517494)
XLA Ops:
  0.6 0.9 %shard_map.133 = bf16[272,128]{1,0:T(8,128)(2,1)S(1)} custom-call(bf16[128,512]{1,0:T(8,128)(2,1)} %own_in.3, bf16[2,512]{1,0:T(2,128)(2,1)} %nodes_in.3), custom_call_target="tpu_custom_call" | custom-call | flops 100000 | bytes 100000 | tf_op jit(solution)/shard_map/pallas_call | solution.py:473
  1.6 5.1 %collective-permute-start.7 = (bf16[272,128]{1,0:T(8,128)(2,1)S(1)}, bf16[272,128]{1,0:T(8,128)(2,1)S(1)}, u32[]{:S(2)}, u32[]{:S(2)}) collective-permute-start(bf16[272,128]{1,0:T(8,128)(2,1)S(1)} %shard_map.133), channel_id=1, source_target_pairs={{0,3},{1,2},{2,1},{3,0},{4,7},{5,6},{6,5},{7,4},{8,11},{9,10},{10,... | collective-permute-start | bytes 208904 | tf_op jit(solution)/shard_map/ppermute | solution.py:500
  6.7 0.0 collective-permute-start.5
  6.7 0.6 %collective-permute-start.3 = (bf16[272,128]{1,0:T(8,128)(2,1)S(1)}, bf16[272,128]{1,0:T(8,128)(2,1)S(1)}, u32[]{:S(2)}, u32[]{:S(2)}) collective-permute-start(bf16[272,128]{1,0:T(8,128)(2,1)S(1)} %shard_map.133), channel_id=1, source_target_pairs={{0,1},{1,0},{2,3},{3,2},{4,5},{5,4},{6,7},{7,6},{8,9},{9,8},{10,11... | collective-permute-start | bytes 208904 | tf_op jit(solution)/shard_map/ppermute | solution.py:500
  7.3 2.1 %shard_map.130 = (f32[64,128]{1,0:T(8,128)}, f32[4,8,640]{2,1,0:T(8,128)S(1)}, f32[4,8,640]{2,1,0:T(8,128)S(1)}) custom-call(f32[64,128]{1,0:T(8,128)} %bitcast.33, f32[32,128]{1,0:T(8,128)} %refs_1_.1, f32[1,32]{1,0:T(1,128)} %bitcast.42, s32[1,32]{1,0:T(1,128)} %refs_3_.1, s32[1,24]{1,0:T(1,128)} %bitcast.43, s32[1,24]{1,0:T(1,128)} %bitcast.44, ...), custom_call_target="tpu_custom_call" | custom-call | flops 100000000 | bytes 1000000 | tf_op jit(solution)/shard_map/pallas_call | solution.py:488
  9.4 0.1 collective-permute-start
  9.5 0.5 %collective-permute-start.8 = (bf16[272,128]{1,0:T(8,128)(2,1)S(1)}, bf16[272,128]{1,0:T(8,128)(2,1)S(1)}, u32[]{:S(2)}, u32[]{:S(2)}) collective-permute-start(bf16[272,128]{1,0:T(8,128)(2,1)S(1)} %collective-permute-done.7.refs_4_), channel_id=1, source_target_pairs={{0,4},{4,0},{8,12},{12,8},{16,20},{20,16},{24,28},{28,24},{1,5},{5... | collective-permute-start | bytes 208904 | tf_op jit(solution)/shard_map/ppermute | solution.py:504
  10.1 2.5 %collective-permute-done.5.refs_2_ = bf16[272,128]{1,0:T(8,128)(2,1)S(1)} collective-permute-done((bf16[272,128]{1,0:T(8,128)(2,1)S(1)}, bf16[272,128]{1,0:T(8,128)(2,1)S(1)}, u32[]{:S(2)}, u32[]{:S(2)}) %collective-permute-start.5) | collective-permute-done | bytes 69664 | tf_op jit(solution)/shard_map/ppermute | solution.py:500
  12.6 0.5 %collective-permute-start.4 = (bf16[272,128]{1,0:T(8,128)(2,1)S(1)}, bf16[272,128]{1,0:T(8,128)(2,1)S(1)}, u32[]{:S(2)}, u32[]{:S(2)}) collective-permute-start(bf16[272,128]{1,0:T(8,128)(2,1)S(1)} %collective-permute-done.3.refs_0_), channel_id=1, source_target_pairs={{0,4},{4,0},{8,12},{12,8},{16,20},{20,16},{24,28},{28,24},{1,5},{5... | collective-permute-start | bytes 208904 | tf_op jit(solution)/shard_map/ppermute | solution.py:504
  13.1 1.6 %collective-permute-start.1 = (f32[4,8,640]{2,1,0:T(8,128)S(1)}, f32[4,8,640]{2,1,0:T(8,128)S(1)}, u32[]{:S(2)}, u32[]{:S(2)}) collective-permute-start(f32[4,8,640]{2,1,0:T(8,128)S(1)} %pad_maximum_fusion), channel_id=1, source_target_pairs={{0,8},{4,12},{8,0},{12,4},{16,24},{20,28},{24,16},{28,20},{1,9},{5... | collective-permute-start | bytes 245768 | tf_op jit(solution)/shard_map/ppermute | solution.py:93
  14.7 0.0 collective-permute-done.8.refs_5_
  14.7 0.0 collective-permute-done.6.refs_3_
  14.7 0.0 collective-permute-done.4.refs_1_
  14.7 0.0 copy-start
  14.7 8.6 %shard_map.134 = (bf16[32,64,256]{2,1,0:T(8,128)(2,1)S(1)}, bf16[32,64,256]{2,1,0:T(8,128)(2,1)S(1)}, f32[32,128]{1,0:T(8,128)S(1)}) custom-call(s32[1,32]{1,0:T(1,128)} %bitcast.45, f32[64,128]{1,0:T(8,128)} %bitcast.34, bf16[128,512]{1,0:T(8,128)(2,1)} %own_in.3, bf16[2,512]{1,0:T(2,128)(2,1)} %nodes_in.3, ...), custom_call_target="tpu_custom_call" | custom-call | flops 10000000000 | bytes 10000000 | tf_op jit(solution)/shard_map/pallas_call | solution.py:509
  23.3 0.1 collective-permute-start.9
  23.4 1.2 %collective-permute-done.9 = f32[32,128]{1,0:T(8,128)S(1)} collective-permute-done((f32[32,128]{1,0:T(8,128)S(1)}, f32[32,128]{1,0:T(8,128)S(1)}, u32[]{:S(2)}, u32[]{:S(2)}) %collective-permute-start.9) | collective-permute-done | bytes 16416 | tf_op jit(solution)/shard_map/ppermute | solution.py:450
  24.6 1.8 %collective-permute-start.12 = (f32[32,128]{1,0:T(8,128)S(1)}, f32[32,128]{1,0:T(8,128)S(1)}, u32[]{:S(2)}, u32[]{:S(2)}) collective-permute-start(f32[32,128]{1,0:T(8,128)S(1)} %add.12.refs_0_), channel_id=1, source_target_pairs={{0,24},{4,28},{8,16},{12,20},{16,8},{20,12},{24,0},{28,4},{1,25},{... | collective-permute-start | bytes 49160 | tf_op jit(solution)/shard_map/ppermute | solution.py:450
  26.4 0.5 %collective-permute-start.11 = (f32[32,128]{1,0:T(8,128)S(1)}, f32[32,128]{1,0:T(8,128)S(1)}, u32[]{:S(2)}, u32[]{:S(2)}) collective-permute-start(f32[32,128]{1,0:T(8,128)S(1)} %add.12.refs_0_), channel_id=1, source_target_pairs={{0,16},{4,20},{8,24},{12,28},{16,0},{20,4},{24,8},{28,12},{1,17},{... | collective-permute-start | bytes 49160 | tf_op jit(solution)/shard_map/ppermute | solution.py:450
  26.9 1.2 %collective-permute-start.10 = (f32[32,128]{1,0:T(8,128)S(1)}, f32[32,128]{1,0:T(8,128)S(1)}, u32[]{:S(2)}, u32[]{:S(2)}) collective-permute-start(f32[32,128]{1,0:T(8,128)S(1)} %add.12.refs_0_), channel_id=1, source_target_pairs={{0,8},{4,12},{8,0},{12,4},{16,24},{20,28},{24,16},{28,20},{1,9},{5... | collective-permute-start | bytes 49160 | tf_op jit(solution)/shard_map/ppermute | solution.py:450
  28.1 0.0 collective-permute-done.1
  28.1 1.6 %collective-permute-start.2 = (f32[4,8,640]{2,1,0:T(8,128)S(1)}, f32[4,8,640]{2,1,0:T(8,128)S(1)}, u32[]{:S(2)}, u32[]{:S(2)}) collective-permute-start(f32[4,8,640]{2,1,0:T(8,128)S(1)} %pad_maximum_fusion.1), channel_id=1, source_target_pairs={{0,16},{4,20},{8,24},{12,28},{16,0},{20,4},{24,8},{28,12},{1,17},{... | collective-permute-start | bytes 245768 | tf_op jit(solution)/shard_map/ppermute | solution.py:93
  29.7 2.3 %shard_map.131.refs_1_.refs_4_ = f32[64,128]{1,0:T(8,128)S(1)} custom-call(f32[64,128]{1,0:T(8,128)S(1)} %bitcast.35, f32[1,8,640]{2,1,0:T(8,128)S(1)} %get-tuple-element.19.refs_0_, f32[1,8,640]{2,1,0:T(8,128)S(1)} %get-tuple-element.17.refs_1_, f32[2,8,640]{2,1,0:T(8,128)S(1)} %get-tuple-element.15.refs_2_), custom_call_target="tpu_custom_call" | custom-call | flops 1000000000 | bytes 10000000 | tf_op jit(solution)/shard_map/pallas_call | solution.py:228
  31.9 0.0 collective-permute-done.11.refs_2_
  32.0 0.0 collective-permute-done.10.refs_1_
  32.0 0.6 %collective-permute-done.2.refs_0_.refs_5_ = f32[4,8,640]{2,1,0:T(8,128)S(1)} collective-permute-done((f32[4,8,640]{2,1,0:T(8,128)S(1)}, f32[4,8,640]{2,1,0:T(8,128)S(1)}, u32[]{:S(2)}, u32[]{:S(2)}) %collective-permute-start.2) | collective-permute-done | bytes 81952 | tf_op jit(solution)/shard_map/ppermute | solution.py:93
  32.6 2.7 %collective-permute-start.15 = (f32[32,128]{1,0:T(8,128)S(1)}, f32[32,128]{1,0:T(8,128)S(1)}, u32[]{:S(2)}, u32[]{:S(2)}) collective-permute-start(f32[32,128]{1,0:T(8,128)S(1)} %shard_map.135), channel_id=1, source_target_pairs={{0,3},{1,2},{2,1},{3,0},{4,7},{5,6},{6,5},{7,4},{8,11},{9,10},{10,... | collective-permute-start | bytes 49160 | tf_op jit(solution)/shard_map/ppermute | solution.py:450
  35.3 0.0 collective-permute-start.14
  35.3 1.7 %collective-permute-start.13 = (f32[32,128]{1,0:T(8,128)S(1)}, f32[32,128]{1,0:T(8,128)S(1)}, u32[]{:S(2)}, u32[]{:S(2)}) collective-permute-start(f32[32,128]{1,0:T(8,128)S(1)} %shard_map.135), channel_id=1, source_target_pairs={{0,1},{1,0},{2,3},{3,2},{4,5},{5,4},{6,7},{7,6},{8,9},{9,8},{10,11... | collective-permute-start | bytes 49160 | tf_op jit(solution)/shard_map/ppermute | solution.py:450
  37.0 2.9 %shard_map.132._ = f32[64,128]{1,0:T(8,128)} custom-call(f32[64,128]{1,0:T(8,128)S(1)} %bitcast.36, f32[4,8,640]{2,1,0:T(8,128)S(1)} %collective-permute-done.2.refs_0_.refs_5_, f32[64,128]{1,0:T(8,128)S(1)} %shard_map.131.refs_1_.refs_4_), custom_call_target="tpu_custom_call" | custom-call | flops 1000000000 | bytes 10000000 | tf_op jit(solution)/shard_map/pallas_call | solution.py:228
  39.9 0.1 collective-permute-done.14
  40.0 3.4 %shard_map.136 = f32[32,128,128]{2,1,0:T(8,128)} custom-call(f32[32,128]{1,0:T(8,128)S(1)} %add_add_fusion.gram_ref, bf16[32,64,256]{2,1,0:T(8,128)(2,1)S(1)} %get-tuple-element.13.high_ref, bf16[32,64,256]{2,1,0:T(8,128)(2,1)S(1)} %get-tuple-element.14.low_ref, f32[64,128]{1,0:T(8,128)} %shard_map.132._), custom_call_target="tpu_custom_call" | custom-call | flops 1000000000 | bytes 10000000 | tf_op jit(solution)/shard_map/pallas_call | solution.py:533
  (18 shorter events, 0.1 us)
Async XLA Ops:
  1.6 7.9 %collective-permute-start.7 = (bf16[272,128]{1,0:T(8,128)(2,1)S(1)}, bf16[272,128]{1,0:T(8,128)(2,1)S(1)}, u32[]{:S(2)}, u32[]{:S(2)}) collective-permute-start(bf16[272,128]{1,0:T(8,128)(2,1)S(1)} %shard_map.133), channel_id=1, source_target_pairs={{0,3},{1,2},{2,1},{3,0},{4,7},{5,6},{6,5},{7,4},{8,11},{9,10},{10,... | collective-permute-start | bytes 208904 | tf_op jit(solution)/shard_map/ppermute | solution.py:500
  6.7 5.9 %collective-permute-start.5 = (bf16[272,128]{1,0:T(8,128)(2,1)S(1)}, bf16[272,128]{1,0:T(8,128)(2,1)S(1)}, u32[]{:S(2)}, u32[]{:S(2)}) collective-permute-start(bf16[272,128]{1,0:T(8,128)(2,1)S(1)} %shard_map.133), channel_id=1, source_target_pairs={{0,2},{1,3},{2,0},{3,1},{4,6},{5,7},{6,4},{7,5},{8,10},{9,11},{10,... | collective-permute-start | bytes 208904 | tf_op jit(solution)/shard_map/ppermute | solution.py:500
  6.7 5.9 %collective-permute-start.3 = (bf16[272,128]{1,0:T(8,128)(2,1)S(1)}, bf16[272,128]{1,0:T(8,128)(2,1)S(1)}, u32[]{:S(2)}, u32[]{:S(2)}) collective-permute-start(bf16[272,128]{1,0:T(8,128)(2,1)S(1)} %shard_map.133), channel_id=1, source_target_pairs={{0,1},{1,0},{2,3},{3,2},{4,5},{5,4},{6,7},{7,6},{8,9},{9,8},{10,11... | collective-permute-start | bytes 208904 | tf_op jit(solution)/shard_map/ppermute | solution.py:500
  9.4 3.7 %collective-permute-start = (f32[4,8,640]{2,1,0:T(8,128)S(1)}, f32[4,8,640]{2,1,0:T(8,128)S(1)}, u32[]{:S(2)}, u32[]{:S(2)}) collective-permute-start(f32[4,8,640]{2,1,0:T(8,128)S(1)} %get-tuple-element.11), channel_id=1, source_target_pairs={{0,4},{4,0},{8,12},{12,8},{16,20},{20,16},{24,28},{28,24},{1,5},{5... | collective-permute-start | bytes 245768 | tf_op jit(solution)/shard_map/ppermute | solution.py:93
  9.5 5.2 %collective-permute-start.8 = (bf16[272,128]{1,0:T(8,128)(2,1)S(1)}, bf16[272,128]{1,0:T(8,128)(2,1)S(1)}, u32[]{:S(2)}, u32[]{:S(2)}) collective-permute-start(bf16[272,128]{1,0:T(8,128)(2,1)S(1)} %collective-permute-done.7.refs_4_), channel_id=1, source_target_pairs={{0,4},{4,0},{8,12},{12,8},{16,20},{20,16},{24,28},{28,24},{1,5},{5... | collective-permute-start | bytes 208904 | tf_op jit(solution)/shard_map/ppermute | solution.py:504
  12.6 2.1 %collective-permute-start.6 = (bf16[272,128]{1,0:T(8,128)(2,1)S(1)}, bf16[272,128]{1,0:T(8,128)(2,1)S(1)}, u32[]{:S(2)}, u32[]{:S(2)}) collective-permute-start(bf16[272,128]{1,0:T(8,128)(2,1)S(1)} %collective-permute-done.5.refs_2_), channel_id=1, source_target_pairs={{0,4},{4,0},{8,12},{12,8},{16,20},{20,16},{24,28},{28,24},{1,5},{5... | collective-permute-start | bytes 208904 | tf_op jit(solution)/shard_map/ppermute | solution.py:504
  12.6 2.1 %collective-permute-start.4 = (bf16[272,128]{1,0:T(8,128)(2,1)S(1)}, bf16[272,128]{1,0:T(8,128)(2,1)S(1)}, u32[]{:S(2)}, u32[]{:S(2)}) collective-permute-start(bf16[272,128]{1,0:T(8,128)(2,1)S(1)} %collective-permute-done.3.refs_0_), channel_id=1, source_target_pairs={{0,4},{4,0},{8,12},{12,8},{16,20},{20,16},{24,28},{28,24},{1,5},{5... | collective-permute-start | bytes 208904 | tf_op jit(solution)/shard_map/ppermute | solution.py:504
  13.1 14.9 %collective-permute-start.1 = (f32[4,8,640]{2,1,0:T(8,128)S(1)}, f32[4,8,640]{2,1,0:T(8,128)S(1)}, u32[]{:S(2)}, u32[]{:S(2)}) collective-permute-start(f32[4,8,640]{2,1,0:T(8,128)S(1)} %pad_maximum_fusion), channel_id=1, source_target_pairs={{0,8},{4,12},{8,0},{12,4},{16,24},{20,28},{24,16},{28,20},{1,9},{5... | collective-permute-start | bytes 245768 | tf_op jit(solution)/shard_map/ppermute | solution.py:93
  14.7 15.0 %copy-start = (f32[32,2,128]{2,1,0:T(2,128)S(1)}, f32[32,2,128]{2,1,0:T(2,128)}, u32[]{:S(2)}) copy-start(f32[32,2,128]{2,1,0:T(2,128)} %param.11) | copy-start | bytes 98308
  23.3 1.2 %collective-permute-start.9 = (f32[32,128]{1,0:T(8,128)S(1)}, f32[32,128]{1,0:T(8,128)S(1)}, u32[]{:S(2)}, u32[]{:S(2)}) collective-permute-start(f32[32,128]{1,0:T(8,128)S(1)} %get-tuple-element.12), channel_id=1, source_target_pairs={{0,4},{4,0},{8,12},{12,8},{16,20},{20,16},{24,28},{28,24},{1,5},{5... | collective-permute-start | bytes 49160 | tf_op jit(solution)/shard_map/ppermute | solution.py:450
  24.6 7.4 %collective-permute-start.12 = (f32[32,128]{1,0:T(8,128)S(1)}, f32[32,128]{1,0:T(8,128)S(1)}, u32[]{:S(2)}, u32[]{:S(2)}) collective-permute-start(f32[32,128]{1,0:T(8,128)S(1)} %add.12.refs_0_), channel_id=1, source_target_pairs={{0,24},{4,28},{8,16},{12,20},{16,8},{20,12},{24,0},{28,4},{1,25},{... | collective-permute-start | bytes 49160 | tf_op jit(solution)/shard_map/ppermute | solution.py:450
  26.4 5.6 %collective-permute-start.11 = (f32[32,128]{1,0:T(8,128)S(1)}, f32[32,128]{1,0:T(8,128)S(1)}, u32[]{:S(2)}, u32[]{:S(2)}) collective-permute-start(f32[32,128]{1,0:T(8,128)S(1)} %add.12.refs_0_), channel_id=1, source_target_pairs={{0,16},{4,20},{8,24},{12,28},{16,0},{20,4},{24,8},{28,12},{1,17},{... | collective-permute-start | bytes 49160 | tf_op jit(solution)/shard_map/ppermute | solution.py:450
  26.9 5.1 %collective-permute-start.10 = (f32[32,128]{1,0:T(8,128)S(1)}, f32[32,128]{1,0:T(8,128)S(1)}, u32[]{:S(2)}, u32[]{:S(2)}) collective-permute-start(f32[32,128]{1,0:T(8,128)S(1)} %add.12.refs_0_), channel_id=1, source_target_pairs={{0,8},{4,12},{8,0},{12,4},{16,24},{20,28},{24,16},{28,20},{1,9},{5... | collective-permute-start | bytes 49160 | tf_op jit(solution)/shard_map/ppermute | solution.py:450
  28.1 4.5 %collective-permute-start.2 = (f32[4,8,640]{2,1,0:T(8,128)S(1)}, f32[4,8,640]{2,1,0:T(8,128)S(1)}, u32[]{:S(2)}, u32[]{:S(2)}) collective-permute-start(f32[4,8,640]{2,1,0:T(8,128)S(1)} %pad_maximum_fusion.1), channel_id=1, source_target_pairs={{0,16},{4,20},{8,24},{12,28},{16,0},{20,4},{24,8},{28,12},{1,17},{... | collective-permute-start | bytes 245768 | tf_op jit(solution)/shard_map/ppermute | solution.py:93
  32.6 7.3 %collective-permute-start.15 = (f32[32,128]{1,0:T(8,128)S(1)}, f32[32,128]{1,0:T(8,128)S(1)}, u32[]{:S(2)}, u32[]{:S(2)}) collective-permute-start(f32[32,128]{1,0:T(8,128)S(1)} %shard_map.135), channel_id=1, source_target_pairs={{0,3},{1,2},{2,1},{3,0},{4,7},{5,6},{6,5},{7,4},{8,11},{9,10},{10,... | collective-permute-start | bytes 49160 | tf_op jit(solution)/shard_map/ppermute | solution.py:450
  35.3 4.6 %collective-permute-start.14 = (f32[32,128]{1,0:T(8,128)S(1)}, f32[32,128]{1,0:T(8,128)S(1)}, u32[]{:S(2)}, u32[]{:S(2)}) collective-permute-start(f32[32,128]{1,0:T(8,128)S(1)} %shard_map.135), channel_id=1, source_target_pairs={{0,2},{1,3},{2,0},{3,1},{4,6},{5,7},{6,4},{7,5},{8,10},{9,11},{10,... | collective-permute-start | bytes 49160 | tf_op jit(solution)/shard_map/ppermute | solution.py:450
  35.3 4.6 %collective-permute-start.13 = (f32[32,128]{1,0:T(8,128)S(1)}, f32[32,128]{1,0:T(8,128)S(1)}, u32[]{:S(2)}, u32[]{:S(2)}) collective-permute-start(f32[32,128]{1,0:T(8,128)S(1)} %shard_map.135), channel_id=1, source_target_pairs={{0,1},{1,0},{2,3},{3,2},{4,5},{5,4},{6,7},{7,6},{8,9},{9,8},{10,11... | collective-permute-start | bytes 49160 | tf_op jit(solution)/shard_map/ppermute | solution.py:450

commit v11 on v10

--- a/solution.py
+++ b/solution.py
@@ -118,8 +118,8 @@
     eye = iota((vesicles, vesicles), 0) == iota((vesicles, vesicles), 1)
     bend = jnp.sum(jnp.where(eye, bend_ref[...], 0.0), axis=1, keepdims=True)
     bend = jnp.concatenate([bend] * 2, axis=0)
-    slope = dot(rows, deriv, precision=HIGHEST)
-    fourth = dot(rows, table_ref[...], precision=HIGHEST)
+    both = dot(rows, jnp.concatenate([deriv, table_ref[...]], axis=1), precision=HIGHEST)
+    slope, fourth = both[:, :rows.shape[1]], both[:, rows.shape[1]:]
     force = dot(tension * slope, deriv, precision=HIGHEST) - bend * fourth
     force_x, force_y = force[:vesicles], force[vesicles:]
     force_ref[pl.ds(0, vesicles, stride=2), :] = force_x
@@ -305,7 +305,7 @@
             total = part if total is None else total + part
         return total
 
-    many = math.gcd(vesicles, 8)
+    many = math.gcd(vesicles, 16)
 
     def group_gram(v):
         both = jnp.concatenate([

time: 43.6 us -> 43.7 us (level)
  transfers between devices with their start and end apart: 16 -> 16, of which waited for: 4 -> 4; matrix products, arithmetic and copies ran while one was open for 0% -> 0% of each run, Pallas kernels for 36% -> 37%
where the time goes in v11:
time: 43.7 us; the launch traced here: 43.4 us
  Pallas kernels  20.3 us (46%)
  starting transfers between devices  18 us (41%)
  waiting for transfers between devices  4.39 us (10%)
  between operations  0.76 us (2%)
    pallas_call x1, Pallas kernels, per_device(): pl.pallas_call(functools.partial(far_kernel, col_count), out_shape=[jax.S...  8.63 us
    ppermute x7, starting transfers between devices, sum_over(): lax.ppermute(value, axis, partners(count, k))  7.95 us
    ppermute x3, starting transfers between devices, per_device(): lax.ppermute(sent, 'col', partners(col_count, k))  5.76 us
    pallas_call x2, Pallas kernels, near_part(): pl.pallas_call(functools.partial(near_kernel, slot_cap, len(pieces)), out...  5.17 us
    pallas_call x1, Pallas kernels, per_device(): pl.pallas_call(functools.partial(basis_kernel, scale_factor, groups), out...  3.42 us
    ppermute x3, starting transfers between devices, cube_exchange(): held.append(lax.ppermute(leaving, axis, partners(count, bit)))  3.21 us
    ppermute x3, waiting for transfers between devices, per_device(): lax.ppermute(sent, 'col', partners(col_count, k))  2.51 us
    pallas_call x1, Pallas kernels, per_device(): pl.pallas_call(functools.partial(force_kernel, clu_count), out_shape=[jax...  2.09 us
  transfers between devices with their start and end apart: 16, of which 4 were waited for; matrix products, arithmetic and copies ran while one was open for 0% of the time, Pallas kernels for 37%

profile of v11, /device:TPU:0, one launch (start us, length us, event | category | flops | bytes accessed | tf_op | source)
XLA Modules:
  0.0 43.4 jit_solution(100783655125684818)
XLA Ops:
  0.6 0.9 %shard_map.133 = bf16[272,128]{1,0:T(8,128)(2,1)S(1)} custom-call(bf16[128,512]{1,0:T(8,128)(2,1)} %own_in.3, bf16[2,512]{1,0:T(2,128)(2,1)} %nodes_in.3), custom_call_target="tpu_custom_call" | custom-call | flops 100000 | bytes 100000 | tf_op jit(solution)/shard_map/pallas_call | solution.py:473
  1.6 5.1 %collective-permute-start.7 = (bf16[272,128]{1,0:T(8,128)(2,1)S(1)}, bf16[272,128]{1,0:T(8,128)(2,1)S(1)}, u32[]{:S(2)}, u32[]{:S(2)}) collective-permute-start(bf16[272,128]{1,0:T(8,128)(2,1)S(1)} %shard_map.133), channel_id=1, source_target_pairs={{0,3},{1,2},{2,1},{3,0},{4,7},{5,6},{6,5},{7,4},{8,11},{9,10},{10,... | collective-permute-start | bytes 208904 | tf_op jit(solution)/shard_map/ppermute | solution.py:500
  6.7 0.6 %collective-permute-start.3 = (bf16[272,128]{1,0:T(8,128)(2,1)S(1)}, bf16[272,128]{1,0:T(8,128)(2,1)S(1)}, u32[]{:S(2)}, u32[]{:S(2)}) collective-permute-start(bf16[272,128]{1,0:T(8,128)(2,1)S(1)} %shard_map.133), channel_id=1, source_target_pairs={{0,1},{1,0},{2,3},{3,2},{4,5},{5,4},{6,7},{7,6},{8,9},{9,8},{10,11... | collective-permute-start | bytes 208904 | tf_op jit(solution)/shard_map/ppermute | solution.py:500
  7.3 2.1 %shard_map.130 = (f32[64,128]{1,0:T(8,128)}, f32[4,8,640]{2,1,0:T(8,128)S(1)}, f32[4,8,640]{2,1,0:T(8,128)S(1)}) custom-call(f32[64,128]{1,0:T(8,128)} %bitcast.33, f32[32,128]{1,0:T(8,128)} %refs_1_.1, f32[1,32]{1,0:T(1,128)} %bitcast.42, s32[1,32]{1,0:T(1,128)} %refs_3_.1, s32[1,24]{1,0:T(1,128)} %bitcast.43, s32[1,24]{1,0:T(1,128)} %bitcast.44, ...), custom_call_target="tpu_custom_call" | custom-call | flops 100000000 | bytes 1000000 | tf_op jit(solution)/shard_map/pallas_call | solution.py:488
  9.4 0.1 collective-permute-start
  9.5 0.0 collective-permute-done.7.refs_4_
  9.6 0.5 %collective-permute-start.8 = (bf16[272,128]{1,0:T(8,128)(2,1)S(1)}, bf16[272,128]{1,0:T(8,128)(2,1)S(1)}, u32[]{:S(2)}, u32[]{:S(2)}) collective-permute-start(bf16[272,128]{1,0:T(8,128)(2,1)S(1)} %collective-permute-done.7.refs_4_), channel_id=1, source_target_pairs={{0,4},{4,0},{8,12},{12,8},{16,20},{20,16},{24,28},{28,24},{1,5},{5... | collective-permute-start | bytes 208904 | tf_op jit(solution)/shard_map/ppermute | solution.py:504
  10.1 2.5 %collective-permute-done.5.refs_2_ = bf16[272,128]{1,0:T(8,128)(2,1)S(1)} collective-permute-done((bf16[272,128]{1,0:T(8,128)(2,1)S(1)}, bf16[272,128]{1,0:T(8,128)(2,1)S(1)}, u32[]{:S(2)}, u32[]{:S(2)}) %collective-permute-start.5) | collective-permute-done | bytes 69664 | tf_op jit(solution)/shard_map/ppermute | solution.py:500
  12.6 0.0 collective-permute-start.6
  12.6 0.0 collective-permute-done.3.refs_0_
  12.6 0.5 %collective-permute-start.4 = (bf16[272,128]{1,0:T(8,128)(2,1)S(1)}, bf16[272,128]{1,0:T(8,128)(2,1)S(1)}, u32[]{:S(2)}, u32[]{:S(2)}) collective-permute-start(bf16[272,128]{1,0:T(8,128)(2,1)S(1)} %collective-permute-done.3.refs_0_), channel_id=1, source_target_pairs={{0,4},{4,0},{8,12},{12,8},{16,20},{20,16},{24,28},{28,24},{1,5},{5... | collective-permute-start | bytes 208904 | tf_op jit(solution)/shard_map/ppermute | solution.py:504
  13.1 0.0 collective-permute-done
  13.1 1.6 %collective-permute-start.1 = (f32[4,8,640]{2,1,0:T(8,128)S(1)}, f32[4,8,640]{2,1,0:T(8,128)S(1)}, u32[]{:S(2)}, u32[]{:S(2)}) collective-permute-start(f32[4,8,640]{2,1,0:T(8,128)S(1)} %pad_maximum_fusion), channel_id=1, source_target_pairs={{0,8},{4,12},{8,0},{12,4},{16,24},{20,28},{24,16},{28,20},{1,9},{5... | collective-permute-start | bytes 245768 | tf_op jit(solution)/shard_map/ppermute | solution.py:93
  14.7 0.0 collective-permute-done.8.refs_5_
  14.7 0.0 collective-permute-done.6.refs_3_
  14.7 0.0 copy-start
  14.7 8.6 %shard_map.134 = (bf16[32,64,256]{2,1,0:T(8,128)(2,1)S(1)}, bf16[32,64,256]{2,1,0:T(8,128)(2,1)S(1)}, f32[32,128]{1,0:T(8,128)S(1)}) custom-call(s32[1,32]{1,0:T(1,128)} %bitcast.45, f32[64,128]{1,0:T(8,128)} %bitcast.34, bf16[128,512]{1,0:T(8,128)(2,1)} %own_in.3, bf16[2,512]{1,0:T(2,128)(2,1)} %nodes_in.3, ...), custom_call_target="tpu_custom_call" | custom-call | flops 10000000000 | bytes 10000000 | tf_op jit(solution)/shard_map/pallas_call | solution.py:509
  23.4 0.1 collective-permute-start.9
  23.4 1.2 %collective-permute-done.9 = f32[32,128]{1,0:T(8,128)S(1)} collective-permute-done((f32[32,128]{1,0:T(8,128)S(1)}, f32[32,128]{1,0:T(8,128)S(1)}, u32[]{:S(2)}, u32[]{:S(2)}) %collective-permute-start.9) | collective-permute-done | bytes 16416 | tf_op jit(solution)/shard_map/ppermute | solution.py:450
  24.6 1.8 %collective-permute-start.12 = (f32[32,128]{1,0:T(8,128)S(1)}, f32[32,128]{1,0:T(8,128)S(1)}, u32[]{:S(2)}, u32[]{:S(2)}) collective-permute-start(f32[32,128]{1,0:T(8,128)S(1)} %add.12.refs_0_), channel_id=1, source_target_pairs={{0,24},{4,28},{8,16},{12,20},{16,8},{20,12},{24,0},{28,4},{1,25},{... | collective-permute-start | bytes 49160 | tf_op jit(solution)/shard_map/ppermute | solution.py:450
  26.4 0.5 %collective-permute-start.11 = (f32[32,128]{1,0:T(8,128)S(1)}, f32[32,128]{1,0:T(8,128)S(1)}, u32[]{:S(2)}, u32[]{:S(2)}) collective-permute-start(f32[32,128]{1,0:T(8,128)S(1)} %add.12.refs_0_), channel_id=1, source_target_pairs={{0,16},{4,20},{8,24},{12,28},{16,0},{20,4},{24,8},{28,12},{1,17},{... | collective-permute-start | bytes 49160 | tf_op jit(solution)/shard_map/ppermute | solution.py:450
  26.9 1.2 %collective-permute-start.10 = (f32[32,128]{1,0:T(8,128)S(1)}, f32[32,128]{1,0:T(8,128)S(1)}, u32[]{:S(2)}, u32[]{:S(2)}) collective-permute-start(f32[32,128]{1,0:T(8,128)S(1)} %add.12.refs_0_), channel_id=1, source_target_pairs={{0,8},{4,12},{8,0},{12,4},{16,24},{20,28},{24,16},{28,20},{1,9},{5... | collective-permute-start | bytes 49160 | tf_op jit(solution)/shard_map/ppermute | solution.py:450
  28.1 0.0 collective-permute-done.1
  28.1 1.6 %collective-permute-start.2 = (f32[4,8,640]{2,1,0:T(8,128)S(1)}, f32[4,8,640]{2,1,0:T(8,128)S(1)}, u32[]{:S(2)}, u32[]{:S(2)}) collective-permute-start(f32[4,8,640]{2,1,0:T(8,128)S(1)} %pad_maximum_fusion.1), channel_id=1, source_target_pairs={{0,16},{4,20},{8,24},{12,28},{16,0},{20,4},{24,8},{28,12},{1,17},{... | collective-permute-start | bytes 245768 | tf_op jit(solution)/shard_map/ppermute | solution.py:93
  29.7 2.3 %shard_map.131.refs_1_.refs_4_ = f32[64,128]{1,0:T(8,128)S(1)} custom-call(f32[64,128]{1,0:T(8,128)S(1)} %bitcast.35, f32[1,8,640]{2,1,0:T(8,128)S(1)} %get-tuple-element.19.refs_0_, f32[1,8,640]{2,1,0:T(8,128)S(1)} %get-tuple-element.17.refs_1_, f32[2,8,640]{2,1,0:T(8,128)S(1)} %get-tuple-element.15.refs_2_), custom_call_target="tpu_custom_call" | custom-call | flops 1000000000 | bytes 10000000 | tf_op jit(solution)/shard_map/pallas_call | solution.py:228
  32.0 0.0 collective-permute-done.11.refs_2_
  32.0 0.6 %collective-permute-done.2.refs_0_.refs_5_ = f32[4,8,640]{2,1,0:T(8,128)S(1)} collective-permute-done((f32[4,8,640]{2,1,0:T(8,128)S(1)}, f32[4,8,640]{2,1,0:T(8,128)S(1)}, u32[]{:S(2)}, u32[]{:S(2)}) %collective-permute-start.2) | collective-permute-done | bytes 81952 | tf_op jit(solution)/shard_map/ppermute | solution.py:93
  32.6 2.7 %collective-permute-start.15 = (f32[32,128]{1,0:T(8,128)S(1)}, f32[32,128]{1,0:T(8,128)S(1)}, u32[]{:S(2)}, u32[]{:S(2)}) collective-permute-start(f32[32,128]{1,0:T(8,128)S(1)} %shard_map.135), channel_id=1, source_target_pairs={{0,3},{1,2},{2,1},{3,0},{4,7},{5,6},{6,5},{7,4},{8,11},{9,10},{10,... | collective-permute-start | bytes 49160 | tf_op jit(solution)/shard_map/ppermute | solution.py:450
  35.4 1.7 %collective-permute-start.13 = (f32[32,128]{1,0:T(8,128)S(1)}, f32[32,128]{1,0:T(8,128)S(1)}, u32[]{:S(2)}, u32[]{:S(2)}) collective-permute-start(f32[32,128]{1,0:T(8,128)S(1)} %shard_map.135), channel_id=1, source_target_pairs={{0,1},{1,0},{2,3},{3,2},{4,5},{5,4},{6,7},{7,6},{8,9},{9,8},{10,11... | collective-permute-start | bytes 49160 | tf_op jit(solution)/shard_map/ppermute | solution.py:450
  37.0 2.9 %shard_map.132._ = f32[64,128]{1,0:T(8,128)} custom-call(f32[64,128]{1,0:T(8,128)S(1)} %bitcast.36, f32[4,8,640]{2,1,0:T(8,128)S(1)} %collective-permute-done.2.refs_0_.refs_5_, f32[64,128]{1,0:T(8,128)S(1)} %shard_map.131.refs_1_.refs_4_), custom_call_target="tpu_custom_call" | custom-call | flops 1000000000 | bytes 10000000 | tf_op jit(solution)/shard_map/pallas_call | solution.py:228
  39.9 0.1 collective-permute-done.14
  40.0 3.4 %shard_map.136 = f32[32,128,128]{2,1,0:T(8,128)} custom-call(f32[32,128]{1,0:T(8,128)S(1)} %add_add_fusion.gram_ref, bf16[32,64,256]{2,1,0:T(8,128)(2,1)S(1)} %get-tuple-element.13.high_ref, bf16[32,64,256]{2,1,0:T(8,128)(2,1)S(1)} %get-tuple-element.14.low_ref, f32[64,128]{1,0:T(8,128)} %shard_map.132._), custom_call_target="tpu_custom_call" | custom-call | flops 1000000000 | bytes 10000000 | tf_op jit(solution)/shard_map/pallas_call | solution.py:533
  (18 shorter events, 0.1 us)
Async XLA Ops:
  1.6 8.0 %collective-permute-start.7 = (bf16[272,128]{1,0:T(8,128)(2,1)S(1)}, bf16[272,128]{1,0:T(8,128)(2,1)S(1)}, u32[]{:S(2)}, u32[]{:S(2)}) collective-permute-start(bf16[272,128]{1,0:T(8,128)(2,1)S(1)} %shard_map.133), channel_id=1, source_target_pairs={{0,3},{1,2},{2,1},{3,0},{4,7},{5,6},{6,5},{7,4},{8,11},{9,10},{10,... | collective-permute-start | bytes 208904 | tf_op jit(solution)/shard_map/ppermute | solution.py:500
  6.7 5.9 %collective-permute-start.5 = (bf16[272,128]{1,0:T(8,128)(2,1)S(1)}, bf16[272,128]{1,0:T(8,128)(2,1)S(1)}, u32[]{:S(2)}, u32[]{:S(2)}) collective-permute-start(bf16[272,128]{1,0:T(8,128)(2,1)S(1)} %shard_map.133), channel_id=1, source_target_pairs={{0,2},{1,3},{2,0},{3,1},{4,6},{5,7},{6,4},{7,5},{8,10},{9,11},{10,... | collective-permute-start | bytes 208904 | tf_op jit(solution)/shard_map/ppermute | solution.py:500
  6.7 5.9 %collective-permute-start.3 = (bf16[272,128]{1,0:T(8,128)(2,1)S(1)}, bf16[272,128]{1,0:T(8,128)(2,1)S(1)}, u32[]{:S(2)}, u32[]{:S(2)}) collective-permute-start(bf16[272,128]{1,0:T(8,128)(2,1)S(1)} %shard_map.133), channel_id=1, source_target_pairs={{0,1},{1,0},{2,3},{3,2},{4,5},{5,4},{6,7},{7,6},{8,9},{9,8},{10,11... | collective-permute-start | bytes 208904 | tf_op jit(solution)/shard_map/ppermute | solution.py:500
  9.4 3.7 %collective-permute-start = (f32[4,8,640]{2,1,0:T(8,128)S(1)}, f32[4,8,640]{2,1,0:T(8,128)S(1)}, u32[]{:S(2)}, u32[]{:S(2)}) collective-permute-start(f32[4,8,640]{2,1,0:T(8,128)S(1)} %get-tuple-element.11), channel_id=1, source_target_pairs={{0,4},{4,0},{8,12},{12,8},{16,20},{20,16},{24,28},{28,24},{1,5},{5... | collective-permute-start | bytes 245768 | tf_op jit(solution)/shard_map/ppermute | solution.py:93
  9.6 5.1 %collective-permute-start.8 = (bf16[272,128]{1,0:T(8,128)(2,1)S(1)}, bf16[272,128]{1,0:T(8,128)(2,1)S(1)}, u32[]{:S(2)}, u32[]{:S(2)}) collective-permute-start(bf16[272,128]{1,0:T(8,128)(2,1)S(1)} %collective-permute-done.7.refs_4_), channel_id=1, source_target_pairs={{0,4},{4,0},{8,12},{12,8},{16,20},{20,16},{24,28},{28,24},{1,5},{5... | collective-permute-start | bytes 208904 | tf_op jit(solution)/shard_map/ppermute | solution.py:504
  12.6 2.1 %collective-permute-start.6 = (bf16[272,128]{1,0:T(8,128)(2,1)S(1)}, bf16[272,128]{1,0:T(8,128)(2,1)S(1)}, u32[]{:S(2)}, u32[]{:S(2)}) collective-permute-start(bf16[272,128]{1,0:T(8,128)(2,1)S(1)} %collective-permute-done.5.refs_2_), channel_id=1, source_target_pairs={{0,4},{4,0},{8,12},{12,8},{16,20},{20,16},{24,28},{28,24},{1,5},{5... | collective-permute-start | bytes 208904 | tf_op jit(solution)/shard_map/ppermute | solution.py:504
  12.6 2.1 %collective-permute-start.4 = (bf16[272,128]{1,0:T(8,128)(2,1)S(1)}, bf16[272,128]{1,0:T(8,128)(2,1)S(1)}, u32[]{:S(2)}, u32[]{:S(2)}) collective-permute-start(bf16[272,128]{1,0:T(8,128)(2,1)S(1)} %collective-permute-done.3.refs_0_), channel_id=1, source_target_pairs={{0,4},{4,0},{8,12},{12,8},{16,20},{20,16},{24,28},{28,24},{1,5},{5... | collective-permute-start | bytes 208904 | tf_op jit(solution)/shard_map/ppermute | solution.py:504
  13.1 15.0 %collective-permute-start.1 = (f32[4,8,640]{2,1,0:T(8,128)S(1)}, f32[4,8,640]{2,1,0:T(8,128)S(1)}, u32[]{:S(2)}, u32[]{:S(2)}) collective-permute-start(f32[4,8,640]{2,1,0:T(8,128)S(1)} %pad_maximum_fusion), channel_id=1, source_target_pairs={{0,8},{4,12},{8,0},{12,4},{16,24},{20,28},{24,16},{28,20},{1,9},{5... | collective-permute-start | bytes 245768 | tf_op jit(solution)/shard_map/ppermute | solution.py:93
  14.7 15.0 %copy-start = (f32[32,2,128]{2,1,0:T(2,128)S(1)}, f32[32,2,128]{2,1,0:T(2,128)}, u32[]{:S(2)}) copy-start(f32[32,2,128]{2,1,0:T(2,128)} %param.11) | copy-start | bytes 98308
  23.4 1.2 %collective-permute-start.9 = (f32[32,128]{1,0:T(8,128)S(1)}, f32[32,128]{1,0:T(8,128)S(1)}, u32[]{:S(2)}, u32[]{:S(2)}) collective-permute-start(f32[32,128]{1,0:T(8,128)S(1)} %get-tuple-element.12), channel_id=1, source_target_pairs={{0,4},{4,0},{8,12},{12,8},{16,20},{20,16},{24,28},{28,24},{1,5},{5... | collective-permute-start | bytes 49160 | tf_op jit(solution)/shard_map/ppermute | solution.py:450
  24.6 7.4 %collective-permute-start.12 = (f32[32,128]{1,0:T(8,128)S(1)}, f32[32,128]{1,0:T(8,128)S(1)}, u32[]{:S(2)}, u32[]{:S(2)}) collective-permute-start(f32[32,128]{1,0:T(8,128)S(1)} %add.12.refs_0_), channel_id=1, source_target_pairs={{0,24},{4,28},{8,16},{12,20},{16,8},{20,12},{24,0},{28,4},{1,25},{... | collective-permute-start | bytes 49160 | tf_op jit(solution)/shard_map/ppermute | solution.py:450
  26.4 5.6 %collective-permute-start.11 = (f32[32,128]{1,0:T(8,128)S(1)}, f32[32,128]{1,0:T(8,128)S(1)}, u32[]{:S(2)}, u32[]{:S(2)}) collective-permute-start(f32[32,128]{1,0:T(8,128)S(1)} %add.12.refs_0_), channel_id=1, source_target_pairs={{0,16},{4,20},{8,24},{12,28},{16,0},{20,4},{24,8},{28,12},{1,17},{... | collective-permute-start | bytes 49160 | tf_op jit(solution)/shard_map/ppermute | solution.py:450
  26.9 5.1 %collective-permute-start.10 = (f32[32,128]{1,0:T(8,128)S(1)}, f32[32,128]{1,0:T(8,128)S(1)}, u32[]{:S(2)}, u32[]{:S(2)}) collective-permute-start(f32[32,128]{1,0:T(8,128)S(1)} %add.12.refs_0_), channel_id=1, source_target_pairs={{0,8},{4,12},{8,0},{12,4},{16,24},{20,28},{24,16},{28,20},{1,9},{5... | collective-permute-start | bytes 49160 | tf_op jit(solution)/shard_map/ppermute | solution.py:450
  28.1 4.5 %collective-permute-start.2 = (f32[4,8,640]{2,1,0:T(8,128)S(1)}, f32[4,8,640]{2,1,0:T(8,128)S(1)}, u32[]{:S(2)}, u32[]{:S(2)}) collective-permute-start(f32[4,8,640]{2,1,0:T(8,128)S(1)} %pad_maximum_fusion.1), channel_id=1, source_target_pairs={{0,16},{4,20},{8,24},{12,28},{16,0},{20,4},{24,8},{28,12},{1,17},{... | collective-permute-start | bytes 245768 | tf_op jit(solution)/shard_map/ppermute | solution.py:93
  32.6 7.3 %collective-permute-start.15 = (f32[32,128]{1,0:T(8,128)S(1)}, f32[32,128]{1,0:T(8,128)S(1)}, u32[]{:S(2)}, u32[]{:S(2)}) collective-permute-start(f32[32,128]{1,0:T(8,128)S(1)} %shard_map.135), channel_id=1, source_target_pairs={{0,3},{1,2},{2,1},{3,0},{4,7},{5,6},{6,5},{7,4},{8,11},{9,10},{10,... | collective-permute-start | bytes 49160 | tf_op jit(solution)/shard_map/ppermute | solution.py:450
  35.4 4.6 %collective-permute-start.14 = (f32[32,128]{1,0:T(8,128)S(1)}, f32[32,128]{1,0:T(8,128)S(1)}, u32[]{:S(2)}, u32[]{:S(2)}) collective-permute-start(f32[32,128]{1,0:T(8,128)S(1)} %shard_map.135), channel_id=1, source_target_pairs={{0,2},{1,3},{2,0},{3,1},{4,6},{5,7},{6,4},{7,5},{8,10},{9,11},{10,... | collective-permute-start | bytes 49160 | tf_op jit(solution)/shard_map/ppermute | solution.py:450
  35.4 4.6 %collective-permute-start.13 = (f32[32,128]{1,0:T(8,128)S(1)}, f32[32,128]{1,0:T(8,128)S(1)}, u32[]{:S(2)}, u32[]{:S(2)}) collective-permute-start(f32[32,128]{1,0:T(8,128)S(1)} %shard_map.135), channel_id=1, source_target_pairs={{0,1},{1,0},{2,3},{3,2},{4,5},{5,4},{6,7},{7,6},{8,9},{9,8},{10,11... | collective-permute-start | bytes 49160 | tf_op jit(solution)/shard_map/ppermute | solution.py:450

commit v12 on v10

--- a/solution.py
+++ b/solution.py
@@ -14,6 +14,7 @@
 BF16 = jnp.bfloat16
 HIGHEST = lax.Precision.HIGHEST
 BLOCK = 8
+DEPTH = 16
 MIB = 1 << 20
 
 NT = (((1,), (1,)), ((), ()))
@@ -238,11 +239,49 @@
     )(flat, *pieces, *before)
 
 
+def parts_of(value, count):
+    parts = []
+    for _ in range(count):
+        part = value.astype(BF16).astype(F32)
+        parts.append(part)
+        value = value - part
+    return parts
+
+
+def source_powers(sx, sy):
+    one = jnp.ones_like(sx)
+    rows = [sx] * 3 + [sy] * 3 + [one] * 3
+    for value in (sx * sx, sy * sy, sx * sy):
+        rows += parts_of(value, 2)
+    return jnp.concatenate(rows + [jnp.zeros_like(sx)], axis=0)
+
+
+def target_factors(pos_ref, factors):
+    vesicles, nodes = pos_ref.shape[0] // 2, pos_ref.shape[1]
+    x = pos_ref[pl.ds(0, vesicles, stride=2), :]
+    y = pos_ref[pl.ds(1, vesicles, stride=2), :]
+    zero = jnp.zeros_like(x)
+    wanted = [
+        (-2.0 * x, -2.0 * y, x * x + y * y + EPS_SQUARED, 1.0, 1.0, 0.0),
+        (4.0 * x, zero, -2.0 * (x * x), -2.0, 0.0, 0.0),
+        (2.0 * y, 2.0 * x, -2.0 * (x * y), 0.0, 0.0, -2.0),
+        (zero, 4.0 * y, -2.0 * (y * y), 0.0, -2.0, 0.0),
+    ]
+    for c, entries in enumerate(wanted):
+        rows = []
+        for value in entries[:3]:
+            rows += parts_of(value, 3)
+        for value in entries[3:]:
+            rows += [jnp.full_like(x, value)] * 2
+        for k, row in enumerate(rows + [zero]):
+            factors[c, pl.ds(k, vesicles, stride=DEPTH), :] = row
+
+
 def far_kernel(col_count, range_in, pos_in, own_in, nodes_in, *refs):
     count = 2 * (col_count - 1)
     piece_refs = refs[:count]
-    (high_ref, low_ref, gram_ref, range_ref, pos_ref, own_nodes, own_rows, basis, spots, wide,
-     sums, sems) = refs[count:]
+    (high_ref, low_ref, gram_ref, range_ref, pos_ref, own_nodes, own_rows, basis, spots, powers,
+     factors, sums, sems) = refs[count:]
     vesicles = pos_ref.shape[0] // 2
     nodes = pos_ref.shape[1]
     rank, sources = own_rows.shape[0] // 2, own_rows.shape[1]
@@ -251,9 +290,7 @@
     columns = sources // nodes
 
     def widen(r):
-        turned = spots[r].T
-        for c in range(2):
-            wide[r, c] = jnp.broadcast_to(turned[:, c:c + 1], (sources, nodes))
+        powers[r] = source_powers(spots[r, 0:1], spots[r, 1:2]).T.astype(BF16)
 
     def lay_out_received():
         for k in range(1, col_count):
@@ -275,23 +312,21 @@
     basis[col, :, sources:] = own_rows[rank:]
     spots[col, 0:2] = own_nodes[...].astype(F32)
     widen(col)
+    target_factors(pos_ref, factors)
     sums[...] = jnp.zeros_like(sums)
 
-    chunk = 32 if sources % 32 == 0 else sources
+    chunk = 64 if sources % 64 == 0 else sources
     depth = 256 if sources % 256 == 0 else sources
 
     def evaluate(v, start):
-        r = range_ref[0, v]
-        tx = pos_ref[pl.ds(2 * v, 1), :]
-        ty = pos_ref[pl.ds(2 * v + 1, 1), :]
-        dx = tx - wide[r, 0, start:start + chunk]
-        dy = ty - wide[r, 1, start:start + chunk]
-        xx, yy = dx * dx, dy * dy
-        spread = xx + yy + EPS_SQUARED
-        log_part = -0.5 * jnp.log(spread)
+        rows_here = pl.ds(pl.multiple_of(v * DEPTH, DEPTH), DEPTH)
+        mine = jnp.concatenate([factors[c, rows_here, :] for c in range(4)], axis=1).astype(BF16)
+        shape = dot(powers[range_ref[0, v], start:start + chunk], mine)
+        spread, xx, xy, yy = [shape[:, c * nodes:(c + 1) * nodes] for c in range(4)]
+        log_part = jnp.log(spread)
         inverse = reciprocal(spread)
-        return ((log_part + xx * inverse).astype(BF16), (dx * dy * inverse).astype(BF16),
-                (log_part + yy * inverse).astype(BF16))
+        return ((log_part + inverse * xx).astype(BF16), (inverse * xy).astype(BF16),
+                (log_part + inverse * yy).astype(BF16))
 
     def sketch(v):
         r = range_ref[0, v]
@@ -519,7 +554,8 @@
             pltpu.VMEM((rows, sources), BF16),
             pltpu.VMEM((col_count, rank, 2 * sources), BF16),
             pltpu.VMEM((col_count, 8, sources), F32),
-            pltpu.VMEM((col_count, 2, sources, nodes), F32),
+            pltpu.VMEM((col_count, sources, DEPTH), BF16),
+            pltpu.VMEM((4, vesicles * DEPTH, nodes), F32),
             pltpu.VMEM((rows, rows), F32),
             pltpu.SemaphoreType.DMA((4,))],
         compiler_params=params(32),
@@ -528,7 +564,7 @@
     gram = sum_over(gram, "clu", step_groups(clu_count, True), [near_first, arrived[-1]])
     gram = sum_over(gram, "col", step_groups(col_count, False))
 
-    scale_factor = math.sqrt(2.0 * nodes * vesicles * clu_count * col_count)
+    scale_factor = -math.sqrt(2.0 * nodes * vesicles * clu_count * col_count)
     groups = math.gcd(vesicles, 8)
     new_basis = pl.pallas_call(
         functools.partial(basis_kernel, scale_factor, groups),

time: 43.6 us -> 52.2 us (1.20)
  Pallas kernels: 20.2 us -> 28.8 us
    pallas_call x1, Pallas kernels: 8.6 us -> 17.2 us  [per_device(): pl.pallas_call(functools.partial(far_kernel, col_count), out_shape=[jax.S...]
  transfers between devices with their start and end apart: 16 -> 16, of which waited for: 4 -> 4; matrix products, arithmetic and copies ran while one was open for 0% -> 0% of each run, Pallas kernels for 36% -> 47%
where the time goes in v12:
time: 52.2 us; the launch traced here: 52 us
  Pallas kernels  28.8 us (55%)
  starting transfers between devices  18 us (34%)
  waiting for transfers between devices  4.41 us (8%)
  between operations  0.76 us (1%)
    pallas_call x1, Pallas kernels, per_device(): pl.pallas_call(functools.partial(far_kernel, col_count), out_shape=[jax.S...  17.2 us
    ppermute x7, starting transfers between devices, sum_over(): lax.ppermute(value, axis, partners(count, k))  7.95 us
    ppermute x3, starting transfers between devices, per_device(): lax.ppermute(sent, 'col', partners(col_count, k))  5.76 us
    pallas_call x2, Pallas kernels, near_part(): pl.pallas_call(functools.partial(near_kernel, slot_cap, len(pieces)), out...  5.17 us
    pallas_call x1, Pallas kernels, per_device(): pl.pallas_call(functools.partial(basis_kernel, scale_factor, groups), out...  3.42 us
    ppermute x3, starting transfers between devices, cube_exchange(): held.append(lax.ppermute(leaving, axis, partners(count, bit)))  3.21 us
    ppermute x3, waiting for transfers between devices, per_device(): lax.ppermute(sent, 'col', partners(col_count, k))  2.54 us
    pallas_call x1, Pallas kernels, per_device(): pl.pallas_call(functools.partial(force_kernel, clu_count), out_shape=[jax...  2.06 us
  transfers between devices with their start and end apart: 16, of which 4 were waited for; matrix products, arithmetic and copies ran while one was open for 0% of the time, Pallas kernels for 47%

profile of v12, /device:TPU:0, one launch (start us, length us, event | category | flops | bytes accessed | tf_op | source)
XLA Modules:
  0.0 52.0 jit_solution(16694428065239447676)
XLA Ops:
  0.6 0.9 %shard_map.133 = bf16[272,128]{1,0:T(8,128)(2,1)S(1)} custom-call(bf16[128,512]{1,0:T(8,128)(2,1)} %own_in.3, bf16[2,512]{1,0:T(2,128)(2,1)} %nodes_in.3), custom_call_target="tpu_custom_call" | custom-call | flops 100000 | bytes 100000 | tf_op jit(solution)/shard_map/pallas_call | solution.py:508
  1.6 5.1 %collective-permute-start.7 = (bf16[272,128]{1,0:T(8,128)(2,1)S(1)}, bf16[272,128]{1,0:T(8,128)(2,1)S(1)}, u32[]{:S(2)}, u32[]{:S(2)}) collective-permute-start(bf16[272,128]{1,0:T(8,128)(2,1)S(1)} %shard_map.133), channel_id=1, source_target_pairs={{0,3},{1,2},{2,1},{3,0},{4,7},{5,6},{6,5},{7,4},{8,11},{9,10},{10,... | collective-permute-start | bytes 208904 | tf_op jit(solution)/shard_map/ppermute | solution.py:535
  6.7 0.0 collective-permute-start.5
  6.7 0.6 %collective-permute-start.3 = (bf16[272,128]{1,0:T(8,128)(2,1)S(1)}, bf16[272,128]{1,0:T(8,128)(2,1)S(1)}, u32[]{:S(2)}, u32[]{:S(2)}) collective-permute-start(bf16[272,128]{1,0:T(8,128)(2,1)S(1)} %shard_map.133), channel_id=1, source_target_pairs={{0,1},{1,0},{2,3},{3,2},{4,5},{5,4},{6,7},{7,6},{8,9},{9,8},{10,11... | collective-permute-start | bytes 208904 | tf_op jit(solution)/shard_map/ppermute | solution.py:535
  7.3 2.1 %shard_map.130 = (f32[64,128]{1,0:T(8,128)}, f32[4,8,640]{2,1,0:T(8,128)S(1)}, f32[4,8,640]{2,1,0:T(8,128)S(1)}) custom-call(f32[64,128]{1,0:T(8,128)} %bitcast.33, f32[32,128]{1,0:T(8,128)} %refs_1_.1, f32[1,32]{1,0:T(1,128)} %bitcast.42, s32[1,32]{1,0:T(1,128)} %refs_3_.1, s32[1,24]{1,0:T(1,128)} %bitcast.43, s32[1,24]{1,0:T(1,128)} %bitcast.44, ...), custom_call_target="tpu_custom_call" | custom-call | flops 100000000 | bytes 1000000 | tf_op jit(solution)/shard_map/pallas_call | solution.py:523
  9.4 0.1 collective-permute-start
  9.5 0.5 %collective-permute-start.8 = (bf16[272,128]{1,0:T(8,128)(2,1)S(1)}, bf16[272,128]{1,0:T(8,128)(2,1)S(1)}, u32[]{:S(2)}, u32[]{:S(2)}) collective-permute-start(bf16[272,128]{1,0:T(8,128)(2,1)S(1)} %collective-permute-done.7.refs_4_), channel_id=1, source_target_pairs={{0,4},{4,0},{8,12},{12,8},{16,20},{20,16},{24,28},{28,24},{1,5},{5... | collective-permute-start | bytes 208904 | tf_op jit(solution)/shard_map/ppermute | solution.py:539
  10.1 2.5 %collective-permute-done.5.refs_2_ = bf16[272,128]{1,0:T(8,128)(2,1)S(1)} collective-permute-done((bf16[272,128]{1,0:T(8,128)(2,1)S(1)}, bf16[272,128]{1,0:T(8,128)(2,1)S(1)}, u32[]{:S(2)}, u32[]{:S(2)}) %collective-permute-start.5) | collective-permute-done | bytes 69664 | tf_op jit(solution)/shard_map/ppermute | solution.py:535
  12.6 0.5 collective-permute-start.4
  13.1 1.6 %collective-permute-start.1 = (f32[4,8,640]{2,1,0:T(8,128)S(1)}, f32[4,8,640]{2,1,0:T(8,128)S(1)}, u32[]{:S(2)}, u32[]{:S(2)}) collective-permute-start(f32[4,8,640]{2,1,0:T(8,128)S(1)} %pad_maximum_fusion), channel_id=1, source_target_pairs={{0,8},{4,12},{8,0},{12,4},{16,24},{20,28},{24,16},{28,20},{1,9},{5... | collective-permute-start | bytes 245768 | tf_op jit(solution)/shard_map/ppermute | solution.py:94
  14.7 0.0 collective-permute-done.8.refs_5_
  14.7 0.0 collective-permute-done.6.refs_3_
  14.7 0.0 collective-permute-done.4.refs_1_
  14.7 0.0 copy-start
  14.7 17.2 %shard_map.134 = (bf16[32,64,256]{2,1,0:T(8,128)(2,1)S(1)}, bf16[32,64,256]{2,1,0:T(8,128)(2,1)S(1)}, f32[32,128]{1,0:T(8,128)S(1)}) custom-call(s32[1,32]{1,0:T(1,128)} %bitcast.45, f32[64,128]{1,0:T(8,128)} %bitcast.34, bf16[128,512]{1,0:T(8,128)(2,1)} %own_in.3, bf16[2,512]{1,0:T(2,128)(2,1)} %nodes_in.3, ...), custom_call_target="tpu_custom_call" | custom-call | flops 10000000000 | bytes 10000000 | tf_op jit(solution)/shard_map/pallas_call | solution.py:544
  32.0 0.1 collective-permute-start.9
  32.1 1.2 %collective-permute-done.9 = f32[32,128]{1,0:T(8,128)S(1)} collective-permute-done((f32[32,128]{1,0:T(8,128)S(1)}, f32[32,128]{1,0:T(8,128)S(1)}, u32[]{:S(2)}, u32[]{:S(2)}) %collective-permute-start.9) | collective-permute-done | bytes 16416 | tf_op jit(solution)/shard_map/ppermute | solution.py:485
  33.2 1.8 %collective-permute-start.12 = (f32[32,128]{1,0:T(8,128)S(1)}, f32[32,128]{1,0:T(8,128)S(1)}, u32[]{:S(2)}, u32[]{:S(2)}) collective-permute-start(f32[32,128]{1,0:T(8,128)S(1)} %add.12.refs_0_), channel_id=1, source_target_pairs={{0,24},{4,28},{8,16},{12,20},{16,8},{20,12},{24,0},{28,4},{1,25},{... | collective-permute-start | bytes 49160 | tf_op jit(solution)/shard_map/ppermute | solution.py:485
  35.0 0.5 collective-permute-start.11
  35.5 1.2 %collective-permute-start.10 = (f32[32,128]{1,0:T(8,128)S(1)}, f32[32,128]{1,0:T(8,128)S(1)}, u32[]{:S(2)}, u32[]{:S(2)}) collective-permute-start(f32[32,128]{1,0:T(8,128)S(1)} %add.12.refs_0_), channel_id=1, source_target_pairs={{0,8},{4,12},{8,0},{12,4},{16,24},{20,28},{24,16},{28,20},{1,9},{5... | collective-permute-start | bytes 49160 | tf_op jit(solution)/shard_map/ppermute | solution.py:485
  36.7 0.0 collective-permute-done.1
  36.7 1.6 %collective-permute-start.2 = (f32[4,8,640]{2,1,0:T(8,128)S(1)}, f32[4,8,640]{2,1,0:T(8,128)S(1)}, u32[]{:S(2)}, u32[]{:S(2)}) collective-permute-start(f32[4,8,640]{2,1,0:T(8,128)S(1)} %pad_maximum_fusion.1), channel_id=1, source_target_pairs={{0,16},{4,20},{8,24},{12,28},{16,0},{20,4},{24,8},{28,12},{1,17},{... | collective-permute-start | bytes 245768 | tf_op jit(solution)/shard_map/ppermute | solution.py:94
  38.3 2.3 %shard_map.131.refs_1_.refs_4_ = f32[64,128]{1,0:T(8,128)S(1)} custom-call(f32[64,128]{1,0:T(8,128)S(1)} %bitcast.35, f32[1,8,640]{2,1,0:T(8,128)S(1)} %get-tuple-element.19.refs_0_, f32[1,8,640]{2,1,0:T(8,128)S(1)} %get-tuple-element.17.refs_1_, f32[2,8,640]{2,1,0:T(8,128)S(1)} %get-tuple-element.15.refs_2_), custom_call_target="tpu_custom_call" | custom-call | flops 1000000000 | bytes 10000000 | tf_op jit(solution)/shard_map/pallas_call | solution.py:229
  40.6 0.0 collective-permute-done.11.refs_2_
  40.6 0.0 collective-permute-done.10.refs_1_
  40.6 0.6 %collective-permute-done.2.refs_0_.refs_5_ = f32[4,8,640]{2,1,0:T(8,128)S(1)} collective-permute-done((f32[4,8,640]{2,1,0:T(8,128)S(1)}, f32[4,8,640]{2,1,0:T(8,128)S(1)}, u32[]{:S(2)}, u32[]{:S(2)}) %collective-permute-start.2) | collective-permute-done | bytes 81952 | tf_op jit(solution)/shard_map/ppermute | solution.py:94
  41.3 2.7 %collective-permute-start.15 = (f32[32,128]{1,0:T(8,128)S(1)}, f32[32,128]{1,0:T(8,128)S(1)}, u32[]{:S(2)}, u32[]{:S(2)}) collective-permute-start(f32[32,128]{1,0:T(8,128)S(1)} %shard_map.135), channel_id=1, source_target_pairs={{0,3},{1,2},{2,1},{3,0},{4,7},{5,6},{6,5},{7,4},{8,11},{9,10},{10,... | collective-permute-start | bytes 49160 | tf_op jit(solution)/shard_map/ppermute | solution.py:485
  44.0 0.0 collective-permute-start.14
  44.0 1.7 %collective-permute-start.13 = (f32[32,128]{1,0:T(8,128)S(1)}, f32[32,128]{1,0:T(8,128)S(1)}, u32[]{:S(2)}, u32[]{:S(2)}) collective-permute-start(f32[32,128]{1,0:T(8,128)S(1)} %shard_map.135), channel_id=1, source_target_pairs={{0,1},{1,0},{2,3},{3,2},{4,5},{5,4},{6,7},{7,6},{8,9},{9,8},{10,11... | collective-permute-start | bytes 49160 | tf_op jit(solution)/shard_map/ppermute | solution.py:485
  45.7 2.9 %shard_map.132._ = f32[64,128]{1,0:T(8,128)} custom-call(f32[64,128]{1,0:T(8,128)S(1)} %bitcast.36, f32[4,8,640]{2,1,0:T(8,128)S(1)} %collective-permute-done.2.refs_0_.refs_5_, f32[64,128]{1,0:T(8,128)S(1)} %shard_map.131.refs_1_.refs_4_), custom_call_target="tpu_custom_call" | custom-call | flops 1000000000 | bytes 10000000 | tf_op jit(solution)/shard_map/pallas_call | solution.py:229
  48.6 0.1 collective-permute-done.14
  48.6 3.4 %shard_map.136 = f32[32,128,128]{2,1,0:T(8,128)} custom-call(f32[32,128]{1,0:T(8,128)S(1)} %add_add_fusion.gram_ref, bf16[32,64,256]{2,1,0:T(8,128)(2,1)S(1)} %get-tuple-element.13.high_ref, bf16[32,64,256]{2,1,0:T(8,128)(2,1)S(1)} %get-tuple-element.14.low_ref, f32[64,128]{1,0:T(8,128)} %shard_map.132._), custom_call_target="tpu_custom_call" | custom-call | flops 1000000000 | bytes 10000000 | tf_op jit(solution)/shard_map/pallas_call | solution.py:569
  (18 shorter events, 0.1 us)
Async XLA Ops:
  1.6 7.9 %collective-permute-start.7 = (bf16[272,128]{1,0:T(8,128)(2,1)S(1)}, bf16[272,128]{1,0:T(8,128)(2,1)S(1)}, u32[]{:S(2)}, u32[]{:S(2)}) collective-permute-start(bf16[272,128]{1,0:T(8,128)(2,1)S(1)} %shard_map.133), channel_id=1, source_target_pairs={{0,3},{1,2},{2,1},{3,0},{4,7},{5,6},{6,5},{7,4},{8,11},{9,10},{10,... | collective-permute-start | bytes 208904 | tf_op jit(solution)/shard_map/ppermute | solution.py:535
  6.7 5.9 %collective-permute-start.5 = (bf16[272,128]{1,0:T(8,128)(2,1)S(1)}, bf16[272,128]{1,0:T(8,128)(2,1)S(1)}, u32[]{:S(2)}, u32[]{:S(2)}) collective-permute-start(bf16[272,128]{1,0:T(8,128)(2,1)S(1)} %shard_map.133), channel_id=1, source_target_pairs={{0,2},{1,3},{2,0},{3,1},{4,6},{5,7},{6,4},{7,5},{8,10},{9,11},{10,... | collective-permute-start | bytes 208904 | tf_op jit(solution)/shard_map/ppermute | solution.py:535
  6.7 5.9 %collective-permute-start.3 = (bf16[272,128]{1,0:T(8,128)(2,1)S(1)}, bf16[272,128]{1,0:T(8,128)(2,1)S(1)}, u32[]{:S(2)}, u32[]{:S(2)}) collective-permute-start(bf16[272,128]{1,0:T(8,128)(2,1)S(1)} %shard_map.133), channel_id=1, source_target_pairs={{0,1},{1,0},{2,3},{3,2},{4,5},{5,4},{6,7},{7,6},{8,9},{9,8},{10,11... | collective-permute-start | bytes 208904 | tf_op jit(solution)/shard_map/ppermute | solution.py:535
  9.4 3.7 %collective-permute-start = (f32[4,8,640]{2,1,0:T(8,128)S(1)}, f32[4,8,640]{2,1,0:T(8,128)S(1)}, u32[]{:S(2)}, u32[]{:S(2)}) collective-permute-start(f32[4,8,640]{2,1,0:T(8,128)S(1)} %get-tuple-element.11), channel_id=1, source_target_pairs={{0,4},{4,0},{8,12},{12,8},{16,20},{20,16},{24,28},{28,24},{1,5},{5... | collective-permute-start | bytes 245768 | tf_op jit(solution)/shard_map/ppermute | solution.py:94
  9.5 5.2 %collective-permute-start.8 = (bf16[272,128]{1,0:T(8,128)(2,1)S(1)}, bf16[272,128]{1,0:T(8,128)(2,1)S(1)}, u32[]{:S(2)}, u32[]{:S(2)}) collective-permute-start(bf16[272,128]{1,0:T(8,128)(2,1)S(1)} %collective-permute-done.7.refs_4_), channel_id=1, source_target_pairs={{0,4},{4,0},{8,12},{12,8},{16,20},{20,16},{24,28},{28,24},{1,5},{5... | collective-permute-start | bytes 208904 | tf_op jit(solution)/shard_map/ppermute | solution.py:539
  12.6 2.1 %collective-permute-start.6 = (bf16[272,128]{1,0:T(8,128)(2,1)S(1)}, bf16[272,128]{1,0:T(8,128)(2,1)S(1)}, u32[]{:S(2)}, u32[]{:S(2)}) collective-permute-start(bf16[272,128]{1,0:T(8,128)(2,1)S(1)} %collective-permute-done.5.refs_2_), channel_id=1, source_target_pairs={{0,4},{4,0},{8,12},{12,8},{16,20},{20,16},{24,28},{28,24},{1,5},{5... | collective-permute-start | bytes 208904 | tf_op jit(solution)/shard_map/ppermute | solution.py:539
  12.6 2.1 %collective-permute-start.4 = (bf16[272,128]{1,0:T(8,128)(2,1)S(1)}, bf16[272,128]{1,0:T(8,128)(2,1)S(1)}, u32[]{:S(2)}, u32[]{:S(2)}) collective-permute-start(bf16[272,128]{1,0:T(8,128)(2,1)S(1)} %collective-permute-done.3.refs_0_), channel_id=1, source_target_pairs={{0,4},{4,0},{8,12},{12,8},{16,20},{20,16},{24,28},{28,24},{1,5},{5... | collective-permute-start | bytes 208904 | tf_op jit(solution)/shard_map/ppermute | solution.py:539
  13.1 23.6 %collective-permute-start.1 = (f32[4,8,640]{2,1,0:T(8,128)S(1)}, f32[4,8,640]{2,1,0:T(8,128)S(1)}, u32[]{:S(2)}, u32[]{:S(2)}) collective-permute-start(f32[4,8,640]{2,1,0:T(8,128)S(1)} %pad_maximum_fusion), channel_id=1, source_target_pairs={{0,8},{4,12},{8,0},{12,4},{16,24},{20,28},{24,16},{28,20},{1,9},{5... | collective-permute-start | bytes 245768 | tf_op jit(solution)/shard_map/ppermute | solution.py:94
  14.7 23.6 %copy-start = (f32[32,2,128]{2,1,0:T(2,128)S(1)}, f32[32,2,128]{2,1,0:T(2,128)}, u32[]{:S(2)}) copy-start(f32[32,2,128]{2,1,0:T(2,128)} %param.11) | copy-start | bytes 98308
  32.0 1.2 %collective-permute-start.9 = (f32[32,128]{1,0:T(8,128)S(1)}, f32[32,128]{1,0:T(8,128)S(1)}, u32[]{:S(2)}, u32[]{:S(2)}) collective-permute-start(f32[32,128]{1,0:T(8,128)S(1)} %get-tuple-element.12), channel_id=1, source_target_pairs={{0,4},{4,0},{8,12},{12,8},{16,20},{20,16},{24,28},{28,24},{1,5},{5... | collective-permute-start | bytes 49160 | tf_op jit(solution)/shard_map/ppermute | solution.py:485
  33.2 7.4 %collective-permute-start.12 = (f32[32,128]{1,0:T(8,128)S(1)}, f32[32,128]{1,0:T(8,128)S(1)}, u32[]{:S(2)}, u32[]{:S(2)}) collective-permute-start(f32[32,128]{1,0:T(8,128)S(1)} %add.12.refs_0_), channel_id=1, source_target_pairs={{0,24},{4,28},{8,16},{12,20},{16,8},{20,12},{24,0},{28,4},{1,25},{... | collective-permute-start | bytes 49160 | tf_op jit(solution)/shard_map/ppermute | solution.py:485
  35.0 5.6 %collective-permute-start.11 = (f32[32,128]{1,0:T(8,128)S(1)}, f32[32,128]{1,0:T(8,128)S(1)}, u32[]{:S(2)}, u32[]{:S(2)}) collective-permute-start(f32[32,128]{1,0:T(8,128)S(1)} %add.12.refs_0_), channel_id=1, source_target_pairs={{0,16},{4,20},{8,24},{12,28},{16,0},{20,4},{24,8},{28,12},{1,17},{... | collective-permute-start | bytes 49160 | tf_op jit(solution)/shard_map/ppermute | solution.py:485
  35.5 5.1 %collective-permute-start.10 = (f32[32,128]{1,0:T(8,128)S(1)}, f32[32,128]{1,0:T(8,128)S(1)}, u32[]{:S(2)}, u32[]{:S(2)}) collective-permute-start(f32[32,128]{1,0:T(8,128)S(1)} %add.12.refs_0_), channel_id=1, source_target_pairs={{0,8},{4,12},{8,0},{12,4},{16,24},{20,28},{24,16},{28,20},{1,9},{5... | collective-permute-start | bytes 49160 | tf_op jit(solution)/shard_map/ppermute | solution.py:485
  36.7 4.5 %collective-permute-start.2 = (f32[4,8,640]{2,1,0:T(8,128)S(1)}, f32[4,8,640]{2,1,0:T(8,128)S(1)}, u32[]{:S(2)}, u32[]{:S(2)}) collective-permute-start(f32[4,8,640]{2,1,0:T(8,128)S(1)} %pad_maximum_fusion.1), channel_id=1, source_target_pairs={{0,16},{4,20},{8,24},{12,28},{16,0},{20,4},{24,8},{28,12},{1,17},{... | collective-permute-start | bytes 245768 | tf_op jit(solution)/shard_map/ppermute | solution.py:94
  41.3 7.3 %collective-permute-start.15 = (f32[32,128]{1,0:T(8,128)S(1)}, f32[32,128]{1,0:T(8,128)S(1)}, u32[]{:S(2)}, u32[]{:S(2)}) collective-permute-start(f32[32,128]{1,0:T(8,128)S(1)} %shard_map.135), channel_id=1, source_target_pairs={{0,3},{1,2},{2,1},{3,0},{4,7},{5,6},{6,5},{7,4},{8,11},{9,10},{10,... | collective-permute-start | bytes 49160 | tf_op jit(solution)/shard_map/ppermute | solution.py:485
  44.0 4.6 %collective-permute-start.14 = (f32[32,128]{1,0:T(8,128)S(1)}, f32[32,128]{1,0:T(8,128)S(1)}, u32[]{:S(2)}, u32[]{:S(2)}) collective-permute-start(f32[32,128]{1,0:T(8,128)S(1)} %shard_map.135), channel_id=1, source_target_pairs={{0,2},{1,3},{2,0},{3,1},{4,6},{5,7},{6,4},{7,5},{8,10},{9,11},{10,... | collective-permute-start | bytes 49160 | tf_op jit(solution)/shard_map/ppermute | solution.py:485
  44.0 4.6 %collective-permute-start.13 = (f32[32,128]{1,0:T(8,128)S(1)}, f32[32,128]{1,0:T(8,128)S(1)}, u32[]{:S(2)}, u32[]{:S(2)}) collective-permute-start(f32[32,128]{1,0:T(8,128)S(1)} %shard_map.135), channel_id=1, source_target_pairs={{0,1},{1,0},{2,3},{3,2},{4,5},{5,4},{6,7},{7,6},{8,9},{9,8},{10,11... | collective-permute-start | bytes 49160 | tf_op jit(solution)/shard_map/ppermute | solution.py:485

commit v13 on v10

--- a/solution.py
+++ b/solution.py
@@ -239,7 +239,7 @@
 
 
 def far_kernel(col_count, range_in, pos_in, own_in, nodes_in, *refs):
-    count = 2 * (col_count - 1)
+    count = col_count
     piece_refs = refs[:count]
     (high_ref, low_ref, gram_ref, range_ref, pos_ref, own_nodes, own_rows, basis, spots, wide,
      sums, sems) = refs[count:]
@@ -258,7 +258,9 @@
     def lay_out_received():
         for k in range(1, col_count):
             where = origin(col, k, col_count)
-            mine, other = piece_refs[2 * k - 2], piece_refs[2 * k - 1]
+            mine = piece_refs[k - 1]
+            height = mine.shape[0]
+            other = piece_refs[-1].at[(k - 1) * height:k * height]
             ends = mine[columns * rank:].astype(F32)
             for c in range(columns):
                 lanes = slice(c * nodes, (c + 1) * nodes)
@@ -499,9 +501,9 @@
 
     moved_halves = [lax.ppermute(sent, "col", partners(col_count, k)) for k in range(1, col_count)]
     arrived = cube_exchange(kept, leaving, "clu")
-    pieces = []
-    for mine in moved_halves:
-        pieces += [mine, lax.ppermute(mine, "clu", [(i, i ^ 1) for i in range(clu_count)])]
+    swapped = lax.ppermute(jnp.concatenate(moved_halves, axis=0), "clu",
+                           [(i, i ^ 1) for i in range(clu_count)])
+    pieces = [*moved_halves, swapped]
 
     near_first = near_part(flat, arrived[:-1], [], slot_cap)
     near = near_part(flat, arrived[-1:], [near_first], slot_cap)
@@ -510,7 +512,7 @@
         functools.partial(far_kernel, col_count),
         out_shape=[jax.ShapeDtypeStruct((vesicles, rank, 2 * nodes), BF16)] * 2
         + [jax.ShapeDtypeStruct((rank // 2, 2 * rank), F32)],
-        in_specs=[far_off_spec()] * 4 + [whole_spec()] * (2 * (col_count - 1)),
+        in_specs=[far_off_spec()] * 4 + [whole_spec()] * col_count,
         out_specs=[whole_spec()] * 3,
         scratch_shapes=[
             pltpu.SMEM((1, vesicles), jnp.int32),

time: 43.6 us -> 45.8 us (1.050)
  waiting for transfers between devices: 4.42 us -> 7.41 us
  starting transfers between devices: 18 us -> 17.1 us
    ppermute x3, waiting for transfers between devices: 0.63 us -> 3.33 us  [cube_exchange(): held.append(lax.ppermute(leaving, axis, partners(count, bit)))]
    ppermute x3 -> x1, starting transfers between devices: 1.06 us -> 0.07 us  [per_device(): lax.ppermute(jnp.concatenate(moved_halves, axis=0), 'clu', [(i, i ^ 1) fo...]
    ppermute x3, waiting for transfers between devices: 2.54 us -> 3.09 us  [per_device(): lax.ppermute(sent, 'col', partners(col_count, k))]
  transfers between devices with their start and end apart: 16 -> 14, of which waited for: 4 -> 4; matrix products, arithmetic and copies ran while one was open for 0% -> 0% of each run, Pallas kernels for 36% -> 16%
where the time goes in v13:
time: 45.8 us; the launch traced here: 45.6 us
  Pallas kernels  20.3 us (44%)
  starting transfers between devices  17.1 us (37%)
  waiting for transfers between devices  7.41 us (16%)
  between operations  0.78 us (2%)
    pallas_call x1, Pallas kernels, per_device(): pl.pallas_call(functools.partial(far_kernel, col_count), out_shape=[jax.S...  8.7 us
    ppermute x7, starting transfers between devices, sum_over(): lax.ppermute(value, axis, partners(count, k))  8.01 us
    ppermute x3, starting transfers between devices, per_device(): lax.ppermute(sent, 'col', partners(col_count, k))  5.76 us
    pallas_call x2, Pallas kernels, near_part(): pl.pallas_call(functools.partial(near_kernel, slot_cap, len(pieces)), out...  5.17 us
    pallas_call x1, Pallas kernels, per_device(): pl.pallas_call(functools.partial(basis_kernel, scale_factor, groups), out...  3.42 us
    ppermute x3, waiting for transfers between devices, cube_exchange(): held.append(lax.ppermute(leaving, axis, partners(count, bit)))  3.33 us
    ppermute x3, starting transfers between devices, cube_exchange(): held.append(lax.ppermute(leaving, axis, partners(count, bit)))  3.22 us
    ppermute x3, waiting for transfers between devices, per_device(): lax.ppermute(sent, 'col', partners(col_count, k))  3.09 us
  transfers between devices with their start and end apart: 14, of which 4 were waited for; matrix products, arithmetic and copies ran while one was open for 0% of the time, Pallas kernels for 16%

profile of v13, /device:TPU:0, one launch (start us, length us, event | category | flops | bytes accessed | tf_op | source)
XLA Modules:
  0.0 45.6 jit_solution(16002512050343492942)
XLA Ops:
  0.6 0.9 %shard_map.133 = bf16[272,128]{1,0:T(8,128)(2,1)S(1)} custom-call(bf16[128,512]{1,0:T(8,128)(2,1)} %own_in.3, bf16[2,512]{1,0:T(2,128)(2,1)} %nodes_in.3), custom_call_target="tpu_custom_call" | custom-call | flops 100000 | bytes 100000 | tf_op jit(solution)/shard_map/pallas_call | solution.py:475
  1.6 5.1 %collective-permute-start.5 = (bf16[272,128]{1,0:T(8,128)(2,1)S(1)}, bf16[272,128]{1,0:T(8,128)(2,1)S(1)}, u32[]{:S(2)}, u32[]{:S(2)}) collective-permute-start(bf16[272,128]{1,0:T(8,128)(2,1)S(1)} %shard_map.133), channel_id=1, source_target_pairs={{0,3},{1,2},{2,1},{3,0},{4,7},{5,6},{6,5},{7,4},{8,11},{9,10},{10,... | collective-permute-start | bytes 208904 | tf_op jit(solution)/shard_map/ppermute | solution.py:502
  6.7 0.0 collective-permute-start.4
  6.7 0.6 %collective-permute-start.3 = (bf16[272,128]{1,0:T(8,128)(2,1)S(1)}, bf16[272,128]{1,0:T(8,128)(2,1)S(1)}, u32[]{:S(2)}, u32[]{:S(2)}) collective-permute-start(bf16[272,128]{1,0:T(8,128)(2,1)S(1)} %shard_map.133), channel_id=1, source_target_pairs={{0,1},{1,0},{2,3},{3,2},{4,5},{5,4},{6,7},{7,6},{8,9},{9,8},{10,11... | collective-permute-start | bytes 208904 | tf_op jit(solution)/shard_map/ppermute | solution.py:502
  7.3 2.1 %shard_map.130 = (f32[64,128]{1,0:T(8,128)}, f32[4,8,640]{2,1,0:T(8,128)S(1)}, f32[4,8,640]{2,1,0:T(8,128)S(1)}) custom-call(f32[64,128]{1,0:T(8,128)} %bitcast.33, f32[32,128]{1,0:T(8,128)} %refs_1_.1, f32[1,32]{1,0:T(1,128)} %bitcast.42, s32[1,32]{1,0:T(1,128)} %refs_3_.1, s32[1,24]{1,0:T(1,128)} %bitcast.43, s32[1,24]{1,0:T(1,128)} %bitcast.44, ...), custom_call_target="tpu_custom_call" | custom-call | flops 100000000 | bytes 1000000 | tf_op jit(solution)/shard_map/pallas_call | solution.py:490
  9.4 0.1 collective-permute-start
  9.5 0.0 collective-permute-done.5.refs_2_
  9.5 3.1 %collective-permute-done.4.refs_1_ = bf16[272,128]{1,0:T(8,128)(2,1)S(1)} collective-permute-done((bf16[272,128]{1,0:T(8,128)(2,1)S(1)}, bf16[272,128]{1,0:T(8,128)(2,1)S(1)}, u32[]{:S(2)}, u32[]{:S(2)}) %collective-permute-start.4) | collective-permute-done | bytes 69664 | tf_op jit(solution)/shard_map/ppermute | solution.py:502
  12.6 0.0 collective-permute-done.3.refs_0_
  12.6 0.1 collective-permute-start.6
  12.7 0.0 collective-permute-done
  12.7 1.6 %collective-permute-start.1 = (f32[4,8,640]{2,1,0:T(8,128)S(1)}, f32[4,8,640]{2,1,0:T(8,128)S(1)}, u32[]{:S(2)}, u32[]{:S(2)}) collective-permute-start(f32[4,8,640]{2,1,0:T(8,128)S(1)} %pad_maximum_fusion.1), channel_id=1, source_target_pairs={{0,8},{4,12},{8,0},{12,4},{16,24},{20,28},{24,16},{28,20},{1,9},{5... | collective-permute-start | bytes 245768 | tf_op jit(solution)/shard_map/ppermute | solution.py:93
  14.3 3.3 %collective-permute-done.1 = f32[4,8,640]{2,1,0:T(8,128)S(1)} collective-permute-done((f32[4,8,640]{2,1,0:T(8,128)S(1)}, f32[4,8,640]{2,1,0:T(8,128)S(1)}, u32[]{:S(2)}, u32[]{:S(2)}) %collective-permute-start.1) | collective-permute-done | bytes 81952 | tf_op jit(solution)/shard_map/ppermute | solution.py:93
  17.7 0.0 copy-start
  17.7 8.7 %shard_map.134 = (bf16[32,64,256]{2,1,0:T(8,128)(2,1)S(1)}, bf16[32,64,256]{2,1,0:T(8,128)(2,1)S(1)}, f32[32,128]{1,0:T(8,128)S(1)}) custom-call(s32[1,32]{1,0:T(1,128)} %bitcast.45, f32[64,128]{1,0:T(8,128)} %bitcast.34, bf16[128,512]{1,0:T(8,128)(2,1)} %own_in.3, bf16[2,512]{1,0:T(2,128)(2,1)} %nodes_in.3, ...), custom_call_target="tpu_custom_call" | custom-call | flops 10000000000 | bytes 10000000 | tf_op jit(solution)/shard_map/pallas_call | solution.py:511
  26.4 0.1 collective-permute-start.7
  26.5 1.6 %collective-permute-start.2 = (f32[4,8,640]{2,1,0:T(8,128)S(1)}, f32[4,8,640]{2,1,0:T(8,128)S(1)}, u32[]{:S(2)}, u32[]{:S(2)}) collective-permute-start(f32[4,8,640]{2,1,0:T(8,128)S(1)} %pad_maximum_fusion.2), channel_id=1, source_target_pairs={{0,16},{4,20},{8,24},{12,28},{16,0},{20,4},{24,8},{28,12},{1,17},{... | collective-permute-start | bytes 245768 | tf_op jit(solution)/shard_map/ppermute | solution.py:93
  28.1 2.0 %collective-permute-start.10 = (f32[32,128]{1,0:T(8,128)S(1)}, f32[32,128]{1,0:T(8,128)S(1)}, u32[]{:S(2)}, u32[]{:S(2)}) collective-permute-start(f32[32,128]{1,0:T(8,128)S(1)} %add.12.refs_0_), channel_id=1, source_target_pairs={{0,24},{4,28},{8,16},{12,20},{16,8},{20,12},{24,0},{28,4},{1,25},{... | collective-permute-start | bytes 49160 | tf_op jit(solution)/shard_map/ppermute | solution.py:452
  30.1 1.0 %collective-permute-start.9 = (f32[32,128]{1,0:T(8,128)S(1)}, f32[32,128]{1,0:T(8,128)S(1)}, u32[]{:S(2)}, u32[]{:S(2)}) collective-permute-start(f32[32,128]{1,0:T(8,128)S(1)} %add.12.refs_0_), channel_id=1, source_target_pairs={{0,16},{4,20},{8,24},{12,28},{16,0},{20,4},{24,8},{28,12},{1,17},{... | collective-permute-start | bytes 49160 | tf_op jit(solution)/shard_map/ppermute | solution.py:452
  31.1 0.5 %collective-permute-start.8 = (f32[32,128]{1,0:T(8,128)S(1)}, f32[32,128]{1,0:T(8,128)S(1)}, u32[]{:S(2)}, u32[]{:S(2)}) collective-permute-start(f32[32,128]{1,0:T(8,128)S(1)} %add.12.refs_0_), channel_id=1, source_target_pairs={{0,8},{4,12},{8,0},{12,4},{16,24},{20,28},{24,16},{28,20},{1,9},{5... | collective-permute-start | bytes 49160 | tf_op jit(solution)/shard_map/ppermute | solution.py:452
  31.6 2.3 %shard_map.131.refs_1_.refs_4_ = f32[64,128]{1,0:T(8,128)S(1)} custom-call(f32[64,128]{1,0:T(8,128)S(1)} %bitcast.35, f32[1,8,640]{2,1,0:T(8,128)S(1)} %get-tuple-element.19.refs_0_, f32[1,8,640]{2,1,0:T(8,128)S(1)} %get-tuple-element.17.refs_1_, f32[2,8,640]{2,1,0:T(8,128)S(1)} %get-tuple-element.15.refs_2_), custom_call_target="tpu_custom_call" | custom-call | flops 1000000000 | bytes 10000000 | tf_op jit(solution)/shard_map/pallas_call | solution.py:228
  33.9 0.0 collective-permute-done.2.refs_0_.refs_5_
  33.9 0.0 collective-permute-done.10.refs_3_
  33.9 0.9 %collective-permute-done.8.refs_1_ = f32[32,128]{1,0:T(8,128)S(1)} collective-permute-done((f32[32,128]{1,0:T(8,128)S(1)}, f32[32,128]{1,0:T(8,128)S(1)}, u32[]{:S(2)}, u32[]{:S(2)}) %collective-permute-start.8) | collective-permute-done | bytes 16416 | tf_op jit(solution)/shard_map/ppermute | solution.py:452
  34.8 2.7 %collective-permute-start.13 = (f32[32,128]{1,0:T(8,128)S(1)}, f32[32,128]{1,0:T(8,128)S(1)}, u32[]{:S(2)}, u32[]{:S(2)}) collective-permute-start(f32[32,128]{1,0:T(8,128)S(1)} %shard_map.135), channel_id=1, source_target_pairs={{0,3},{1,2},{2,1},{3,0},{4,7},{5,6},{6,5},{7,4},{8,11},{9,10},{10,... | collective-permute-start | bytes 49160 | tf_op jit(solution)/shard_map/ppermute | solution.py:452
  37.5 0.0 collective-permute-start.12
  37.5 1.7 %collective-permute-start.11 = (f32[32,128]{1,0:T(8,128)S(1)}, f32[32,128]{1,0:T(8,128)S(1)}, u32[]{:S(2)}, u32[]{:S(2)}) collective-permute-start(f32[32,128]{1,0:T(8,128)S(1)} %shard_map.135), channel_id=1, source_target_pairs={{0,1},{1,0},{2,3},{3,2},{4,5},{5,4},{6,7},{7,6},{8,9},{9,8},{10,11... | collective-permute-start | bytes 49160 | tf_op jit(solution)/shard_map/ppermute | solution.py:452
  39.2 2.9 %shard_map.132._ = f32[64,128]{1,0:T(8,128)} custom-call(f32[64,128]{1,0:T(8,128)S(1)} %bitcast.36, f32[4,8,640]{2,1,0:T(8,128)S(1)} %collective-permute-done.2.refs_0_.refs_5_, f32[64,128]{1,0:T(8,128)S(1)} %shard_map.131.refs_1_.refs_4_), custom_call_target="tpu_custom_call" | custom-call | flops 1000000000 | bytes 10000000 | tf_op jit(solution)/shard_map/pallas_call | solution.py:228
  42.1 0.0 collective-permute-done.13
  42.1 0.1 collective-permute-done.12
  42.2 0.0 collective-permute-done.11
  42.2 3.4 %shard_map.136 = f32[32,128,128]{2,1,0:T(8,128)} custom-call(f32[32,128]{1,0:T(8,128)S(1)} %add_add_fusion.gram_ref, bf16[32,64,256]{2,1,0:T(8,128)(2,1)S(1)} %get-tuple-element.13.high_ref, bf16[32,64,256]{2,1,0:T(8,128)(2,1)S(1)} %get-tuple-element.14.low_ref, f32[64,128]{1,0:T(8,128)} %shard_map.132._), custom_call_target="tpu_custom_call" | custom-call | flops 1000000000 | bytes 10000000 | tf_op jit(solution)/shard_map/pallas_call | solution.py:535
  (15 shorter events, 0.1 us)
Async XLA Ops:
  1.6 7.9 %collective-permute-start.5 = (bf16[272,128]{1,0:T(8,128)(2,1)S(1)}, bf16[272,128]{1,0:T(8,128)(2,1)S(1)}, u32[]{:S(2)}, u32[]{:S(2)}) collective-permute-start(bf16[272,128]{1,0:T(8,128)(2,1)S(1)} %shard_map.133), channel_id=1, source_target_pairs={{0,3},{1,2},{2,1},{3,0},{4,7},{5,6},{6,5},{7,4},{8,11},{9,10},{10,... | collective-permute-start | bytes 208904 | tf_op jit(solution)/shard_map/ppermute | solution.py:502
  6.7 5.9 %collective-permute-start.4 = (bf16[272,128]{1,0:T(8,128)(2,1)S(1)}, bf16[272,128]{1,0:T(8,128)(2,1)S(1)}, u32[]{:S(2)}, u32[]{:S(2)}) collective-permute-start(bf16[272,128]{1,0:T(8,128)(2,1)S(1)} %shard_map.133), channel_id=1, source_target_pairs={{0,2},{1,3},{2,0},{3,1},{4,6},{5,7},{6,4},{7,5},{8,10},{9,11},{10,... | collective-permute-start | bytes 208904 | tf_op jit(solution)/shard_map/ppermute | solution.py:502
  6.7 5.9 %collective-permute-start.3 = (bf16[272,128]{1,0:T(8,128)(2,1)S(1)}, bf16[272,128]{1,0:T(8,128)(2,1)S(1)}, u32[]{:S(2)}, u32[]{:S(2)}) collective-permute-start(bf16[272,128]{1,0:T(8,128)(2,1)S(1)} %shard_map.133), channel_id=1, source_target_pairs={{0,1},{1,0},{2,3},{3,2},{4,5},{5,4},{6,7},{7,6},{8,9},{9,8},{10,11... | collective-permute-start | bytes 208904 | tf_op jit(solution)/shard_map/ppermute | solution.py:502
  9.4 3.3 %collective-permute-start = (f32[4,8,640]{2,1,0:T(8,128)S(1)}, f32[4,8,640]{2,1,0:T(8,128)S(1)}, u32[]{:S(2)}, u32[]{:S(2)}) collective-permute-start(f32[4,8,640]{2,1,0:T(8,128)S(1)} %get-tuple-element.11), channel_id=1, source_target_pairs={{0,4},{4,0},{8,12},{12,8},{16,20},{20,16},{24,28},{28,24},{1,5},{5... | collective-permute-start | bytes 245768 | tf_op jit(solution)/shard_map/ppermute | solution.py:93
  12.6 5.0 %collective-permute-start.6 = (bf16[816,128]{1,0:T(8,128)(2,1)S(1)}, bf16[816,128]{1,0:T(8,128)(2,1)S(1)}, u32[]{:S(2)}, u32[]{:S(2)}) collective-permute-start(bf16[816,128]{1,0:T(8,128)(2,1)S(1)} %pad_maximum_fusion), channel_id=1, source_target_pairs={{0,4},{4,0},{8,12},{12,8},{16,20},{20,16},{24,28},{28,24},{1,5},{5... | collective-permute-start | bytes 626696 | tf_op jit(solution)/shard_map/ppermute | solution.py:504
  12.7 4.9 %collective-permute-start.1 = (f32[4,8,640]{2,1,0:T(8,128)S(1)}, f32[4,8,640]{2,1,0:T(8,128)S(1)}, u32[]{:S(2)}, u32[]{:S(2)}) collective-permute-start(f32[4,8,640]{2,1,0:T(8,128)S(1)} %pad_maximum_fusion.1), channel_id=1, source_target_pairs={{0,8},{4,12},{8,0},{12,4},{16,24},{20,28},{24,16},{28,20},{1,9},{5... | collective-permute-start | bytes 245768 | tf_op jit(solution)/shard_map/ppermute | solution.py:93
  17.7 14.0 %copy-start = (f32[32,2,128]{2,1,0:T(2,128)S(1)}, f32[32,2,128]{2,1,0:T(2,128)}, u32[]{:S(2)}) copy-start(f32[32,2,128]{2,1,0:T(2,128)} %param.11) | copy-start | bytes 98308
  26.4 1.7 %collective-permute-start.7 = (f32[32,128]{1,0:T(8,128)S(1)}, f32[32,128]{1,0:T(8,128)S(1)}, u32[]{:S(2)}, u32[]{:S(2)}) collective-permute-start(f32[32,128]{1,0:T(8,128)S(1)} %get-tuple-element.12), channel_id=1, source_target_pairs={{0,4},{4,0},{8,12},{12,8},{16,20},{20,16},{24,28},{28,24},{1,5},{5... | collective-permute-start | bytes 49160 | tf_op jit(solution)/shard_map/ppermute | solution.py:452
  26.5 7.4 %collective-permute-start.2 = (f32[4,8,640]{2,1,0:T(8,128)S(1)}, f32[4,8,640]{2,1,0:T(8,128)S(1)}, u32[]{:S(2)}, u32[]{:S(2)}) collective-permute-start(f32[4,8,640]{2,1,0:T(8,128)S(1)} %pad_maximum_fusion.2), channel_id=1, source_target_pairs={{0,16},{4,20},{8,24},{12,28},{16,0},{20,4},{24,8},{28,12},{1,17},{... | collective-permute-start | bytes 245768 | tf_op jit(solution)/shard_map/ppermute | solution.py:93
  28.1 5.8 %collective-permute-start.10 = (f32[32,128]{1,0:T(8,128)S(1)}, f32[32,128]{1,0:T(8,128)S(1)}, u32[]{:S(2)}, u32[]{:S(2)}) collective-permute-start(f32[32,128]{1,0:T(8,128)S(1)} %add.12.refs_0_), channel_id=1, source_target_pairs={{0,24},{4,28},{8,16},{12,20},{16,8},{20,12},{24,0},{28,4},{1,25},{... | collective-permute-start | bytes 49160 | tf_op jit(solution)/shard_map/ppermute | solution.py:452
  30.1 3.8 %collective-permute-start.9 = (f32[32,128]{1,0:T(8,128)S(1)}, f32[32,128]{1,0:T(8,128)S(1)}, u32[]{:S(2)}, u32[]{:S(2)}) collective-permute-start(f32[32,128]{1,0:T(8,128)S(1)} %add.12.refs_0_), channel_id=1, source_target_pairs={{0,16},{4,20},{8,24},{12,28},{16,0},{20,4},{24,8},{28,12},{1,17},{... | collective-permute-start | bytes 49160 | tf_op jit(solution)/shard_map/ppermute | solution.py:452
  31.1 3.7 %collective-permute-start.8 = (f32[32,128]{1,0:T(8,128)S(1)}, f32[32,128]{1,0:T(8,128)S(1)}, u32[]{:S(2)}, u32[]{:S(2)}) collective-permute-start(f32[32,128]{1,0:T(8,128)S(1)} %add.12.refs_0_), channel_id=1, source_target_pairs={{0,8},{4,12},{8,0},{12,4},{16,24},{20,28},{24,16},{28,20},{1,9},{5... | collective-permute-start | bytes 49160 | tf_op jit(solution)/shard_map/ppermute | solution.py:452
  34.8 7.3 %collective-permute-start.13 = (f32[32,128]{1,0:T(8,128)S(1)}, f32[32,128]{1,0:T(8,128)S(1)}, u32[]{:S(2)}, u32[]{:S(2)}) collective-permute-start(f32[32,128]{1,0:T(8,128)S(1)} %shard_map.135), channel_id=1, source_target_pairs={{0,3},{1,2},{2,1},{3,0},{4,7},{5,6},{6,5},{7,4},{8,11},{9,10},{10,... | collective-permute-start | bytes 49160 | tf_op jit(solution)/shard_map/ppermute | solution.py:452
  37.5 4.6 %collective-permute-start.12 = (f32[32,128]{1,0:T(8,128)S(1)}, f32[32,128]{1,0:T(8,128)S(1)}, u32[]{:S(2)}, u32[]{:S(2)}) collective-permute-start(f32[32,128]{1,0:T(8,128)S(1)} %shard_map.135), channel_id=1, source_target_pairs={{0,2},{1,3},{2,0},{3,1},{4,6},{5,7},{6,4},{7,5},{8,10},{9,11},{10,... | collective-permute-start | bytes 49160 | tf_op jit(solution)/shard_map/ppermute | solution.py:452
  37.5 4.6 %collective-permute-start.11 = (f32[32,128]{1,0:T(8,128)S(1)}, f32[32,128]{1,0:T(8,128)S(1)}, u32[]{:S(2)}, u32[]{:S(2)}) collective-permute-start(f32[32,128]{1,0:T(8,128)S(1)} %shard_map.135), channel_id=1, source_target_pairs={{0,1},{1,0},{2,3},{3,2},{4,5},{5,4},{6,7},{7,6},{8,9},{9,8},{10,11... | collective-permute-start | bytes 49160 | tf_op jit(solution)/shard_map/ppermute | solution.py:452

commit v14 on v10

--- a/solution.py
+++ b/solution.py
@@ -339,7 +339,7 @@
     eye = (iota((size, size), 0) == iota((size, size), 1)).astype(F32)
     rest = jnp.concatenate([gram, eye], axis=1)
     done = []
-    step = 8
+    step = 16
     for start in range(0, size, step):
         height = size - start
         columns = [jnp.broadcast_to(rest[:, start + j:start + j + 1], (height, 2 * size))

time: 43.6 us -> 43.4 us (level)
  transfers between devices with their start and end apart: 16 -> 16, of which waited for: 4 -> 4; matrix products, arithmetic and copies ran while one was open for 0% -> 0% of each run, Pallas kernels for 36% -> 37%
where the time goes in v14:
time: 43.4 us; the launch traced here: 43.2 us
  Pallas kernels  20 us (46%)
  starting transfers between devices  18 us (41%)
  waiting for transfers between devices  4.42 us (10%)
  between operations  0.76 us (2%)
    pallas_call x1, Pallas kernels, per_device(): pl.pallas_call(functools.partial(far_kernel, col_count), out_shape=[jax.S...  8.6 us
    ppermute x7, starting transfers between devices, sum_over(): lax.ppermute(value, axis, partners(count, k))  7.95 us
    ppermute x3, starting transfers between devices, per_device(): lax.ppermute(sent, 'col', partners(col_count, k))  5.76 us
    pallas_call x2, Pallas kernels, near_part(): pl.pallas_call(functools.partial(near_kernel, slot_cap, len(pieces)), out...  5.17 us
    ppermute x3, starting transfers between devices, cube_exchange(): held.append(lax.ppermute(leaving, axis, partners(count, bit)))  3.2 us
    pallas_call x1, Pallas kernels, per_device(): pl.pallas_call(functools.partial(basis_kernel, scale_factor, groups), out...  3.18 us
    ppermute x3, waiting for transfers between devices, per_device(): lax.ppermute(sent, 'col', partners(col_count, k))  2.54 us
    pallas_call x1, Pallas kernels, per_device(): pl.pallas_call(functools.partial(force_kernel, clu_count), out_shape=[jax...  2.06 us
  transfers between devices with their start and end apart: 16, of which 4 were waited for; matrix products, arithmetic and copies ran while one was open for 0% of the time, Pallas kernels for 37%

profile of v14, /device:TPU:0, one launch (start us, length us, event | category | flops | bytes accessed | tf_op | source)
XLA Modules:
  0.0 43.2 jit_solution(2991017159653158348)
XLA Ops:
  0.6 0.9 %shard_map.133 = bf16[272,128]{1,0:T(8,128)(2,1)S(1)} custom-call(bf16[128,512]{1,0:T(8,128)(2,1)} %own_in.3, bf16[2,512]{1,0:T(2,128)(2,1)} %nodes_in.3), custom_call_target="tpu_custom_call" | custom-call | flops 100000 | bytes 100000 | tf_op jit(solution)/shard_map/pallas_call | solution.py:473
  1.6 5.1 %collective-permute-start.7 = (bf16[272,128]{1,0:T(8,128)(2,1)S(1)}, bf16[272,128]{1,0:T(8,128)(2,1)S(1)}, u32[]{:S(2)}, u32[]{:S(2)}) collective-permute-start(bf16[272,128]{1,0:T(8,128)(2,1)S(1)} %shard_map.133), channel_id=1, source_target_pairs={{0,3},{1,2},{2,1},{3,0},{4,7},{5,6},{6,5},{7,4},{8,11},{9,10},{10,... | collective-permute-start | bytes 208904 | tf_op jit(solution)/shard_map/ppermute | solution.py:500
  6.7 0.0 collective-permute-start.5
  6.7 0.6 %collective-permute-start.3 = (bf16[272,128]{1,0:T(8,128)(2,1)S(1)}, bf16[272,128]{1,0:T(8,128)(2,1)S(1)}, u32[]{:S(2)}, u32[]{:S(2)}) collective-permute-start(bf16[272,128]{1,0:T(8,128)(2,1)S(1)} %shard_map.133), channel_id=1, source_target_pairs={{0,1},{1,0},{2,3},{3,2},{4,5},{5,4},{6,7},{7,6},{8,9},{9,8},{10,11... | collective-permute-start | bytes 208904 | tf_op jit(solution)/shard_map/ppermute | solution.py:500
  7.3 2.1 %shard_map.130 = (f32[64,128]{1,0:T(8,128)}, f32[4,8,640]{2,1,0:T(8,128)S(1)}, f32[4,8,640]{2,1,0:T(8,128)S(1)}) custom-call(f32[64,128]{1,0:T(8,128)} %bitcast.33, f32[32,128]{1,0:T(8,128)} %refs_1_.1, f32[1,32]{1,0:T(1,128)} %bitcast.42, s32[1,32]{1,0:T(1,128)} %refs_3_.1, s32[1,24]{1,0:T(1,128)} %bitcast.43, s32[1,24]{1,0:T(1,128)} %bitcast.44, ...), custom_call_target="tpu_custom_call" | custom-call | flops 100000000 | bytes 1000000 | tf_op jit(solution)/shard_map/pallas_call | solution.py:488
  9.4 0.1 collective-permute-start
  9.5 0.5 %collective-permute-start.8 = (bf16[272,128]{1,0:T(8,128)(2,1)S(1)}, bf16[272,128]{1,0:T(8,128)(2,1)S(1)}, u32[]{:S(2)}, u32[]{:S(2)}) collective-permute-start(bf16[272,128]{1,0:T(8,128)(2,1)S(1)} %collective-permute-done.7.refs_4_), channel_id=1, source_target_pairs={{0,4},{4,0},{8,12},{12,8},{16,20},{20,16},{24,28},{28,24},{1,5},{5... | collective-permute-start | bytes 208904 | tf_op jit(solution)/shard_map/ppermute | solution.py:504
  10.1 2.5 %collective-permute-done.5.refs_2_ = bf16[272,128]{1,0:T(8,128)(2,1)S(1)} collective-permute-done((bf16[272,128]{1,0:T(8,128)(2,1)S(1)}, bf16[272,128]{1,0:T(8,128)(2,1)S(1)}, u32[]{:S(2)}, u32[]{:S(2)}) %collective-permute-start.5) | collective-permute-done | bytes 69664 | tf_op jit(solution)/shard_map/ppermute | solution.py:500
  12.6 0.5 %collective-permute-start.4 = (bf16[272,128]{1,0:T(8,128)(2,1)S(1)}, bf16[272,128]{1,0:T(8,128)(2,1)S(1)}, u32[]{:S(2)}, u32[]{:S(2)}) collective-permute-start(bf16[272,128]{1,0:T(8,128)(2,1)S(1)} %collective-permute-done.3.refs_0_), channel_id=1, source_target_pairs={{0,4},{4,0},{8,12},{12,8},{16,20},{20,16},{24,28},{28,24},{1,5},{5... | collective-permute-start | bytes 208904 | tf_op jit(solution)/shard_map/ppermute | solution.py:504
  13.1 1.6 %collective-permute-start.1 = (f32[4,8,640]{2,1,0:T(8,128)S(1)}, f32[4,8,640]{2,1,0:T(8,128)S(1)}, u32[]{:S(2)}, u32[]{:S(2)}) collective-permute-start(f32[4,8,640]{2,1,0:T(8,128)S(1)} %pad_maximum_fusion), channel_id=1, source_target_pairs={{0,8},{4,12},{8,0},{12,4},{16,24},{20,28},{24,16},{28,20},{1,9},{5... | collective-permute-start | bytes 245768 | tf_op jit(solution)/shard_map/ppermute | solution.py:93
  14.7 0.0 collective-permute-done.6.refs_3_
  14.7 0.0 collective-permute-done.4.refs_1_
  14.7 0.0 copy-start
  14.7 8.6 %shard_map.134 = (bf16[32,64,256]{2,1,0:T(8,128)(2,1)S(1)}, bf16[32,64,256]{2,1,0:T(8,128)(2,1)S(1)}, f32[32,128]{1,0:T(8,128)S(1)}) custom-call(s32[1,32]{1,0:T(1,128)} %bitcast.45, f32[64,128]{1,0:T(8,128)} %bitcast.34, bf16[128,512]{1,0:T(8,128)(2,1)} %own_in.3, bf16[2,512]{1,0:T(2,128)(2,1)} %nodes_in.3, ...), custom_call_target="tpu_custom_call" | custom-call | flops 10000000000 | bytes 10000000 | tf_op jit(solution)/shard_map/pallas_call | solution.py:509
  23.3 0.1 collective-permute-start.9
  23.4 1.2 %collective-permute-done.9 = f32[32,128]{1,0:T(8,128)S(1)} collective-permute-done((f32[32,128]{1,0:T(8,128)S(1)}, f32[32,128]{1,0:T(8,128)S(1)}, u32[]{:S(2)}, u32[]{:S(2)}) %collective-permute-start.9) | collective-permute-done | bytes 16416 | tf_op jit(solution)/shard_map/ppermute | solution.py:450
  24.6 1.8 %collective-permute-start.12 = (f32[32,128]{1,0:T(8,128)S(1)}, f32[32,128]{1,0:T(8,128)S(1)}, u32[]{:S(2)}, u32[]{:S(2)}) collective-permute-start(f32[32,128]{1,0:T(8,128)S(1)} %add.12.refs_0_), channel_id=1, source_target_pairs={{0,24},{4,28},{8,16},{12,20},{16,8},{20,12},{24,0},{28,4},{1,25},{... | collective-permute-start | bytes 49160 | tf_op jit(solution)/shard_map/ppermute | solution.py:450
  26.4 0.5 %collective-permute-start.11 = (f32[32,128]{1,0:T(8,128)S(1)}, f32[32,128]{1,0:T(8,128)S(1)}, u32[]{:S(2)}, u32[]{:S(2)}) collective-permute-start(f32[32,128]{1,0:T(8,128)S(1)} %add.12.refs_0_), channel_id=1, source_target_pairs={{0,16},{4,20},{8,24},{12,28},{16,0},{20,4},{24,8},{28,12},{1,17},{... | collective-permute-start | bytes 49160 | tf_op jit(solution)/shard_map/ppermute | solution.py:450
  26.9 1.2 %collective-permute-start.10 = (f32[32,128]{1,0:T(8,128)S(1)}, f32[32,128]{1,0:T(8,128)S(1)}, u32[]{:S(2)}, u32[]{:S(2)}) collective-permute-start(f32[32,128]{1,0:T(8,128)S(1)} %add.12.refs_0_), channel_id=1, source_target_pairs={{0,8},{4,12},{8,0},{12,4},{16,24},{20,28},{24,16},{28,20},{1,9},{5... | collective-permute-start | bytes 49160 | tf_op jit(solution)/shard_map/ppermute | solution.py:450
  28.1 0.0 collective-permute-done.1
  28.1 1.6 %collective-permute-start.2 = (f32[4,8,640]{2,1,0:T(8,128)S(1)}, f32[4,8,640]{2,1,0:T(8,128)S(1)}, u32[]{:S(2)}, u32[]{:S(2)}) collective-permute-start(f32[4,8,640]{2,1,0:T(8,128)S(1)} %pad_maximum_fusion.1), channel_id=1, source_target_pairs={{0,16},{4,20},{8,24},{12,28},{16,0},{20,4},{24,8},{28,12},{1,17},{... | collective-permute-start | bytes 245768 | tf_op jit(solution)/shard_map/ppermute | solution.py:93
  29.7 2.3 %shard_map.131.refs_1_.refs_4_ = f32[64,128]{1,0:T(8,128)S(1)} custom-call(f32[64,128]{1,0:T(8,128)S(1)} %bitcast.35, f32[1,8,640]{2,1,0:T(8,128)S(1)} %get-tuple-element.19.refs_0_, f32[1,8,640]{2,1,0:T(8,128)S(1)} %get-tuple-element.17.refs_1_, f32[2,8,640]{2,1,0:T(8,128)S(1)} %get-tuple-element.15.refs_2_), custom_call_target="tpu_custom_call" | custom-call | flops 1000000000 | bytes 10000000 | tf_op jit(solution)/shard_map/pallas_call | solution.py:228
  31.9 0.0 collective-permute-done.11.refs_2_
  32.0 0.0 collective-permute-done.10.refs_1_
  32.0 0.6 %collective-permute-done.2.refs_0_.refs_5_ = f32[4,8,640]{2,1,0:T(8,128)S(1)} collective-permute-done((f32[4,8,640]{2,1,0:T(8,128)S(1)}, f32[4,8,640]{2,1,0:T(8,128)S(1)}, u32[]{:S(2)}, u32[]{:S(2)}) %collective-permute-start.2) | collective-permute-done | bytes 81952 | tf_op jit(solution)/shard_map/ppermute | solution.py:93
  32.6 2.7 %collective-permute-start.15 = (f32[32,128]{1,0:T(8,128)S(1)}, f32[32,128]{1,0:T(8,128)S(1)}, u32[]{:S(2)}, u32[]{:S(2)}) collective-permute-start(f32[32,128]{1,0:T(8,128)S(1)} %shard_map.135), channel_id=1, source_target_pairs={{0,3},{1,2},{2,1},{3,0},{4,7},{5,6},{6,5},{7,4},{8,11},{9,10},{10,... | collective-permute-start | bytes 49160 | tf_op jit(solution)/shard_map/ppermute | solution.py:450
  35.3 0.0 collective-permute-start.14
  35.3 1.7 %collective-permute-start.13 = (f32[32,128]{1,0:T(8,128)S(1)}, f32[32,128]{1,0:T(8,128)S(1)}, u32[]{:S(2)}, u32[]{:S(2)}) collective-permute-start(f32[32,128]{1,0:T(8,128)S(1)} %shard_map.135), channel_id=1, source_target_pairs={{0,1},{1,0},{2,3},{3,2},{4,5},{5,4},{6,7},{7,6},{8,9},{9,8},{10,11... | collective-permute-start | bytes 49160 | tf_op jit(solution)/shard_map/ppermute | solution.py:450
  37.0 2.9 %shard_map.132._ = f32[64,128]{1,0:T(8,128)} custom-call(f32[64,128]{1,0:T(8,128)S(1)} %bitcast.36, f32[4,8,640]{2,1,0:T(8,128)S(1)} %collective-permute-done.2.refs_0_.refs_5_, f32[64,128]{1,0:T(8,128)S(1)} %shard_map.131.refs_1_.refs_4_), custom_call_target="tpu_custom_call" | custom-call | flops 1000000000 | bytes 10000000 | tf_op jit(solution)/shard_map/pallas_call | solution.py:228
  39.9 0.0 collective-permute-done.15
  39.9 0.1 collective-permute-done.14
  40.0 3.2 %shard_map.136 = f32[32,128,128]{2,1,0:T(8,128)} custom-call(f32[32,128]{1,0:T(8,128)S(1)} %add_add_fusion.gram_ref, bf16[32,64,256]{2,1,0:T(8,128)(2,1)S(1)} %get-tuple-element.13.high_ref, bf16[32,64,256]{2,1,0:T(8,128)(2,1)S(1)} %get-tuple-element.14.low_ref, f32[64,128]{1,0:T(8,128)} %shard_map.132._), custom_call_target="tpu_custom_call" | custom-call | flops 1000000000 | bytes 10000000 | tf_op jit(solution)/shard_map/pallas_call | solution.py:533
  (18 shorter events, 0.1 us)
Async XLA Ops:
  1.6 7.9 %collective-permute-start.7 = (bf16[272,128]{1,0:T(8,128)(2,1)S(1)}, bf16[272,128]{1,0:T(8,128)(2,1)S(1)}, u32[]{:S(2)}, u32[]{:S(2)}) collective-permute-start(bf16[272,128]{1,0:T(8,128)(2,1)S(1)} %shard_map.133), channel_id=1, source_target_pairs={{0,3},{1,2},{2,1},{3,0},{4,7},{5,6},{6,5},{7,4},{8,11},{9,10},{10,... | collective-permute-start | bytes 208904 | tf_op jit(solution)/shard_map/ppermute | solution.py:500
  6.7 5.9 %collective-permute-start.5 = (bf16[272,128]{1,0:T(8,128)(2,1)S(1)}, bf16[272,128]{1,0:T(8,128)(2,1)S(1)}, u32[]{:S(2)}, u32[]{:S(2)}) collective-permute-start(bf16[272,128]{1,0:T(8,128)(2,1)S(1)} %shard_map.133), channel_id=1, source_target_pairs={{0,2},{1,3},{2,0},{3,1},{4,6},{5,7},{6,4},{7,5},{8,10},{9,11},{10,... | collective-permute-start | bytes 208904 | tf_op jit(solution)/shard_map/ppermute | solution.py:500
  6.7 5.9 %collective-permute-start.3 = (bf16[272,128]{1,0:T(8,128)(2,1)S(1)}, bf16[272,128]{1,0:T(8,128)(2,1)S(1)}, u32[]{:S(2)}, u32[]{:S(2)}) collective-permute-start(bf16[272,128]{1,0:T(8,128)(2,1)S(1)} %shard_map.133), channel_id=1, source_target_pairs={{0,1},{1,0},{2,3},{3,2},{4,5},{5,4},{6,7},{7,6},{8,9},{9,8},{10,11... | collective-permute-start | bytes 208904 | tf_op jit(solution)/shard_map/ppermute | solution.py:500
  9.4 3.7 %collective-permute-start = (f32[4,8,640]{2,1,0:T(8,128)S(1)}, f32[4,8,640]{2,1,0:T(8,128)S(1)}, u32[]{:S(2)}, u32[]{:S(2)}) collective-permute-start(f32[4,8,640]{2,1,0:T(8,128)S(1)} %get-tuple-element.11), channel_id=1, source_target_pairs={{0,4},{4,0},{8,12},{12,8},{16,20},{20,16},{24,28},{28,24},{1,5},{5... | collective-permute-start | bytes 245768 | tf_op jit(solution)/shard_map/ppermute | solution.py:93
  9.5 5.2 %collective-permute-start.8 = (bf16[272,128]{1,0:T(8,128)(2,1)S(1)}, bf16[272,128]{1,0:T(8,128)(2,1)S(1)}, u32[]{:S(2)}, u32[]{:S(2)}) collective-permute-start(bf16[272,128]{1,0:T(8,128)(2,1)S(1)} %collective-permute-done.7.refs_4_), channel_id=1, source_target_pairs={{0,4},{4,0},{8,12},{12,8},{16,20},{20,16},{24,28},{28,24},{1,5},{5... | collective-permute-start | bytes 208904 | tf_op jit(solution)/shard_map/ppermute | solution.py:504
  12.6 2.1 %collective-permute-start.6 = (bf16[272,128]{1,0:T(8,128)(2,1)S(1)}, bf16[272,128]{1,0:T(8,128)(2,1)S(1)}, u32[]{:S(2)}, u32[]{:S(2)}) collective-permute-start(bf16[272,128]{1,0:T(8,128)(2,1)S(1)} %collective-permute-done.5.refs_2_), channel_id=1, source_target_pairs={{0,4},{4,0},{8,12},{12,8},{16,20},{20,16},{24,28},{28,24},{1,5},{5... | collective-permute-start | bytes 208904 | tf_op jit(solution)/shard_map/ppermute | solution.py:504
  12.6 2.1 %collective-permute-start.4 = (bf16[272,128]{1,0:T(8,128)(2,1)S(1)}, bf16[272,128]{1,0:T(8,128)(2,1)S(1)}, u32[]{:S(2)}, u32[]{:S(2)}) collective-permute-start(bf16[272,128]{1,0:T(8,128)(2,1)S(1)} %collective-permute-done.3.refs_0_), channel_id=1, source_target_pairs={{0,4},{4,0},{8,12},{12,8},{16,20},{20,16},{24,28},{28,24},{1,5},{5... | collective-permute-start | bytes 208904 | tf_op jit(solution)/shard_map/ppermute | solution.py:504
  13.1 14.9 %collective-permute-start.1 = (f32[4,8,640]{2,1,0:T(8,128)S(1)}, f32[4,8,640]{2,1,0:T(8,128)S(1)}, u32[]{:S(2)}, u32[]{:S(2)}) collective-permute-start(f32[4,8,640]{2,1,0:T(8,128)S(1)} %pad_maximum_fusion), channel_id=1, source_target_pairs={{0,8},{4,12},{8,0},{12,4},{16,24},{20,28},{24,16},{28,20},{1,9},{5... | collective-permute-start | bytes 245768 | tf_op jit(solution)/shard_map/ppermute | solution.py:93
  14.7 15.0 %copy-start = (f32[32,2,128]{2,1,0:T(2,128)S(1)}, f32[32,2,128]{2,1,0:T(2,128)}, u32[]{:S(2)}) copy-start(f32[32,2,128]{2,1,0:T(2,128)} %param.11) | copy-start | bytes 98308
  23.3 1.2 %collective-permute-start.9 = (f32[32,128]{1,0:T(8,128)S(1)}, f32[32,128]{1,0:T(8,128)S(1)}, u32[]{:S(2)}, u32[]{:S(2)}) collective-permute-start(f32[32,128]{1,0:T(8,128)S(1)} %get-tuple-element.12), channel_id=1, source_target_pairs={{0,4},{4,0},{8,12},{12,8},{16,20},{20,16},{24,28},{28,24},{1,5},{5... | collective-permute-start | bytes 49160 | tf_op jit(solution)/shard_map/ppermute | solution.py:450
  24.6 7.4 %collective-permute-start.12 = (f32[32,128]{1,0:T(8,128)S(1)}, f32[32,128]{1,0:T(8,128)S(1)}, u32[]{:S(2)}, u32[]{:S(2)}) collective-permute-start(f32[32,128]{1,0:T(8,128)S(1)} %add.12.refs_0_), channel_id=1, source_target_pairs={{0,24},{4,28},{8,16},{12,20},{16,8},{20,12},{24,0},{28,4},{1,25},{... | collective-permute-start | bytes 49160 | tf_op jit(solution)/shard_map/ppermute | solution.py:450
  26.4 5.6 %collective-permute-start.11 = (f32[32,128]{1,0:T(8,128)S(1)}, f32[32,128]{1,0:T(8,128)S(1)}, u32[]{:S(2)}, u32[]{:S(2)}) collective-permute-start(f32[32,128]{1,0:T(8,128)S(1)} %add.12.refs_0_), channel_id=1, source_target_pairs={{0,16},{4,20},{8,24},{12,28},{16,0},{20,4},{24,8},{28,12},{1,17},{... | collective-permute-start | bytes 49160 | tf_op jit(solution)/shard_map/ppermute | solution.py:450
  26.9 5.1 %collective-permute-start.10 = (f32[32,128]{1,0:T(8,128)S(1)}, f32[32,128]{1,0:T(8,128)S(1)}, u32[]{:S(2)}, u32[]{:S(2)}) collective-permute-start(f32[32,128]{1,0:T(8,128)S(1)} %add.12.refs_0_), channel_id=1, source_target_pairs={{0,8},{4,12},{8,0},{12,4},{16,24},{20,28},{24,16},{28,20},{1,9},{5... | collective-permute-start | bytes 49160 | tf_op jit(solution)/shard_map/ppermute | solution.py:450
  28.1 4.5 %collective-permute-start.2 = (f32[4,8,640]{2,1,0:T(8,128)S(1)}, f32[4,8,640]{2,1,0:T(8,128)S(1)}, u32[]{:S(2)}, u32[]{:S(2)}) collective-permute-start(f32[4,8,640]{2,1,0:T(8,128)S(1)} %pad_maximum_fusion.1), channel_id=1, source_target_pairs={{0,16},{4,20},{8,24},{12,28},{16,0},{20,4},{24,8},{28,12},{1,17},{... | collective-permute-start | bytes 245768 | tf_op jit(solution)/shard_map/ppermute | solution.py:93
  32.6 7.3 %collective-permute-start.15 = (f32[32,128]{1,0:T(8,128)S(1)}, f32[32,128]{1,0:T(8,128)S(1)}, u32[]{:S(2)}, u32[]{:S(2)}) collective-permute-start(f32[32,128]{1,0:T(8,128)S(1)} %shard_map.135), channel_id=1, source_target_pairs={{0,3},{1,2},{2,1},{3,0},{4,7},{5,6},{6,5},{7,4},{8,11},{9,10},{10,... | collective-permute-start | bytes 49160 | tf_op jit(solution)/shard_map/ppermute | solution.py:450
  35.3 4.6 %collective-permute-start.14 = (f32[32,128]{1,0:T(8,128)S(1)}, f32[32,128]{1,0:T(8,128)S(1)}, u32[]{:S(2)}, u32[]{:S(2)}) collective-permute-start(f32[32,128]{1,0:T(8,128)S(1)} %shard_map.135), channel_id=1, source_target_pairs={{0,2},{1,3},{2,0},{3,1},{4,6},{5,7},{6,4},{7,5},{8,10},{9,11},{10,... | collective-permute-start | bytes 49160 | tf_op jit(solution)/shard_map/ppermute | solution.py:450
  35.3 4.6 %collective-permute-start.13 = (f32[32,128]{1,0:T(8,128)S(1)}, f32[32,128]{1,0:T(8,128)S(1)}, u32[]{:S(2)}, u32[]{:S(2)}) collective-permute-start(f32[32,128]{1,0:T(8,128)S(1)} %shard_map.135), channel_id=1, source_target_pairs={{0,1},{1,0},{2,3},{3,2},{4,5},{5,4},{6,7},{7,6},{8,9},{9,8},{10,11... | collective-permute-start | bytes 49160 | tf_op jit(solution)/shard_map/ppermute | solution.py:450
